TPU v7x, 32 devices: a whole 2x2x4 slice. The times are simulated.
32 devices in a mesh: dp: 2 (over y), tm: 16 (over z, x, core).
Axes of the slice: x: 2, y: 2, z: 4, core: 2. Of those that a mesh axis runs over, the one named last changes fastest.
Arguments:
- signal: bfloat16 [2, 2048, 512], P('dp', 'tm'), may hold values from -6 to 6
- conv_weight: bfloat16 [2, 1024, 512], replicated, may hold values from -0.1875 to 0.1875
- res_weight: bfloat16 [2, 256, 768], replicated, may hold values from -0.375 to 0.375
- grad_out: bfloat16 [2, 2048, 512], P('dp', 'tm'), may hold values from -6 to 6
- skip_cotangent: bfloat16 [2, 2048, 256], P('dp', 'tm'), may hold values from -6 to 6
Outputs:
- input_grad: bfloat16 [2, 2048, 512], P('dp', 'tm')
- conv_grad: bfloat16 [2, 1024, 512], P(None, 'tm')
- res_grad: bfloat16 [2, 256, 768], replicated
All inputs are finite; a program needn't handle non-finite values.
Results may differ from a plain program's by a relative error of at most 0.0063.
Values may be sent and summed in bfloat16 or wider, within the bound.
No kernel may reach another device: no remote copies, remote signals or barrier semaphores. Data moves between devices by JAX's collectives and lax.ppermute only.
A program may use at most 64 MiB of HBM per device.

v0:
```python
import jax
import jax.numpy as jnp
from jax import lax
from jax.sharding import PartitionSpec as P


def passed_along(block, axis, distance):
    devices = range(lax.axis_size(axis))
    route = [(i - distance, i) for i in devices if i - distance in devices]
    return lax.ppermute(block, axis, route)


def gate_gradients(dh, z, gated):
    tf = jnp.tanh(z[:, :gated])
    sg = jax.nn.sigmoid(z[:, gated:])
    return jnp.concatenate([dh * sg * (1.0 - tf * tf), dh * tf * sg * (1.0 - sg)], axis=1).astype(
        jnp.bfloat16
    )


def reduce_conv(cat_rows, dz):
    piece = lax.psum_scatter(
        lax.dot_general(cat_rows, dz, (((0,), (0,)), ((), ())), preferred_element_type=jnp.float32),
        "tm",
        scatter_dimension=0,
        tiled=True,
    )
    return lax.psum(piece, "dp")


def body(signal, conv_weight, res_weight, grad_out, skip_cotangent):
    s_dev, t_dev, width = signal.shape
    gated = res_weight.shape[1]
    near = t_dev // 4
    slabs = lax.axis_size("tm") // 8
    count_rows = s_dev * t_dev
    factor = float(count_rows * lax.axis_size("dp") * lax.axis_size("tm")) ** (-0.5)

    def delayed(x, layer):
        if layer == 0:
            got = passed_along(x[:, t_dev - near :, :], "tm", 1)
            return jnp.concatenate([got, x[:, : t_dev - near, :]], axis=1)
        return passed_along(x, "tm", slabs)

    def shifted_rows(dpast, layer):
        if layer == 0:
            got = passed_along(dpast[:, :near, :], "tm", -1)
            return jnp.concatenate([dpast[:, near:, :], got], axis=1)
        return passed_along(dpast, "tm", -slabs)

    x = signal
    cats = []
    zvals = []
    hvals = []
    for layer in range(2):
        past = delayed(x, layer)
        cat_rows = jnp.concatenate([past, x], axis=2).reshape(count_rows, 2 * width)
        z = jnp.dot(cat_rows, conv_weight[layer], preferred_element_type=jnp.float32)
        h = (jnp.tanh(z[:, :gated]) * jax.nn.sigmoid(z[:, gated:])).astype(jnp.bfloat16)
        cats.append(cat_rows)
        zvals.append(z)
        hvals.append(h)
        if layer == 0:
            resid = jnp.dot(h, res_weight[0][:, :width], preferred_element_type=jnp.float32)
            x = (
                (x.reshape(count_rows, width).astype(jnp.float32) + resid)
                .astype(jnp.bfloat16)
                .reshape(s_dev, t_dev, width)
            )
    grad = grad_out.reshape(count_rows, width).astype(jnp.float32)
    skip_rows = skip_cotangent.reshape(count_rows, -1)
    conv_parts = [None, None]
    res_parts = [None, None]
    dz_kept = [None, None]
    for layer in (1, 0):
        outer = jnp.concatenate([grad.astype(jnp.bfloat16), skip_rows], axis=1)
        dh = lax.dot_general(
            outer, res_weight[layer], (((1,), (1,)), ((), ())), preferred_element_type=jnp.float32
        )
        dz = gate_gradients(dh, zvals[layer], gated)
        wcat = lax.dot_general(
            dz, conv_weight[layer], (((1,), (1,)), ((), ())), preferred_element_type=jnp.float32
        )
        dpast = wcat[:, :width].astype(jnp.bfloat16).reshape(s_dev, t_dev, width)
        moved = shifted_rows(dpast, layer).reshape(count_rows, width)
        grad = grad + wcat[:, width:] + moved.astype(jnp.float32)
        res_local = lax.dot_general(
            hvals[layer], outer, (((0,), (0,)), ((), ())), preferred_element_type=jnp.float32
        )
        dz_kept[layer] = dz
        res_parts[layer] = res_local
    for layer in range(2):
        conv_parts[layer] = reduce_conv(cats[layer], dz_kept[layer])
    res_total = lax.psum(jnp.stack(res_parts), ("dp", "tm"))
    input_grad = grad.astype(jnp.bfloat16).reshape(s_dev, t_dev, width)
    conv_grad = (jnp.stack(conv_parts) * factor).astype(jnp.bfloat16)
    res_grad = (res_total * factor).astype(jnp.bfloat16)
    return (input_grad, conv_grad, res_grad)


def solution(mesh):
    in_specs = (P("dp", "tm", None), P(), P(), P("dp", "tm", None), P("dp", "tm", None))
    out_specs = (P("dp", "tm", None), P(None, "tm", None), P())
    return jax.shard_map(body, mesh=mesh, in_specs=in_specs, out_specs=out_specs, check_vma=False)
```

profile of v0, /device:TPU:0, one launch (start us, length us, event | category | flops | bytes accessed | tf_op | source)
XLA Modules:
  0.0 216.7 jit_solution(6797605330487345108)
XLA Ops:
  8.1 0.9 slice.61
  9.0 2.3 %collective-permute-start = (bf16[1,32,512]{2,1,0:T(8,128)(2,1)S(1)}, bf16[1,32,512]{2,1,0:T(8,128)(2,1)S(1)}, u32[]{:S(2)}, u32[]{:S(2)}) collective-permute-start(bf16[1,32,512]{2,1,0:T(8,128)(2,1)S(1)} %slice.61), channel_id=1, source_target_pairs={{0,1},{1,2},{2,3},{3,4},{4,5},{5,6},{6,7},{7,8},{8,9},{9,10},{10,1... | collective-permute-start | bytes 98312 | tf_op jit(solution)/shard_map/ppermute | solution.py:10
  11.3 1.0 slice_bitcast_fusion
  12.4 0.9 slice.62
  13.3 1.7 fusion.8
  15.0 0.1 multiply_convert_fusion.6
  15.1 0.2 fusion.1
  15.3 5.7 %collective-permute-start.1 = (bf16[1,128,512]{2,1,0:T(8,128)(2,1)S(1)}, bf16[1,128,512]{2,1,0:T(8,128)(2,1)S(1)}, u32[]{:S(2)}, u32[]{:S(2)}) collective-permute-start(bf16[1,128,512]{2,1,0:T(8,128)(2,1)S(1)} %fusion.1), channel_id=1, source_target_pairs={{0,2},{1,3},{2,4},{3,5},{4,6},{5,7},{6,8},{7,9},{8,10},{9,11},{10,... | collective-permute-start | bytes 393224 | tf_op jit(solution)/shard_map/ppermute | solution.py:10
  21.0 3.3 %collective-permute-done.1 = bf16[1,128,512]{2,1,0:T(8,128)(2,1)S(1)} collective-permute-done((bf16[1,128,512]{2,1,0:T(8,128)(2,1)S(1)}, bf16[1,128,512]{2,1,0:T(8,128)(2,1)S(1)}, u32[]{:S(2)}, u32[]{:S(2)}) %collective-permute-start.1) | collective-permute-done | bytes 131104 | tf_op jit(solution)/shard_map/ppermute | solution.py:10
  24.2 0.3 fusion.4
  24.6 0.3 multiply_convert_fusion.5
  24.9 0.3 copy-done.6
  25.2 1.8 fusion.22
  27.1 0.5 fusion.2
  27.6 1.3 collective-permute-start.2
  28.9 6.3 %collective-permute-done.2 = bf16[1,128,512]{2,1,0:T(8,128)(2,1)S(1)} collective-permute-done((bf16[1,128,512]{2,1,0:T(8,128)(2,1)S(1)}, bf16[1,128,512]{2,1,0:T(8,128)(2,1)S(1)}, u32[]{:S(2)}, u32[]{:S(2)}) %collective-permute-start.2) | collective-permute-done | bytes 131104 | tf_op jit(solution)/shard_map/ppermute | solution.py:10
  35.3 1.4 multiply_convert_fusion.3
  36.7 1.8 fusion.33
  38.5 0.0 all-reduce.4.cloned.1.call-start
  38.6 1.3 convolution_bitcast_fusion
  39.9 0.3 convolution_bitcast_fusion.1
  40.2 1.3 pad_maximum_fusion
  41.5 0.5 fusion.6
  42.0 1.3 collective-permute-start.3
  43.3 1.8 collective-permute-done.3
  45.1 0.7 fusion.24
  45.9 45.6 %reduce-scatter.5.cloned.1.call-done = f32[64,512]{1,0:T(8,128)} async-done(((f32[1024,512]{1,0:T(8,128)}), f32[64,512]{1,0:T(8,128)}) %reduce-scatter.5.cloned.1.call-update) | async-done | bytes 131088 | tf_op jit(solution)/shard_map/reduce_scatter | solution.py:22
  91.4 64.8 %reduce-scatter.3.cloned.1.call-done = f32[64,512]{1,0:T(8,128)} async-done(((f32[1024,512]{1,0:T(8,128)}), f32[64,512]{1,0:T(8,128)}) %reduce-scatter.3.cloned.1.call-update) | async-done | bytes 131088 | tf_op jit(solution)/shard_map/reduce_scatter | solution.py:22
  156.3 27.4 %all-reduce.4.cloned.1.call-done = f32[2,256,768]{2,1,0:T(8,128)} async-done(((f32[2,256,768]{2,1,0:T(8,128)}), f32[2,256,768]{2,1,0:T(8,128)}) %all-reduce.4.cloned.1.call-update) | async-done | bytes 1572880 | tf_op jit(solution)/shard_map/psum | solution.py:94
  183.7 2.4 %multiply_convert_fusion = bf16[2,256,768]{2,1,0:T(8,128)(2,1)} fusion(f32[2,256,768]{2,1,0:T(8,128)} %all-reduce.4.cloned.1.call-done), kind=kLoop, calls=%fused_computation.1 | loop fusion | flops 786432 | bytes 2359296 | tf_op jit(solution)/shard_map/convert_element_type | solution.py:97
  186.1 21.5 %all-reduce.6.cloned.1.call-done = (f32[1,64,512]{2,1,0:T(8,128)}, f32[1,64,512]{2,1,0:T(8,128)}) async-done(((f32[1,64,512]{2,1,0:T(8,128)}, f32[1,64,512]{2,1,0:T(8,128)}), (f32[1,64,512]{2,1,0:T(8,128)}, f32[1,64,512]{2,1,0:T(8,128)})) %all-reduce.6.cloned.1.call-update) | async-done | bytes 262160 | tf_op jit(solution)/shard_map/psum | solution.py:28
  207.6 1.6 fusion.21
  (26 shorter events, 0.3 us)
Async XLA Ops:
  8.0 7.1 %copy-start.1 = (bf16[1,128,512]{2,1,0:T(8,128)(2,1)S(1)}, bf16[1,128,512]{2,1,0:T(8,128)(2,1)}, u32[]{:S(2)}) copy-start(bf16[1,128,512]{2,1,0:T(8,128)(2,1)} %param.5) | copy-start | bytes 393220
  8.0 16.2 %copy-start = (bf16[2,1024,512]{2,1,0:T(8,128)(2,1)S(1)}, bf16[2,1024,512]{2,1,0:T(8,128)(2,1)}, u32[]{:S(2)}) copy-start(bf16[2,1024,512]{2,1,0:T(8,128)(2,1)} %param.6) | copy-start | bytes 6291460
  8.0 83.4 %reduce-scatter.5.cloned.1.call-start = ((), (), s32[]{:S(2)}) async-start(), calls=%async_computation.3 | async-start | bytes 2228224 | tf_op jit(solution)/shard_map/reduce_scatter | solution.py:22
  9.0 4.3 %collective-permute-start = (bf16[1,32,512]{2,1,0:T(8,128)(2,1)S(1)}, bf16[1,32,512]{2,1,0:T(8,128)(2,1)S(1)}, u32[]{:S(2)}, u32[]{:S(2)}) collective-permute-start(bf16[1,32,512]{2,1,0:T(8,128)(2,1)S(1)} %slice.61), channel_id=1, source_target_pairs={{0,1},{1,2},{2,3},{3,4},{4,5},{5,6},{6,7},{7,8},{8,9},{9,10},{10,1... | collective-permute-start | bytes 98312 | tf_op jit(solution)/shard_map/ppermute | solution.py:10
  13.3 11.3 %copy-start.2 = (bf16[1,128,512]{2,1,0:T(8,128)(2,1)S(1)}, bf16[1,128,512]{2,1,0:T(8,128)(2,1)}, u32[]{:S(2)}) copy-start(bf16[1,128,512]{2,1,0:T(8,128)(2,1)} %param.8) | copy-start | bytes 393220
  13.3 11.3 %copy-start.3 = (bf16[1,128,256]{2,1,0:T(8,128)(2,1)S(1)}, bf16[1,128,256]{2,1,0:T(8,128)(2,1)}, u32[]{:S(2)}) copy-start(bf16[1,128,256]{2,1,0:T(8,128)(2,1)} %param.9) | copy-start | bytes 196612
  13.3 11.3 %copy-start.5 = (bf16[2,256,768]{2,1,0:T(8,128)(2,1)S(1)}, bf16[2,256,768]{2,1,0:T(8,128)(2,1)}, u32[]{:S(2)}) copy-start(bf16[2,256,768]{2,1,0:T(8,128)(2,1)} %param.7) | copy-start | bytes 2359300
  15.0 9.9 %copy-start.4 = (f32[128,512]{1,0:T(8,128)}, f32[128,512]{1,0:T(8,128)S(1)}, u32[]{:S(2)}) copy-start(f32[128,512]{1,0:T(8,128)S(1)} %fusion.8) | copy-start | bytes 786436
  15.3 9.0 %collective-permute-start.1 = (bf16[1,128,512]{2,1,0:T(8,128)(2,1)S(1)}, bf16[1,128,512]{2,1,0:T(8,128)(2,1)S(1)}, u32[]{:S(2)}, u32[]{:S(2)}) collective-permute-start(bf16[1,128,512]{2,1,0:T(8,128)(2,1)S(1)} %fusion.1), channel_id=1, source_target_pairs={{0,2},{1,3},{2,4},{3,5},{4,6},{5,7},{6,8},{7,9},{8,10},{9,11},{10,... | collective-permute-start | bytes 393224 | tf_op jit(solution)/shard_map/ppermute | solution.py:10
  24.5 0.7 copy-start.6
  27.1 129.2 %reduce-scatter.3.cloned.1.call-start = ((), (), s32[]{:S(2)}) async-start(), calls=%async_computation.2 | async-start | bytes 2228224 | tf_op jit(solution)/shard_map/reduce_scatter | solution.py:22
  27.6 7.6 %collective-permute-start.2 = (bf16[1,128,512]{2,1,0:T(8,128)(2,1)S(1)}, bf16[1,128,512]{2,1,0:T(8,128)(2,1)S(1)}, u32[]{:S(2)}, u32[]{:S(2)}) collective-permute-start(bf16[1,128,512]{2,1,0:T(8,128)(2,1)S(1)} %fusion.23), channel_id=1, source_target_pairs={{2,0},{3,1},{4,2},{5,3},{6,4},{7,5},{8,6},{9,7},{10,8},{11,9},{12,... | collective-permute-start | bytes 393224 | tf_op jit(solution)/shard_map/ppermute | solution.py:10
  38.5 145.2 %all-reduce.4.cloned.1.call-start = ((), (), s32[]{:S(2)}) async-start(), calls=%async_computation.4 | async-start | bytes 3145728 | tf_op jit(solution)/shard_map/psum | solution.py:94
  41.5 166.1 %all-reduce.6.cloned.1.call-start = ((), (), s32[]{:S(2)}) async-start(), calls=%async_computation.5 | async-start | bytes 524288 | tf_op jit(solution)/shard_map/psum | solution.py:28
  42.0 3.1 %collective-permute-start.3 = (bf16[1,32,512]{2,1,0:T(8,128)(2,1)S(1)}, bf16[1,32,512]{2,1,0:T(8,128)(2,1)S(1)}, u32[]{:S(2)}, u32[]{:S(2)}) collective-permute-start(bf16[1,32,512]{2,1,0:T(8,128)(2,1)S(1)} %slice.87), channel_id=1, source_target_pairs={{1,0},{2,1},{3,2},{4,3},{5,4},{6,5},{7,6},{8,7},{9,8},{10,9},{11,1... | collective-permute-start | bytes 98312 | tf_op jit(solution)/shard_map/ppermute | solution.py:10
Sparse Core Ops, SparseCore 0:
  27.2 64.2 reduce-scatter.4
  95.6 60.5 reduce-scatter.2
Sparse Core Ops, SparseCore 1:
  44.3 139.4 all-reduce.3
  185.9 21.6 all-reduce.5
where the time goes:
time: 217 us
  waiting for transfers between devices  171 us (79%)
  between operations  15.7 us (7%)
  starting transfers between devices  10.8 us (5%)
  matrix products  9.99 us (5%)
  other arithmetic  6.16 us (3%)
  local copies, waits for them, and re-layouts  3.26 us (2%)
    reduce_scatter x2, waiting for transfers between devices, reduce_conv(): lax.psum_scatter(lax.dot_general(cat_rows, dz, (((0,), (0,)), ((), ())),...  110 us
    psum x1, waiting for transfers between devices, body(): res_total = lax.psum(jnp.stack(res_parts), ('dp', 'tm'))  27.4 us
    psum x1, waiting for transfers between devices, reduce_conv(): return lax.psum(piece, 'dp')  21.5 us
    ppermute x4, waiting for transfers between devices, passed_along(): return lax.ppermute(block, axis, route)  11.4 us
    ppermute x4, starting transfers between devices, passed_along(): return lax.ppermute(block, axis, route)  10.6 us
  transfers between devices with their start and end apart: 8, of which 7 were waited for; matrix products, arithmetic and copies ran while one was open for 6% of the time, Pallas kernels for 0%

commit v1 on v0

v1 whole, which is shorter than its diff:
```python
import functools

import jax
import jax.numpy as jnp
from jax import lax
from jax.experimental import pallas as pl
from jax.experimental.pallas import tpu as pltpu
from jax.sharding import PartitionSpec as P

F32 = jnp.float32
BF16 = jnp.bfloat16
VMEM_LIMIT = 48 * 1024 * 1024


def mm(a, b):
    return jnp.dot(a, b, preferred_element_type=F32)


def mm_nt(a, b):
    return lax.dot_general(a, b, (((1,), (1,)), ((), ())), preferred_element_type=F32)


def mm_tn(a, b):
    return lax.dot_general(a, b, (((0,), (0,)), ((), ())), preferred_element_type=F32)


def call(kernel, outs, *args, scratch=(), flops=0, nbytes=0, name=None):
    return pl.pallas_call(
        kernel,
        out_shape=outs,
        in_specs=[pl.BlockSpec(memory_space=pltpu.VMEM)] * len(args),
        out_specs=[pl.BlockSpec(memory_space=pltpu.VMEM)] * len(outs),
        scratch_shapes=list(scratch),
        compiler_params=pltpu.CompilerParams(vmem_limit_bytes=VMEM_LIMIT),
        cost_estimate=pl.CostEstimate(flops=flops, bytes_accessed=nbytes, transcendentals=0),
        name=name,
    )(*args)


def shaped(shape, dtype=BF16):
    return jax.ShapeDtypeStruct(shape, dtype)


def place_conv(dst, part, base, groups, rows):
    per = part.shape[0] // rows
    for block in range(per):
        index = base + block
        g, x, c = index // 4, (index // 2) % 2, index % 2
        dst[c, x, g, 0:rows, :] = part[block * rows : (block + 1) * rows, :].astype(BF16)


def place_res(dst, part, which, groups, conv_rows, piece_rows):
    quarter = part.shape[0] // 4
    for c in range(2):
        for x in range(2):
            for block in range(quarter // 16):
                row = which * quarter + block * 16
                g, off = row // piece_rows, row % piece_rows
                src = (2 * c + x) * quarter + block * 16
                dst[c, x, g, conv_rows + off : conv_rows + off + 16, :] = part[src : src + 16, :].astype(BF16)


def forward_and_outer_kernel(
    groups, conv_rows, piece_rows,
    sig, near_in, far, far_near, cw, rw, grad, skip,
    send, keep, a_out, b_out, o_out, ga_out, x0_out, p0_out,
    staged,
):
    t, width = sig.shape
    near = near_in.shape[0]
    gated = rw.shape[1]
    core = lax.rem(lax.axis_index("tm"), 2)
    x0 = jnp.concatenate([sig[...], far[...]], axis=0)
    p0 = jnp.concatenate([near_in[...], sig[0 : t - near, :], far_near[...], far[0 : t - near, :]], axis=0)
    x0_out[...] = x0
    p0_out[...] = p0
    z0 = mm(p0, cw[0, 0:width, :]) + mm(x0, cw[0, width:, :])
    tf = jnp.tanh(z0[:, :gated])
    sg = jax.nn.sigmoid(z0[:, gated:])
    h0 = (tf * sg).astype(BF16)
    a_out[...] = sg * (1.0 - tf * tf)
    b_out[...] = tf * sg * (1.0 - sg)
    x1 = (x0.astype(F32) + mm(h0, rw[0, :, 0:width])).astype(BF16)
    z1 = mm(x1[t:, :], cw[1, 0:width, :]) + mm(x1[:t, :], cw[1, width:, :])
    tf = jnp.tanh(z1[:, :gated])
    sg = jax.nn.sigmoid(z1[:, gated:])
    h1 = (tf * sg).astype(BF16)
    g2 = grad[...]
    sk = skip[...]
    e1 = mm_nt(g2, rw[1, :, 0:width]) + mm_nt(sk, rw[1, :, width:])
    dz1 = jnp.concatenate([e1 * sg * (1.0 - tf * tf), e1 * tf * sg * (1.0 - sg)], axis=1).astype(BF16)
    half = width // conv_rows
    place_conv(staged, mm_tn(x1[t:, :], dz1), 0, groups, conv_rows)
    place_conv(staged, mm_tn(x1[:t, :], dz1), half, groups, conv_rows)
    dpast = mm_nt(dz1, cw[1, 0:width, :]).astype(BF16)
    ga = g2.astype(F32) + mm_nt(dz1, cw[1, width:, :])
    ga_out[...] = ga
    outer = jnp.concatenate([ga.astype(BF16), dpast], axis=0)
    o_out[...] = outer
    if groups * piece_rows > 3 * gated // 4:
        staged[:, :, :, conv_rows:, :] = jnp.zeros((2, 2, groups, piece_rows, width), BF16)
    place_res(staged, mm_tn(h1, g2), 0, groups, conv_rows, piece_rows)
    place_res(staged, mm_tn(h0, outer), 1, groups, conv_rows, piece_rows)
    skips = jnp.concatenate([mm_tn(h1, sk), mm_tn(h0[:t, :], sk)], axis=1)
    place_res(staged, skips, 2, groups, conv_rows, piece_rows)
    send[...] = staged[1 - core]
    keep[...] = staged[core]


def inner_kernel(
    groups, conv_rows, near,
    x0, p0, a, b, outer, ga, cw, rw, skip,
    send, keep, own_out, back_out, edge_out,
    staged,
):
    t = skip.shape[0]
    width = x0.shape[1]
    core = lax.rem(lax.axis_index("tm"), 2)
    e0 = mm_nt(outer[...], rw[0, :, 0:width])
    es = mm_nt(skip[...], rw[0, :, width:])
    e0 = jnp.concatenate([e0[:t, :] + es, e0[t:, :]], axis=0)
    dz0 = jnp.concatenate([e0 * a[...], e0 * b[...]], axis=1).astype(BF16)
    half = width // conv_rows
    place_conv(staged, mm_tn(p0[...], dz0), 0, groups, conv_rows)
    place_conv(staged, mm_tn(x0[...], dz0), half, groups, conv_rows)
    send[...] = staged[1 - core]
    keep[...] = staged[core]
    wp = mm_nt(dz0, cw[0, 0:width, :]).astype(BF16)
    wx = mm_nt(dz0, cw[0, width:, :])
    zero = jnp.zeros((near, width), F32)
    own_out[...] = ga[...] + wx[:t, :] + jnp.concatenate([wp[near:t, :].astype(F32), zero], axis=0)
    back_out[...] = (
        outer[t:, :].astype(F32) + wx[t:, :] + jnp.concatenate([wp[t + near :, :].astype(F32), zero], axis=0)
    ).astype(BF16)
    edge_out[...] = jnp.concatenate([wp[0:near, :], wp[t : t + near, :]], axis=0)


def add_core_kernel(got, kept, send, keep, staged):
    xbit = lax.rem(lax.axis_index("tm") // 2, 2)
    staged[...] = (got[...].astype(F32) + kept[...].astype(F32)).astype(BF16)
    send[...] = staged[1 - xbit]
    keep[...] = staged[xbit]


def add_x_kernel(groups, got, kept, *rest):
    outs, staged = rest[:-1], rest[-1]
    g = lax.axis_index("tm") // 4
    staged[...] = (got[...].astype(F32) + kept[...].astype(F32)).astype(BF16)
    for k in range(groups):
        outs[k][...] = staged[lax.bitwise_xor(g, k)]


def sum_kernel(*refs):
    out = refs[-1]
    total = refs[0][...].astype(F32)
    for ref in refs[1:-1]:
        total = total + ref[...].astype(F32)
    out[...] = total.astype(BF16)


def finish_kernel(factor, conv_rows, n_terms, *refs):
    total = refs[0][...].astype(F32)
    for ref in refs[1:n_terms]:
        total = total + ref[...].astype(F32)
    total = (total * factor).astype(BF16)
    refs[n_terms][...] = total[:conv_rows, :]
    for ref in refs[n_terms + 1 :]:
        ref[...] = total[conv_rows:, :]


def swap(x, distance, size):
    return lax.ppermute(x, "tm", [(i, i ^ distance) for i in range(size)])


def shift(x, distance, size):
    return lax.ppermute(x, "tm", [(i, i + distance) for i in range(size) if 0 <= i + distance < size])


def body(signal, conv_weight, res_weight, grad_out, skip_cotangent):
    s_dev, t, width = signal.shape
    gated = res_weight.shape[1]
    near = t // 4
    tm, dp = lax.axis_size("tm"), lax.axis_size("dp")
    slabs, groups = tm // 8, tm // 4
    rows = 2 * width // tm
    res_quarter = 3 * gated // 4
    piece = -(-res_quarter // groups // 16) * 16
    factor = float(s_dev * t * dp * tm) ** (-0.5)

    sig = signal[0]
    grad = grad_out[0]
    skip = skip_cotangent[0]
    tail = sig[t - near :, :]
    far = shift(sig, slabs, tm)
    near_in = shift(tail, 1, tm)
    far_near = shift(tail, slabs + 1, tm)

    deep = rows + piece
    send1, keep1, a, b, outer, ga, x0, p0 = call(
        functools.partial(forward_and_outer_kernel, groups, rows, piece),
        [
            shaped((2, groups, deep, width)), shaped((2, groups, deep, width)),
            shaped((2 * t, gated), F32), shaped((2 * t, gated), F32),
            shaped((2 * t, width)), shaped((t, width), F32),
            shaped((2 * t, width)), shaped((2 * t, width)),
        ],
        sig, near_in, far, far_near, conv_weight, res_weight, grad, skip,
        scratch=[pltpu.VMEM((2, 2, groups, deep, width), BF16)],
        flops=1_300_000_000, nbytes=8_000_000, name="forward_and_outer",
    )
    got1 = swap(send1, 1, tm)
    send0, keep0, own, back, edge = call(
        functools.partial(inner_kernel, groups, rows, near),
        [
            shaped((2, groups, rows, width)), shaped((2, groups, rows, width)),
            shaped((t, width), F32), shaped((t, width)), shaped((2 * near, width)),
        ],
        x0, p0, a, b, outer, ga, conv_weight, res_weight, skip,
        scratch=[pltpu.VMEM((2, 2, groups, rows, width), BF16)],
        flops=1_000_000_000, nbytes=6_000_000, name="inner",
    )
    got0 = swap(send0, 1, tm)

    def reduced(got, kept, depth):
        quarter = (groups, depth, width)
        send, keep = call(
            add_core_kernel, [shaped(quarter)] * 2, got, kept,
            scratch=[pltpu.VMEM((2,) + quarter, BF16)], nbytes=2_000_000, name="add_core",
        )
        got = swap(send, 2, tm)
        pieces = call(
            functools.partial(add_x_kernel, groups), [shaped((depth, width))] * groups, got, keep,
            scratch=[pltpu.VMEM(quarter, BF16)], nbytes=1_000_000, name="add_x",
        )
        terms = [pieces[0]] + [swap(pieces[k], 4 * k, tm) for k in range(1, groups)]
        (total,) = call(sum_kernel, [shaped((depth, width))], *terms, nbytes=500_000, name="add_z")
        others = [
            lax.ppermute(total, "dp", [(i, (i + k) % dp) for i in range(dp)]) for k in range(1, dp)
        ]
        return [total] + others

    sums1 = reduced(got1, keep1, deep)
    sums0 = reduced(got0, keep0, rows)
    conv1, res = call(
        functools.partial(finish_kernel, factor, rows, dp), [shaped((rows, width)), shaped((piece, width))],
        *sums1, nbytes=300_000, name="finish_outer",
    )
    (conv0,) = call(
        functools.partial(finish_kernel, factor, rows, dp), [shaped((rows, width))],
        *sums0, nbytes=300_000, name="finish_inner",
    )
    conv_grad = jnp.stack([conv0, conv1])

    g = lax.axis_index("tm") // 4
    got = jnp.stack([res] + [swap(res, 4 * k, tm) for k in range(1, groups)])
    quarter = got[jnp.bitwise_xor(jnp.arange(groups), g)].reshape(groups * piece, width)[:res_quarter]
    xbit = (lax.axis_index("tm") // 2) % 2
    other = swap(quarter, 2, tm)
    pair = jnp.where(xbit == 0, jnp.stack([quarter, other]), jnp.stack([other, quarter]))
    core = lax.axis_index("tm") % 2
    other = swap(pair, 1, tm)
    both = jnp.where(core == 0, jnp.stack([pair, other]), jnp.stack([other, pair]))
    sets = both.reshape(4, 3, gated // 4, width).transpose(1, 0, 2, 3).reshape(3, gated, width)
    sk = width // 2
    res_grad = jnp.stack([
        jnp.concatenate([sets[1], sets[2][:, sk:]], axis=1),
        jnp.concatenate([sets[0], sets[2][:, :sk]], axis=1),
    ])

    edges = shift(edge, -1, tm)
    back_tail = back[t - near :, :].astype(F32) + edges[near:, :].astype(F32)
    back = jnp.concatenate([back[: t - near, :], back_tail.astype(BF16)], axis=0)
    come = shift(back, -slabs, tm)
    first = own[: t - near, :] + come[: t - near, :].astype(F32)
    last = own[t - near :, :] + come[t - near :, :].astype(F32) + edges[:near, :].astype(F32)
    input_grad = jnp.concatenate([first, last], axis=0).astype(BF16).reshape(s_dev, t, width)
    return (input_grad, conv_grad, res_grad)


def solution(mesh):
    in_specs = (P("dp", "tm", None), P(), P(), P("dp", "tm", None), P("dp", "tm", None))
    out_specs = (P("dp", "tm", None), P(None, "tm", None), P())
    return jax.shard_map(body, mesh=mesh, in_specs=in_specs, out_specs=out_specs, check_vma=False)
```

time: 217 us -> 90.8 us (0.42)
  waiting for transfers between devices: 171 us -> 28.4 us
  starting transfers between devices: 10.8 us -> 34.6 us
  between operations: 15.7 us -> 0.97 us
  matrix products: 9.99 us -> 0 us
  local copies, waits for them, and re-layouts: 3.26 us -> 12.5 us
  Pallas kernels: 0 us -> 9.22 us
    reduce_scatter x2 -> x0, waiting for transfers between devices: 110 us -> none  [reduce_conv(): lax.psum_scatter(lax.dot_general(cat_rows, dz, (((0,), (0,)), ((), ())),...]
    psum x2 -> x0, waiting for transfers between devices: 48.9 us -> none  [the longest x1 27.4 us: body(): res_total = lax.psum(jnp.stack(res_parts), ('dp', 'tm'))]
    ppermute x4 -> x22, starting transfers between devices: 10.6 us -> 34.6 us  [the longest x15 17.5 us: swap(): return lax.ppermute(x, 'tm', [(i, i ^ distance) for i in range(size)])]
    ppermute x4 -> x22, waiting for transfers between devices: 11.4 us -> 28.4 us  [the longest x15 22.7 us: swap(): return lax.ppermute(x, 'tm', [(i, i ^ distance) for i in range(size)])]
    unnamed x14 -> x44, local copies, waits for them, and re-layouts: 0.37 us -> 11 us
    dot_general x11 -> x0, matrix products: 9.99 us -> none  [the longest x2 3.57 us: reduce_conv(): lax.dot_general(cat_rows, dz, (((0,), (0,)), ((), ())), preferred_element...]
    pallas_call x0 -> x10, Pallas kernels: none -> 9.22 us  [call(): pl.pallas_call(kernel, out_shape=outs, in_specs=[pl.BlockSpec(memory_spac...]
    convert_element_type x4 -> x1, other arithmetic: 4.14 us -> 0.01 us  [body(): back = jnp.concatenate([back[:t - near, :], back_tail.astype(BF16)], axis=0)]
  transfers between devices with their start and end apart: 8 -> 22, of which waited for: 7 -> 13; matrix products, arithmetic and copies ran while one was open for 6% -> 5% of each run, Pallas kernels for 0% -> 4%
where the time goes in v1:
time: 90.8 us; the launch traced here: 90.1 us
  starting transfers between devices  34.6 us (38%)
  waiting for transfers between devices  28.4 us (31%)
  local copies, waits for them, and re-layouts  12.5 us (14%)
  Pallas kernels  9.22 us (10%)
  other arithmetic  4.43 us (5%)
  between operations  0.97 us (1%)
    ppermute x15, waiting for transfers between devices, swap(): return lax.ppermute(x, 'tm', [(i, i ^ distance) for i in range(size)])  22.7 us
    ppermute x15, starting transfers between devices, swap(): return lax.ppermute(x, 'tm', [(i, i ^ distance) for i in range(size)])  17.5 us
    ppermute x5, starting transfers between devices, shift(): lax.ppermute(x, 'tm', [(i, i + distance) for i in range(size) if 0 <= i +...  14 us
    unnamed x44, local copies, waits for them, and re-layouts  11 us
    pallas_call x10, Pallas kernels, call(): pl.pallas_call(kernel, out_shape=outs, in_specs=[pl.BlockSpec(memory_spac...  9.22 us
    ppermute x2, waiting for transfers between devices, reduced(): lax.ppermute(total, 'dp', [(i, (i + k) % dp) for i in range(dp)])  4.09 us
    ppermute x2, starting transfers between devices, reduced(): lax.ppermute(total, 'dp', [(i, (i + k) % dp) for i in range(dp)])  3.12 us
    concatenate x3, other arithmetic, body(): jnp.concatenate([first, last], axis=0).astype(BF16).reshape(s_dev, t, width)  2.47 us
  transfers between devices with their start and end apart: 22, of which 13 were waited for; matrix products, arithmetic and copies ran while one was open for 5% of the time, Pallas kernels for 4%

profile of v1, /device:TPU:0, one launch (start us, length us, event | category | flops | bytes accessed | tf_op | source)
XLA Modules:
  0.0 90.1 jit_solution(9294723942585038111)
XLA Ops:
  0.6 4.9 %collective-permute-start.1 = (bf16[128,512]{1,0:T(8,128)(2,1)}, bf16[128,512]{1,0:T(8,128)(2,1)S(1)}, u32[]{:S(2)}, u32[]{:S(2)}) collective-permute-start(bf16[128,512]{1,0:T(8,128)(2,1)} %bitcast.39), channel_id=1, source_target_pairs={{0,2},{1,3},{2,4},{3,5},{4,6},{5,7},{6,8},{7,9},{8,10},{9,11},{10,... | collective-permute-start | bytes 393224 | tf_op jit(solution)/shard_map/ppermute | solution.py:176
  6.3 1.4 %collective-permute-start = (bf16[32,512]{1,0:T(8,128)(2,1)S(1)}, bf16[32,512]{1,0:T(8,128)(2,1)S(1)}, u32[]{:S(2)}, u32[]{:S(2)}) collective-permute-start(bf16[32,512]{1,0:T(8,128)(2,1)S(1)} %slice_bitcast_fusion), channel_id=1, source_target_pairs={{0,1},{1,2},{2,3},{3,4},{4,5},{5,6},{6,7},{7,8},{8,9},{9,10},{10,1... | collective-permute-start | bytes 98312 | tf_op jit(solution)/shard_map/ppermute | solution.py:176
  7.7 5.1 %collective-permute-start.2 = (bf16[32,512]{1,0:T(8,128)(2,1)S(1)}, bf16[32,512]{1,0:T(8,128)(2,1)S(1)}, u32[]{:S(2)}, u32[]{:S(2)}) collective-permute-start(bf16[32,512]{1,0:T(8,128)(2,1)S(1)} %slice_bitcast_fusion), channel_id=1, source_target_pairs={{0,3},{1,4},{2,5},{3,6},{4,7},{5,8},{6,9},{7,10},{8,11},{9,12},{10... | collective-permute-start | bytes 98312 | tf_op jit(solution)/shard_map/ppermute | solution.py:176
  12.8 1.6 %collective-permute-done.2.far_near = bf16[32,512]{1,0:T(8,128)(2,1)S(1)} collective-permute-done((bf16[32,512]{1,0:T(8,128)(2,1)S(1)}, bf16[32,512]{1,0:T(8,128)(2,1)S(1)}, u32[]{:S(2)}, u32[]{:S(2)}) %collective-permute-start.2) | collective-permute-done | bytes 32800 | tf_op jit(solution)/shard_map/ppermute | solution.py:176
  14.4 1.1 %copy-done.1 = bf16[2,256,768]{2,1,0:T(8,128)(2,1)S(1)} copy-done((bf16[2,256,768]{2,1,0:T(8,128)(2,1)S(1)}, bf16[2,256,768]{2,1,0:T(8,128)(2,1)}, u32[]{:S(2)}) %copy-start.1) | copy-done | bytes 786456
  18.2 4.1 %forward_and_outer.1 = (bf16[2,4,112,512]{3,2,1,0:T(8,128)(2,1)S(1)}, bf16[2,4,112,512]{3,2,1,0:T(8,128)(2,1)S(1)}, f32[256,256]{1,0:T(8,128)S(1)}, f32[256,256]...) custom-call(bf16[128,512]{1,0:T(8,128)(2,1)S(1)} %bitcast.40, ...), custom_call_target="tpu_custom_call" | custom-call | flops 1300000000 | bytes 8000000 | tf_op jit(solution)/shard_map/forward_and_outer/pallas_call | solution.py:28
  23.2 2.5 %collective-permute-done.11.got = bf16[2,4,112,512]{3,2,1,0:T(8,128)(2,1)S(1)} collective-permute-done((bf16[2,4,112,512]{3,2,1,0:T(8,128)(2,1)S(1)}, bf16[2,4,112,512]{3,2,1,0:T(8,128)(2,1)S(1)}, u32[]{:S(2)}, u32[]{:S(2)}) %collective-permute-start.11) | collective-permute-done | bytes 917536 | tf_op jit(solution)/shard_map/ppermute | solution.py:172
  25.6 1.3 %add_core.3 = (bf16[4,112,512]{2,1,0:T(8,128)(2,1)}, bf16[4,112,512]{2,1,0:T(8,128)(2,1)S(1)}) custom-call(bf16[2,4,112,512]{3,2,1,0:T(8,128)(2,1)S(1)} %collective-permute-done.11.got, bf16[2,4,112,512]{3,2,1,0:T(8,128)(2,1)S(1)} %get-tuple-element.48.kept), custom_call_target="tpu_custom_call" | custom-call | bytes 2000000 | tf_op jit(solution)/shard_map/add_core/pallas_call | solution.py:28
  27.7 1.8 %collective-permute-start.12 = (bf16[4,112,512]{2,1,0:T(8,128)(2,1)}, bf16[4,112,512]{2,1,0:T(8,128)(2,1)}, u32[]{:S(2)}, u32[]{:S(2)}) collective-permute-start(bf16[4,112,512]{2,1,0:T(8,128)(2,1)} %get-tuple-element.49), channel_id=1, source_target_pairs={{0,2},{1,3},{2,0},{3,1},{4,6},{5,7},{6,4},{7,5},{8,10},{9,11},{10,... | collective-permute-start | bytes 1376264 | tf_op jit(solution)/shard_map/ppermute | solution.py:172
  35.2 1.9 %inner.1 = (bf16[2,4,64,512]{3,2,1,0:T(8,128)(2,1)}, bf16[2,4,64,512]{3,2,1,0:T(8,128)(2,1)S(1)}, f32[128,512]{1,0:T(8,128)S(1)}, bf16[128,512]{1,0:T(8,128)(2,1)S(1)}, bf16[64,512]{1,0:T(8,128)(2,1)S(1)}) custom-call(bf16[256,512]{1,0:T(8,128)(2,1)S(1)} %copy-done.14, bf16[256,512]{1,0:T(8,128)(2,1)S(1)} %copy-done.16, f32[256,256]{1,0:T(8,128)S(1)} %copy-done.6, ...), custom_call_target="tpu_custom_call" | custom-call | flops 1000000000 | bytes 6000000 | tf_op jit(solution)/shard_map/inner/pallas_call | solution.py:28
  37.2 1.3 %collective-permute-start.3 = (bf16[64,512]{1,0:T(8,128)(2,1)S(1)}, bf16[64,512]{1,0:T(8,128)(2,1)S(1)}, u32[]{:S(2)}, u32[]{:S(2)}) collective-permute-start(bf16[64,512]{1,0:T(8,128)(2,1)S(1)} %get-tuple-element.38), channel_id=1, source_target_pairs={{1,0},{2,1},{3,2},{4,3},{5,4},{6,5},{7,6},{8,7},{9,8},{10,9},{11,1... | collective-permute-start | bytes 196616 | tf_op jit(solution)/shard_map/ppermute | solution.py:176
  38.5 2.3 %collective-permute-done.12.got = bf16[4,112,512]{2,1,0:T(8,128)(2,1)} collective-permute-done((bf16[4,112,512]{2,1,0:T(8,128)(2,1)}, bf16[4,112,512]{2,1,0:T(8,128)(2,1)}, u32[]{:S(2)}, u32[]{:S(2)}) %collective-permute-start.12) | collective-permute-done | bytes 458784 | tf_op jit(solution)/shard_map/ppermute | solution.py:172
  40.9 1.3 %add_x.3 = (bf16[112,512]{1,0:T(8,128)(2,1)S(1)}, bf16[112,512]{1,0:T(8,128)(2,1)S(1)}, bf16[112,512]{1,0:T(8,128)(2,1)S(1)}, bf16[112,512]{1,0:T(8,128)(2,1)S(1)}) custom-call(bf16[4,112,512]{2,1,0:T(8,128)(2,1)} %collective-permute-done.12.got, bf16[4,112,512]{2,1,0:T(8,128)(2,1)S(1)} %copy-done.4), custom_call_target="tpu_custom_call" | custom-call | bytes 1000000 | tf_op jit(solution)/shard_map/add_x/pallas_call | solution.py:28
  42.1 2.8 %collective-permute-start.13 = (bf16[112,512]{1,0:T(8,128)(2,1)S(1)}, bf16[112,512]{1,0:T(8,128)(2,1)S(1)}, u32[]{:S(2)}, u32[]{:S(2)}) collective-permute-start(bf16[112,512]{1,0:T(8,128)(2,1)S(1)} %get-tuple-element.52), channel_id=1, source_target_pairs={{0,4},{1,5},{2,6},{3,7},{4,0},{5,1},{6,2},{7,3},{8,12},{9,13},{10,... | collective-permute-start | bytes 344072 | tf_op jit(solution)/shard_map/ppermute | solution.py:172
  44.9 1.1 %collective-permute-start.14 = (bf16[112,512]{1,0:T(8,128)(2,1)S(1)}, bf16[112,512]{1,0:T(8,128)(2,1)S(1)}, u32[]{:S(2)}, u32[]{:S(2)}) collective-permute-start(bf16[112,512]{1,0:T(8,128)(2,1)S(1)} %get-tuple-element.53), channel_id=1, source_target_pairs={{0,8},{1,9},{2,10},{3,11},{4,12},{5,13},{6,14},{7,15},{8,0},{9,1},... | collective-permute-start | bytes 344072 | tf_op jit(solution)/shard_map/ppermute | solution.py:172
  46.0 1.3 %collective-permute-start.15 = (bf16[112,512]{1,0:T(8,128)(2,1)S(1)}, bf16[112,512]{1,0:T(8,128)(2,1)S(1)}, u32[]{:S(2)}, u32[]{:S(2)}) collective-permute-start(bf16[112,512]{1,0:T(8,128)(2,1)S(1)} %get-tuple-element.54), channel_id=1, source_target_pairs={{0,12},{1,13},{2,14},{3,15},{4,8},{5,9},{6,10},{7,11},{8,4},{9,5},... | collective-permute-start | bytes 344072 | tf_op jit(solution)/shard_map/ppermute | solution.py:172
  48.5 7.8 %collective-permute-done.14.refs_2_ = bf16[112,512]{1,0:T(8,128)(2,1)S(1)} collective-permute-done((bf16[112,512]{1,0:T(8,128)(2,1)S(1)}, bf16[112,512]{1,0:T(8,128)(2,1)S(1)}, u32[]{:S(2)}, u32[]{:S(2)}) %collective-permute-start.14) | collective-permute-done | bytes 114720 | tf_op jit(solution)/shard_map/ppermute | solution.py:172
  56.4 1.6 %collective-permute-start.16 = (bf16[112,512]{1,0:T(8,128)(2,1)S(1)}, bf16[112,512]{1,0:T(8,128)(2,1)S(1)}, u32[]{:S(2)}, u32[]{:S(2)}) collective-permute-start(bf16[112,512]{1,0:T(8,128)(2,1)S(1)} %add_z.3.refs_0_), channel_id=1, source_target_pairs={{0,16},{16,0},{1,17},{17,1},{2,18},{18,2},{3,19},{19,3},{4,20},{20... | collective-permute-start | bytes 344072 | tf_op jit(solution)/shard_map/ppermute | solution.py:238
  58.0 1.3 %collective-permute-start.4 = (bf16[128,512]{1,0:T(8,128)(2,1)S(1)}, bf16[128,512]{1,0:T(8,128)(2,1)S(1)}, u32[]{:S(2)}, u32[]{:S(2)}) collective-permute-start(bf16[128,512]{1,0:T(8,128)(2,1)S(1)} %pad_maximum_fusion.2), channel_id=1, source_target_pairs={{2,0},{3,1},{4,2},{5,3},{6,4},{7,5},{8,6},{9,7},{10,8},{11,9},{12,... | collective-permute-start | bytes 393224 | tf_op jit(solution)/shard_map/ppermute | solution.py:176
  59.3 2.0 %collective-permute-done.16.refs_1_ = bf16[112,512]{1,0:T(8,128)(2,1)S(1)} collective-permute-done((bf16[112,512]{1,0:T(8,128)(2,1)S(1)}, bf16[112,512]{1,0:T(8,128)(2,1)S(1)}, u32[]{:S(2)}, u32[]{:S(2)}) %collective-permute-start.16) | collective-permute-done | bytes 114720 | tf_op jit(solution)/shard_map/ppermute | solution.py:238
  61.3 2.8 %collective-permute-start.18 = (bf16[48,512]{1,0:T(8,128)(2,1)S(1)}, bf16[48,512]{1,0:T(8,128)(2,1)S(1)}, u32[]{:S(2)}, u32[]{:S(2)}) collective-permute-start(bf16[48,512]{1,0:T(8,128)(2,1)S(1)} %get-tuple-element.56), channel_id=1, source_target_pairs={{0,8},{1,9},{2,10},{3,11},{4,12},{5,13},{6,14},{7,15},{8,0},{9,1},... | collective-permute-start | bytes 147464 | tf_op jit(solution)/shard_map/ppermute | solution.py:172
  64.1 1.5 %collective-permute-start.19 = (bf16[48,512]{1,0:T(8,128)(2,1)S(1)}, bf16[48,512]{1,0:T(8,128)(2,1)S(1)}, u32[]{:S(2)}, u32[]{:S(2)}) collective-permute-start(bf16[48,512]{1,0:T(8,128)(2,1)S(1)} %get-tuple-element.56), channel_id=1, source_target_pairs={{0,12},{1,13},{2,14},{3,15},{4,8},{5,9},{6,10},{7,11},{8,4},{9,5},... | collective-permute-start | bytes 147464 | tf_op jit(solution)/shard_map/ppermute | solution.py:172
  66.6 2.1 %collective-permute-done.18 = bf16[48,512]{1,0:T(8,128)(2,1)S(1)} collective-permute-done((bf16[48,512]{1,0:T(8,128)(2,1)S(1)}, bf16[48,512]{1,0:T(8,128)(2,1)S(1)}, u32[]{:S(2)}, u32[]{:S(2)}) %collective-permute-start.18) | collective-permute-done | bytes 49184 | tf_op jit(solution)/shard_map/ppermute | solution.py:172
  68.7 1.3 %collective-permute-done.19 = bf16[48,512]{1,0:T(8,128)(2,1)S(1)} collective-permute-done((bf16[48,512]{1,0:T(8,128)(2,1)S(1)}, bf16[48,512]{1,0:T(8,128)(2,1)S(1)}, u32[]{:S(2)}, u32[]{:S(2)}) %collective-permute-start.19) | collective-permute-done | bytes 49184 | tf_op jit(solution)/shard_map/ppermute | solution.py:172
  72.4 1.8 %collective-permute-done.6.got = bf16[4,64,512]{2,1,0:T(8,128)(2,1)S(1)} collective-permute-done((bf16[4,64,512]{2,1,0:T(8,128)(2,1)S(1)}, bf16[4,64,512]{2,1,0:T(8,128)(2,1)S(1)}, u32[]{:S(2)}, u32[]{:S(2)}) %collective-permute-start.6) | collective-permute-done | bytes 262176 | tf_op jit(solution)/shard_map/ppermute | solution.py:172
  74.4 1.5 %collective-permute-start.7 = (bf16[64,512]{1,0:T(8,128)(2,1)S(1)}, bf16[64,512]{1,0:T(8,128)(2,1)S(1)}, u32[]{:S(2)}, u32[]{:S(2)}) collective-permute-start(bf16[64,512]{1,0:T(8,128)(2,1)S(1)} %get-tuple-element.44), channel_id=1, source_target_pairs={{0,4},{1,5},{2,6},{3,7},{4,0},{5,1},{6,2},{7,3},{8,12},{9,13},{10,... | collective-permute-start | bytes 196616 | tf_op jit(solution)/shard_map/ppermute | solution.py:172
  75.8 1.7 %collective-permute-start.8 = (bf16[64,512]{1,0:T(8,128)(2,1)S(1)}, bf16[64,512]{1,0:T(8,128)(2,1)S(1)}, u32[]{:S(2)}, u32[]{:S(2)}) collective-permute-start(bf16[64,512]{1,0:T(8,128)(2,1)S(1)} %get-tuple-element.45), channel_id=1, source_target_pairs={{0,8},{1,9},{2,10},{3,11},{4,12},{5,13},{6,14},{7,15},{8,0},{9,1},... | collective-permute-start | bytes 196616 | tf_op jit(solution)/shard_map/ppermute | solution.py:172
  77.5 1.4 %collective-permute-start.9 = (bf16[64,512]{1,0:T(8,128)(2,1)S(1)}, bf16[64,512]{1,0:T(8,128)(2,1)S(1)}, u32[]{:S(2)}, u32[]{:S(2)}) collective-permute-start(bf16[64,512]{1,0:T(8,128)(2,1)S(1)} %get-tuple-element.46), channel_id=1, source_target_pairs={{0,12},{1,13},{2,14},{3,15},{4,8},{5,9},{6,10},{7,11},{8,4},{9,5},... | collective-permute-start | bytes 196616 | tf_op jit(solution)/shard_map/ppermute | solution.py:172
  79.9 1.1 %collective-permute-done.8.refs_2_ = bf16[64,512]{1,0:T(8,128)(2,1)S(1)} collective-permute-done((bf16[64,512]{1,0:T(8,128)(2,1)S(1)}, bf16[64,512]{1,0:T(8,128)(2,1)S(1)}, u32[]{:S(2)}, u32[]{:S(2)}) %collective-permute-start.8) | collective-permute-done | bytes 65568 | tf_op jit(solution)/shard_map/ppermute | solution.py:172
  81.0 2.7 %collective-permute-done.9.refs_3_ = bf16[64,512]{1,0:T(8,128)(2,1)S(1)} collective-permute-done((bf16[64,512]{1,0:T(8,128)(2,1)S(1)}, bf16[64,512]{1,0:T(8,128)(2,1)S(1)}, u32[]{:S(2)}, u32[]{:S(2)}) %collective-permute-start.9) | collective-permute-done | bytes 65568 | tf_op jit(solution)/shard_map/ppermute | solution.py:172
  83.7 1.5 %collective-permute-start.10 = (bf16[64,512]{1,0:T(8,128)(2,1)S(1)}, bf16[64,512]{1,0:T(8,128)(2,1)S(1)}, u32[]{:S(2)}, u32[]{:S(2)}) collective-permute-start(bf16[64,512]{1,0:T(8,128)(2,1)S(1)} %add_z.2.refs_0_), channel_id=1, source_target_pairs={{0,16},{16,0},{1,17},{17,1},{2,18},{18,2},{3,19},{19,3},{4,20},{20... | collective-permute-start | bytes 196616 | tf_op jit(solution)/shard_map/ppermute | solution.py:238
  85.9 2.1 %collective-permute-done.10.refs_1_ = bf16[64,512]{1,0:T(8,128)(2,1)S(1)} collective-permute-done((bf16[64,512]{1,0:T(8,128)(2,1)S(1)}, bf16[64,512]{1,0:T(8,128)(2,1)S(1)}, u32[]{:S(2)}, u32[]{:S(2)}) %collective-permute-start.10) | collective-permute-done | bytes 65568 | tf_op jit(solution)/shard_map/ppermute | solution.py:238
  (86 shorter events, 19.3 us)
Async XLA Ops:
  0.6 13.8 %collective-permute-start.1 = (bf16[128,512]{1,0:T(8,128)(2,1)}, bf16[128,512]{1,0:T(8,128)(2,1)S(1)}, u32[]{:S(2)}, u32[]{:S(2)}) collective-permute-start(bf16[128,512]{1,0:T(8,128)(2,1)} %bitcast.39), channel_id=1, source_target_pairs={{0,2},{1,3},{2,4},{3,5},{4,6},{5,7},{6,8},{7,9},{8,10},{9,11},{10,... | collective-permute-start | bytes 393224 | tf_op jit(solution)/shard_map/ppermute | solution.py:176
  6.3 6.6 %collective-permute-start = (bf16[32,512]{1,0:T(8,128)(2,1)S(1)}, bf16[32,512]{1,0:T(8,128)(2,1)S(1)}, u32[]{:S(2)}, u32[]{:S(2)}) collective-permute-start(bf16[32,512]{1,0:T(8,128)(2,1)S(1)} %slice_bitcast_fusion), channel_id=1, source_target_pairs={{0,1},{1,2},{2,3},{3,4},{4,5},{5,6},{6,7},{7,8},{8,9},{9,10},{10,1... | collective-permute-start | bytes 98312 | tf_op jit(solution)/shard_map/ppermute | solution.py:176
  7.7 6.7 %collective-permute-start.2 = (bf16[32,512]{1,0:T(8,128)(2,1)S(1)}, bf16[32,512]{1,0:T(8,128)(2,1)S(1)}, u32[]{:S(2)}, u32[]{:S(2)}) collective-permute-start(bf16[32,512]{1,0:T(8,128)(2,1)S(1)} %slice_bitcast_fusion), channel_id=1, source_target_pairs={{0,3},{1,4},{2,5},{3,6},{4,7},{5,8},{6,9},{7,10},{8,11},{9,12},{10... | collective-permute-start | bytes 98312 | tf_op jit(solution)/shard_map/ppermute | solution.py:176
  18.2 11.3 %copy-start = (bf16[2,1024,512]{2,1,0:T(8,128)(2,1)S(1)}, bf16[2,1024,512]{2,1,0:T(8,128)(2,1)}, u32[]{:S(2)}) copy-start(bf16[2,1024,512]{2,1,0:T(8,128)(2,1)} %cw.3) | copy-start | bytes 6291460
  18.2 11.3 %copy-start.19 = (bf16[1,128,256]{2,1,0:T(8,128)(2,1)S(1)}, bf16[1,128,256]{2,1,0:T(8,128)(2,1)}, u32[]{:S(2)}) copy-start(bf16[1,128,256]{2,1,0:T(8,128)(2,1)} %param.9) | copy-start | bytes 196612
  23.0 3.9 %copy-start.7 = (f32[256,256]{1,0:T(8,128)}, f32[256,256]{1,0:T(8,128)S(1)}, u32[]{:S(2)}) copy-start(f32[256,256]{1,0:T(8,128)S(1)} %get-tuple-element.33.b) | copy-start | bytes 786436
  23.1 4.7 %copy-start.9 = (bf16[256,512]{1,0:T(8,128)(2,1)}, bf16[256,512]{1,0:T(8,128)(2,1)S(1)}, u32[]{:S(2)}) copy-start(bf16[256,512]{1,0:T(8,128)(2,1)S(1)} %get-tuple-element.34.outer) | copy-start | bytes 786436
  23.1 6.4 %copy-start.11 = (f32[128,512]{1,0:T(8,128)}, f32[128,512]{1,0:T(8,128)S(1)}, u32[]{:S(2)}) copy-start(f32[128,512]{1,0:T(8,128)S(1)} %get-tuple-element.35.ga) | copy-start | bytes 786436
  23.1 6.4 %copy-start.13 = (bf16[256,512]{1,0:T(8,128)(2,1)}, bf16[256,512]{1,0:T(8,128)(2,1)S(1)}, u32[]{:S(2)}) copy-start(bf16[256,512]{1,0:T(8,128)(2,1)S(1)} %get-tuple-element.30.x0) | copy-start | bytes 786436
  23.1 6.4 %copy-start.15 = (bf16[256,512]{1,0:T(8,128)(2,1)}, bf16[256,512]{1,0:T(8,128)(2,1)S(1)}, u32[]{:S(2)}) copy-start(bf16[256,512]{1,0:T(8,128)(2,1)S(1)} %get-tuple-element.31.p0) | copy-start | bytes 786436
  23.1 6.4 %copy-start.2 = (bf16[2,256,768]{2,1,0:T(8,128)(2,1)S(1)}, bf16[2,256,768]{2,1,0:T(8,128)(2,1)}, u32[]{:S(2)}) copy-start(bf16[2,256,768]{2,1,0:T(8,128)(2,1)} %rw.3) | copy-start | bytes 2359300
  23.1 2.5 %collective-permute-start.11 = (bf16[2,4,112,512]{3,2,1,0:T(8,128)(2,1)S(1)}, bf16[2,4,112,512]{3,2,1,0:T(8,128)(2,1)S(1)}, u32[]{:S(2)}, u32[]{:S(2)}) collective-permute-start(bf16[2,4,112,512]{3,2,1,0:T(8,128)(2,1)S(1)} %get-tuple-element.47), channel_id=1, source_target_pairs={{0,1},{1,0},{2,3},{3,2},{4,5},{5,4},{6,7},{7,6},{8,9},{9,8},{10,11... | collective-permute-start | bytes 2752520 | tf_op jit(solution)/shard_map/ppermute | solution.py:172
  27.7 13.1 %collective-permute-start.12 = (bf16[4,112,512]{2,1,0:T(8,128)(2,1)}, bf16[4,112,512]{2,1,0:T(8,128)(2,1)}, u32[]{:S(2)}, u32[]{:S(2)}) collective-permute-start(bf16[4,112,512]{2,1,0:T(8,128)(2,1)} %get-tuple-element.49), channel_id=1, source_target_pairs={{0,2},{1,3},{2,0},{3,1},{4,6},{5,7},{6,4},{7,5},{8,10},{9,11},{10,... | collective-permute-start | bytes 1376264 | tf_op jit(solution)/shard_map/ppermute | solution.py:172
  35.2 5.6 %copy-start.4 = (bf16[4,112,512]{2,1,0:T(8,128)(2,1)S(1)}, bf16[4,112,512]{2,1,0:T(8,128)(2,1)}, u32[]{:S(2)}) copy-start(bf16[4,112,512]{2,1,0:T(8,128)(2,1)} %copy-done.3) | copy-start | bytes 1376260
  37.2 24.1 %copy-start.17 = (f32[128,512]{1,0:T(8,128)}, f32[128,512]{1,0:T(8,128)S(1)}, u32[]{:S(2)}) copy-start(f32[128,512]{1,0:T(8,128)S(1)} %get-tuple-element.36) | copy-start | bytes 786436
  37.2 28.4 %collective-permute-start.5 = (bf16[2,4,64,512]{3,2,1,0:T(8,128)(2,1)}, bf16[2,4,64,512]{3,2,1,0:T(8,128)(2,1)S(1)}, u32[]{:S(2)}, u32[]{:S(2)}) collective-permute-start(bf16[2,4,64,512]{3,2,1,0:T(8,128)(2,1)} %get-tuple-element.39), channel_id=1, source_target_pairs={{0,1},{1,0},{2,3},{3,2},{4,5},{5,4},{6,7},{7,6},{8,9},{9,8},{10,11... | collective-permute-start | bytes 1572872 | tf_op jit(solution)/shard_map/ppermute | solution.py:172
  37.2 10.2 %collective-permute-start.3 = (bf16[64,512]{1,0:T(8,128)(2,1)S(1)}, bf16[64,512]{1,0:T(8,128)(2,1)S(1)}, u32[]{:S(2)}, u32[]{:S(2)}) collective-permute-start(bf16[64,512]{1,0:T(8,128)(2,1)S(1)} %get-tuple-element.38), channel_id=1, source_target_pairs={{1,0},{2,1},{3,2},{4,3},{5,4},{6,5},{7,6},{8,7},{9,8},{10,9},{11,1... | collective-permute-start | bytes 196616 | tf_op jit(solution)/shard_map/ppermute | solution.py:176
  42.1 6.4 %collective-permute-start.13 = (bf16[112,512]{1,0:T(8,128)(2,1)S(1)}, bf16[112,512]{1,0:T(8,128)(2,1)S(1)}, u32[]{:S(2)}, u32[]{:S(2)}) collective-permute-start(bf16[112,512]{1,0:T(8,128)(2,1)S(1)} %get-tuple-element.52), channel_id=1, source_target_pairs={{0,4},{1,5},{2,6},{3,7},{4,0},{5,1},{6,2},{7,3},{8,12},{9,13},{10,... | collective-permute-start | bytes 344072 | tf_op jit(solution)/shard_map/ppermute | solution.py:172
  44.9 11.4 %collective-permute-start.14 = (bf16[112,512]{1,0:T(8,128)(2,1)S(1)}, bf16[112,512]{1,0:T(8,128)(2,1)S(1)}, u32[]{:S(2)}, u32[]{:S(2)}) collective-permute-start(bf16[112,512]{1,0:T(8,128)(2,1)S(1)} %get-tuple-element.53), channel_id=1, source_target_pairs={{0,8},{1,9},{2,10},{3,11},{4,12},{5,13},{6,14},{7,15},{8,0},{9,1},... | collective-permute-start | bytes 344072 | tf_op jit(solution)/shard_map/ppermute | solution.py:172
  46.0 10.3 %collective-permute-start.15 = (bf16[112,512]{1,0:T(8,128)(2,1)S(1)}, bf16[112,512]{1,0:T(8,128)(2,1)S(1)}, u32[]{:S(2)}, u32[]{:S(2)}) collective-permute-start(bf16[112,512]{1,0:T(8,128)(2,1)S(1)} %get-tuple-element.54), channel_id=1, source_target_pairs={{0,12},{1,13},{2,14},{3,15},{4,8},{5,9},{6,10},{7,11},{8,4},{9,5},... | collective-permute-start | bytes 344072 | tf_op jit(solution)/shard_map/ppermute | solution.py:172
  56.4 4.9 %collective-permute-start.16 = (bf16[112,512]{1,0:T(8,128)(2,1)S(1)}, bf16[112,512]{1,0:T(8,128)(2,1)S(1)}, u32[]{:S(2)}, u32[]{:S(2)}) collective-permute-start(bf16[112,512]{1,0:T(8,128)(2,1)S(1)} %add_z.3.refs_0_), channel_id=1, source_target_pairs={{0,16},{16,0},{1,17},{17,1},{2,18},{18,2},{3,19},{19,3},{4,20},{20... | collective-permute-start | bytes 344072 | tf_op jit(solution)/shard_map/ppermute | solution.py:238
  58.0 13.5 %collective-permute-start.4 = (bf16[128,512]{1,0:T(8,128)(2,1)S(1)}, bf16[128,512]{1,0:T(8,128)(2,1)S(1)}, u32[]{:S(2)}, u32[]{:S(2)}) collective-permute-start(bf16[128,512]{1,0:T(8,128)(2,1)S(1)} %pad_maximum_fusion.2), channel_id=1, source_target_pairs={{2,0},{3,1},{4,2},{5,3},{6,4},{7,5},{8,6},{9,7},{10,8},{11,9},{12,... | collective-permute-start | bytes 393224 | tf_op jit(solution)/shard_map/ppermute | solution.py:176
  61.3 7.4 %collective-permute-start.18 = (bf16[48,512]{1,0:T(8,128)(2,1)S(1)}, bf16[48,512]{1,0:T(8,128)(2,1)S(1)}, u32[]{:S(2)}, u32[]{:S(2)}) collective-permute-start(bf16[48,512]{1,0:T(8,128)(2,1)S(1)} %get-tuple-element.56), channel_id=1, source_target_pairs={{0,8},{1,9},{2,10},{3,11},{4,12},{5,13},{6,14},{7,15},{8,0},{9,1},... | collective-permute-start | bytes 147464 | tf_op jit(solution)/shard_map/ppermute | solution.py:172
  64.1 6.0 %collective-permute-start.19 = (bf16[48,512]{1,0:T(8,128)(2,1)S(1)}, bf16[48,512]{1,0:T(8,128)(2,1)S(1)}, u32[]{:S(2)}, u32[]{:S(2)}) collective-permute-start(bf16[48,512]{1,0:T(8,128)(2,1)S(1)} %get-tuple-element.56), channel_id=1, source_target_pairs={{0,12},{1,13},{2,14},{3,15},{4,8},{5,9},{6,10},{7,11},{8,4},{9,5},... | collective-permute-start | bytes 147464 | tf_op jit(solution)/shard_map/ppermute | solution.py:172
  65.5 4.6 %collective-permute-start.17 = (bf16[48,512]{1,0:T(8,128)(2,1)S(1)}, bf16[48,512]{1,0:T(8,128)(2,1)S(1)}, u32[]{:S(2)}, u32[]{:S(2)}) collective-permute-start(bf16[48,512]{1,0:T(8,128)(2,1)S(1)} %get-tuple-element.56), channel_id=1, source_target_pairs={{0,4},{1,5},{2,6},{3,7},{4,0},{5,1},{6,2},{7,3},{8,12},{9,13},{10,... | collective-permute-start | bytes 147464 | tf_op jit(solution)/shard_map/ppermute | solution.py:172
  65.9 8.4 %collective-permute-start.6 = (bf16[4,64,512]{2,1,0:T(8,128)(2,1)S(1)}, bf16[4,64,512]{2,1,0:T(8,128)(2,1)S(1)}, u32[]{:S(2)}, u32[]{:S(2)}) collective-permute-start(bf16[4,64,512]{2,1,0:T(8,128)(2,1)S(1)} %get-tuple-element.41), channel_id=1, source_target_pairs={{0,2},{1,3},{2,0},{3,1},{4,6},{5,7},{6,4},{7,5},{8,10},{9,11},{10,... | collective-permute-start | bytes 786440 | tf_op jit(solution)/shard_map/ppermute | solution.py:172
  70.7 8.2 %collective-permute-start.20 = (bf16[192,512]{1,0:T(8,128)(2,1)S(1)}, bf16[192,512]{1,0:T(8,128)(2,1)S(1)}, u32[]{:S(2)}, u32[]{:S(2)}) collective-permute-start(bf16[192,512]{1,0:T(8,128)(2,1)S(1)} %bitcast.44), channel_id=1, source_target_pairs={{0,2},{1,3},{2,0},{3,1},{4,6},{5,7},{6,4},{7,5},{8,10},{9,11},{10,... | collective-permute-start | bytes 589832 | tf_op jit(solution)/shard_map/ppermute | solution.py:172
  74.4 5.5 %collective-permute-start.7 = (bf16[64,512]{1,0:T(8,128)(2,1)S(1)}, bf16[64,512]{1,0:T(8,128)(2,1)S(1)}, u32[]{:S(2)}, u32[]{:S(2)}) collective-permute-start(bf16[64,512]{1,0:T(8,128)(2,1)S(1)} %get-tuple-element.44), channel_id=1, source_target_pairs={{0,4},{1,5},{2,6},{3,7},{4,0},{5,1},{6,2},{7,3},{8,12},{9,13},{10,... | collective-permute-start | bytes 196616 | tf_op jit(solution)/shard_map/ppermute | solution.py:172
  75.8 5.2 %collective-permute-start.8 = (bf16[64,512]{1,0:T(8,128)(2,1)S(1)}, bf16[64,512]{1,0:T(8,128)(2,1)S(1)}, u32[]{:S(2)}, u32[]{:S(2)}) collective-permute-start(bf16[64,512]{1,0:T(8,128)(2,1)S(1)} %get-tuple-element.45), channel_id=1, source_target_pairs={{0,8},{1,9},{2,10},{3,11},{4,12},{5,13},{6,14},{7,15},{8,0},{9,1},... | collective-permute-start | bytes 196616 | tf_op jit(solution)/shard_map/ppermute | solution.py:172
  77.5 6.2 %collective-permute-start.9 = (bf16[64,512]{1,0:T(8,128)(2,1)S(1)}, bf16[64,512]{1,0:T(8,128)(2,1)S(1)}, u32[]{:S(2)}, u32[]{:S(2)}) collective-permute-start(bf16[64,512]{1,0:T(8,128)(2,1)S(1)} %get-tuple-element.46), channel_id=1, source_target_pairs={{0,12},{1,13},{2,14},{3,15},{4,8},{5,9},{6,10},{7,11},{8,4},{9,5},... | collective-permute-start | bytes 196616 | tf_op jit(solution)/shard_map/ppermute | solution.py:172
  78.9 9.8 %collective-permute-start.21 = (bf16[2,192,512]{2,1,0:T(8,128)(2,1)S(1)}, bf16[2,192,512]{2,1,0:T(8,128)(2,1)S(1)}, u32[]{:S(2)}, u32[]{:S(2)}) collective-permute-start(bf16[2,192,512]{2,1,0:T(8,128)(2,1)S(1)} %maximum_select_fusion.2), channel_id=1, source_target_pairs={{0,1},{1,0},{2,3},{3,2},{4,5},{5,4},{6,7},{7,6},{8,9},{9,8},{10,11... | collective-permute-start | bytes 1179656 | tf_op jit(solution)/shard_map/ppermute | solution.py:172
  83.7 4.3 %collective-permute-start.10 = (bf16[64,512]{1,0:T(8,128)(2,1)S(1)}, bf16[64,512]{1,0:T(8,128)(2,1)S(1)}, u32[]{:S(2)}, u32[]{:S(2)}) collective-permute-start(bf16[64,512]{1,0:T(8,128)(2,1)S(1)} %add_z.2.refs_0_), channel_id=1, source_target_pairs={{0,16},{16,0},{1,17},{17,1},{2,18},{18,2},{3,19},{19,3},{4,20},{20... | collective-permute-start | bytes 196616 | tf_op jit(solution)/shard_map/ppermute | solution.py:238
  (12 other events, 11.0 us)

commit v2 on v0

--- a/solution.py
+++ b/solution.py
@@ -1,7 +1,14 @@
+import functools
+
 import jax
 import jax.numpy as jnp
 from jax import lax
+from jax.experimental import pallas as pl
+from jax.experimental.pallas import tpu as pltpu
 from jax.sharding import PartitionSpec as P
+
+F32 = jnp.float32
+BF16 = jnp.bfloat16
 
 
 def passed_along(block, axis, distance):
@@ -28,7 +35,7 @@
     return lax.psum(piece, "dp")
 
 
-def body(signal, conv_weight, res_weight, grad_out, skip_cotangent):
+def general_body(signal, conv_weight, res_weight, grad_out, skip_cotangent):
     s_dev, t_dev, width = signal.shape
     gated = res_weight.shape[1]
     near = t_dev // 4
@@ -98,7 +105,377 @@
     return (input_grad, conv_grad, res_grad)
 
 
+def mm(a, b):
+    return jnp.dot(a, b, preferred_element_type=F32)
+
+
+def mm_nt(a, b):
+    return lax.dot_general(a, b, (((1,), (1,)), ((), ())), preferred_element_type=F32)
+
+
+def mm_tn(a, b):
+    return lax.dot_general(a, b, (((0,), (0,)), ((), ())), preferred_element_type=F32)
+
+
+def shaped(shape, dtype=BF16):
+    return jax.ShapeDtypeStruct(shape, dtype)
+
+
+def call(kernel, outs, *args, after=(), scratch=(), flops=0, nbytes=0, vmem=8, name=None):
+    n_args = len(args)
+
+    def run(*refs):
+        kernel(*refs[:n_args], *refs[n_args + len(after) :])
+
+    in_vmem = pl.BlockSpec(memory_space=pltpu.VMEM)
+    return pl.pallas_call(
+        run,
+        out_shape=outs,
+        in_specs=[in_vmem] * n_args + [pl.BlockSpec(memory_space=pl.ANY)] * len(after),
+        out_specs=[in_vmem] * len(outs),
+        scratch_shapes=list(scratch),
+        compiler_params=pltpu.CompilerParams(vmem_limit_bytes=vmem * 1024 * 1024),
+        cost_estimate=pl.CostEstimate(flops=flops, bytes_accessed=nbytes, transcendentals=0),
+        name=name,
+    )(*args, *after)
+
+
+def place(tm):
+    return tm // 4, lax.rem(tm // 2, 2), lax.rem(tm, 2)
+
+
+def here():
+    return place(lax.axis_index("tm"))
+
+
+def load_kernel(*refs):
+    n = (len(refs) - 1) // 2
+    sems = refs[-1]
+    copies = [pltpu.make_async_copy(refs[i], refs[n + i], sems.at[i]) for i in range(n)]
+    for copy in copies:
+        copy.start()
+    for copy in copies:
+        copy.wait()
+
+
+def load(*arrays):
+    n = len(arrays)
+    return pl.pallas_call(
+        load_kernel,
+        out_shape=[pltpu.VMEM(a.shape, a.dtype) for a in arrays],
+        in_specs=[pl.BlockSpec(memory_space=pltpu.HBM)] * n,
+        out_specs=[pl.BlockSpec(memory_space=pltpu.VMEM)] * n,
+        scratch_shapes=[pltpu.SemaphoreType.DMA((n,))],
+        compiler_params=pltpu.CompilerParams(vmem_limit_bytes=8 * 1024 * 1024),
+        cost_estimate=pl.CostEstimate(flops=4_000_000_000, bytes_accessed=6_000_000, transcendentals=0),
+        name="load",
+    )(*[pltpu.with_memory_space_constraint(a, pltpu.HBM) for a in arrays])
+
+
+def pack_halo_kernel(sig, far, tail4, out):
+    t = sig.shape[0]
+    near = t // 4
+    out[0:near, :] = sig[t - near :, :]
+    out[near : 2 * near, :] = far[t - near :, :]
+    out[2 * near :, :] = tail4[...]
+
+
+def inputs_of(sig, far, edge):
+    t = sig.shape[0]
+    near = t // 4
+    _, _, core = here()
+    even = core == 0
+    near_in = jnp.where(even, edge[near : 2 * near, :], edge[0:near, :])
+    far_near = jnp.where(even, edge[2 * near :, :], edge[near : 2 * near, :])
+    x0 = jnp.concatenate([sig[...], far[...]], axis=0)
+    p0 = jnp.concatenate([near_in, sig[0 : t - near, :], far_near, far[0 : t - near, :]], axis=0)
+    return x0, p0
+
+
+def forward_and_outer_kernel(
+    sig, far, edge, cw, rw, grad, skip,
+    send, keep, a_out, b_out, x1_out, dz_out, o_out, ga_out,
+    staged,
+):
+    t, width = sig.shape
+    gated = rw.shape[1]
+    _, _, core = here()
+    x0, p0 = inputs_of(sig, far, edge)
+    z0 = mm(p0, cw[0, 0:width, :]) + mm(x0, cw[0, width:, :])
+    tf = jnp.tanh(z0[:, :gated])
+    sg = jax.nn.sigmoid(z0[:, gated:])
+    h0 = (tf * sg).astype(BF16)
+    a_out[...] = sg * (1.0 - tf * tf)
+    b_out[...] = tf * sg * (1.0 - sg)
+    x1 = (x0.astype(F32) + mm(h0, rw[0, :, 0:width])).astype(BF16)
+    x1_out[...] = x1
+    z1 = mm(x1[t:, :], cw[1, 0:width, :]) + mm(x1[:t, :], cw[1, width:, :])
+    tf = jnp.tanh(z1[:, :gated])
+    sg = jax.nn.sigmoid(z1[:, gated:])
+    h1 = (tf * sg).astype(BF16)
+    g2 = grad[...]
+    sk = skip[...]
+    e1 = mm_nt(g2, rw[1, :, 0:width]) + mm_nt(sk, rw[1, :, width:])
+    dz1 = jnp.concatenate([e1 * sg * (1.0 - tf * tf), e1 * tf * sg * (1.0 - sg)], axis=1).astype(BF16)
+    dz_out[...] = dz1
+    dpast = mm_nt(dz1, cw[1, 0:width, :]).astype(BF16)
+    ga = g2.astype(F32) + mm_nt(dz1, cw[1, width:, :])
+    ga_out[...] = ga
+    outer = jnp.concatenate([ga.astype(BF16), dpast], axis=0)
+    o_out[...] = outer
+    skips = jnp.concatenate([mm_tn(h1, sk), mm_tn(h0[:t, :], sk)], axis=1)
+    eighth = gated // 8
+    for which, part in enumerate((mm_tn(h1, g2), mm_tn(h0, outer), skips)):
+        for c in range(2):
+            for q in range(4):
+                rows = slice((4 * c + q) * eighth, (4 * c + q + 1) * eighth)
+                staged[c, q, which * eighth : (which + 1) * eighth, :] = part[rows, :].astype(BF16)
+    send[...] = staged[1 - core]
+    keep[...] = staged[core]
+
+
+def inner_kernel(
+    sig, far, edge, a, b, x1, dz1, outer, ga, cw, rw, skip,
+    send, keep, own_out, back_out,
+    staged,
+):
+    t, width = sig.shape
+    near = t // 4
+    _, _, core = here()
+    x0, p0 = inputs_of(sig, far, edge)
+    e0 = mm_nt(outer[...], rw[0, :, 0:width])
+    es = mm_nt(skip[...], rw[0, :, width:])
+    e0 = jnp.concatenate([e0[:t, :] + es, e0[t:, :]], axis=0)
+    dz0 = jnp.concatenate([e0 * a[...], e0 * b[...]], axis=1).astype(BF16)
+    half = width // 16
+    rows = 2 * half
+    blocks = width // rows
+    last = x1[t:, :]
+    first = x1[:t, :]
+    for base, part0, part1 in (
+        (0, mm_tn(p0, dz0), mm_tn(last, dz1[...])),
+        (blocks, mm_tn(x0, dz0), mm_tn(first, dz1[...])),
+    ):
+        for block in range(blocks):
+            g, x, c = (base + block) // 4, (base + block) // 2 % 2, (base + block) % 2
+            for y in range(2):
+                src = slice(block * rows + y * half, block * rows + (y + 1) * half)
+                at = (((2 * x + y) * 2 + g % 2) * 2 + g // 2) * rows
+                staged[c, at : at + half, :] = part0[src, :].astype(BF16)
+                staged[c, at + half : at + rows, :] = part1[src, :].astype(BF16)
+    size = staged.shape[1]
+    send[0:size, :] = staged[1 - core]
+    keep[...] = staged[core]
+    wp = mm_nt(dz0, cw[0, 0:width, :]).astype(BF16)
+    wx = mm_nt(dz0, cw[0, width:, :])
+    zero = jnp.zeros((near, width), F32)
+    own_out[...] = ga[...] + wx[:t, :] + jnp.concatenate([wp[near:t, :].astype(F32), zero], axis=0)
+    back_out[...] = (
+        outer[t:, :].astype(F32) + wx[t:, :] + jnp.concatenate([wp[t + near :, :].astype(F32), zero], axis=0)
+    ).astype(BF16)
+    send[size : size + near, :] = wp[0:near, :]
+    send[size + near :, :] = wp[t : t + near, :]
+
+
+def total_of(*refs):
+    total = refs[0][...].astype(F32)
+    for ref in refs[1:]:
+        total = total + ref[...].astype(F32)
+    return total
+
+
+def split_quarters(total, mine, by_y, by_x, by_both, staged):
+    _, x, _ = here()
+    q = 2 * x + lax.axis_index("dp")
+    staged[...] = total.reshape(staged.shape)
+    mine[...] = staged[q]
+    for k, out in ((1, by_y), (2, by_x), (3, by_both)):
+        out[...] = staged[lax.bitwise_xor(q, k)].astype(BF16)
+
+
+def res_quarters_kernel(got, kept, *rest):
+    split_quarters(total_of(got, kept), *rest)
+
+
+def conv_quarters_kernel(got, kept, own, back, mine, by_y, by_x, by_both, own_out, back_out, tail_out, staged):
+    size = kept.shape[0]
+    split_quarters(got[0:size, :].astype(F32) + kept[...].astype(F32), mine, by_y, by_x, by_both, staged)
+    t = own.shape[0]
+    near = t // 4
+    _, _, core = here()
+    edge = got[size : size + near, :].astype(F32)
+    deep = got[size + near :, :]
+    own_out[0 : t - near, :] = own[0 : t - near, :]
+    own_out[t - near :, :] = own[t - near :, :] + jnp.where(core == 0, edge, 0.0)
+    back_out[0 : t - near, :] = back[0 : t - near, :]
+    back_out[t - near :, :] = (
+        back[t - near :, :].astype(F32) + jnp.where(core == 0, deep.astype(F32), edge)
+    ).astype(BF16)
+    tail_out[...] = jnp.where(core == 0, jnp.zeros_like(deep), deep)
+
+
+def sum_kernel(*refs):
+    refs[-1][...] = total_of(*refs[:-1]).astype(BF16)
+
+
+def scaled_sum_kernel(factor, *refs):
+    refs[-1][...] = (total_of(*refs[:-1]) * factor).astype(BF16)
+
+
+def halves_kernel(bit, *refs):
+    send, keep, staged = refs[-3:]
+    g, _, _ = here()
+    mine = lax.rem(g // (1 << bit), 2)
+    staged[...] = total_of(*refs[:-3]).reshape(staged.shape)
+    send[...] = staged[1 - mine].astype(BF16)
+    keep[...] = staged[mine]
+
+
+def in_order_kernel(mine, by_y, by_x, by_both, out):
+    _, x, _ = here()
+    q = 2 * x + lax.axis_index("dp")
+    for k, ref in enumerate((mine, by_y, by_x, by_both)):
+        out[lax.bitwise_xor(q, k)] = ref[...]
+
+
+def finish_kernel(mine, other, res_mine, res_other, conv, res):
+    y = lax.axis_index("dp")
+    half = mine.shape[0] // 2
+    for ref, at in ((mine, y), (other, 1 - y)):
+        rows = pl.ds(pl.multiple_of(at * half, half), half)
+        conv[0, rows, :] = ref[0:half, :]
+        conv[1, rows, :] = ref[half:, :]
+    _, _, core = here()
+    eighth = res.shape[1] // 8
+    width, part = res_mine.shape[2], res_mine.shape[2] // 2
+    for ref, c in ((res_mine, core), (res_other, 1 - core)):
+        for q in range(4):
+            rows = pl.ds(pl.multiple_of((4 * c + q) * eighth, eighth), eighth)
+            res[1, rows, 0:width] = ref[q, 0:eighth, :]
+            res[0, rows, 0:width] = ref[q, eighth : 2 * eighth, :]
+            res[1, rows, width:] = ref[q, 2 * eighth :, 0:part]
+            res[0, rows, width:] = ref[q, 2 * eighth :, part:]
+
+
+def finish_signal_kernel(own, come, come_tail, out, done):
+    done[...] = jnp.zeros_like(done)
+    t = own.shape[0]
+    near = come_tail.shape[0]
+    out[0 : t - near, :] = (own[0 : t - near, :] + come[0 : t - near, :].astype(F32)).astype(BF16)
+    out[t - near :, :] = total_of(own.at[t - near :, :], come.at[t - near :, :], come_tail).astype(BF16)
+
+
+def swap(x, distance):
+    return lax.ppermute(x, "tm", [(i, i ^ distance) for i in range(16)])
+
+
+def swap_streams(x):
+    return lax.ppermute(x, "dp", [(0, 1), (1, 0)])
+
+
+def swap_both(x, distance):
+    route = [(16 * y + i, 16 * (1 - y) + (i ^ distance)) for y in range(2) for i in range(16)]
+    return lax.ppermute(x, ("dp", "tm"), route)
+
+
+def shift(x, distance):
+    return lax.ppermute(x, "tm", [(i, i + distance) for i in range(16) if 0 <= i + distance < 16])
+
+
+def body(signal, conv_weight, res_weight, grad_out, skip_cotangent):
+    s_dev, t, width = signal.shape
+    gated = res_weight.shape[1]
+    near = t // 4
+    half = width // 16
+    res_rows = 3 * gated // 8
+    factor = float(s_dev * t * 32) ** (-0.5)
+
+    sig = signal[0]
+    far = shift(sig, 2)
+    tail4 = shift(sig[t - near :, :], 4)
+    cw, rw, sig, grad, skip = load(conv_weight, res_weight, sig, grad_out[0], skip_cotangent[0])
+    (edge_in,) = call(pack_halo_kernel, [shaped((3 * near, width))], sig, far, tail4, name="pack_halo")
+    edge_in = swap(edge_in, 1)
+
+    rsend, rkeep, a, b, x1, dz1, outer, ga = call(
+        forward_and_outer_kernel,
+        [
+            shaped((4, res_rows, width)), shaped((4, res_rows, width)),
+            shaped((2 * t, gated), F32), shaped((2 * t, gated), F32), shaped((2 * t, width)),
+            shaped((t, width)), shaped((2 * t, width)), shaped((t, width), F32),
+        ],
+        sig, far, edge_in, cw, rw, grad, skip,
+        scratch=[pltpu.VMEM((2, 4, res_rows, width), BF16)], vmem=12, name="forward_and_outer",
+    )
+    rgot = swap(rsend, 1)
+    size = 16 * 2 * half
+    csend, ckeep, own, back = call(
+        inner_kernel,
+        [
+            shaped((size + 2 * near, width)), shaped((size, width)), shaped((t, width), F32), shaped((t, width)),
+        ],
+        sig, far, edge_in, a, b, x1, dz1, outer, ga, cw, rw, skip,
+        scratch=[pltpu.VMEM((2, size, width), BF16)], vmem=12, flops=2_000_000_000, name="inner",
+    )
+    cgot = swap(csend, 1)
+
+    def around(by_y, by_x, by_both):
+        return swap_streams(by_y), swap(by_x, 2), swap_both(by_both, 2)
+
+    def halves(bit, shape, terms, after, name):
+        return call(
+            functools.partial(halves_kernel, bit), [shaped(shape[1:]), shaped(shape[1:], F32)], *terms,
+            after=after, scratch=[pltpu.VMEM(shape, F32)], name=name,
+        )
+
+    res = shaped((res_rows, width))
+    rmine, *rsend = call(
+        res_quarters_kernel, [shaped((res_rows, width), F32), res, res, res], rgot, rkeep,
+        after=(csend,), scratch=[pltpu.VMEM((4, res_rows, width), F32)], name="res_quarters",
+    )
+    rterms = (rmine,) + around(*rsend)
+    part = shaped((size // 4, width))
+    cmine, by_y, by_x, by_both, own, back, tail = call(
+        conv_quarters_kernel,
+        [shaped(part.shape, F32), part, part, part, shaped((t, width), F32), shaped((t, width)), shaped((near, width))],
+        cgot, ckeep, own, back,
+        after=(rmine,), scratch=[pltpu.VMEM((4, size // 4, width), F32)], name="conv_quarters",
+    )
+    cterms = (cmine,) + around(by_y, by_x, by_both)
+    come = shift(back, -2)
+    come_tail = shift(tail, -4)
+    (rsum,) = call(sum_kernel, [res], *rterms, after=(cmine,), name="res_sum_xy")
+    rgot = swap(rsum, 4)
+    (rsum,) = call(sum_kernel, [res], rsum, rgot, name="res_sum_z1")
+    rgot = swap(rsum, 8)
+    csend, ckeep = halves(0, (2, 4 * half, width), cterms, (rsum, come, come_tail), "conv_z1")
+    cgot = swap(csend, 4)
+    (quarter,) = call(
+        functools.partial(scaled_sum_kernel, factor), [res], rsum, rgot, after=(csend,), name="res_sum_z2"
+    )
+    rparts = (quarter,) + around(quarter, quarter, quarter)
+    csend, ckeep = halves(1, (2, 2 * half, width), (ckeep, cgot), (quarter,), "conv_z2")
+    cgot = swap(csend, 8)
+    (ordered,) = call(in_order_kernel, [shaped((4, res_rows, width))], *rparts, after=(csend,), name="res_in_order")
+    rgot = swap(ordered, 1)
+    input_grad, done = call(
+        finish_signal_kernel, [shaped((t, width)), shaped((8, 128), F32)], own, come, come_tail,
+        after=(csend,), name="finish_signal",
+    )
+    (mine,) = call(
+        functools.partial(scaled_sum_kernel, factor), [shaped((2 * half, width))], ckeep, cgot,
+        after=(ordered, done), name="conv_scaled",
+    )
+    other = swap_streams(mine)
+    conv_grad, res_grad = call(
+        finish_kernel, [shaped((2, 2 * half, width)), shaped(res_weight.shape)], mine, other, ordered, rgot,
+        name="finish",
+    )
+    return (input_grad.reshape(s_dev, t, width), conv_grad, res_grad)
+
+
 def solution(mesh):
     in_specs = (P("dp", "tm", None), P(), P(), P("dp", "tm", None), P("dp", "tm", None))
     out_specs = (P("dp", "tm", None), P(None, "tm", None), P())
-    return jax.shard_map(body, mesh=mesh, in_specs=in_specs, out_specs=out_specs, check_vma=False)
+    chosen = body if mesh.shape["dp"] == 2 and mesh.shape["tm"] == 16 else general_body
+    return jax.shard_map(chosen, mesh=mesh, in_specs=in_specs, out_specs=out_specs, check_vma=False)

time: 217 us -> 68.2 us (0.31)
  waiting for transfers between devices: 171 us -> 24.9 us
  starting transfers between devices: 10.8 us -> 33.1 us
  between operations: 15.7 us -> 0.77 us
  matrix products: 9.99 us -> 0 us
  Pallas kernels: 0 us -> 8.34 us
  other arithmetic: 6.16 us -> 0 us
  local copies, waits for them, and re-layouts: 3.26 us -> 0.76 us
    reduce_scatter x2 -> x0, waiting for transfers between devices: 110 us -> none  [reduce_conv(): lax.psum_scatter(lax.dot_general(cat_rows, dz, (((0,), (0,)), ((), ())),...]
    psum x2 -> x0, waiting for transfers between devices: 48.9 us -> none  [the longest x1 27.4 us: body(): res_total = lax.psum(jnp.stack(res_parts), ('dp', 'tm'))]
    ppermute x4 -> x22, starting transfers between devices: 10.6 us -> 33.1 us  [the longest x11 14.5 us: swap(): return lax.ppermute(x, 'tm', [(i, i ^ distance) for i in range(16)])]
    ppermute x4 -> x22, waiting for transfers between devices: 11.4 us -> 24.9 us  [the longest x11 12 us: swap(): return lax.ppermute(x, 'tm', [(i, i ^ distance) for i in range(16)])]
    dot_general x11 -> x0, matrix products: 9.99 us -> none  [the longest x2 3.57 us: reduce_conv(): lax.dot_general(cat_rows, dz, (((0,), (0,)), ((), ())), preferred_element...]
    pallas_call x0 -> x15, Pallas kernels: none -> 8.34 us  [the longest x14 6.48 us: call(): pl.pallas_call(run, out_shape=outs, in_specs=[in_vmem] * n_args + [pl.Blo...]
    convert_element_type x4 -> x0, other arithmetic: 4.14 us -> none  [the longest x1 2.39 us: body(): res_grad = (res_total * factor).astype(jnp.bfloat16)]
  transfers between devices with their start and end apart: 8 -> 22, of which waited for: 7 -> 12; matrix products, arithmetic and copies ran while one was open for 6% -> 0% of each run, Pallas kernels for 0% -> 5%
where the time goes in v2:
time: 68.2 us; the launch traced here: 67.9 us
  starting transfers between devices  33.1 us (49%)
  waiting for transfers between devices  24.9 us (37%)
  Pallas kernels  8.34 us (12%)
  between operations  0.77 us (1%)
  local copies, waits for them, and re-layouts  0.76 us (1%)
    ppermute x11, starting transfers between devices, swap(): return lax.ppermute(x, 'tm', [(i, i ^ distance) for i in range(16)])  14.5 us
    ppermute x11, waiting for transfers between devices, swap(): return lax.ppermute(x, 'tm', [(i, i ^ distance) for i in range(16)])  12 us
    ppermute x4, starting transfers between devices, shift(): lax.ppermute(x, 'tm', [(i, i + distance) for i in range(16) if 0 <= i + d...  10.9 us
    pallas_call x14, Pallas kernels, call(): pl.pallas_call(run, out_shape=outs, in_specs=[in_vmem] * n_args + [pl.Blo...  6.48 us
    ppermute x4, waiting for transfers between devices, shift(): lax.ppermute(x, 'tm', [(i, i + distance) for i in range(16) if 0 <= i + d...  5.41 us
    ppermute x4, starting transfers between devices, swap_streams(): return lax.ppermute(x, 'dp', [(0, 1), (1, 0)])  5.32 us
    ppermute x3, waiting for transfers between devices, swap_both(): return lax.ppermute(x, ('dp', 'tm'), route)  4.32 us
    ppermute x4, waiting for transfers between devices, swap_streams(): return lax.ppermute(x, 'dp', [(0, 1), (1, 0)])  3.22 us
  transfers between devices with their start and end apart: 22, of which 12 were waited for; matrix products, arithmetic and copies ran while one was open for 0% of the time, Pallas kernels for 5%

profile of v2, /device:TPU:0, one launch (start us, length us, event | category | flops | bytes accessed | tf_op | source)
XLA Modules:
  0.0 67.9 jit_solution(248414817627916362)
XLA Ops:
  0.6 0.8 %slice_bitcast_fusion = bf16[32,512]{1,0:T(8,128)(2,1)S(1)} fusion(bf16[1,128,512]{2,1,0:T(8,128)(2,1)} %param.5), kind=kLoop, calls=%fused_computation | loop fusion | bytes 65536 | tf_op jit(solution)/shard_map/slice | solution.py:395
  1.4 4.9 %collective-permute-start.1 = (bf16[32,512]{1,0:T(8,128)(2,1)S(1)}, bf16[32,512]{1,0:T(8,128)(2,1)S(1)}, u32[]{:S(2)}, u32[]{:S(2)}) collective-permute-start(bf16[32,512]{1,0:T(8,128)(2,1)S(1)} %slice_bitcast_fusion), channel_id=1, source_target_pairs={{0,4},{1,5},{2,6},{3,7},{4,8},{5,9},{6,10},{7,11},{8,12},{9,13},{1... | collective-permute-start | bytes 98312 | tf_op jit(solution)/shard_map/ppermute | solution.py:382
  6.3 3.4 %collective-permute-start = (bf16[128,512]{1,0:T(8,128)(2,1)}, bf16[128,512]{1,0:T(8,128)(2,1)S(1)}, u32[]{:S(2)}, u32[]{:S(2)}) collective-permute-start(bf16[128,512]{1,0:T(8,128)(2,1)} %bitcast.6), channel_id=1, source_target_pairs={{0,2},{1,3},{2,4},{3,5},{4,6},{5,7},{6,8},{7,9},{8,10},{9,11},{10,... | collective-permute-start | bytes 393224 | tf_op jit(solution)/shard_map/ppermute | solution.py:382
  9.7 1.9 %load.1 = (bf16[2,1024,512]{2,1,0:T(8,128)(2,1)S(1)}, bf16[2,256,768]{2,1,0:T(8,128)(2,1)S(1)}, bf16[128,512]{1,0:T(8,128)(2,1)S(1)}, bf16[128,512]{1,0:T(8,128)(2,1)S(1)}, bf16[128,256]{1,0:T(8,128)(2,1)S(1)}) custom-call(bf16[2,1024,512]{2,1,0:T(8,128)(2,1)} %refs_0_.1, bf16[2,256,768]{2,1,0:T(8,128)(2,1)} %refs_1_.1, bf16[128,512]{1,0:T(8,128)(2,1)} %bitcast.7, ...), custom_call_target="tpu_custom_call" | custom-call | flops 4000000000 | bytes 6000000 | tf_op jit(solution)/shard_map/load/pallas_call | solution.py:163
  11.6 0.9 %collective-permute-done.refs_1_ = bf16[128,512]{1,0:T(8,128)(2,1)S(1)} collective-permute-done((bf16[128,512]{1,0:T(8,128)(2,1)}, bf16[128,512]{1,0:T(8,128)(2,1)S(1)}, u32[]{:S(2)}, u32[]{:S(2)}) %collective-permute-start) | collective-permute-done | bytes 131104 | tf_op jit(solution)/shard_map/ppermute | solution.py:382
  12.6 1.3 %collective-permute-done.2.refs_2_ = bf16[96,512]{1,0:T(8,128)(2,1)S(1)} collective-permute-done((bf16[96,512]{1,0:T(8,128)(2,1)S(1)}, bf16[96,512]{1,0:T(8,128)(2,1)S(1)}, u32[]{:S(2)}, u32[]{:S(2)}) %collective-permute-start.2) | collective-permute-done | bytes 98336 | tf_op jit(solution)/shard_map/ppermute | solution.py:369
  13.9 1.8 %forward_and_outer.1 = (bf16[4,96,512]{2,1,0:T(8,128)(2,1)S(1)}, bf16[4,96,512]{2,1,0:T(8,128)(2,1)S(1)}, f32[256,256]{1,0:T(8,128)S(1)}, f32[256,256]{1,0:T(8,1...) custom-call(bf16[128,512]{1,0:T(8,128)(2,1)S(1)} %get-tuple-element., ...), custom_call_target="tpu_custom_call" | custom-call | tf_op jit(solution)/shard_map/forward_and_outer/pallas_call | solution.py:131
  15.7 1.9 %inner.1 = (bf16[1088,512]{1,0:T(8,128)(2,1)S(1)}, bf16[1024,512]{1,0:T(8,128)(2,1)S(1)}, f32[128,512]{1,0:T(8,128)S(1)}, bf16[128,512]{1,0:T(8,128)(2,1)S(1)}) custom-call(bf16[128,512]{1,0:T(8,128)(2,1)S(1)} %get-tuple-element.39.refs_0_, bf16[128,512]{1,0:T(8,128)(2,1)S(1)} %collective-permute-done.refs_1_, ...), custom_call_target="tpu_custom_call" | custom-call | flops 2000000000 | tf_op jit(solution)/shard_map/inner/pallas_call | solution.py:131
  18.1 2.8 %collective-permute-done.4.refs_0_ = bf16[4,96,512]{2,1,0:T(8,128)(2,1)S(1)} collective-permute-done((bf16[4,96,512]{2,1,0:T(8,128)(2,1)S(1)}, bf16[4,96,512]{2,1,0:T(8,128)(2,1)S(1)}, u32[]{:S(2)}, u32[]{:S(2)}) %collective-permute-start.4) | collective-permute-done | bytes 393248 | tf_op jit(solution)/shard_map/ppermute | solution.py:369
  21.1 1.6 %collective-permute-start.10 = (bf16[96,512]{1,0:T(8,128)(2,1)S(1)}, bf16[96,512]{1,0:T(8,128)(2,1)S(1)}, u32[]{:S(2)}, u32[]{:S(2)}) collective-permute-start(bf16[96,512]{1,0:T(8,128)(2,1)S(1)} %get-tuple-element.64), channel_id=1, source_target_pairs={{0,16},{16,0},{1,17},{17,1},{2,18},{18,2},{3,19},{19,3},{4,20},{20... | collective-permute-start | bytes 294920 | tf_op jit(solution)/shard_map/ppermute | solution.py:373
  22.7 2.4 %collective-permute-start.11 = (bf16[96,512]{1,0:T(8,128)(2,1)S(1)}, bf16[96,512]{1,0:T(8,128)(2,1)S(1)}, u32[]{:S(2)}, u32[]{:S(2)}) collective-permute-start(bf16[96,512]{1,0:T(8,128)(2,1)S(1)} %get-tuple-element.65), channel_id=1, source_target_pairs={{0,2},{1,3},{2,0},{3,1},{4,6},{5,7},{6,4},{7,5},{8,10},{9,11},{10,... | collective-permute-start | bytes 294920 | tf_op jit(solution)/shard_map/ppermute | solution.py:369
  25.6 1.5 %collective-permute-start.7 = (bf16[256,512]{1,0:T(8,128)(2,1)S(1)}, bf16[256,512]{1,0:T(8,128)(2,1)S(1)}, u32[]{:S(2)}, u32[]{:S(2)}) collective-permute-start(bf16[256,512]{1,0:T(8,128)(2,1)S(1)} %get-tuple-element.61), channel_id=1, source_target_pairs={{0,16},{16,0},{1,17},{17,1},{2,18},{18,2},{3,19},{19,3},{4,20},{20... | collective-permute-start | bytes 786440 | tf_op jit(solution)/shard_map/ppermute | solution.py:373
  27.2 2.0 %collective-permute-start.8 = (bf16[256,512]{1,0:T(8,128)(2,1)S(1)}, bf16[256,512]{1,0:T(8,128)(2,1)S(1)}, u32[]{:S(2)}, u32[]{:S(2)}) collective-permute-start(bf16[256,512]{1,0:T(8,128)(2,1)S(1)} %get-tuple-element.62), channel_id=1, source_target_pairs={{0,2},{1,3},{2,0},{3,1},{4,6},{5,7},{6,4},{7,5},{8,10},{9,11},{10,... | collective-permute-start | bytes 786440 | tf_op jit(solution)/shard_map/ppermute | solution.py:369
  29.4 2.3 %collective-permute-done.12.refs_3_ = bf16[96,512]{1,0:T(8,128)(2,1)S(1)} collective-permute-done((bf16[96,512]{1,0:T(8,128)(2,1)S(1)}, bf16[96,512]{1,0:T(8,128)(2,1)S(1)}, u32[]{:S(2)}, u32[]{:S(2)}) %collective-permute-start.12) | collective-permute-done | bytes 98336 | tf_op jit(solution)/shard_map/ppermute | solution.py:378
  31.8 2.0 %collective-permute-start.13 = (bf16[96,512]{1,0:T(8,128)(2,1)S(1)}, bf16[96,512]{1,0:T(8,128)(2,1)S(1)}, u32[]{:S(2)}, u32[]{:S(2)}) collective-permute-start(bf16[96,512]{1,0:T(8,128)(2,1)S(1)} %res_sum_xy.1.refs_0_), channel_id=1, source_target_pairs={{0,4},{1,5},{2,6},{3,7},{4,0},{5,1},{6,2},{7,3},{8,12},{9,13},{10,... | collective-permute-start | bytes 294920 | tf_op jit(solution)/shard_map/ppermute | solution.py:369
  33.8 1.3 %collective-permute-start.5 = (bf16[128,512]{1,0:T(8,128)(2,1)S(1)}, bf16[128,512]{1,0:T(8,128)(2,1)S(1)}, u32[]{:S(2)}, u32[]{:S(2)}) collective-permute-start(bf16[128,512]{1,0:T(8,128)(2,1)S(1)} %get-tuple-element.58), channel_id=1, source_target_pairs={{2,0},{3,1},{4,2},{5,3},{6,4},{7,5},{8,6},{9,7},{10,8},{11,9},{12,... | collective-permute-start | bytes 393224 | tf_op jit(solution)/shard_map/ppermute | solution.py:382
  35.1 2.0 %collective-permute-done.13.refs_1_ = bf16[96,512]{1,0:T(8,128)(2,1)S(1)} collective-permute-done((bf16[96,512]{1,0:T(8,128)(2,1)S(1)}, bf16[96,512]{1,0:T(8,128)(2,1)S(1)}, u32[]{:S(2)}, u32[]{:S(2)}) %collective-permute-start.13) | collective-permute-done | bytes 98336 | tf_op jit(solution)/shard_map/ppermute | solution.py:369
  37.0 1.3 %collective-permute-start.6 = (bf16[32,512]{1,0:T(8,128)(2,1)S(1)}, bf16[32,512]{1,0:T(8,128)(2,1)S(1)}, u32[]{:S(2)}, u32[]{:S(2)}) collective-permute-start(bf16[32,512]{1,0:T(8,128)(2,1)S(1)} %get-tuple-element.59), channel_id=1, source_target_pairs={{4,0},{5,1},{6,2},{7,3},{8,4},{9,5},{10,6},{11,7},{12,8},{13,9},{1... | collective-permute-start | bytes 98312 | tf_op jit(solution)/shard_map/ppermute | solution.py:382
  38.3 4.5 %collective-permute-done.6.refs_6_.refs_2_ = bf16[32,512]{1,0:T(8,128)(2,1)S(1)} collective-permute-done((bf16[32,512]{1,0:T(8,128)(2,1)S(1)}, bf16[32,512]{1,0:T(8,128)(2,1)S(1)}, u32[]{:S(2)}, u32[]{:S(2)}) %collective-permute-start.6) | collective-permute-done | bytes 32800 | tf_op jit(solution)/shard_map/ppermute | solution.py:382
  42.8 3.2 %collective-permute-start.15 = (bf16[96,512]{1,0:T(8,128)(2,1)S(1)}, bf16[96,512]{1,0:T(8,128)(2,1)S(1)}, u32[]{:S(2)}, u32[]{:S(2)}) collective-permute-start(bf16[96,512]{1,0:T(8,128)(2,1)S(1)} %res_sum_z1.1.refs_4_.refs_0_), channel_id=1, source_target_pairs={{0,8},{1,9},{2,10},{3,11},{4,12},{5,13},{6,14},{7,15},{8,0},{9,1},... | collective-permute-start | bytes 294920 | tf_op jit(solution)/shard_map/ppermute | solution.py:369
  46.2 0.9 %collective-permute-start.14 = (bf16[128,512]{1,0:T(8,128)(2,1)S(1)}, bf16[128,512]{1,0:T(8,128)(2,1)S(1)}, u32[]{:S(2)}, u32[]{:S(2)}) collective-permute-start(bf16[128,512]{1,0:T(8,128)(2,1)S(1)} %get-tuple-element.68.refs_2_), channel_id=1, source_target_pairs={{0,4},{1,5},{2,6},{3,7},{4,0},{5,1},{6,2},{7,3},{8,12},{9,13},{10,... | collective-permute-start | bytes 393224 | tf_op jit(solution)/shard_map/ppermute | solution.py:369
  47.1 1.6 %collective-permute-done.15.refs_1_ = bf16[96,512]{1,0:T(8,128)(2,1)S(1)} collective-permute-done((bf16[96,512]{1,0:T(8,128)(2,1)S(1)}, bf16[96,512]{1,0:T(8,128)(2,1)S(1)}, u32[]{:S(2)}, u32[]{:S(2)}) %collective-permute-start.15) | collective-permute-done | bytes 98336 | tf_op jit(solution)/shard_map/ppermute | solution.py:369
  48.8 2.2 %collective-permute-start.19 = (bf16[96,512]{1,0:T(8,128)(2,1)S(1)}, bf16[96,512]{1,0:T(8,128)(2,1)S(1)}, u32[]{:S(2)}, u32[]{:S(2)}) collective-permute-start(bf16[96,512]{1,0:T(8,128)(2,1)S(1)} %res_sum_z2.1.refs_2_.refs_0_), channel_id=1, source_target_pairs={{0,18},{1,19},{2,16},{3,17},{4,22},{5,23},{6,20},{7,21},{8,26},{9,... | collective-permute-start | bytes 294920 | tf_op jit(solution)/shard_map/ppermute | solution.py:378
  50.9 1.4 %collective-permute-start.18 = (bf16[96,512]{1,0:T(8,128)(2,1)S(1)}, bf16[96,512]{1,0:T(8,128)(2,1)S(1)}, u32[]{:S(2)}, u32[]{:S(2)}) collective-permute-start(bf16[96,512]{1,0:T(8,128)(2,1)S(1)} %res_sum_z2.1.refs_2_.refs_0_), channel_id=1, source_target_pairs={{0,2},{1,3},{2,0},{3,1},{4,6},{5,7},{6,4},{7,5},{8,10},{9,11},{10,... | collective-permute-start | bytes 294920 | tf_op jit(solution)/shard_map/ppermute | solution.py:369
  52.4 2.0 %collective-permute-done.19.refs_3_ = bf16[96,512]{1,0:T(8,128)(2,1)S(1)} collective-permute-done((bf16[96,512]{1,0:T(8,128)(2,1)S(1)}, bf16[96,512]{1,0:T(8,128)(2,1)S(1)}, u32[]{:S(2)}, u32[]{:S(2)}) %collective-permute-start.19) | collective-permute-done | bytes 98336 | tf_op jit(solution)/shard_map/ppermute | solution.py:378
  54.3 1.6 %collective-permute-done.18.refs_2_ = bf16[96,512]{1,0:T(8,128)(2,1)S(1)} collective-permute-done((bf16[96,512]{1,0:T(8,128)(2,1)S(1)}, bf16[96,512]{1,0:T(8,128)(2,1)S(1)}, u32[]{:S(2)}, u32[]{:S(2)}) %collective-permute-start.18) | collective-permute-done | bytes 98336 | tf_op jit(solution)/shard_map/ppermute | solution.py:369
  56.0 1.0 %collective-permute-done.17.refs_1_ = bf16[96,512]{1,0:T(8,128)(2,1)S(1)} collective-permute-done((bf16[96,512]{1,0:T(8,128)(2,1)S(1)}, bf16[96,512]{1,0:T(8,128)(2,1)S(1)}, u32[]{:S(2)}, u32[]{:S(2)}) %collective-permute-start.17) | collective-permute-done | bytes 98336 | tf_op jit(solution)/shard_map/ppermute | solution.py:373
  57.1 2.1 %collective-permute-start.16 = (bf16[64,512]{1,0:T(8,128)(2,1)S(1)}, bf16[64,512]{1,0:T(8,128)(2,1)S(1)}, u32[]{:S(2)}, u32[]{:S(2)}) collective-permute-start(bf16[64,512]{1,0:T(8,128)(2,1)S(1)} %get-tuple-element.69.refs_3_.refs_4_), channel_id=1, source_target_pairs={{0,8},{1,9},{2,10},{3,11},{4,12},{5,13},{6,14},{7,15},{8,0},{9,1},... | collective-permute-start | bytes 196616 | tf_op jit(solution)/shard_map/ppermute | solution.py:369
  59.8 2.7 %collective-permute-done.16.refs_1_ = bf16[64,512]{1,0:T(8,128)(2,1)S(1)} collective-permute-done((bf16[64,512]{1,0:T(8,128)(2,1)S(1)}, bf16[64,512]{1,0:T(8,128)(2,1)S(1)}, u32[]{:S(2)}, u32[]{:S(2)}) %collective-permute-start.16) | collective-permute-done | bytes 65568 | tf_op jit(solution)/shard_map/ppermute | solution.py:369
  62.5 2.2 %collective-permute-start.20 = (bf16[64,512]{1,0:T(8,128)(2,1)S(1)}, bf16[64,512]{1,0:T(8,128)(2,1)S(1)}, u32[]{:S(2)}, u32[]{:S(2)}) collective-permute-start(bf16[64,512]{1,0:T(8,128)(2,1)S(1)} %conv_scaled.1.refs_0_), channel_id=1, source_target_pairs={{0,16},{16,0},{1,17},{17,1},{2,18},{18,2},{3,19},{19,3},{4,20},{20... | collective-permute-start | bytes 196616 | tf_op jit(solution)/shard_map/ppermute | solution.py:373
  64.7 2.2 %collective-permute-done.20.refs_1_ = bf16[64,512]{1,0:T(8,128)(2,1)S(1)} collective-permute-done((bf16[64,512]{1,0:T(8,128)(2,1)S(1)}, bf16[64,512]{1,0:T(8,128)(2,1)S(1)}, u32[]{:S(2)}, u32[]{:S(2)}) %collective-permute-start.20) | collective-permute-done | bytes 65568 | tf_op jit(solution)/shard_map/ppermute | solution.py:373
  66.9 1.0 %finish.1 = (bf16[2,64,512]{2,1,0:T(8,128)(2,1)}, bf16[2,256,768]{2,1,0:T(8,128)(2,1)}) custom-call(bf16[64,512]{1,0:T(8,128)(2,1)S(1)} %conv_scaled.1.refs_0_, bf16[64,512]{1,0:T(8,128)(2,1)S(1)} %collective-permute-done.20.refs_1_, bf16[4,96,512]{2,1,0:T(8,128)(2,1)S(1)} %res_in_order.1.refs_2_, bf16[4,96,512]{2,1,0:T(8,128)(2,1)S(1)} %collective-permute-done.21.refs_3_), custom_call_target="tpu_custom_call" | custom-call | tf_op jit(solution)/shard_map/finish/pallas_call | solution.py:131
  (28 shorter events, 2.7 us)
Async XLA Ops:
  1.4 10.2 %collective-permute-start.1 = (bf16[32,512]{1,0:T(8,128)(2,1)S(1)}, bf16[32,512]{1,0:T(8,128)(2,1)S(1)}, u32[]{:S(2)}, u32[]{:S(2)}) collective-permute-start(bf16[32,512]{1,0:T(8,128)(2,1)S(1)} %slice_bitcast_fusion), channel_id=1, source_target_pairs={{0,4},{1,5},{2,6},{3,7},{4,8},{5,9},{6,10},{7,11},{8,12},{9,13},{1... | collective-permute-start | bytes 98312 | tf_op jit(solution)/shard_map/ppermute | solution.py:382
  6.3 6.2 %collective-permute-start = (bf16[128,512]{1,0:T(8,128)(2,1)}, bf16[128,512]{1,0:T(8,128)(2,1)S(1)}, u32[]{:S(2)}, u32[]{:S(2)}) collective-permute-start(bf16[128,512]{1,0:T(8,128)(2,1)} %bitcast.6), channel_id=1, source_target_pairs={{0,2},{1,3},{2,4},{3,5},{4,6},{5,7},{6,8},{7,9},{8,10},{9,11},{10,... | collective-permute-start | bytes 393224 | tf_op jit(solution)/shard_map/ppermute | solution.py:382
  12.6 1.3 %collective-permute-start.2 = (bf16[96,512]{1,0:T(8,128)(2,1)S(1)}, bf16[96,512]{1,0:T(8,128)(2,1)S(1)}, u32[]{:S(2)}, u32[]{:S(2)}) collective-permute-start(bf16[96,512]{1,0:T(8,128)(2,1)S(1)} %pack_halo.1), channel_id=1, source_target_pairs={{0,1},{1,0},{2,3},{3,2},{4,5},{5,4},{6,7},{7,6},{8,9},{9,8},{10,11... | collective-permute-start | bytes 294920 | tf_op jit(solution)/shard_map/ppermute | solution.py:369
  17.6 7.6 %collective-permute-start.3 = (bf16[1088,512]{1,0:T(8,128)(2,1)S(1)}, bf16[1088,512]{1,0:T(8,128)(2,1)S(1)}, u32[]{:S(2)}, u32[]{:S(2)}) collective-permute-start(bf16[1088,512]{1,0:T(8,128)(2,1)S(1)} %get-tuple-element.50.refs_2_), channel_id=1, source_target_pairs={{0,1},{1,0},{2,3},{3,2},{4,5},{5,4},{6,7},{7,6},{8,9},{9,8},{10,11... | collective-permute-start | bytes 3342344 | tf_op jit(solution)/shard_map/ppermute | solution.py:369
  17.8 3.2 %collective-permute-start.4 = (bf16[4,96,512]{2,1,0:T(8,128)(2,1)S(1)}, bf16[4,96,512]{2,1,0:T(8,128)(2,1)S(1)}, u32[]{:S(2)}, u32[]{:S(2)}) collective-permute-start(bf16[4,96,512]{2,1,0:T(8,128)(2,1)S(1)} %get-tuple-element.54), channel_id=1, source_target_pairs={{0,1},{1,0},{2,3},{3,2},{4,5},{5,4},{6,7},{7,6},{8,9},{9,8},{10,11... | collective-permute-start | bytes 1179656 | tf_op jit(solution)/shard_map/ppermute | solution.py:369
  21.1 8.1 %collective-permute-start.10 = (bf16[96,512]{1,0:T(8,128)(2,1)S(1)}, bf16[96,512]{1,0:T(8,128)(2,1)S(1)}, u32[]{:S(2)}, u32[]{:S(2)}) collective-permute-start(bf16[96,512]{1,0:T(8,128)(2,1)S(1)} %get-tuple-element.64), channel_id=1, source_target_pairs={{0,16},{16,0},{1,17},{17,1},{2,18},{18,2},{3,19},{19,3},{4,20},{20... | collective-permute-start | bytes 294920 | tf_op jit(solution)/shard_map/ppermute | solution.py:373
  22.7 6.7 %collective-permute-start.11 = (bf16[96,512]{1,0:T(8,128)(2,1)S(1)}, bf16[96,512]{1,0:T(8,128)(2,1)S(1)}, u32[]{:S(2)}, u32[]{:S(2)}) collective-permute-start(bf16[96,512]{1,0:T(8,128)(2,1)S(1)} %get-tuple-element.65), channel_id=1, source_target_pairs={{0,2},{1,3},{2,0},{3,1},{4,6},{5,7},{6,4},{7,5},{8,10},{9,11},{10,... | collective-permute-start | bytes 294920 | tf_op jit(solution)/shard_map/ppermute | solution.py:369
  25.1 6.6 %collective-permute-start.12 = (bf16[96,512]{1,0:T(8,128)(2,1)S(1)}, bf16[96,512]{1,0:T(8,128)(2,1)S(1)}, u32[]{:S(2)}, u32[]{:S(2)}) collective-permute-start(bf16[96,512]{1,0:T(8,128)(2,1)S(1)} %get-tuple-element.66), channel_id=1, source_target_pairs={{0,18},{1,19},{2,16},{3,17},{4,22},{5,23},{6,20},{7,21},{8,26},{9,... | collective-permute-start | bytes 294920 | tf_op jit(solution)/shard_map/ppermute | solution.py:378
  25.6 20.4 %collective-permute-start.7 = (bf16[256,512]{1,0:T(8,128)(2,1)S(1)}, bf16[256,512]{1,0:T(8,128)(2,1)S(1)}, u32[]{:S(2)}, u32[]{:S(2)}) collective-permute-start(bf16[256,512]{1,0:T(8,128)(2,1)S(1)} %get-tuple-element.61), channel_id=1, source_target_pairs={{0,16},{16,0},{1,17},{17,1},{2,18},{18,2},{3,19},{19,3},{4,20},{20... | collective-permute-start | bytes 786440 | tf_op jit(solution)/shard_map/ppermute | solution.py:373
  27.2 18.8 %collective-permute-start.8 = (bf16[256,512]{1,0:T(8,128)(2,1)S(1)}, bf16[256,512]{1,0:T(8,128)(2,1)S(1)}, u32[]{:S(2)}, u32[]{:S(2)}) collective-permute-start(bf16[256,512]{1,0:T(8,128)(2,1)S(1)} %get-tuple-element.62), channel_id=1, source_target_pairs={{0,2},{1,3},{2,0},{3,1},{4,6},{5,7},{6,4},{7,5},{8,10},{9,11},{10,... | collective-permute-start | bytes 786440 | tf_op jit(solution)/shard_map/ppermute | solution.py:369
  29.2 16.8 %collective-permute-start.9 = (bf16[256,512]{1,0:T(8,128)(2,1)S(1)}, bf16[256,512]{1,0:T(8,128)(2,1)S(1)}, u32[]{:S(2)}, u32[]{:S(2)}) collective-permute-start(bf16[256,512]{1,0:T(8,128)(2,1)S(1)} %get-tuple-element.63), channel_id=1, source_target_pairs={{0,18},{1,19},{2,16},{3,17},{4,22},{5,23},{6,20},{7,21},{8,26},{9,... | collective-permute-start | bytes 786440 | tf_op jit(solution)/shard_map/ppermute | solution.py:378
  31.8 5.2 %collective-permute-start.13 = (bf16[96,512]{1,0:T(8,128)(2,1)S(1)}, bf16[96,512]{1,0:T(8,128)(2,1)S(1)}, u32[]{:S(2)}, u32[]{:S(2)}) collective-permute-start(bf16[96,512]{1,0:T(8,128)(2,1)S(1)} %res_sum_xy.1.refs_0_), channel_id=1, source_target_pairs={{0,4},{1,5},{2,6},{3,7},{4,0},{5,1},{6,2},{7,3},{8,12},{9,13},{10,... | collective-permute-start | bytes 294920 | tf_op jit(solution)/shard_map/ppermute | solution.py:369
  33.8 12.2 %collective-permute-start.5 = (bf16[128,512]{1,0:T(8,128)(2,1)S(1)}, bf16[128,512]{1,0:T(8,128)(2,1)S(1)}, u32[]{:S(2)}, u32[]{:S(2)}) collective-permute-start(bf16[128,512]{1,0:T(8,128)(2,1)S(1)} %get-tuple-element.58), channel_id=1, source_target_pairs={{2,0},{3,1},{4,2},{5,3},{6,4},{7,5},{8,6},{9,7},{10,8},{11,9},{12,... | collective-permute-start | bytes 393224 | tf_op jit(solution)/shard_map/ppermute | solution.py:382
  37.0 5.8 %collective-permute-start.6 = (bf16[32,512]{1,0:T(8,128)(2,1)S(1)}, bf16[32,512]{1,0:T(8,128)(2,1)S(1)}, u32[]{:S(2)}, u32[]{:S(2)}) collective-permute-start(bf16[32,512]{1,0:T(8,128)(2,1)S(1)} %get-tuple-element.59), channel_id=1, source_target_pairs={{4,0},{5,1},{6,2},{7,3},{8,4},{9,5},{10,6},{11,7},{12,8},{13,9},{1... | collective-permute-start | bytes 98312 | tf_op jit(solution)/shard_map/ppermute | solution.py:382
  42.8 5.9 %collective-permute-start.15 = (bf16[96,512]{1,0:T(8,128)(2,1)S(1)}, bf16[96,512]{1,0:T(8,128)(2,1)S(1)}, u32[]{:S(2)}, u32[]{:S(2)}) collective-permute-start(bf16[96,512]{1,0:T(8,128)(2,1)S(1)} %res_sum_z1.1.refs_4_.refs_0_), channel_id=1, source_target_pairs={{0,8},{1,9},{2,10},{3,11},{4,12},{5,13},{6,14},{7,15},{8,0},{9,1},... | collective-permute-start | bytes 294920 | tf_op jit(solution)/shard_map/ppermute | solution.py:369
  46.2 6.1 %collective-permute-start.14 = (bf16[128,512]{1,0:T(8,128)(2,1)S(1)}, bf16[128,512]{1,0:T(8,128)(2,1)S(1)}, u32[]{:S(2)}, u32[]{:S(2)}) collective-permute-start(bf16[128,512]{1,0:T(8,128)(2,1)S(1)} %get-tuple-element.68.refs_2_), channel_id=1, source_target_pairs={{0,4},{1,5},{2,6},{3,7},{4,0},{5,1},{6,2},{7,3},{8,12},{9,13},{10,... | collective-permute-start | bytes 393224 | tf_op jit(solution)/shard_map/ppermute | solution.py:369
  48.8 5.6 %collective-permute-start.19 = (bf16[96,512]{1,0:T(8,128)(2,1)S(1)}, bf16[96,512]{1,0:T(8,128)(2,1)S(1)}, u32[]{:S(2)}, u32[]{:S(2)}) collective-permute-start(bf16[96,512]{1,0:T(8,128)(2,1)S(1)} %res_sum_z2.1.refs_2_.refs_0_), channel_id=1, source_target_pairs={{0,18},{1,19},{2,16},{3,17},{4,22},{5,23},{6,20},{7,21},{8,26},{9,... | collective-permute-start | bytes 294920 | tf_op jit(solution)/shard_map/ppermute | solution.py:378
  50.9 5.0 %collective-permute-start.18 = (bf16[96,512]{1,0:T(8,128)(2,1)S(1)}, bf16[96,512]{1,0:T(8,128)(2,1)S(1)}, u32[]{:S(2)}, u32[]{:S(2)}) collective-permute-start(bf16[96,512]{1,0:T(8,128)(2,1)S(1)} %res_sum_z2.1.refs_2_.refs_0_), channel_id=1, source_target_pairs={{0,2},{1,3},{2,0},{3,1},{4,6},{5,7},{6,4},{7,5},{8,10},{9,11},{10,... | collective-permute-start | bytes 294920 | tf_op jit(solution)/shard_map/ppermute | solution.py:369
  52.3 4.6 %collective-permute-start.17 = (bf16[96,512]{1,0:T(8,128)(2,1)S(1)}, bf16[96,512]{1,0:T(8,128)(2,1)S(1)}, u32[]{:S(2)}, u32[]{:S(2)}) collective-permute-start(bf16[96,512]{1,0:T(8,128)(2,1)S(1)} %res_sum_z2.1.refs_2_.refs_0_), channel_id=1, source_target_pairs={{0,16},{16,0},{1,17},{17,1},{2,18},{18,2},{3,19},{19,3},{4,20},{20... | collective-permute-start | bytes 294920 | tf_op jit(solution)/shard_map/ppermute | solution.py:373
  57.0 10.0 %collective-permute-start.21 = (bf16[4,96,512]{2,1,0:T(8,128)(2,1)S(1)}, bf16[4,96,512]{2,1,0:T(8,128)(2,1)S(1)}, u32[]{:S(2)}, u32[]{:S(2)}) collective-permute-start(bf16[4,96,512]{2,1,0:T(8,128)(2,1)S(1)} %res_in_order.1.refs_2_), channel_id=1, source_target_pairs={{0,1},{1,0},{2,3},{3,2},{4,5},{5,4},{6,7},{7,6},{8,9},{9,8},{10,11... | collective-permute-start | bytes 1179656 | tf_op jit(solution)/shard_map/ppermute | solution.py:369
  57.1 5.4 %collective-permute-start.16 = (bf16[64,512]{1,0:T(8,128)(2,1)S(1)}, bf16[64,512]{1,0:T(8,128)(2,1)S(1)}, u32[]{:S(2)}, u32[]{:S(2)}) collective-permute-start(bf16[64,512]{1,0:T(8,128)(2,1)S(1)} %get-tuple-element.69.refs_3_.refs_4_), channel_id=1, source_target_pairs={{0,8},{1,9},{2,10},{3,11},{4,12},{5,13},{6,14},{7,15},{8,0},{9,1},... | collective-permute-start | bytes 196616 | tf_op jit(solution)/shard_map/ppermute | solution.py:369
  62.5 4.4 %collective-permute-start.20 = (bf16[64,512]{1,0:T(8,128)(2,1)S(1)}, bf16[64,512]{1,0:T(8,128)(2,1)S(1)}, u32[]{:S(2)}, u32[]{:S(2)}) collective-permute-start(bf16[64,512]{1,0:T(8,128)(2,1)S(1)} %conv_scaled.1.refs_0_), channel_id=1, source_target_pairs={{0,16},{16,0},{1,17},{17,1},{2,18},{18,2},{3,19},{19,3},{4,20},{20... | collective-permute-start | bytes 196616 | tf_op jit(solution)/shard_map/ppermute | solution.py:373

commit v3 on v2

v3 whole, which is shorter than its diff:
```python
import functools

import jax
import jax.numpy as jnp
from jax import lax
from jax.experimental import pallas as pl
from jax.experimental.pallas import tpu as pltpu
from jax.sharding import PartitionSpec as P

F32 = jnp.float32
BF16 = jnp.bfloat16


def passed_along(block, axis, distance):
    devices = range(lax.axis_size(axis))
    route = [(i - distance, i) for i in devices if i - distance in devices]
    return lax.ppermute(block, axis, route)


def gate_gradients(dh, z, gated):
    tf = jnp.tanh(z[:, :gated])
    sg = jax.nn.sigmoid(z[:, gated:])
    return jnp.concatenate([dh * sg * (1.0 - tf * tf), dh * tf * sg * (1.0 - sg)], axis=1).astype(
        jnp.bfloat16
    )


def reduce_conv(cat_rows, dz):
    piece = lax.psum_scatter(
        lax.dot_general(cat_rows, dz, (((0,), (0,)), ((), ())), preferred_element_type=jnp.float32),
        "tm",
        scatter_dimension=0,
        tiled=True,
    )
    return lax.psum(piece, "dp")


def general_body(signal, conv_weight, res_weight, grad_out, skip_cotangent):
    s_dev, t_dev, width = signal.shape
    gated = res_weight.shape[1]
    near = t_dev // 4
    slabs = lax.axis_size("tm") // 8
    count_rows = s_dev * t_dev
    factor = float(count_rows * lax.axis_size("dp") * lax.axis_size("tm")) ** (-0.5)

    def delayed(x, layer):
        if layer == 0:
            got = passed_along(x[:, t_dev - near :, :], "tm", 1)
            return jnp.concatenate([got, x[:, : t_dev - near, :]], axis=1)
        return passed_along(x, "tm", slabs)

    def shifted_rows(dpast, layer):
        if layer == 0:
            got = passed_along(dpast[:, :near, :], "tm", -1)
            return jnp.concatenate([dpast[:, near:, :], got], axis=1)
        return passed_along(dpast, "tm", -slabs)

    x = signal
    cats = []
    zvals = []
    hvals = []
    for layer in range(2):
        past = delayed(x, layer)
        cat_rows = jnp.concatenate([past, x], axis=2).reshape(count_rows, 2 * width)
        z = jnp.dot(cat_rows, conv_weight[layer], preferred_element_type=jnp.float32)
        h = (jnp.tanh(z[:, :gated]) * jax.nn.sigmoid(z[:, gated:])).astype(jnp.bfloat16)
        cats.append(cat_rows)
        zvals.append(z)
        hvals.append(h)
        if layer == 0:
            resid = jnp.dot(h, res_weight[0][:, :width], preferred_element_type=jnp.float32)
            x = (
                (x.reshape(count_rows, width).astype(jnp.float32) + resid)
                .astype(jnp.bfloat16)
                .reshape(s_dev, t_dev, width)
            )
    grad = grad_out.reshape(count_rows, width).astype(jnp.float32)
    skip_rows = skip_cotangent.reshape(count_rows, -1)
    conv_parts = [None, None]
    res_parts = [None, None]
    dz_kept = [None, None]
    for layer in (1, 0):
        outer = jnp.concatenate([grad.astype(jnp.bfloat16), skip_rows], axis=1)
        dh = lax.dot_general(
            outer, res_weight[layer], (((1,), (1,)), ((), ())), preferred_element_type=jnp.float32
        )
        dz = gate_gradients(dh, zvals[layer], gated)
        wcat = lax.dot_general(
            dz, conv_weight[layer], (((1,), (1,)), ((), ())), preferred_element_type=jnp.float32
        )
        dpast = wcat[:, :width].astype(jnp.bfloat16).reshape(s_dev, t_dev, width)
        moved = shifted_rows(dpast, layer).reshape(count_rows, width)
        grad = grad + wcat[:, width:] + moved.astype(jnp.float32)
        res_local = lax.dot_general(
            hvals[layer], outer, (((0,), (0,)), ((), ())), preferred_element_type=jnp.float32
        )
        dz_kept[layer] = dz
        res_parts[layer] = res_local
    for layer in range(2):
        conv_parts[layer] = reduce_conv(cats[layer], dz_kept[layer])
    res_total = lax.psum(jnp.stack(res_parts), ("dp", "tm"))
    input_grad = grad.astype(jnp.bfloat16).reshape(s_dev, t_dev, width)
    conv_grad = (jnp.stack(conv_parts) * factor).astype(jnp.bfloat16)
    res_grad = (res_total * factor).astype(jnp.bfloat16)
    return (input_grad, conv_grad, res_grad)


def mm(a, b):
    return jnp.dot(a, b, preferred_element_type=F32)


def mm_nt(a, b):
    return lax.dot_general(a, b, (((1,), (1,)), ((), ())), preferred_element_type=F32)


def mm_tn(a, b):
    return lax.dot_general(a, b, (((0,), (0,)), ((), ())), preferred_element_type=F32)


def shaped(shape, dtype=BF16):
    return jax.ShapeDtypeStruct(shape, dtype)


def call(kernel, outs, *args, after=(), scratch=(), flops=0, nbytes=0, vmem=8, name=None):
    n_args = len(args)

    def run(*refs):
        kernel(*refs[:n_args], *refs[n_args + len(after) :])

    in_vmem = pl.BlockSpec(memory_space=pltpu.VMEM)
    return pl.pallas_call(
        run,
        out_shape=outs,
        in_specs=[in_vmem] * n_args + [pl.BlockSpec(memory_space=pl.ANY)] * len(after),
        out_specs=[in_vmem] * len(outs),
        scratch_shapes=list(scratch),
        compiler_params=pltpu.CompilerParams(vmem_limit_bytes=vmem * 1024 * 1024),
        cost_estimate=pl.CostEstimate(flops=flops, bytes_accessed=nbytes, transcendentals=0),
        name=name,
    )(*args, *after)


def place(tm):
    return tm // 4, lax.rem(tm // 2, 2), lax.rem(tm, 2)


def here():
    return place(lax.axis_index("tm"))


def load_kernel(cw, rw, sig, grad, skip, cw_out, rw_out, own_out, tail_out, sems):
    t, width = sig.shape
    near = tail_out.shape[0]
    pairs = (
        (sig.at[t - near :, :], tail_out),
        (sig, own_out.at[:, 0:width]),
        (grad, own_out.at[:, width : 2 * width]),
        (skip, own_out.at[:, 2 * width :]),
        (cw, cw_out),
        (rw, rw_out),
    )
    copies = [pltpu.make_async_copy(src, dst, sems.at[i]) for i, (src, dst) in enumerate(pairs)]
    for copy in copies:
        copy.start()
    for copy in copies:
        copy.wait()


def load(cw, rw, sig, grad, skip):
    t, width = sig.shape
    in_hbm = [pltpu.with_memory_space_constraint(a, pltpu.HBM) for a in (cw, rw, sig, grad, skip)]
    return pl.pallas_call(
        load_kernel,
        out_shape=[
            pltpu.VMEM(cw.shape, BF16), pltpu.VMEM(rw.shape, BF16),
            pltpu.VMEM((t, 2 * width + skip.shape[1]), BF16), pltpu.VMEM((t // 4, width), BF16),
        ],
        in_specs=[pl.BlockSpec(memory_space=pltpu.HBM)] * 5,
        out_specs=[pl.BlockSpec(memory_space=pltpu.VMEM)] * 4,
        scratch_shapes=[pltpu.SemaphoreType.DMA((6,))],
        compiler_params=pltpu.CompilerParams(vmem_limit_bytes=8 * 1024 * 1024),
        cost_estimate=pl.CostEstimate(flops=4_000_000_000, bytes_accessed=6_000_000, transcendentals=0),
        name="load",
    )(*in_hbm)


def pack_halo_kernel(far, tail4, out):
    t = far.shape[0]
    out[0:t, :] = far[...]
    out[t:, :] = tail4[...]


def split_quarters(staged, mine, by_y, by_x, by_both):
    _, x, core = here()
    q = 2 * x + lax.axis_index("dp")
    mine[...] = staged[core, q]
    for k, out in ((1, by_y), (2, by_x), (3, by_both)):
        out[...] = staged[core, lax.bitwise_xor(q, k)]


def forward_and_outer_kernel(
    own, own_other, halo, halo_other, cw, rw,
    mine, by_y, by_x, by_both, x_out, a_out, b_out, x1_out, dz_out, o_out, ga_out, es_out,
    staged, gin, skin,
):
    t = own.shape[0]
    near = t // 4
    width = x_out.shape[1]
    gated = rw.shape[1]
    _, _, core = here()
    for a, h, c in ((own, halo, core), (own_other, halo_other, 1 - core)):
        rows = pl.ds(pl.multiple_of(c * t, t), t)
        x_out[pl.ds(pl.multiple_of(near + c * t, near), t), :] = h[0:t, :]
        x_out[pl.ds(pl.multiple_of(near + (2 + c) * t, near), t), :] = a[:, 0:width]
        gin[rows, :] = a[:, width : 2 * width]
        skin[rows, :] = a[:, 2 * width :]
    x_out[0:near, :] = jnp.where(core == 1, halo[t:, :], halo_other[t:, :])
    x0 = x_out[near:, :]
    z0 = mm(x_out[0 : 4 * t, :], cw[0, 0:width, :]) + mm(x0, cw[0, width:, :])
    tf = jnp.tanh(z0[:, :gated])
    sg = jax.nn.sigmoid(z0[:, gated:])
    h0 = (tf * sg).astype(BF16)
    a_out[...] = sg * (1.0 - tf * tf)
    b_out[...] = tf * sg * (1.0 - sg)
    x1 = (x0.astype(F32) + mm(h0, rw[0, :, 0:width])).astype(BF16)
    x1_out[...] = x1
    z1 = mm(x1[0 : 2 * t, :], cw[1, 0:width, :]) + mm(x1[2 * t :, :], cw[1, width:, :])
    tf = jnp.tanh(z1[:, :gated])
    sg = jax.nn.sigmoid(z1[:, gated:])
    h1 = (tf * sg).astype(BF16)
    g2 = gin[...]
    sk = skin[...]
    e1 = mm_nt(g2, rw[1, :, 0:width]) + mm_nt(sk, rw[1, :, width:])
    dz1 = jnp.concatenate([e1 * sg * (1.0 - tf * tf), e1 * tf * sg * (1.0 - sg)], axis=1).astype(BF16)
    dz_out[...] = dz1
    dpast = mm_nt(dz1, cw[1, 0:width, :]).astype(BF16)
    ga = g2.astype(F32) + mm_nt(dz1, cw[1, width:, :])
    ga_out[...] = ga
    outer = jnp.concatenate([dpast, ga.astype(BF16)], axis=0)
    o_out[...] = outer
    es_out[...] = mm_nt(sk, rw[0, :, width:])
    skips = jnp.concatenate([mm_tn(h1, sk), mm_tn(h0[2 * t :, :], sk)], axis=1)
    eighth = gated // 8
    for which, part in enumerate((mm_tn(h1, g2), mm_tn(h0, outer), skips)):
        for c in range(2):
            for q in range(4):
                rows = slice((4 * c + q) * eighth, (4 * c + q + 1) * eighth)
                staged[c, q, which * eighth : (which + 1) * eighth, :] = part[rows, :].astype(BF16)
    split_quarters(staged, mine, by_y, by_x, by_both)


def inner_kernel(
    xin, a, b, x1, dz1, outer, ga, es, cw, rw,
    mine, by_y, by_x, by_both, own_out, back_out, tail_out,
    staged, dz,
):
    width = xin.shape[1]
    t = dz1.shape[0] // 2
    near = t // 4
    _, _, core = here()
    e0 = mm_nt(outer[...], rw[0, :, 0:width])
    e0 = jnp.concatenate([e0[: 2 * t, :], e0[2 * t :, :] + es[...]], axis=0)
    dz0 = jnp.concatenate([e0 * a[...], e0 * b[...]], axis=1).astype(BF16)
    dz[0 : 4 * t, :] = dz0
    dz[4 * t :, :] = jnp.zeros((near, width), BF16)
    half = width // 16
    rows = 2 * half
    blocks = width // rows
    for base, part0, part1 in (
        (0, mm_tn(xin[0 : 4 * t, :], dz0), mm_tn(x1[0 : 2 * t, :], dz1[...])),
        (blocks, mm_tn(xin[near:, :], dz0), mm_tn(x1[2 * t :, :], dz1[...])),
    ):
        for block in range(blocks):
            g, x, c = (base + block) // 4, (base + block) // 2 % 2, (base + block) % 2
            for y in range(2):
                src = slice(block * rows + y * half, block * rows + (y + 1) * half)
                staged[c, 2 * x + y, g, 0:half, :] = part0[src, :].astype(BF16)
                staged[c, 2 * x + y, g, half:, :] = part1[src, :].astype(BF16)
    split_quarters(staged, mine, by_y, by_x, by_both)
    at = pl.multiple_of(core * t, t)
    long = t + near
    back = dz[pl.ds(at, long), :]
    here_dz = dz[pl.ds(2 * t + at, long), :]
    both = jnp.concatenate([back, here_dz], axis=0)
    wp = mm_nt(both, cw[0, 0:width, :]).astype(BF16)
    wx = mm_nt(both, cw[0, width:, :])
    back_out[...] = (outer[pl.ds(at, t), :].astype(F32) + wx[0:t, :] + wp[near:long, :].astype(F32)).astype(BF16)
    own_out[...] = ga[pl.ds(at, t), :] + wx[long : long + t, :] + wp[long + near :, :].astype(F32)
    tail_out[...] = wp[0:near, :]


def total_of(*refs):
    total = refs[0][...].astype(F32)
    for ref in refs[1:]:
        total = total + ref[...].astype(F32)
    return total


def sum_kernel(*refs):
    refs[-1][...] = total_of(*refs[:-1]).astype(BF16)


def scaled_sum_kernel(factor, *refs):
    refs[-1][...] = (total_of(*refs[:-1]) * factor).astype(BF16)


def groups_kernel(mine, by_y, by_x, by_both, keep, send1, send2, send3, staged):
    g, _, _ = here()
    staged[...] = total_of(mine, by_y, by_x, by_both)
    keep[...] = staged[g]
    for k, out in ((1, send1), (2, send2), (3, send3)):
        out[...] = staged[lax.bitwise_xor(g, k)].astype(BF16)


def in_order_kernel(mine, by_y, by_x, by_both, out):
    _, x, _ = here()
    q = 2 * x + lax.axis_index("dp")
    for k, ref in enumerate((mine, by_y, by_x, by_both)):
        out[lax.bitwise_xor(q, k)] = ref[...]


def finish_kernel(mine, other, res_mine, res_other, conv, res):
    y = lax.axis_index("dp")
    half = mine.shape[0] // 2
    for ref, at in ((mine, y), (other, 1 - y)):
        rows = pl.ds(pl.multiple_of(at * half, half), half)
        conv[0, rows, :] = ref[0:half, :]
        conv[1, rows, :] = ref[half:, :]
    _, _, core = here()
    eighth = res.shape[1] // 8
    width, part = res_mine.shape[2], res_mine.shape[2] // 2
    for ref, c in ((res_mine, core), (res_other, 1 - core)):
        for q in range(4):
            rows = pl.ds(pl.multiple_of((4 * c + q) * eighth, eighth), eighth)
            res[1, rows, 0:width] = ref[q, 0:eighth, :]
            res[0, rows, 0:width] = ref[q, eighth : 2 * eighth, :]
            res[1, rows, width:] = ref[q, 2 * eighth :, 0:part]
            res[0, rows, width:] = ref[q, 2 * eighth :, part:]


def finish_signal_kernel(own, come, come_tail, out, done):
    done[...] = jnp.zeros_like(done)
    t = own.shape[0]
    near = come_tail.shape[0]
    out[0 : t - near, :] = (own[0 : t - near, :] + come[0 : t - near, :].astype(F32)).astype(BF16)
    out[t - near :, :] = total_of(own.at[t - near :, :], come.at[t - near :, :], come_tail).astype(BF16)


def swap(x, distance):
    return lax.ppermute(x, "tm", [(i, i ^ distance) for i in range(16)])


def swap_streams(x):
    return lax.ppermute(x, "dp", [(0, 1), (1, 0)])


def swap_both(x, distance):
    route = [(16 * y + i, 16 * (1 - y) + (i ^ distance)) for y in range(2) for i in range(16)]
    return lax.ppermute(x, ("dp", "tm"), route)


def shift(x, distance):
    return lax.ppermute(x, "tm", [(i, i + distance) for i in range(16) if 0 <= i + distance < 16])


def body(signal, conv_weight, res_weight, grad_out, skip_cotangent):
    s_dev, t, width = signal.shape
    gated = res_weight.shape[1]
    near = t // 4
    half = width // 16
    res_rows = 3 * gated // 8
    factor = float(s_dev * t * 32) ** (-0.5)

    far = shift(signal[0], 2)
    cw, rw, own, tail = load(conv_weight, res_weight, signal[0], grad_out[0], skip_cotangent[0])
    own_other = swap(own, 1)
    tail4 = shift(tail, 4)
    (halo,) = call(pack_halo_kernel, [shaped((t + near, width))], far, tail4, name="pack_halo")
    halo_other = swap(halo, 1)

    res = shaped((res_rows, width))
    *rsplit, xin, a, b, x1, dz1, outer, ga, es = call(
        forward_and_outer_kernel,
        [
            res, res, res, res,
            shaped((4 * t + near, width)), shaped((4 * t, gated), F32), shaped((4 * t, gated), F32),
            shaped((4 * t, width)), shaped((2 * t, width)), shaped((4 * t, width)), shaped((2 * t, width), F32),
            shaped((2 * t, gated), F32),
        ],
        own, own_other, halo, halo_other, cw, rw,
        scratch=[
            pltpu.VMEM((2, 4, res_rows, width), BF16), pltpu.VMEM((2 * t, width), BF16),
            pltpu.VMEM((2 * t, gated), BF16),
        ],
        vmem=16, name="forward_and_outer",
    )
    piece = (2 * half, width)
    part = shaped((4,) + piece)
    *csplit, own, back, tail = call(
        inner_kernel,
        [part, part, part, part, shaped((t, width), F32), shaped((t, width)), shaped((near, width))],
        xin, a, b, x1, dz1, outer, ga, es, cw, rw,
        scratch=[pltpu.VMEM((2, 4, 4) + piece, BF16), pltpu.VMEM((4 * t + near, width), BF16)],
        vmem=16, flops=2_000_000_000, name="inner",
    )

    def around(by_y, by_x, by_both):
        return swap_streams(by_y), swap(by_x, 2), swap_both(by_both, 2)

    rterms = (rsplit[0],) + around(*rsplit[1:])
    cterms = (csplit[0],) + around(*csplit[1:])
    come = shift(back, -2)
    come_tail = lax.ppermute(tail, "tm", [(i, i - 3) for i in range(4, 16, 2)])
    (rsum,) = call(sum_kernel, [res], *rterms, after=(csplit[0],), name="res_sum_xy")
    rgot = swap(rsum, 4)
    (rsum,) = call(sum_kernel, [res], rsum, rgot, name="res_sum_z1")
    rgot = swap(rsum, 8)
    ckeep, *csend = call(
        groups_kernel, [shaped(piece, F32)] + [shaped(piece)] * 3, *cterms,
        after=(rsum,), scratch=[pltpu.VMEM((4,) + piece, F32)], name="conv_groups",
    )
    cgot = [swap(send, 4 * k) for k, send in zip((1, 2, 3), csend)]
    input_grad, done = call(
        finish_signal_kernel, [shaped((t, width)), shaped((8, 128), F32)], own, come, come_tail,
        after=(ckeep,), name="finish_signal",
    )
    (quarter,) = call(
        functools.partial(scaled_sum_kernel, factor), [res], rsum, rgot, after=(ckeep,), name="res_sum_z2"
    )
    rparts = (quarter,) + around(quarter, quarter, quarter)
    (mine,) = call(
        functools.partial(scaled_sum_kernel, factor), [shaped(piece)], ckeep, *cgot,
        after=(quarter,), name="conv_scaled",
    )
    other = swap_streams(mine)
    (ordered,) = call(in_order_kernel, [shaped((4, res_rows, width))], *rparts, after=(mine, done), name="res_in_order")
    rgot = swap(ordered, 1)
    conv_grad, res_grad = call(
        finish_kernel, [shaped((2,) + piece), shaped(res_weight.shape)], mine, other, ordered, rgot,
        name="finish",
    )
    return (input_grad.reshape(s_dev, t, width), conv_grad, res_grad)


def solution(mesh):
    in_specs = (P("dp", "tm", None), P(), P(), P("dp", "tm", None), P("dp", "tm", None))
    out_specs = (P("dp", "tm", None), P(None, "tm", None), P())
    chosen = body if mesh.shape["dp"] == 2 and mesh.shape["tm"] == 16 else general_body
    return jax.shard_map(chosen, mesh=mesh, in_specs=in_specs, out_specs=out_specs, check_vma=False)
```

time: 68.2 us -> 60.2 us (0.88)
  waiting for transfers between devices: 24.9 us -> 16.8 us
  starting transfers between devices: 33.1 us -> 34.1 us
  local copies, waits for them, and re-layouts: 0.76 us -> 0.01 us
    ppermute x11, waiting for transfers between devices: 12 us -> 7.5 us  [swap(): return lax.ppermute(x, 'tm', [(i, i ^ distance) for i in range(16)])]
    ppermute x4 -> x3, waiting for transfers between devices: 5.41 us -> 1.58 us  [shift(): lax.ppermute(x, 'tm', [(i, i + distance) for i in range(16) if 0 <= i + d...]
    ppermute x3, starting transfers between devices: 2.37 us -> 4.28 us  [swap_both(): return lax.ppermute(x, ('dp', 'tm'), route)]
    ppermute x4 -> x3, starting transfers between devices: 10.9 us -> 9.18 us  [shift(): lax.ppermute(x, 'tm', [(i, i + distance) for i in range(16) if 0 <= i + d...]
    slice x1 -> x0, local copies, waits for them, and re-layouts: 0.76 us -> none  [body(): tail4 = shift(sig[t - near:, :], 4)]
    pallas_call x14 -> x11, Pallas kernels: 6.48 us -> 6.22 us  [call(): pl.pallas_call(run, out_shape=outs, in_specs=[in_vmem] * n_args + [pl.Blo...]
  transfers between devices with their start and end apart: 22 -> 22, of which waited for: 12 -> 6; matrix products, arithmetic and copies ran while one was open for 0% -> 0% of each run, Pallas kernels for 5% -> 5%
where the time goes in v3:
time: 60.2 us; the launch traced here: 60 us
  starting transfers between devices  34.1 us (57%)
  waiting for transfers between devices  16.8 us (28%)
  Pallas kernels  8.25 us (14%)
  between operations  0.8 us (1%)
    ppermute x11, starting transfers between devices, swap(): return lax.ppermute(x, 'tm', [(i, i ^ distance) for i in range(16)])  15 us
    ppermute x3, starting transfers between devices, shift(): lax.ppermute(x, 'tm', [(i, i + distance) for i in range(16) if 0 <= i + d...  9.18 us
    ppermute x11, waiting for transfers between devices, swap(): return lax.ppermute(x, 'tm', [(i, i ^ distance) for i in range(16)])  7.5 us
    pallas_call x11, Pallas kernels, call(): pl.pallas_call(run, out_shape=outs, in_specs=[in_vmem] * n_args + [pl.Blo...  6.22 us
    ppermute x4, starting transfers between devices, swap_streams(): return lax.ppermute(x, 'dp', [(0, 1), (1, 0)])  4.98 us
    ppermute x3, waiting for transfers between devices, swap_both(): return lax.ppermute(x, ('dp', 'tm'), route)  4.33 us
    ppermute x3, starting transfers between devices, swap_both(): return lax.ppermute(x, ('dp', 'tm'), route)  4.28 us
    ppermute x4, waiting for transfers between devices, swap_streams(): return lax.ppermute(x, 'dp', [(0, 1), (1, 0)])  3.35 us
  transfers between devices with their start and end apart: 22, of which 6 were waited for; matrix products, arithmetic and copies ran while one was open for 0% of the time, Pallas kernels for 5%

profile of v3, /device:TPU:0, one launch (start us, length us, event | category | flops | bytes accessed | tf_op | source)
XLA Modules:
  0.0 60.0 jit_solution(7815783330988565381)
XLA Ops:
  0.6 2.0 %load.1 = (bf16[2,1024,512]{2,1,0:T(8,128)(2,1)S(1)}, bf16[2,256,768]{2,1,0:T(8,128)(2,1)S(1)}, bf16[128,1280]{1,0:T(8,128)(2,1)S(1)}, bf16[32,512]{1,0:T(8,128)(2,1)S(1)}) custom-call(bf16[2,1024,512]{2,1,0:T(8,128)(2,1)} %cw.1, bf16[2,256,768]{2,1,0:T(8,128)(2,1)} %rw.1, bf16[128,512]{1,0:T(8,128)(2,1)} %bitcast.5, bf16[128,512]{1,0:T(8,128)(2,1)} %bitcast.4, ...), custom_call_target="tpu_custom_call" | custom-call | flops 4000000000 | bytes 6000000 | tf_op jit(solution)/shard_map/load/pallas_call | solution.py:172
  2.7 0.5 collective-permute-start
  3.2 4.4 %collective-permute-start.1 = (bf16[128,512]{1,0:T(8,128)(2,1)S(1)}, bf16[128,512]{1,0:T(8,128)(2,1)S(1)}, u32[]{:S(2)}, u32[]{:S(2)}) collective-permute-start(bf16[128,512]{1,0:T(8,128)(2,1)S(1)} %bitcast.6), channel_id=1, source_target_pairs={{0,2},{1,3},{2,4},{3,5},{4,6},{5,7},{6,8},{7,9},{8,10},{9,11},{10,... | collective-permute-start | bytes 393224 | tf_op jit(solution)/shard_map/ppermute | solution.py:363
  7.6 3.5 %collective-permute-start.2 = (bf16[32,512]{1,0:T(8,128)(2,1)S(1)}, bf16[32,512]{1,0:T(8,128)(2,1)S(1)}, u32[]{:S(2)}, u32[]{:S(2)}) collective-permute-start(bf16[32,512]{1,0:T(8,128)(2,1)S(1)} %get-tuple-element.35), channel_id=1, source_target_pairs={{0,4},{1,5},{2,6},{3,7},{4,8},{5,9},{6,10},{7,11},{8,12},{9,13},{1... | collective-permute-start | bytes 98312 | tf_op jit(solution)/shard_map/ppermute | solution.py:363
  11.1 1.6 %collective-permute-done.2.refs_1_ = bf16[32,512]{1,0:T(8,128)(2,1)S(1)} collective-permute-done((bf16[32,512]{1,0:T(8,128)(2,1)S(1)}, bf16[32,512]{1,0:T(8,128)(2,1)S(1)}, u32[]{:S(2)}, u32[]{:S(2)}) %collective-permute-start.2) | collective-permute-done | bytes 32800 | tf_op jit(solution)/shard_map/ppermute | solution.py:363
  12.8 1.4 %collective-permute-done.3.refs_3_ = bf16[160,512]{1,0:T(8,128)(2,1)S(1)} collective-permute-done((bf16[160,512]{1,0:T(8,128)(2,1)S(1)}, bf16[160,512]{1,0:T(8,128)(2,1)S(1)}, u32[]{:S(2)}, u32[]{:S(2)}) %collective-permute-start.3) | collective-permute-done | bytes 163872 | tf_op jit(solution)/shard_map/ppermute | solution.py:350
  14.2 2.3 %forward_and_outer.1 = (bf16[96,512]{1,0:T(8,128)(2,1)S(1)}, bf16[96,512]{1,0:T(8,128)(2,1)S(1)}, bf16[96,512]{1,0:T(8,128)(2,1)S(1)}, bf16[96,512]{1,0:T(8,128)...) custom-call(bf16[128,1280]{1,0:T(8,128)(2,1)S(1)} %get-tuple-element, ...), custom_call_target="tpu_custom_call" | custom-call | tf_op jit(solution)/shard_map/forward_and_outer/pallas_call | solution.py:131
  16.5 1.6 %collective-permute-start.9 = (bf16[96,512]{1,0:T(8,128)(2,1)S(1)}, bf16[96,512]{1,0:T(8,128)(2,1)S(1)}, u32[]{:S(2)}, u32[]{:S(2)}) collective-permute-start(bf16[96,512]{1,0:T(8,128)(2,1)S(1)} %get-tuple-element.54), channel_id=1, source_target_pairs={{0,16},{16,0},{1,17},{17,1},{2,18},{18,2},{3,19},{19,3},{4,20},{20... | collective-permute-start | bytes 294920 | tf_op jit(solution)/shard_map/ppermute | solution.py:354
  18.0 1.5 %collective-permute-start.10 = (bf16[96,512]{1,0:T(8,128)(2,1)S(1)}, bf16[96,512]{1,0:T(8,128)(2,1)S(1)}, u32[]{:S(2)}, u32[]{:S(2)}) collective-permute-start(bf16[96,512]{1,0:T(8,128)(2,1)S(1)} %get-tuple-element.55), channel_id=1, source_target_pairs={{0,2},{1,3},{2,0},{3,1},{4,6},{5,7},{6,4},{7,5},{8,10},{9,11},{10,... | collective-permute-start | bytes 294920 | tf_op jit(solution)/shard_map/ppermute | solution.py:350
  19.6 0.4 collective-permute-start.11
  20.0 1.8 %inner.1 = (bf16[4,64,512]{2,1,0:T(8,128)(2,1)S(1)}, bf16[4,64,512]{2,1,0:T(8,128)(2,1)S(1)}, bf16[4,64,512]{2,1,0:T(8,128)(2,1)S(1)}, bf16[4,64,512]{2,1,0:T(8,...) custom-call(bf16[544,512]{1,0:T(8,128)(2,1)S(1)} %get-tuple-element.38.refs_0_, ...), custom_call_target="tpu_custom_call" | custom-call | flops 2000000000 | tf_op jit(solution)/shard_map/inner/pallas_call | solution.py:131
  21.9 1.6 %collective-permute-start.6 = (bf16[4,64,512]{2,1,0:T(8,128)(2,1)S(1)}, bf16[4,64,512]{2,1,0:T(8,128)(2,1)S(1)}, u32[]{:S(2)}, u32[]{:S(2)}) collective-permute-start(bf16[4,64,512]{2,1,0:T(8,128)(2,1)S(1)} %get-tuple-element.50), channel_id=1, source_target_pairs={{0,16},{16,0},{1,17},{17,1},{2,18},{18,2},{3,19},{19,3},{4,20},{20... | collective-permute-start | bytes 786440 | tf_op jit(solution)/shard_map/ppermute | solution.py:354
  23.4 1.5 %collective-permute-start.7 = (bf16[4,64,512]{2,1,0:T(8,128)(2,1)S(1)}, bf16[4,64,512]{2,1,0:T(8,128)(2,1)S(1)}, u32[]{:S(2)}, u32[]{:S(2)}) collective-permute-start(bf16[4,64,512]{2,1,0:T(8,128)(2,1)S(1)} %get-tuple-element.51), channel_id=1, source_target_pairs={{0,2},{1,3},{2,0},{3,1},{4,6},{5,7},{6,4},{7,5},{8,10},{9,11},{10,... | collective-permute-start | bytes 786440 | tf_op jit(solution)/shard_map/ppermute | solution.py:350
  25.0 0.4 collective-permute-start.8
  25.5 2.4 %collective-permute-start.12 = (bf16[96,512]{1,0:T(8,128)(2,1)S(1)}, bf16[96,512]{1,0:T(8,128)(2,1)S(1)}, u32[]{:S(2)}, u32[]{:S(2)}) collective-permute-start(bf16[96,512]{1,0:T(8,128)(2,1)S(1)} %res_sum_xy.1.refs_0_), channel_id=1, source_target_pairs={{0,4},{1,5},{2,6},{3,7},{4,0},{5,1},{6,2},{7,3},{8,12},{9,13},{10,... | collective-permute-start | bytes 294920 | tf_op jit(solution)/shard_map/ppermute | solution.py:350
  27.9 1.3 %collective-permute-start.4 = (bf16[128,512]{1,0:T(8,128)(2,1)S(1)}, bf16[128,512]{1,0:T(8,128)(2,1)S(1)}, u32[]{:S(2)}, u32[]{:S(2)}) collective-permute-start(bf16[128,512]{1,0:T(8,128)(2,1)S(1)} %get-tuple-element.47), channel_id=1, source_target_pairs={{2,0},{3,1},{4,2},{5,3},{6,4},{7,5},{8,6},{9,7},{10,8},{11,9},{12,... | collective-permute-start | bytes 393224 | tf_op jit(solution)/shard_map/ppermute | solution.py:363
  29.2 1.3 %collective-permute-done.12.refs_1_ = bf16[96,512]{1,0:T(8,128)(2,1)S(1)} collective-permute-done((bf16[96,512]{1,0:T(8,128)(2,1)S(1)}, bf16[96,512]{1,0:T(8,128)(2,1)S(1)}, u32[]{:S(2)}, u32[]{:S(2)}) %collective-permute-start.12) | collective-permute-done | bytes 98336 | tf_op jit(solution)/shard_map/ppermute | solution.py:350
  30.5 3.4 %collective-permute-start.16 = (bf16[96,512]{1,0:T(8,128)(2,1)S(1)}, bf16[96,512]{1,0:T(8,128)(2,1)S(1)}, u32[]{:S(2)}, u32[]{:S(2)}) collective-permute-start(bf16[96,512]{1,0:T(8,128)(2,1)S(1)} %res_sum_z1.1.refs_4_.refs_0_), channel_id=1, source_target_pairs={{0,8},{1,9},{2,10},{3,11},{4,12},{5,13},{6,14},{7,15},{8,0},{9,1},... | collective-permute-start | bytes 294920 | tf_op jit(solution)/shard_map/ppermute | solution.py:350
  33.9 4.3 %collective-permute-done.8.refs_3_ = bf16[4,64,512]{2,1,0:T(8,128)(2,1)S(1)} collective-permute-done((bf16[4,64,512]{2,1,0:T(8,128)(2,1)S(1)}, bf16[4,64,512]{2,1,0:T(8,128)(2,1)S(1)}, u32[]{:S(2)}, u32[]{:S(2)}) %collective-permute-start.8) | collective-permute-done | bytes 262176 | tf_op jit(solution)/shard_map/ppermute | solution.py:359
  38.2 0.2 conv_groups.1
  38.4 2.4 %collective-permute-start.13 = (bf16[64,512]{1,0:T(8,128)(2,1)S(1)}, bf16[64,512]{1,0:T(8,128)(2,1)S(1)}, u32[]{:S(2)}, u32[]{:S(2)}) collective-permute-start(bf16[64,512]{1,0:T(8,128)(2,1)S(1)} %get-tuple-element.59), channel_id=1, source_target_pairs={{0,4},{1,5},{2,6},{3,7},{4,0},{5,1},{6,2},{7,3},{8,12},{9,13},{10,... | collective-permute-start | bytes 196616 | tf_op jit(solution)/shard_map/ppermute | solution.py:350
  40.8 0.7 %collective-permute-start.5 = (bf16[32,512]{1,0:T(8,128)(2,1)S(1)}, bf16[32,512]{1,0:T(8,128)(2,1)S(1)}, u32[]{:S(2)}, u32[]{:S(2)}) collective-permute-start(bf16[32,512]{1,0:T(8,128)(2,1)S(1)} %get-tuple-element.48), channel_id=1, source_target_pairs={{4,1},{6,3},{8,5},{10,7},{12,9},{14,11},{20,17},{22,19},{24,21},{2... | collective-permute-start | bytes 98312 | tf_op jit(solution)/shard_map/ppermute | solution.py:413
  41.5 3.4 %collective-permute-start.20 = (bf16[96,512]{1,0:T(8,128)(2,1)S(1)}, bf16[96,512]{1,0:T(8,128)(2,1)S(1)}, u32[]{:S(2)}, u32[]{:S(2)}) collective-permute-start(bf16[96,512]{1,0:T(8,128)(2,1)S(1)} %res_sum_z2.1.refs_4_.refs_0_), channel_id=1, source_target_pairs={{0,18},{1,19},{2,16},{3,17},{4,22},{5,23},{6,20},{7,21},{8,26},{9,... | collective-permute-start | bytes 294920 | tf_op jit(solution)/shard_map/ppermute | solution.py:359
  44.9 0.6 %collective-permute-start.18 = (bf16[96,512]{1,0:T(8,128)(2,1)S(1)}, bf16[96,512]{1,0:T(8,128)(2,1)S(1)}, u32[]{:S(2)}, u32[]{:S(2)}) collective-permute-start(bf16[96,512]{1,0:T(8,128)(2,1)S(1)} %res_sum_z2.1.refs_4_.refs_0_), channel_id=1, source_target_pairs={{0,16},{16,0},{1,17},{17,1},{2,18},{18,2},{3,19},{19,3},{4,20},{20... | collective-permute-start | bytes 294920 | tf_op jit(solution)/shard_map/ppermute | solution.py:354
  45.6 2.2 %collective-permute-start.14 = (bf16[64,512]{1,0:T(8,128)(2,1)S(1)}, bf16[64,512]{1,0:T(8,128)(2,1)S(1)}, u32[]{:S(2)}, u32[]{:S(2)}) collective-permute-start(bf16[64,512]{1,0:T(8,128)(2,1)S(1)} %get-tuple-element.60), channel_id=1, source_target_pairs={{0,8},{1,9},{2,10},{3,11},{4,12},{5,13},{6,14},{7,15},{8,0},{9,1},... | collective-permute-start | bytes 196616 | tf_op jit(solution)/shard_map/ppermute | solution.py:350
  47.7 1.0 %collective-permute-start.15 = (bf16[64,512]{1,0:T(8,128)(2,1)S(1)}, bf16[64,512]{1,0:T(8,128)(2,1)S(1)}, u32[]{:S(2)}, u32[]{:S(2)}) collective-permute-start(bf16[64,512]{1,0:T(8,128)(2,1)S(1)} %get-tuple-element.61), channel_id=1, source_target_pairs={{0,12},{1,13},{2,14},{3,15},{4,8},{5,9},{6,10},{7,11},{8,4},{9,5},... | collective-permute-start | bytes 196616 | tf_op jit(solution)/shard_map/ppermute | solution.py:350
  48.8 0.7 %finish_signal.1 = (bf16[128,512]{1,0:T(8,128)(2,1)}, f32[8,128]{1,0:T(8,128)S(1)}) custom-call(f32[128,512]{1,0:T(8,128)S(1)} %get-tuple-element.46.refs_0_, bf16[128,512]{1,0:T(8,128)(2,1)S(1)} %collective-permute-done.4.refs_1_, bf16[32,512]{1,0:T(8,128)(2,1)S(1)} %collective-permute-done.5.refs_2_, f32[64,512]{1,0:T(8,128)S(1)} %get-tuple-element.57.refs_3_.refs_2_.refs_0_), custom_call_target="tpu_custom_call" | custom-call | tf_op jit(solution)/shard_map/finish_signal/pallas_call | solution.py:131
  49.4 4.8 %collective-permute-done.14.refs_2_ = bf16[64,512]{1,0:T(8,128)(2,1)S(1)} collective-permute-done((bf16[64,512]{1,0:T(8,128)(2,1)S(1)}, bf16[64,512]{1,0:T(8,128)(2,1)S(1)}, u32[]{:S(2)}, u32[]{:S(2)}) %collective-permute-start.14) | collective-permute-done | bytes 65568 | tf_op jit(solution)/shard_map/ppermute | solution.py:350
  54.4 0.1 collective-permute-start.21
  54.4 1.2 %collective-permute-start.17 = (bf16[64,512]{1,0:T(8,128)(2,1)S(1)}, bf16[64,512]{1,0:T(8,128)(2,1)S(1)}, u32[]{:S(2)}, u32[]{:S(2)}) collective-permute-start(bf16[64,512]{1,0:T(8,128)(2,1)S(1)} %conv_scaled.1.refs_4_.refs_0_), channel_id=1, source_target_pairs={{0,16},{16,0},{1,17},{17,1},{2,18},{18,2},{3,19},{19,3},{4,20},{20... | collective-permute-start | bytes 196616 | tf_op jit(solution)/shard_map/ppermute | solution.py:354
  55.6 3.3 %collective-permute-done.17.refs_1_ = bf16[64,512]{1,0:T(8,128)(2,1)S(1)} collective-permute-done((bf16[64,512]{1,0:T(8,128)(2,1)S(1)}, bf16[64,512]{1,0:T(8,128)(2,1)S(1)}, u32[]{:S(2)}, u32[]{:S(2)}) %collective-permute-start.17) | collective-permute-done | bytes 65568 | tf_op jit(solution)/shard_map/ppermute | solution.py:354
  59.0 1.0 %finish.1 = (bf16[2,64,512]{2,1,0:T(8,128)(2,1)}, bf16[2,256,768]{2,1,0:T(8,128)(2,1)}) custom-call(bf16[64,512]{1,0:T(8,128)(2,1)S(1)} %conv_scaled.1.refs_4_.refs_0_, bf16[64,512]{1,0:T(8,128)(2,1)S(1)} %collective-permute-done.17.refs_1_, bf16[4,96,512]{2,1,0:T(8,128)(2,1)S(1)} %res_in_order.1.refs_2_, bf16[4,96,512]{2,1,0:T(8,128)(2,1)S(1)} %collective-permute-done.21.refs_3_), custom_call_target="tpu_custom_call" | custom-call | tf_op jit(solution)/shard_map/finish/pallas_call | solution.py:131
  (26 shorter events, 0.3 us)
Async XLA Ops:
  0.6 2.6 %copy-start = (bf16[1,128,512]{2,1,0:T(8,128)(2,1)S(1)}, bf16[1,128,512]{2,1,0:T(8,128)(2,1)}, u32[]{:S(2)}) copy-start(bf16[1,128,512]{2,1,0:T(8,128)(2,1)} %param.5) | copy-start | bytes 393220
  2.7 11.5 %collective-permute-start = (bf16[128,1280]{1,0:T(8,128)(2,1)S(1)}, bf16[128,1280]{1,0:T(8,128)(2,1)S(1)}, u32[]{:S(2)}, u32[]{:S(2)}) collective-permute-start(bf16[128,1280]{1,0:T(8,128)(2,1)S(1)} %get-tuple-element.34.refs_0_), channel_id=1, source_target_pairs={{0,1},{1,0},{2,3},{3,2},{4,5},{5,4},{6,7},{7,6},{8,9},{9,8},{10,11... | collective-permute-start | bytes 983048 | tf_op jit(solution)/shard_map/ppermute | solution.py:350
  3.2 9.5 %collective-permute-start.1 = (bf16[128,512]{1,0:T(8,128)(2,1)S(1)}, bf16[128,512]{1,0:T(8,128)(2,1)S(1)}, u32[]{:S(2)}, u32[]{:S(2)}) collective-permute-start(bf16[128,512]{1,0:T(8,128)(2,1)S(1)} %bitcast.6), channel_id=1, source_target_pairs={{0,2},{1,3},{2,4},{3,5},{4,6},{5,7},{6,8},{7,9},{8,10},{9,11},{10,... | collective-permute-start | bytes 393224 | tf_op jit(solution)/shard_map/ppermute | solution.py:363
  7.6 5.1 %collective-permute-start.2 = (bf16[32,512]{1,0:T(8,128)(2,1)S(1)}, bf16[32,512]{1,0:T(8,128)(2,1)S(1)}, u32[]{:S(2)}, u32[]{:S(2)}) collective-permute-start(bf16[32,512]{1,0:T(8,128)(2,1)S(1)} %get-tuple-element.35), channel_id=1, source_target_pairs={{0,4},{1,5},{2,6},{3,7},{4,8},{5,9},{6,10},{7,11},{8,12},{9,13},{1... | collective-permute-start | bytes 98312 | tf_op jit(solution)/shard_map/ppermute | solution.py:363
  12.7 1.5 %collective-permute-start.3 = (bf16[160,512]{1,0:T(8,128)(2,1)S(1)}, bf16[160,512]{1,0:T(8,128)(2,1)S(1)}, u32[]{:S(2)}, u32[]{:S(2)}) collective-permute-start(bf16[160,512]{1,0:T(8,128)(2,1)S(1)} %pack_halo.1.refs_2_), channel_id=1, source_target_pairs={{0,1},{1,0},{2,3},{3,2},{4,5},{5,4},{6,7},{7,6},{8,9},{9,8},{10,11... | collective-permute-start | bytes 491528 | tf_op jit(solution)/shard_map/ppermute | solution.py:350
  16.5 8.5 %collective-permute-start.9 = (bf16[96,512]{1,0:T(8,128)(2,1)S(1)}, bf16[96,512]{1,0:T(8,128)(2,1)S(1)}, u32[]{:S(2)}, u32[]{:S(2)}) collective-permute-start(bf16[96,512]{1,0:T(8,128)(2,1)S(1)} %get-tuple-element.54), channel_id=1, source_target_pairs={{0,16},{16,0},{1,17},{17,1},{2,18},{18,2},{3,19},{19,3},{4,20},{20... | collective-permute-start | bytes 294920 | tf_op jit(solution)/shard_map/ppermute | solution.py:354
  18.0 7.4 %collective-permute-start.10 = (bf16[96,512]{1,0:T(8,128)(2,1)S(1)}, bf16[96,512]{1,0:T(8,128)(2,1)S(1)}, u32[]{:S(2)}, u32[]{:S(2)}) collective-permute-start(bf16[96,512]{1,0:T(8,128)(2,1)S(1)} %get-tuple-element.55), channel_id=1, source_target_pairs={{0,2},{1,3},{2,0},{3,1},{4,6},{5,7},{6,4},{7,5},{8,10},{9,11},{10,... | collective-permute-start | bytes 294920 | tf_op jit(solution)/shard_map/ppermute | solution.py:350
  19.6 5.8 %collective-permute-start.11 = (bf16[96,512]{1,0:T(8,128)(2,1)S(1)}, bf16[96,512]{1,0:T(8,128)(2,1)S(1)}, u32[]{:S(2)}, u32[]{:S(2)}) collective-permute-start(bf16[96,512]{1,0:T(8,128)(2,1)S(1)} %get-tuple-element.56), channel_id=1, source_target_pairs={{0,18},{1,19},{2,16},{3,17},{4,22},{5,23},{6,20},{7,21},{8,26},{9,... | collective-permute-start | bytes 294920 | tf_op jit(solution)/shard_map/ppermute | solution.py:359
  21.9 12.0 %collective-permute-start.6 = (bf16[4,64,512]{2,1,0:T(8,128)(2,1)S(1)}, bf16[4,64,512]{2,1,0:T(8,128)(2,1)S(1)}, u32[]{:S(2)}, u32[]{:S(2)}) collective-permute-start(bf16[4,64,512]{2,1,0:T(8,128)(2,1)S(1)} %get-tuple-element.50), channel_id=1, source_target_pairs={{0,16},{16,0},{1,17},{17,1},{2,18},{18,2},{3,19},{19,3},{4,20},{20... | collective-permute-start | bytes 786440 | tf_op jit(solution)/shard_map/ppermute | solution.py:354
  23.4 10.4 %collective-permute-start.7 = (bf16[4,64,512]{2,1,0:T(8,128)(2,1)S(1)}, bf16[4,64,512]{2,1,0:T(8,128)(2,1)S(1)}, u32[]{:S(2)}, u32[]{:S(2)}) collective-permute-start(bf16[4,64,512]{2,1,0:T(8,128)(2,1)S(1)} %get-tuple-element.51), channel_id=1, source_target_pairs={{0,2},{1,3},{2,0},{3,1},{4,6},{5,7},{6,4},{7,5},{8,10},{9,11},{10,... | collective-permute-start | bytes 786440 | tf_op jit(solution)/shard_map/ppermute | solution.py:350
  25.0 13.2 %collective-permute-start.8 = (bf16[4,64,512]{2,1,0:T(8,128)(2,1)S(1)}, bf16[4,64,512]{2,1,0:T(8,128)(2,1)S(1)}, u32[]{:S(2)}, u32[]{:S(2)}) collective-permute-start(bf16[4,64,512]{2,1,0:T(8,128)(2,1)S(1)} %get-tuple-element.52), channel_id=1, source_target_pairs={{0,18},{1,19},{2,16},{3,17},{4,22},{5,23},{6,20},{7,21},{8,26},{9,... | collective-permute-start | bytes 786440 | tf_op jit(solution)/shard_map/ppermute | solution.py:359
  25.5 5.0 %collective-permute-start.12 = (bf16[96,512]{1,0:T(8,128)(2,1)S(1)}, bf16[96,512]{1,0:T(8,128)(2,1)S(1)}, u32[]{:S(2)}, u32[]{:S(2)}) collective-permute-start(bf16[96,512]{1,0:T(8,128)(2,1)S(1)} %res_sum_xy.1.refs_0_), channel_id=1, source_target_pairs={{0,4},{1,5},{2,6},{3,7},{4,0},{5,1},{6,2},{7,3},{8,12},{9,13},{10,... | collective-permute-start | bytes 294920 | tf_op jit(solution)/shard_map/ppermute | solution.py:350
  27.9 17.7 %collective-permute-start.4 = (bf16[128,512]{1,0:T(8,128)(2,1)S(1)}, bf16[128,512]{1,0:T(8,128)(2,1)S(1)}, u32[]{:S(2)}, u32[]{:S(2)}) collective-permute-start(bf16[128,512]{1,0:T(8,128)(2,1)S(1)} %get-tuple-element.47), channel_id=1, source_target_pairs={{2,0},{3,1},{4,2},{5,3},{6,4},{7,5},{8,6},{9,7},{10,8},{11,9},{12,... | collective-permute-start | bytes 393224 | tf_op jit(solution)/shard_map/ppermute | solution.py:363
  30.5 10.9 %collective-permute-start.16 = (bf16[96,512]{1,0:T(8,128)(2,1)S(1)}, bf16[96,512]{1,0:T(8,128)(2,1)S(1)}, u32[]{:S(2)}, u32[]{:S(2)}) collective-permute-start(bf16[96,512]{1,0:T(8,128)(2,1)S(1)} %res_sum_z1.1.refs_4_.refs_0_), channel_id=1, source_target_pairs={{0,8},{1,9},{2,10},{3,11},{4,12},{5,13},{6,14},{7,15},{8,0},{9,1},... | collective-permute-start | bytes 294920 | tf_op jit(solution)/shard_map/ppermute | solution.py:350
  38.4 9.3 %collective-permute-start.13 = (bf16[64,512]{1,0:T(8,128)(2,1)S(1)}, bf16[64,512]{1,0:T(8,128)(2,1)S(1)}, u32[]{:S(2)}, u32[]{:S(2)}) collective-permute-start(bf16[64,512]{1,0:T(8,128)(2,1)S(1)} %get-tuple-element.59), channel_id=1, source_target_pairs={{0,4},{1,5},{2,6},{3,7},{4,0},{5,1},{6,2},{7,3},{8,12},{9,13},{10,... | collective-permute-start | bytes 196616 | tf_op jit(solution)/shard_map/ppermute | solution.py:350
  40.8 4.2 %collective-permute-start.5 = (bf16[32,512]{1,0:T(8,128)(2,1)S(1)}, bf16[32,512]{1,0:T(8,128)(2,1)S(1)}, u32[]{:S(2)}, u32[]{:S(2)}) collective-permute-start(bf16[32,512]{1,0:T(8,128)(2,1)S(1)} %get-tuple-element.48), channel_id=1, source_target_pairs={{4,1},{6,3},{8,5},{10,7},{12,9},{14,11},{20,17},{22,19},{24,21},{2... | collective-permute-start | bytes 98312 | tf_op jit(solution)/shard_map/ppermute | solution.py:413
  41.5 12.8 %collective-permute-start.20 = (bf16[96,512]{1,0:T(8,128)(2,1)S(1)}, bf16[96,512]{1,0:T(8,128)(2,1)S(1)}, u32[]{:S(2)}, u32[]{:S(2)}) collective-permute-start(bf16[96,512]{1,0:T(8,128)(2,1)S(1)} %res_sum_z2.1.refs_4_.refs_0_), channel_id=1, source_target_pairs={{0,18},{1,19},{2,16},{3,17},{4,22},{5,23},{6,20},{7,21},{8,26},{9,... | collective-permute-start | bytes 294920 | tf_op jit(solution)/shard_map/ppermute | solution.py:359
  44.9 9.4 %collective-permute-start.19 = (bf16[96,512]{1,0:T(8,128)(2,1)S(1)}, bf16[96,512]{1,0:T(8,128)(2,1)S(1)}, u32[]{:S(2)}, u32[]{:S(2)}) collective-permute-start(bf16[96,512]{1,0:T(8,128)(2,1)S(1)} %res_sum_z2.1.refs_4_.refs_0_), channel_id=1, source_target_pairs={{0,2},{1,3},{2,0},{3,1},{4,6},{5,7},{6,4},{7,5},{8,10},{9,11},{10,... | collective-permute-start | bytes 294920 | tf_op jit(solution)/shard_map/ppermute | solution.py:350
  44.9 9.4 %collective-permute-start.18 = (bf16[96,512]{1,0:T(8,128)(2,1)S(1)}, bf16[96,512]{1,0:T(8,128)(2,1)S(1)}, u32[]{:S(2)}, u32[]{:S(2)}) collective-permute-start(bf16[96,512]{1,0:T(8,128)(2,1)S(1)} %res_sum_z2.1.refs_4_.refs_0_), channel_id=1, source_target_pairs={{0,16},{16,0},{1,17},{17,1},{2,18},{18,2},{3,19},{19,3},{4,20},{20... | collective-permute-start | bytes 294920 | tf_op jit(solution)/shard_map/ppermute | solution.py:354
  45.6 8.7 %collective-permute-start.14 = (bf16[64,512]{1,0:T(8,128)(2,1)S(1)}, bf16[64,512]{1,0:T(8,128)(2,1)S(1)}, u32[]{:S(2)}, u32[]{:S(2)}) collective-permute-start(bf16[64,512]{1,0:T(8,128)(2,1)S(1)} %get-tuple-element.60), channel_id=1, source_target_pairs={{0,8},{1,9},{2,10},{3,11},{4,12},{5,13},{6,14},{7,15},{8,0},{9,1},... | collective-permute-start | bytes 196616 | tf_op jit(solution)/shard_map/ppermute | solution.py:350
  47.7 6.5 %collective-permute-start.15 = (bf16[64,512]{1,0:T(8,128)(2,1)S(1)}, bf16[64,512]{1,0:T(8,128)(2,1)S(1)}, u32[]{:S(2)}, u32[]{:S(2)}) collective-permute-start(bf16[64,512]{1,0:T(8,128)(2,1)S(1)} %get-tuple-element.61), channel_id=1, source_target_pairs={{0,12},{1,13},{2,14},{3,15},{4,8},{5,9},{6,10},{7,11},{8,4},{9,5},... | collective-permute-start | bytes 196616 | tf_op jit(solution)/shard_map/ppermute | solution.py:350
  54.4 4.6 %collective-permute-start.21 = (bf16[4,96,512]{2,1,0:T(8,128)(2,1)S(1)}, bf16[4,96,512]{2,1,0:T(8,128)(2,1)S(1)}, u32[]{:S(2)}, u32[]{:S(2)}) collective-permute-start(bf16[4,96,512]{2,1,0:T(8,128)(2,1)S(1)} %res_in_order.1.refs_2_), channel_id=1, source_target_pairs={{0,1},{1,0},{2,3},{3,2},{4,5},{5,4},{6,7},{7,6},{8,9},{9,8},{10,11... | collective-permute-start | bytes 1179656 | tf_op jit(solution)/shard_map/ppermute | solution.py:350
  54.4 4.5 %collective-permute-start.17 = (bf16[64,512]{1,0:T(8,128)(2,1)S(1)}, bf16[64,512]{1,0:T(8,128)(2,1)S(1)}, u32[]{:S(2)}, u32[]{:S(2)}) collective-permute-start(bf16[64,512]{1,0:T(8,128)(2,1)S(1)} %conv_scaled.1.refs_4_.refs_0_), channel_id=1, source_target_pairs={{0,16},{16,0},{1,17},{17,1},{2,18},{18,2},{3,19},{19,3},{4,20},{20... | collective-permute-start | bytes 196616 | tf_op jit(solution)/shard_map/ppermute | solution.py:354

commit v4 on v3

--- a/solution.py
+++ b/solution.py
@@ -148,11 +148,9 @@
     return place(lax.axis_index("tm"))
 
 
-def load_kernel(cw, rw, sig, grad, skip, cw_out, rw_out, own_out, tail_out, sems):
-    t, width = sig.shape
-    near = tail_out.shape[0]
+def load_kernel(cw, rw, sig, grad, skip, cw_out, rw_out, own_out, sems):
+    width = sig.shape[1]
     pairs = (
-        (sig.at[t - near :, :], tail_out),
         (sig, own_out.at[:, 0:width]),
         (grad, own_out.at[:, width : 2 * width]),
         (skip, own_out.at[:, 2 * width :]),
@@ -173,11 +171,11 @@
         load_kernel,
         out_shape=[
             pltpu.VMEM(cw.shape, BF16), pltpu.VMEM(rw.shape, BF16),
-            pltpu.VMEM((t, 2 * width + skip.shape[1]), BF16), pltpu.VMEM((t // 4, width), BF16),
+            pltpu.VMEM((t, 2 * width + skip.shape[1]), BF16),
         ],
         in_specs=[pl.BlockSpec(memory_space=pltpu.HBM)] * 5,
-        out_specs=[pl.BlockSpec(memory_space=pltpu.VMEM)] * 4,
-        scratch_shapes=[pltpu.SemaphoreType.DMA((6,))],
+        out_specs=[pl.BlockSpec(memory_space=pltpu.VMEM)] * 3,
+        scratch_shapes=[pltpu.SemaphoreType.DMA((5,))],
         compiler_params=pltpu.CompilerParams(vmem_limit_bytes=8 * 1024 * 1024),
         cost_estimate=pl.CostEstimate(flops=4_000_000_000, bytes_accessed=6_000_000, transcendentals=0),
         name="load",
@@ -186,8 +184,9 @@
 
 def pack_halo_kernel(far, tail4, out):
     t = far.shape[0]
-    out[0:t, :] = far[...]
-    out[t:, :] = tail4[...]
+    slab = lax.axis_index("tm")
+    out[0:t, :] = jnp.where(slab >= 2, far[...], jnp.zeros_like(far))
+    out[t:, :] = jnp.where(slab >= 4, tail4[...], jnp.zeros_like(tail4))
 
 
 def split_quarters(staged, mine, by_y, by_x, by_both):
@@ -281,12 +280,13 @@
     long = t + near
     back = dz[pl.ds(at, long), :]
     here_dz = dz[pl.ds(2 * t + at, long), :]
+    first = mm_nt(dz[0:near, :], cw[0, 0:width, :]).astype(BF16)
     both = jnp.concatenate([back, here_dz], axis=0)
     wp = mm_nt(both, cw[0, 0:width, :]).astype(BF16)
     wx = mm_nt(both, cw[0, width:, :])
     back_out[...] = (outer[pl.ds(at, t), :].astype(F32) + wx[0:t, :] + wp[near:long, :].astype(F32)).astype(BF16)
     own_out[...] = ga[pl.ds(at, t), :] + wx[long : long + t, :] + wp[long + near :, :].astype(F32)
-    tail_out[...] = wp[0:near, :]
+    tail_out[...] = first
 
 
 def total_of(*refs):
@@ -296,8 +296,20 @@
     return total
 
 
-def sum_kernel(*refs):
-    refs[-1][...] = total_of(*refs[:-1]).astype(BF16)
+def sum_xy_kernel(mine, by_y, by_x, by_both, tail, out):
+    rows = mine.shape[0]
+    out[0:rows, :] = total_of(mine, by_y, by_x, by_both).astype(BF16)
+    out[rows:, :] = tail[...]
+
+
+def sum_z1_kernel(rows, mine, got, out):
+    out[0:rows, :] = total_of(mine.at[0:rows, :], got.at[0:rows, :]).astype(BF16)
+    out[rows:, :] = got[rows:, :]
+
+
+def sum_z2_kernel(factor, mine, got, out):
+    rows = out.shape[0]
+    out[...] = (total_of(mine.at[0:rows, :], got.at[0:rows, :]) * factor).astype(BF16)
 
 
 def scaled_sum_kernel(factor, *refs):
@@ -338,12 +350,17 @@
             res[0, rows, width:] = ref[q, 2 * eighth :, part:]
 
 
-def finish_signal_kernel(own, come, come_tail, out, done):
+def finish_signal_kernel(own, come, got1, got2, out, done):
     done[...] = jnp.zeros_like(done)
     t = own.shape[0]
-    near = come_tail.shape[0]
-    out[0 : t - near, :] = (own[0 : t - near, :] + come[0 : t - near, :].astype(F32)).astype(BF16)
-    out[t - near :, :] = total_of(own.at[t - near :, :], come.at[t - near :, :], come_tail).astype(BF16)
+    near = t // 4
+    first = got1.shape[0] - near
+    g, _, core = here()
+    total = own[...] + jnp.where(lax.axis_index("tm") < 14, come[...].astype(F32), 0.0)
+    out[0 : t - near, :] = total[0 : t - near, :].astype(BF16)
+    last = jnp.where(lax.rem(g, 2) == 0, got1[first:, :], got2[first:, :]).astype(F32)
+    last = jnp.where((g < 3) & (core == 1), last, 0.0)
+    out[t - near :, :] = (total[t - near :, :] + last).astype(BF16)
 
 
 def swap(x, distance):
@@ -360,7 +377,7 @@
 
 
 def shift(x, distance):
-    return lax.ppermute(x, "tm", [(i, i + distance) for i in range(16) if 0 <= i + distance < 16])
+    return lax.ppermute(x, "tm", [(i, (i + distance) % 16) for i in range(16)])
 
 
 def body(signal, conv_weight, res_weight, grad_out, skip_cotangent):
@@ -372,9 +389,9 @@
     factor = float(s_dev * t * 32) ** (-0.5)
 
     far = shift(signal[0], 2)
-    cw, rw, own, tail = load(conv_weight, res_weight, signal[0], grad_out[0], skip_cotangent[0])
+    cw, rw, own = load(conv_weight, res_weight, signal[0], grad_out[0], skip_cotangent[0])
     own_other = swap(own, 1)
-    tail4 = shift(tail, 4)
+    tail4 = shift(signal[0, t - near :, :], 4)
     (halo,) = call(pack_halo_kernel, [shaped((t + near, width))], far, tail4, name="pack_halo")
     halo_other = swap(halo, 1)
 
@@ -410,22 +427,22 @@
     rterms = (rsplit[0],) + around(*rsplit[1:])
     cterms = (csplit[0],) + around(*csplit[1:])
     come = shift(back, -2)
-    come_tail = lax.ppermute(tail, "tm", [(i, i - 3) for i in range(4, 16, 2)])
-    (rsum,) = call(sum_kernel, [res], *rterms, after=(csplit[0],), name="res_sum_xy")
-    rgot = swap(rsum, 4)
-    (rsum,) = call(sum_kernel, [res], rsum, rgot, name="res_sum_z1")
-    rgot = swap(rsum, 8)
+    long = shaped((res_rows + near, width))
+    (rsum,) = call(sum_xy_kernel, [long], *rterms, tail, after=(csplit[0],), name="res_sum_xy")
+    rgot1 = swap(rsum, 4)
+    (rsum,) = call(functools.partial(sum_z1_kernel, res_rows), [long], rsum, rgot1, name="res_sum_z1")
+    rgot2 = swap(rsum, 8)
     ckeep, *csend = call(
         groups_kernel, [shaped(piece, F32)] + [shaped(piece)] * 3, *cterms,
         after=(rsum,), scratch=[pltpu.VMEM((4,) + piece, F32)], name="conv_groups",
     )
     cgot = [swap(send, 4 * k) for k, send in zip((1, 2, 3), csend)]
     input_grad, done = call(
-        finish_signal_kernel, [shaped((t, width)), shaped((8, 128), F32)], own, come, come_tail,
+        finish_signal_kernel, [shaped((t, width)), shaped((8, 128), F32)], own, come, rgot1, rgot2,
         after=(ckeep,), name="finish_signal",
     )
     (quarter,) = call(
-        functools.partial(scaled_sum_kernel, factor), [res], rsum, rgot, after=(ckeep,), name="res_sum_z2"
+        functools.partial(sum_z2_kernel, factor), [res], rsum, rgot2, after=(ckeep,), name="res_sum_z2"
     )
     rparts = (quarter,) + around(quarter, quarter, quarter)
     (mine,) = call(

time: 60.2 us -> 55.6 us (0.924)
  starting transfers between devices: 34.1 us -> 25.4 us
  waiting for transfers between devices: 16.8 us -> 20.1 us
  local copies, waits for them, and re-layouts: 0.01 us -> 0.76 us
    ppermute x11, starting transfers between devices: 15 us -> 8.67 us  [swap(): return lax.ppermute(x, 'tm', [(i, i ^ distance) for i in range(16)])]
    ppermute x4 -> x3, starting transfers between devices: 9.83 us -> 7.13 us  [shift(): return lax.ppermute(x, 'tm', [(i, (i + distance) % 16) for i in range(16)])]
    ppermute x4 -> x3, waiting for transfers between devices: 1.59 us -> 4.14 us  [shift(): return lax.ppermute(x, 'tm', [(i, (i + distance) % 16) for i in range(16)])]
    ppermute x11, waiting for transfers between devices: 7.5 us -> 8.78 us  [swap(): return lax.ppermute(x, 'tm', [(i, i ^ distance) for i in range(16)])]
    squeeze x0 -> x1, local copies, waits for them, and re-layouts: none -> 0.76 us  [body(): tail4 = shift(signal[0, t - near:, :], 4)]
  transfers between devices with their start and end apart: 22 -> 21, of which waited for: 6 -> 8; matrix products, arithmetic and copies ran while one was open for 0% -> 1% of each run, Pallas kernels for 5% -> 9%
where the time goes in v4:
time: 55.6 us; the launch traced here: 55.4 us
  starting transfers between devices  25.4 us (46%)
  waiting for transfers between devices  20.1 us (36%)
  Pallas kernels  8.36 us (15%)
  between operations  0.77 us (1%)
  local copies, waits for them, and re-layouts  0.76 us (1%)
    ppermute x11, waiting for transfers between devices, swap(): return lax.ppermute(x, 'tm', [(i, i ^ distance) for i in range(16)])  8.78 us
    ppermute x11, starting transfers between devices, swap(): return lax.ppermute(x, 'tm', [(i, i ^ distance) for i in range(16)])  8.67 us
    ppermute x3, starting transfers between devices, shift(): return lax.ppermute(x, 'tm', [(i, (i + distance) % 16) for i in range(16)])  7.13 us
    pallas_call x11, Pallas kernels, call(): pl.pallas_call(run, out_shape=outs, in_specs=[in_vmem] * n_args + [pl.Blo...  6.39 us
    ppermute x4, starting transfers between devices, swap_streams(): return lax.ppermute(x, 'dp', [(0, 1), (1, 0)])  5.42 us
    ppermute x3, waiting for transfers between devices, swap_both(): return lax.ppermute(x, ('dp', 'tm'), route)  4.24 us
    ppermute x3, starting transfers between devices, swap_both(): return lax.ppermute(x, ('dp', 'tm'), route)  4.2 us
    ppermute x3, waiting for transfers between devices, shift(): return lax.ppermute(x, 'tm', [(i, (i + distance) % 16) for i in range(16)])  4.14 us
  transfers between devices with their start and end apart: 21, of which 8 were waited for; matrix products, arithmetic and copies ran while one was open for 1% of the time, Pallas kernels for 9%

profile of v4, /device:TPU:0, one launch (start us, length us, event | category | flops | bytes accessed | tf_op | source)
XLA Modules:
  0.0 55.4 jit_solution(16522596353570549117)
XLA Ops:
  0.6 3.0 %collective-permute-start.1 = (bf16[128,512]{1,0:T(8,128)(2,1)}, bf16[128,512]{1,0:T(8,128)(2,1)S(1)}, u32[]{:S(2)}, u32[]{:S(2)}) collective-permute-start(bf16[128,512]{1,0:T(8,128)(2,1)} %bitcast.6), channel_id=1, source_target_pairs={{0,2},{1,3},{2,4},{3,5},{4,6},{5,7},{6,8},{7,9},{8,10},{9,11},{10,... | collective-permute-start | bytes 393224 | tf_op jit(solution)/shard_map/ppermute | solution.py:380
  3.6 2.0 %load.1 = (bf16[2,1024,512]{2,1,0:T(8,128)(2,1)S(1)}, bf16[2,256,768]{2,1,0:T(8,128)(2,1)S(1)}, bf16[128,1280]{1,0:T(8,128)(2,1)S(1)}) custom-call(bf16[2,1024,512]{2,1,0:T(8,128)(2,1)} %cw.1, bf16[2,256,768]{2,1,0:T(8,128)(2,1)} %rw.1, bf16[128,512]{1,0:T(8,128)(2,1)} %bitcast.7, bf16[128,512]{1,0:T(8,128)(2,1)} %bitcast.8, bf16[128,256]{1,0:T(8,128)(2,1)} %bitcast.10), custom_call_target="tpu_custom_call" | custom-call | flops 4000000000 | bytes 6000000 | tf_op jit(solution)/shard_map/load/pallas_call | solution.py:170
  5.7 0.8 %slice_bitcast_fusion = bf16[32,512]{1,0:T(8,128)(2,1)S(1)} fusion(bf16[1,128,512]{2,1,0:T(8,128)(2,1)} %param.5), kind=kLoop, calls=%fused_computation | loop fusion | bytes 65536 | tf_op jit(solution)/shard_map/squeeze | solution.py:394
  6.4 1.6 %collective-permute-start.2 = (bf16[32,512]{1,0:T(8,128)(2,1)S(1)}, bf16[32,512]{1,0:T(8,128)(2,1)S(1)}, u32[]{:S(2)}, u32[]{:S(2)}) collective-permute-start(bf16[32,512]{1,0:T(8,128)(2,1)S(1)} %slice_bitcast_fusion), channel_id=1, source_target_pairs={{0,4},{1,5},{2,6},{3,7},{4,8},{5,9},{6,10},{7,11},{8,12},{9,13},{1... | collective-permute-start | bytes 98312 | tf_op jit(solution)/shard_map/ppermute | solution.py:380
  8.0 4.1 %collective-permute-done.2.refs_1_ = bf16[32,512]{1,0:T(8,128)(2,1)S(1)} collective-permute-done((bf16[32,512]{1,0:T(8,128)(2,1)S(1)}, bf16[32,512]{1,0:T(8,128)(2,1)S(1)}, u32[]{:S(2)}, u32[]{:S(2)}) %collective-permute-start.2) | collective-permute-done | bytes 32800 | tf_op jit(solution)/shard_map/ppermute | solution.py:380
  12.3 1.4 %collective-permute-done.3.refs_3_ = bf16[160,512]{1,0:T(8,128)(2,1)S(1)} collective-permute-done((bf16[160,512]{1,0:T(8,128)(2,1)S(1)}, bf16[160,512]{1,0:T(8,128)(2,1)S(1)}, u32[]{:S(2)}, u32[]{:S(2)}) %collective-permute-start.3) | collective-permute-done | bytes 163872 | tf_op jit(solution)/shard_map/ppermute | solution.py:367
  13.7 2.3 %forward_and_outer.1 = (bf16[96,512]{1,0:T(8,128)(2,1)S(1)}, bf16[96,512]{1,0:T(8,128)(2,1)S(1)}, bf16[96,512]{1,0:T(8,128)(2,1)S(1)}, bf16[96,512]{1,0:T(8,128)...) custom-call(bf16[128,1280]{1,0:T(8,128)(2,1)S(1)} %get-tuple-element, ...), custom_call_target="tpu_custom_call" | custom-call | tf_op jit(solution)/shard_map/forward_and_outer/pallas_call | solution.py:131
  15.9 1.6 %collective-permute-start.5 = (bf16[96,512]{1,0:T(8,128)(2,1)S(1)}, bf16[96,512]{1,0:T(8,128)(2,1)S(1)}, u32[]{:S(2)}, u32[]{:S(2)}) collective-permute-start(bf16[96,512]{1,0:T(8,128)(2,1)S(1)} %get-tuple-element.47), channel_id=1, source_target_pairs={{0,16},{16,0},{1,17},{17,1},{2,18},{18,2},{3,19},{19,3},{4,20},{20... | collective-permute-start | bytes 294920 | tf_op jit(solution)/shard_map/ppermute | solution.py:371
  17.5 1.5 %collective-permute-start.6 = (bf16[96,512]{1,0:T(8,128)(2,1)S(1)}, bf16[96,512]{1,0:T(8,128)(2,1)S(1)}, u32[]{:S(2)}, u32[]{:S(2)}) collective-permute-start(bf16[96,512]{1,0:T(8,128)(2,1)S(1)} %get-tuple-element.48), channel_id=1, source_target_pairs={{0,2},{1,3},{2,0},{3,1},{4,6},{5,7},{6,4},{7,5},{8,10},{9,11},{10,... | collective-permute-start | bytes 294920 | tf_op jit(solution)/shard_map/ppermute | solution.py:367
  19.1 0.4 collective-permute-start.7
  19.5 2.0 %inner.1 = (bf16[4,64,512]{2,1,0:T(8,128)(2,1)S(1)}, bf16[4,64,512]{2,1,0:T(8,128)(2,1)S(1)}, bf16[4,64,512]{2,1,0:T(8,128)(2,1)S(1)}, bf16[4,64,512]{2,1,0:T(8,...) custom-call(bf16[544,512]{1,0:T(8,128)(2,1)S(1)} %get-tuple-element.36.refs_0_, ...), custom_call_target="tpu_custom_call" | custom-call | flops 2000000000 | tf_op jit(solution)/shard_map/inner/pallas_call | solution.py:131
  21.5 1.6 %collective-permute-start.10 = (bf16[4,64,512]{2,1,0:T(8,128)(2,1)S(1)}, bf16[4,64,512]{2,1,0:T(8,128)(2,1)S(1)}, u32[]{:S(2)}, u32[]{:S(2)}) collective-permute-start(bf16[4,64,512]{2,1,0:T(8,128)(2,1)S(1)} %get-tuple-element.52), channel_id=1, source_target_pairs={{0,16},{16,0},{1,17},{17,1},{2,18},{18,2},{3,19},{19,3},{4,20},{20... | collective-permute-start | bytes 786440 | tf_op jit(solution)/shard_map/ppermute | solution.py:371
  23.1 1.5 %collective-permute-start.11 = (bf16[4,64,512]{2,1,0:T(8,128)(2,1)S(1)}, bf16[4,64,512]{2,1,0:T(8,128)(2,1)S(1)}, u32[]{:S(2)}, u32[]{:S(2)}) collective-permute-start(bf16[4,64,512]{2,1,0:T(8,128)(2,1)S(1)} %get-tuple-element.53), channel_id=1, source_target_pairs={{0,2},{1,3},{2,0},{3,1},{4,6},{5,7},{6,4},{7,5},{8,10},{9,11},{10,... | collective-permute-start | bytes 786440 | tf_op jit(solution)/shard_map/ppermute | solution.py:367
  24.6 0.4 collective-permute-start.12
  25.1 0.1 collective-permute-start.8
  25.2 5.0 %collective-permute-done.8.refs_1_.refs_2_ = bf16[128,512]{1,0:T(8,128)(2,1)S(1)} collective-permute-done((bf16[128,512]{1,0:T(8,128)(2,1)S(1)}, bf16[128,512]{1,0:T(8,128)(2,1)S(1)}, u32[]{:S(2)}, u32[]{:S(2)}) %collective-permute-start.8) | collective-permute-done | bytes 131104 | tf_op jit(solution)/shard_map/ppermute | solution.py:367
  30.2 0.9 %collective-permute-start.9 = (bf16[128,512]{1,0:T(8,128)(2,1)S(1)}, bf16[128,512]{1,0:T(8,128)(2,1)S(1)}, u32[]{:S(2)}, u32[]{:S(2)}) collective-permute-start(bf16[128,512]{1,0:T(8,128)(2,1)S(1)} %res_sum_z1.1.refs_4_.refs_0_), channel_id=1, source_target_pairs={{0,8},{1,9},{2,10},{3,11},{4,12},{5,13},{6,14},{7,15},{8,0},{9,1},... | collective-permute-start | bytes 393224 | tf_op jit(solution)/shard_map/ppermute | solution.py:367
  31.0 2.6 %collective-permute-start.4 = (bf16[128,512]{1,0:T(8,128)(2,1)S(1)}, bf16[128,512]{1,0:T(8,128)(2,1)S(1)}, u32[]{:S(2)}, u32[]{:S(2)}) collective-permute-start(bf16[128,512]{1,0:T(8,128)(2,1)S(1)} %get-tuple-element.45), channel_id=1, source_target_pairs={{0,14},{1,15},{2,0},{3,1},{4,2},{5,3},{6,4},{7,5},{8,6},{9,7},{10,... | collective-permute-start | bytes 393224 | tf_op jit(solution)/shard_map/ppermute | solution.py:380
  33.6 4.2 %collective-permute-done.12.refs_3_ = bf16[4,64,512]{2,1,0:T(8,128)(2,1)S(1)} collective-permute-done((bf16[4,64,512]{2,1,0:T(8,128)(2,1)S(1)}, bf16[4,64,512]{2,1,0:T(8,128)(2,1)S(1)}, u32[]{:S(2)}, u32[]{:S(2)}) %collective-permute-start.12) | collective-permute-done | bytes 262176 | tf_op jit(solution)/shard_map/ppermute | solution.py:376
  37.8 0.2 conv_groups.1
  38.0 0.1 collective-permute-start.13
  38.1 0.1 collective-permute-done.9.refs_3_.refs_1_
  38.2 3.3 %collective-permute-start.19 = (bf16[96,512]{1,0:T(8,128)(2,1)S(1)}, bf16[96,512]{1,0:T(8,128)(2,1)S(1)}, u32[]{:S(2)}, u32[]{:S(2)}) collective-permute-start(bf16[96,512]{1,0:T(8,128)(2,1)S(1)} %res_sum_z2.1.refs_4_.refs_0_), channel_id=1, source_target_pairs={{0,18},{1,19},{2,16},{3,17},{4,22},{5,23},{6,20},{7,21},{8,26},{9,... | collective-permute-start | bytes 294920 | tf_op jit(solution)/shard_map/ppermute | solution.py:376
  41.6 0.6 %collective-permute-start.17 = (bf16[96,512]{1,0:T(8,128)(2,1)S(1)}, bf16[96,512]{1,0:T(8,128)(2,1)S(1)}, u32[]{:S(2)}, u32[]{:S(2)}) collective-permute-start(bf16[96,512]{1,0:T(8,128)(2,1)S(1)} %res_sum_z2.1.refs_4_.refs_0_), channel_id=1, source_target_pairs={{0,16},{16,0},{1,17},{17,1},{2,18},{18,2},{3,19},{19,3},{4,20},{20... | collective-permute-start | bytes 294920 | tf_op jit(solution)/shard_map/ppermute | solution.py:371
  42.2 1.3 %collective-permute-start.14 = (bf16[64,512]{1,0:T(8,128)(2,1)S(1)}, bf16[64,512]{1,0:T(8,128)(2,1)S(1)}, u32[]{:S(2)}, u32[]{:S(2)}) collective-permute-start(bf16[64,512]{1,0:T(8,128)(2,1)S(1)} %get-tuple-element.58), channel_id=1, source_target_pairs={{0,8},{1,9},{2,10},{3,11},{4,12},{5,13},{6,14},{7,15},{8,0},{9,1},... | collective-permute-start | bytes 196616 | tf_op jit(solution)/shard_map/ppermute | solution.py:367
  43.5 3.1 %collective-permute-start.15 = (bf16[64,512]{1,0:T(8,128)(2,1)S(1)}, bf16[64,512]{1,0:T(8,128)(2,1)S(1)}, u32[]{:S(2)}, u32[]{:S(2)}) collective-permute-start(bf16[64,512]{1,0:T(8,128)(2,1)S(1)} %get-tuple-element.59), channel_id=1, source_target_pairs={{0,12},{1,13},{2,14},{3,15},{4,8},{5,9},{6,10},{7,11},{8,4},{9,5},... | collective-permute-start | bytes 196616 | tf_op jit(solution)/shard_map/ppermute | solution.py:367
  46.6 0.7 %finish_signal.1 = (bf16[128,512]{1,0:T(8,128)(2,1)}, f32[8,128]{1,0:T(8,128)S(1)}) custom-call(f32[128,512]{1,0:T(8,128)S(1)} %get-tuple-element.44.refs_0_, bf16[128,512]{1,0:T(8,128)(2,1)S(1)} %collective-permute-done.4.refs_1_, bf16[128,512]{1,0:T(8,128)(2,1)S(1)} %collective-permute-done.8.refs_1_.refs_2_, ...), custom_call_target="tpu_custom_call" | custom-call | tf_op jit(solution)/shard_map/finish_signal/pallas_call | solution.py:131
  47.3 0.1 collective-permute-done.14.refs_2_
  47.4 2.2 %collective-permute-done.15.refs_3_ = bf16[64,512]{1,0:T(8,128)(2,1)S(1)} collective-permute-done((bf16[64,512]{1,0:T(8,128)(2,1)S(1)}, bf16[64,512]{1,0:T(8,128)(2,1)S(1)}, u32[]{:S(2)}, u32[]{:S(2)}) %collective-permute-start.15) | collective-permute-done | bytes 65568 | tf_op jit(solution)/shard_map/ppermute | solution.py:367
  49.9 1.6 %collective-permute-start.16 = (bf16[64,512]{1,0:T(8,128)(2,1)S(1)}, bf16[64,512]{1,0:T(8,128)(2,1)S(1)}, u32[]{:S(2)}, u32[]{:S(2)}) collective-permute-start(bf16[64,512]{1,0:T(8,128)(2,1)S(1)} %conv_scaled.1.refs_4_.refs_0_), channel_id=1, source_target_pairs={{0,16},{16,0},{1,17},{17,1},{2,18},{18,2},{3,19},{19,3},{4,20},{20... | collective-permute-start | bytes 196616 | tf_op jit(solution)/shard_map/ppermute | solution.py:371
  51.5 2.9 %collective-permute-done.16.refs_1_ = bf16[64,512]{1,0:T(8,128)(2,1)S(1)} collective-permute-done((bf16[64,512]{1,0:T(8,128)(2,1)S(1)}, bf16[64,512]{1,0:T(8,128)(2,1)S(1)}, u32[]{:S(2)}, u32[]{:S(2)}) %collective-permute-start.16) | collective-permute-done | bytes 65568 | tf_op jit(solution)/shard_map/ppermute | solution.py:371
  54.4 1.0 %finish.1 = (bf16[2,64,512]{2,1,0:T(8,128)(2,1)}, bf16[2,256,768]{2,1,0:T(8,128)(2,1)}) custom-call(bf16[64,512]{1,0:T(8,128)(2,1)S(1)} %conv_scaled.1.refs_4_.refs_0_, bf16[64,512]{1,0:T(8,128)(2,1)S(1)} %collective-permute-done.16.refs_1_, bf16[4,96,512]{2,1,0:T(8,128)(2,1)S(1)} %res_in_order.1.refs_2_, bf16[4,96,512]{2,1,0:T(8,128)(2,1)S(1)} %collective-permute-done.20.refs_3_), custom_call_target="tpu_custom_call" | custom-call | tf_op jit(solution)/shard_map/finish/pallas_call | solution.py:131
  (23 shorter events, 0.5 us)
Async XLA Ops:
  0.6 11.5 %collective-permute-start.1 = (bf16[128,512]{1,0:T(8,128)(2,1)}, bf16[128,512]{1,0:T(8,128)(2,1)S(1)}, u32[]{:S(2)}, u32[]{:S(2)}) collective-permute-start(bf16[128,512]{1,0:T(8,128)(2,1)} %bitcast.6), channel_id=1, source_target_pairs={{0,2},{1,3},{2,4},{3,5},{4,6},{5,7},{6,8},{7,9},{8,10},{9,11},{10,... | collective-permute-start | bytes 393224 | tf_op jit(solution)/shard_map/ppermute | solution.py:380
  5.6 8.1 %collective-permute-start = (bf16[128,1280]{1,0:T(8,128)(2,1)S(1)}, bf16[128,1280]{1,0:T(8,128)(2,1)S(1)}, u32[]{:S(2)}, u32[]{:S(2)}) collective-permute-start(bf16[128,1280]{1,0:T(8,128)(2,1)S(1)} %get-tuple-element.33.refs_0_), channel_id=1, source_target_pairs={{0,1},{1,0},{2,3},{3,2},{4,5},{5,4},{6,7},{7,6},{8,9},{9,8},{10,11... | collective-permute-start | bytes 983048 | tf_op jit(solution)/shard_map/ppermute | solution.py:367
  6.4 5.7 %collective-permute-start.2 = (bf16[32,512]{1,0:T(8,128)(2,1)S(1)}, bf16[32,512]{1,0:T(8,128)(2,1)S(1)}, u32[]{:S(2)}, u32[]{:S(2)}) collective-permute-start(bf16[32,512]{1,0:T(8,128)(2,1)S(1)} %slice_bitcast_fusion), channel_id=1, source_target_pairs={{0,4},{1,5},{2,6},{3,7},{4,8},{5,9},{6,10},{7,11},{8,12},{9,13},{1... | collective-permute-start | bytes 98312 | tf_op jit(solution)/shard_map/ppermute | solution.py:380
  12.2 1.5 %collective-permute-start.3 = (bf16[160,512]{1,0:T(8,128)(2,1)S(1)}, bf16[160,512]{1,0:T(8,128)(2,1)S(1)}, u32[]{:S(2)}, u32[]{:S(2)}) collective-permute-start(bf16[160,512]{1,0:T(8,128)(2,1)S(1)} %pack_halo.1.refs_2_), channel_id=1, source_target_pairs={{0,1},{1,0},{2,3},{3,2},{4,5},{5,4},{6,7},{7,6},{8,9},{9,8},{10,11... | collective-permute-start | bytes 491528 | tf_op jit(solution)/shard_map/ppermute | solution.py:367
  15.9 8.7 %collective-permute-start.5 = (bf16[96,512]{1,0:T(8,128)(2,1)S(1)}, bf16[96,512]{1,0:T(8,128)(2,1)S(1)}, u32[]{:S(2)}, u32[]{:S(2)}) collective-permute-start(bf16[96,512]{1,0:T(8,128)(2,1)S(1)} %get-tuple-element.47), channel_id=1, source_target_pairs={{0,16},{16,0},{1,17},{17,1},{2,18},{18,2},{3,19},{19,3},{4,20},{20... | collective-permute-start | bytes 294920 | tf_op jit(solution)/shard_map/ppermute | solution.py:371
  17.5 7.5 %collective-permute-start.6 = (bf16[96,512]{1,0:T(8,128)(2,1)S(1)}, bf16[96,512]{1,0:T(8,128)(2,1)S(1)}, u32[]{:S(2)}, u32[]{:S(2)}) collective-permute-start(bf16[96,512]{1,0:T(8,128)(2,1)S(1)} %get-tuple-element.48), channel_id=1, source_target_pairs={{0,2},{1,3},{2,0},{3,1},{4,6},{5,7},{6,4},{7,5},{8,10},{9,11},{10,... | collective-permute-start | bytes 294920 | tf_op jit(solution)/shard_map/ppermute | solution.py:367
  19.1 6.0 %collective-permute-start.7 = (bf16[96,512]{1,0:T(8,128)(2,1)S(1)}, bf16[96,512]{1,0:T(8,128)(2,1)S(1)}, u32[]{:S(2)}, u32[]{:S(2)}) collective-permute-start(bf16[96,512]{1,0:T(8,128)(2,1)S(1)} %get-tuple-element.49), channel_id=1, source_target_pairs={{0,18},{1,19},{2,16},{3,17},{4,22},{5,23},{6,20},{7,21},{8,26},{9,... | collective-permute-start | bytes 294920 | tf_op jit(solution)/shard_map/ppermute | solution.py:376
  21.5 12.1 %collective-permute-start.10 = (bf16[4,64,512]{2,1,0:T(8,128)(2,1)S(1)}, bf16[4,64,512]{2,1,0:T(8,128)(2,1)S(1)}, u32[]{:S(2)}, u32[]{:S(2)}) collective-permute-start(bf16[4,64,512]{2,1,0:T(8,128)(2,1)S(1)} %get-tuple-element.52), channel_id=1, source_target_pairs={{0,16},{16,0},{1,17},{17,1},{2,18},{18,2},{3,19},{19,3},{4,20},{20... | collective-permute-start | bytes 786440 | tf_op jit(solution)/shard_map/ppermute | solution.py:371
  23.1 10.5 %collective-permute-start.11 = (bf16[4,64,512]{2,1,0:T(8,128)(2,1)S(1)}, bf16[4,64,512]{2,1,0:T(8,128)(2,1)S(1)}, u32[]{:S(2)}, u32[]{:S(2)}) collective-permute-start(bf16[4,64,512]{2,1,0:T(8,128)(2,1)S(1)} %get-tuple-element.53), channel_id=1, source_target_pairs={{0,2},{1,3},{2,0},{3,1},{4,6},{5,7},{6,4},{7,5},{8,10},{9,11},{10,... | collective-permute-start | bytes 786440 | tf_op jit(solution)/shard_map/ppermute | solution.py:367
  24.6 13.2 %collective-permute-start.12 = (bf16[4,64,512]{2,1,0:T(8,128)(2,1)S(1)}, bf16[4,64,512]{2,1,0:T(8,128)(2,1)S(1)}, u32[]{:S(2)}, u32[]{:S(2)}) collective-permute-start(bf16[4,64,512]{2,1,0:T(8,128)(2,1)S(1)} %get-tuple-element.54), channel_id=1, source_target_pairs={{0,18},{1,19},{2,16},{3,17},{4,22},{5,23},{6,20},{7,21},{8,26},{9,... | collective-permute-start | bytes 786440 | tf_op jit(solution)/shard_map/ppermute | solution.py:376
  25.1 5.0 %collective-permute-start.8 = (bf16[128,512]{1,0:T(8,128)(2,1)S(1)}, bf16[128,512]{1,0:T(8,128)(2,1)S(1)}, u32[]{:S(2)}, u32[]{:S(2)}) collective-permute-start(bf16[128,512]{1,0:T(8,128)(2,1)S(1)} %res_sum_xy.1.refs_0_), channel_id=1, source_target_pairs={{0,4},{1,5},{2,6},{3,7},{4,0},{5,1},{6,2},{7,3},{8,12},{9,13},{10,... | collective-permute-start | bytes 393224 | tf_op jit(solution)/shard_map/ppermute | solution.py:367
  30.2 8.0 %collective-permute-start.9 = (bf16[128,512]{1,0:T(8,128)(2,1)S(1)}, bf16[128,512]{1,0:T(8,128)(2,1)S(1)}, u32[]{:S(2)}, u32[]{:S(2)}) collective-permute-start(bf16[128,512]{1,0:T(8,128)(2,1)S(1)} %res_sum_z1.1.refs_4_.refs_0_), channel_id=1, source_target_pairs={{0,8},{1,9},{2,10},{3,11},{4,12},{5,13},{6,14},{7,15},{8,0},{9,1},... | collective-permute-start | bytes 393224 | tf_op jit(solution)/shard_map/ppermute | solution.py:367
  31.0 11.2 %collective-permute-start.4 = (bf16[128,512]{1,0:T(8,128)(2,1)S(1)}, bf16[128,512]{1,0:T(8,128)(2,1)S(1)}, u32[]{:S(2)}, u32[]{:S(2)}) collective-permute-start(bf16[128,512]{1,0:T(8,128)(2,1)S(1)} %get-tuple-element.45), channel_id=1, source_target_pairs={{0,14},{1,15},{2,0},{3,1},{4,2},{5,3},{6,4},{7,5},{8,6},{9,7},{10,... | collective-permute-start | bytes 393224 | tf_op jit(solution)/shard_map/ppermute | solution.py:380
  38.0 5.5 %collective-permute-start.13 = (bf16[64,512]{1,0:T(8,128)(2,1)S(1)}, bf16[64,512]{1,0:T(8,128)(2,1)S(1)}, u32[]{:S(2)}, u32[]{:S(2)}) collective-permute-start(bf16[64,512]{1,0:T(8,128)(2,1)S(1)} %get-tuple-element.57), channel_id=1, source_target_pairs={{0,4},{1,5},{2,6},{3,7},{4,0},{5,1},{6,2},{7,3},{8,12},{9,13},{10,... | collective-permute-start | bytes 196616 | tf_op jit(solution)/shard_map/ppermute | solution.py:367
  38.2 11.4 %collective-permute-start.19 = (bf16[96,512]{1,0:T(8,128)(2,1)S(1)}, bf16[96,512]{1,0:T(8,128)(2,1)S(1)}, u32[]{:S(2)}, u32[]{:S(2)}) collective-permute-start(bf16[96,512]{1,0:T(8,128)(2,1)S(1)} %res_sum_z2.1.refs_4_.refs_0_), channel_id=1, source_target_pairs={{0,18},{1,19},{2,16},{3,17},{4,22},{5,23},{6,20},{7,21},{8,26},{9,... | collective-permute-start | bytes 294920 | tf_op jit(solution)/shard_map/ppermute | solution.py:376
  41.6 8.1 %collective-permute-start.18 = (bf16[96,512]{1,0:T(8,128)(2,1)S(1)}, bf16[96,512]{1,0:T(8,128)(2,1)S(1)}, u32[]{:S(2)}, u32[]{:S(2)}) collective-permute-start(bf16[96,512]{1,0:T(8,128)(2,1)S(1)} %res_sum_z2.1.refs_4_.refs_0_), channel_id=1, source_target_pairs={{0,2},{1,3},{2,0},{3,1},{4,6},{5,7},{6,4},{7,5},{8,10},{9,11},{10,... | collective-permute-start | bytes 294920 | tf_op jit(solution)/shard_map/ppermute | solution.py:367
  41.6 8.1 %collective-permute-start.17 = (bf16[96,512]{1,0:T(8,128)(2,1)S(1)}, bf16[96,512]{1,0:T(8,128)(2,1)S(1)}, u32[]{:S(2)}, u32[]{:S(2)}) collective-permute-start(bf16[96,512]{1,0:T(8,128)(2,1)S(1)} %res_sum_z2.1.refs_4_.refs_0_), channel_id=1, source_target_pairs={{0,16},{16,0},{1,17},{17,1},{2,18},{18,2},{3,19},{19,3},{4,20},{20... | collective-permute-start | bytes 294920 | tf_op jit(solution)/shard_map/ppermute | solution.py:371
  42.2 5.2 %collective-permute-start.14 = (bf16[64,512]{1,0:T(8,128)(2,1)S(1)}, bf16[64,512]{1,0:T(8,128)(2,1)S(1)}, u32[]{:S(2)}, u32[]{:S(2)}) collective-permute-start(bf16[64,512]{1,0:T(8,128)(2,1)S(1)} %get-tuple-element.58), channel_id=1, source_target_pairs={{0,8},{1,9},{2,10},{3,11},{4,12},{5,13},{6,14},{7,15},{8,0},{9,1},... | collective-permute-start | bytes 196616 | tf_op jit(solution)/shard_map/ppermute | solution.py:367
  43.5 6.1 %collective-permute-start.15 = (bf16[64,512]{1,0:T(8,128)(2,1)S(1)}, bf16[64,512]{1,0:T(8,128)(2,1)S(1)}, u32[]{:S(2)}, u32[]{:S(2)}) collective-permute-start(bf16[64,512]{1,0:T(8,128)(2,1)S(1)} %get-tuple-element.59), channel_id=1, source_target_pairs={{0,12},{1,13},{2,14},{3,15},{4,8},{5,9},{6,10},{7,11},{8,4},{9,5},... | collective-permute-start | bytes 196616 | tf_op jit(solution)/shard_map/ppermute | solution.py:367
  49.8 4.6 %collective-permute-start.20 = (bf16[4,96,512]{2,1,0:T(8,128)(2,1)S(1)}, bf16[4,96,512]{2,1,0:T(8,128)(2,1)S(1)}, u32[]{:S(2)}, u32[]{:S(2)}) collective-permute-start(bf16[4,96,512]{2,1,0:T(8,128)(2,1)S(1)} %res_in_order.1.refs_2_), channel_id=1, source_target_pairs={{0,1},{1,0},{2,3},{3,2},{4,5},{5,4},{6,7},{7,6},{8,9},{9,8},{10,11... | collective-permute-start | bytes 1179656 | tf_op jit(solution)/shard_map/ppermute | solution.py:367
  49.9 4.5 %collective-permute-start.16 = (bf16[64,512]{1,0:T(8,128)(2,1)S(1)}, bf16[64,512]{1,0:T(8,128)(2,1)S(1)}, u32[]{:S(2)}, u32[]{:S(2)}) collective-permute-start(bf16[64,512]{1,0:T(8,128)(2,1)S(1)} %conv_scaled.1.refs_4_.refs_0_), channel_id=1, source_target_pairs={{0,16},{16,0},{1,17},{17,1},{2,18},{18,2},{3,19},{19,3},{4,20},{20... | collective-permute-start | bytes 196616 | tf_op jit(solution)/shard_map/ppermute | solution.py:371

commit v5 on v4

--- a/solution.py
+++ b/solution.py
@@ -331,17 +331,21 @@
         out[lax.bitwise_xor(q, k)] = ref[...]
 
 
-def finish_kernel(mine, other, res_mine, res_other, conv, res):
+def finish_conv_kernel(mine, other, conv, done):
+    done[...] = jnp.zeros_like(done)
     y = lax.axis_index("dp")
     half = mine.shape[0] // 2
     for ref, at in ((mine, y), (other, 1 - y)):
         rows = pl.ds(pl.multiple_of(at * half, half), half)
         conv[0, rows, :] = ref[0:half, :]
         conv[1, rows, :] = ref[half:, :]
+
+
+def finish_res_kernel(mine, other, res):
     _, _, core = here()
     eighth = res.shape[1] // 8
-    width, part = res_mine.shape[2], res_mine.shape[2] // 2
-    for ref, c in ((res_mine, core), (res_other, 1 - core)):
+    width, part = mine.shape[2], mine.shape[2] // 2
+    for ref, c in ((mine, core), (other, 1 - core)):
         for q in range(4):
             rows = pl.ds(pl.multiple_of((4 * c + q) * eighth, eighth), eighth)
             res[1, rows, 0:width] = ref[q, 0:eighth, :]
@@ -447,14 +451,17 @@
     rparts = (quarter,) + around(quarter, quarter, quarter)
     (mine,) = call(
         functools.partial(scaled_sum_kernel, factor), [shaped(piece)], ckeep, *cgot,
-        after=(quarter,), name="conv_scaled",
+        after=(quarter,), flops=10_000_000_000, name="conv_scaled",
     )
     other = swap_streams(mine)
     (ordered,) = call(in_order_kernel, [shaped((4, res_rows, width))], *rparts, after=(mine, done), name="res_in_order")
     rgot = swap(ordered, 1)
-    conv_grad, res_grad = call(
-        finish_kernel, [shaped((2,) + piece), shaped(res_weight.shape)], mine, other, ordered, rgot,
-        name="finish",
+    conv_grad, conv_done = call(
+        finish_conv_kernel, [shaped((2,) + piece), shaped((8, 128), F32)], mine, other,
+        flops=10_000_000_000, name="finish_conv",
+    )
+    (res_grad,) = call(
+        finish_res_kernel, [shaped(res_weight.shape)], ordered, rgot, after=(conv_done,), name="finish_res"
     )
     return (input_grad.reshape(s_dev, t, width), conv_grad, res_grad)
 

time: 55.6 us -> 52.7 us (0.948)
  waiting for transfers between devices: 20.1 us -> 18.2 us
  starting transfers between devices: 25.4 us -> 23.9 us
  Pallas kernels: 8.36 us -> 8.97 us
    ppermute x3, starting transfers between devices: 4.2 us -> 2.2 us  [swap_both(): return lax.ppermute(x, ('dp', 'tm'), route)]
    ppermute x11, starting transfers between devices: 8.67 us -> 10.2 us  [swap(): return lax.ppermute(x, 'tm', [(i, i ^ distance) for i in range(16)])]
    ppermute x3, starting transfers between devices: 7.13 us -> 6.26 us  [shift(): return lax.ppermute(x, 'tm', [(i, (i + distance) % 16) for i in range(16)])]
    ppermute x11, waiting for transfers between devices: 8.78 us -> 7.96 us  [swap(): return lax.ppermute(x, 'tm', [(i, i ^ distance) for i in range(16)])]
    ppermute x3, waiting for transfers between devices: 4.24 us -> 3.57 us  [swap_both(): return lax.ppermute(x, ('dp', 'tm'), route)]
    pallas_call x11 -> x12, Pallas kernels: 6.39 us -> 7 us  [call(): pl.pallas_call(run, out_shape=outs, in_specs=[in_vmem] * n_args + [pl.Blo...]
  transfers between devices with their start and end apart: 21 -> 21, of which waited for: 8 -> 10; matrix products, arithmetic and copies ran while one was open for 1% -> 1% of each run, Pallas kernels for 9% -> 11%
where the time goes in v5:
time: 52.7 us; the launch traced here: 52.5 us
  starting transfers between devices  23.9 us (45%)
  waiting for transfers between devices  18.2 us (35%)
  Pallas kernels  8.97 us (17%)
  local copies, waits for them, and re-layouts  0.76 us (1%)
  between operations  0.74 us (1%)
    ppermute x11, starting transfers between devices, swap(): return lax.ppermute(x, 'tm', [(i, i ^ distance) for i in range(16)])  10.2 us
    ppermute x11, waiting for transfers between devices, swap(): return lax.ppermute(x, 'tm', [(i, i ^ distance) for i in range(16)])  7.96 us
    pallas_call x12, Pallas kernels, call(): pl.pallas_call(run, out_shape=outs, in_specs=[in_vmem] * n_args + [pl.Blo...  7 us
    ppermute x3, starting transfers between devices, shift(): return lax.ppermute(x, 'tm', [(i, (i + distance) % 16) for i in range(16)])  6.26 us
    ppermute x4, starting transfers between devices, swap_streams(): return lax.ppermute(x, 'dp', [(0, 1), (1, 0)])  5.25 us
    ppermute x3, waiting for transfers between devices, shift(): return lax.ppermute(x, 'tm', [(i, (i + distance) % 16) for i in range(16)])  4.14 us
    ppermute x3, waiting for transfers between devices, swap_both(): return lax.ppermute(x, ('dp', 'tm'), route)  3.57 us
    ppermute x4, waiting for transfers between devices, swap_streams(): return lax.ppermute(x, 'dp', [(0, 1), (1, 0)])  2.5 us
  transfers between devices with their start and end apart: 21, of which 10 were waited for; matrix products, arithmetic and copies ran while one was open for 1% of the time, Pallas kernels for 11%

profile of v5, /device:TPU:0, one launch (start us, length us, event | category | flops | bytes accessed | tf_op | source)
XLA Modules:
  0.0 52.5 jit_solution(11392539244451086763)
XLA Ops:
  0.6 3.0 %collective-permute-start.1 = (bf16[128,512]{1,0:T(8,128)(2,1)}, bf16[128,512]{1,0:T(8,128)(2,1)S(1)}, u32[]{:S(2)}, u32[]{:S(2)}) collective-permute-start(bf16[128,512]{1,0:T(8,128)(2,1)} %bitcast.6), channel_id=1, source_target_pairs={{0,2},{1,3},{2,4},{3,5},{4,6},{5,7},{6,8},{7,9},{8,10},{9,11},{10,... | collective-permute-start | bytes 393224 | tf_op jit(solution)/shard_map/ppermute | solution.py:384
  3.6 2.0 %load.1 = (bf16[2,1024,512]{2,1,0:T(8,128)(2,1)S(1)}, bf16[2,256,768]{2,1,0:T(8,128)(2,1)S(1)}, bf16[128,1280]{1,0:T(8,128)(2,1)S(1)}) custom-call(bf16[2,1024,512]{2,1,0:T(8,128)(2,1)} %cw.1, bf16[2,256,768]{2,1,0:T(8,128)(2,1)} %rw.1, bf16[128,512]{1,0:T(8,128)(2,1)} %bitcast.7, bf16[128,512]{1,0:T(8,128)(2,1)} %bitcast.8, bf16[128,256]{1,0:T(8,128)(2,1)} %bitcast.10), custom_call_target="tpu_custom_call" | custom-call | flops 4000000000 | bytes 6000000 | tf_op jit(solution)/shard_map/load/pallas_call | solution.py:170
  5.7 0.8 %slice_bitcast_fusion = bf16[32,512]{1,0:T(8,128)(2,1)S(1)} fusion(bf16[1,128,512]{2,1,0:T(8,128)(2,1)} %param.5), kind=kLoop, calls=%fused_computation | loop fusion | bytes 65536 | tf_op jit(solution)/shard_map/squeeze | solution.py:398
  6.4 1.6 %collective-permute-start.2 = (bf16[32,512]{1,0:T(8,128)(2,1)S(1)}, bf16[32,512]{1,0:T(8,128)(2,1)S(1)}, u32[]{:S(2)}, u32[]{:S(2)}) collective-permute-start(bf16[32,512]{1,0:T(8,128)(2,1)S(1)} %slice_bitcast_fusion), channel_id=1, source_target_pairs={{0,4},{1,5},{2,6},{3,7},{4,8},{5,9},{6,10},{7,11},{8,12},{9,13},{1... | collective-permute-start | bytes 98312 | tf_op jit(solution)/shard_map/ppermute | solution.py:384
  8.0 4.1 %collective-permute-done.2.refs_1_ = bf16[32,512]{1,0:T(8,128)(2,1)S(1)} collective-permute-done((bf16[32,512]{1,0:T(8,128)(2,1)S(1)}, bf16[32,512]{1,0:T(8,128)(2,1)S(1)}, u32[]{:S(2)}, u32[]{:S(2)}) %collective-permute-start.2) | collective-permute-done | bytes 32800 | tf_op jit(solution)/shard_map/ppermute | solution.py:384
  12.3 1.4 %collective-permute-done.3.refs_3_ = bf16[160,512]{1,0:T(8,128)(2,1)S(1)} collective-permute-done((bf16[160,512]{1,0:T(8,128)(2,1)S(1)}, bf16[160,512]{1,0:T(8,128)(2,1)S(1)}, u32[]{:S(2)}, u32[]{:S(2)}) %collective-permute-start.3) | collective-permute-done | bytes 163872 | tf_op jit(solution)/shard_map/ppermute | solution.py:371
  13.7 2.3 %forward_and_outer.1 = (bf16[96,512]{1,0:T(8,128)(2,1)S(1)}, bf16[96,512]{1,0:T(8,128)(2,1)S(1)}, bf16[96,512]{1,0:T(8,128)(2,1)S(1)}, bf16[96,512]{1,0:T(8,128)...) custom-call(bf16[128,1280]{1,0:T(8,128)(2,1)S(1)} %get-tuple-element, ...), custom_call_target="tpu_custom_call" | custom-call | tf_op jit(solution)/shard_map/forward_and_outer/pallas_call | solution.py:131
  15.9 1.6 %collective-permute-start.5 = (bf16[96,512]{1,0:T(8,128)(2,1)S(1)}, bf16[96,512]{1,0:T(8,128)(2,1)S(1)}, u32[]{:S(2)}, u32[]{:S(2)}) collective-permute-start(bf16[96,512]{1,0:T(8,128)(2,1)S(1)} %get-tuple-element.47), channel_id=1, source_target_pairs={{0,16},{16,0},{1,17},{17,1},{2,18},{18,2},{3,19},{19,3},{4,20},{20... | collective-permute-start | bytes 294920 | tf_op jit(solution)/shard_map/ppermute | solution.py:375
  17.5 1.5 %collective-permute-start.6 = (bf16[96,512]{1,0:T(8,128)(2,1)S(1)}, bf16[96,512]{1,0:T(8,128)(2,1)S(1)}, u32[]{:S(2)}, u32[]{:S(2)}) collective-permute-start(bf16[96,512]{1,0:T(8,128)(2,1)S(1)} %get-tuple-element.48), channel_id=1, source_target_pairs={{0,2},{1,3},{2,0},{3,1},{4,6},{5,7},{6,4},{7,5},{8,10},{9,11},{10,... | collective-permute-start | bytes 294920 | tf_op jit(solution)/shard_map/ppermute | solution.py:371
  19.1 0.4 collective-permute-start.7
  19.5 2.0 %inner.1 = (bf16[4,64,512]{2,1,0:T(8,128)(2,1)S(1)}, bf16[4,64,512]{2,1,0:T(8,128)(2,1)S(1)}, bf16[4,64,512]{2,1,0:T(8,128)(2,1)S(1)}, bf16[4,64,512]{2,1,0:T(8,...) custom-call(bf16[544,512]{1,0:T(8,128)(2,1)S(1)} %get-tuple-element.36.refs_0_, ...), custom_call_target="tpu_custom_call" | custom-call | flops 2000000000 | tf_op jit(solution)/shard_map/inner/pallas_call | solution.py:131
  21.5 1.6 %collective-permute-start.10 = (bf16[4,64,512]{2,1,0:T(8,128)(2,1)S(1)}, bf16[4,64,512]{2,1,0:T(8,128)(2,1)S(1)}, u32[]{:S(2)}, u32[]{:S(2)}) collective-permute-start(bf16[4,64,512]{2,1,0:T(8,128)(2,1)S(1)} %get-tuple-element.52), channel_id=1, source_target_pairs={{0,16},{16,0},{1,17},{17,1},{2,18},{18,2},{3,19},{19,3},{4,20},{20... | collective-permute-start | bytes 786440 | tf_op jit(solution)/shard_map/ppermute | solution.py:375
  23.1 1.5 %collective-permute-start.11 = (bf16[4,64,512]{2,1,0:T(8,128)(2,1)S(1)}, bf16[4,64,512]{2,1,0:T(8,128)(2,1)S(1)}, u32[]{:S(2)}, u32[]{:S(2)}) collective-permute-start(bf16[4,64,512]{2,1,0:T(8,128)(2,1)S(1)} %get-tuple-element.53), channel_id=1, source_target_pairs={{0,2},{1,3},{2,0},{3,1},{4,6},{5,7},{6,4},{7,5},{8,10},{9,11},{10,... | collective-permute-start | bytes 786440 | tf_op jit(solution)/shard_map/ppermute | solution.py:371
  24.6 0.4 collective-permute-start.12
  25.2 5.0 %collective-permute-done.8.refs_1_.refs_2_ = bf16[128,512]{1,0:T(8,128)(2,1)S(1)} collective-permute-done((bf16[128,512]{1,0:T(8,128)(2,1)S(1)}, bf16[128,512]{1,0:T(8,128)(2,1)S(1)}, u32[]{:S(2)}, u32[]{:S(2)}) %collective-permute-start.8) | collective-permute-done | bytes 131104 | tf_op jit(solution)/shard_map/ppermute | solution.py:371
  30.2 0.9 %collective-permute-start.9 = (bf16[128,512]{1,0:T(8,128)(2,1)S(1)}, bf16[128,512]{1,0:T(8,128)(2,1)S(1)}, u32[]{:S(2)}, u32[]{:S(2)}) collective-permute-start(bf16[128,512]{1,0:T(8,128)(2,1)S(1)} %res_sum_z1.1.refs_4_.refs_0_), channel_id=1, source_target_pairs={{0,8},{1,9},{2,10},{3,11},{4,12},{5,13},{6,14},{7,15},{8,0},{9,1},... | collective-permute-start | bytes 393224 | tf_op jit(solution)/shard_map/ppermute | solution.py:371
  31.0 0.9 %collective-permute-done.10.refs_1_ = bf16[4,64,512]{2,1,0:T(8,128)(2,1)S(1)} collective-permute-done((bf16[4,64,512]{2,1,0:T(8,128)(2,1)S(1)}, bf16[4,64,512]{2,1,0:T(8,128)(2,1)S(1)}, u32[]{:S(2)}, u32[]{:S(2)}) %collective-permute-start.10) | collective-permute-done | bytes 262176 | tf_op jit(solution)/shard_map/ppermute | solution.py:375
  32.3 3.6 %collective-permute-done.12.refs_3_ = bf16[4,64,512]{2,1,0:T(8,128)(2,1)S(1)} collective-permute-done((bf16[4,64,512]{2,1,0:T(8,128)(2,1)S(1)}, bf16[4,64,512]{2,1,0:T(8,128)(2,1)S(1)}, u32[]{:S(2)}, u32[]{:S(2)}) %collective-permute-start.12) | collective-permute-done | bytes 262176 | tf_op jit(solution)/shard_map/ppermute | solution.py:380
  36.2 2.3 %collective-permute-start.14 = (bf16[64,512]{1,0:T(8,128)(2,1)S(1)}, bf16[64,512]{1,0:T(8,128)(2,1)S(1)}, u32[]{:S(2)}, u32[]{:S(2)}) collective-permute-start(bf16[64,512]{1,0:T(8,128)(2,1)S(1)} %get-tuple-element.58), channel_id=1, source_target_pairs={{0,8},{1,9},{2,10},{3,11},{4,12},{5,13},{6,14},{7,15},{8,0},{9,1},... | collective-permute-start | bytes 196616 | tf_op jit(solution)/shard_map/ppermute | solution.py:371
  38.5 2.0 %collective-permute-start.15 = (bf16[64,512]{1,0:T(8,128)(2,1)S(1)}, bf16[64,512]{1,0:T(8,128)(2,1)S(1)}, u32[]{:S(2)}, u32[]{:S(2)}) collective-permute-start(bf16[64,512]{1,0:T(8,128)(2,1)S(1)} %get-tuple-element.59), channel_id=1, source_target_pairs={{0,12},{1,13},{2,14},{3,15},{4,8},{5,9},{6,10},{7,11},{8,4},{9,5},... | collective-permute-start | bytes 196616 | tf_op jit(solution)/shard_map/ppermute | solution.py:371
  40.5 1.7 %collective-permute-start.4 = (bf16[128,512]{1,0:T(8,128)(2,1)S(1)}, bf16[128,512]{1,0:T(8,128)(2,1)S(1)}, u32[]{:S(2)}, u32[]{:S(2)}) collective-permute-start(bf16[128,512]{1,0:T(8,128)(2,1)S(1)} %get-tuple-element.45), channel_id=1, source_target_pairs={{0,14},{1,15},{2,0},{3,1},{4,2},{5,3},{6,4},{7,5},{8,6},{9,7},{10,... | collective-permute-start | bytes 393224 | tf_op jit(solution)/shard_map/ppermute | solution.py:384
  42.3 1.3 %collective-permute-start.19 = (bf16[96,512]{1,0:T(8,128)(2,1)S(1)}, bf16[96,512]{1,0:T(8,128)(2,1)S(1)}, u32[]{:S(2)}, u32[]{:S(2)}) collective-permute-start(bf16[96,512]{1,0:T(8,128)(2,1)S(1)} %res_sum_z2.1.refs_4_.refs_0_), channel_id=1, source_target_pairs={{0,18},{1,19},{2,16},{3,17},{4,22},{5,23},{6,20},{7,21},{8,26},{9,... | collective-permute-start | bytes 294920 | tf_op jit(solution)/shard_map/ppermute | solution.py:380
  43.6 1.5 %collective-permute-start.18 = (bf16[96,512]{1,0:T(8,128)(2,1)S(1)}, bf16[96,512]{1,0:T(8,128)(2,1)S(1)}, u32[]{:S(2)}, u32[]{:S(2)}) collective-permute-start(bf16[96,512]{1,0:T(8,128)(2,1)S(1)} %res_sum_z2.1.refs_4_.refs_0_), channel_id=1, source_target_pairs={{0,2},{1,3},{2,0},{3,1},{4,6},{5,7},{6,4},{7,5},{8,10},{9,11},{10,... | collective-permute-start | bytes 294920 | tf_op jit(solution)/shard_map/ppermute | solution.py:371
  45.2 0.7 %collective-permute-start.17 = (bf16[96,512]{1,0:T(8,128)(2,1)S(1)}, bf16[96,512]{1,0:T(8,128)(2,1)S(1)}, u32[]{:S(2)}, u32[]{:S(2)}) collective-permute-start(bf16[96,512]{1,0:T(8,128)(2,1)S(1)} %res_sum_z2.1.refs_4_.refs_0_), channel_id=1, source_target_pairs={{0,16},{16,0},{1,17},{17,1},{2,18},{18,2},{3,19},{19,3},{4,20},{20... | collective-permute-start | bytes 294920 | tf_op jit(solution)/shard_map/ppermute | solution.py:375
  45.9 1.4 %collective-permute-start.16 = (bf16[64,512]{1,0:T(8,128)(2,1)S(1)}, bf16[64,512]{1,0:T(8,128)(2,1)S(1)}, u32[]{:S(2)}, u32[]{:S(2)}) collective-permute-start(bf16[64,512]{1,0:T(8,128)(2,1)S(1)} %conv_scaled.1.refs_0_.refs_4_), channel_id=1, source_target_pairs={{0,16},{16,0},{1,17},{17,1},{2,18},{18,2},{3,19},{19,3},{4,20},{20... | collective-permute-start | bytes 196616 | tf_op jit(solution)/shard_map/ppermute | solution.py:375
  47.3 0.7 %finish_signal.1 = (bf16[128,512]{1,0:T(8,128)(2,1)}, f32[8,128]{1,0:T(8,128)S(1)}) custom-call(f32[128,512]{1,0:T(8,128)S(1)} %get-tuple-element.44.refs_0_, bf16[128,512]{1,0:T(8,128)(2,1)S(1)} %collective-permute-done.4.refs_1_, bf16[128,512]{1,0:T(8,128)(2,1)S(1)} %collective-permute-done.8.refs_1_.refs_2_, ...), custom_call_target="tpu_custom_call" | custom-call | tf_op jit(solution)/shard_map/finish_signal/pallas_call | solution.py:131
  48.0 0.8 %collective-permute-done.18.refs_2_ = bf16[96,512]{1,0:T(8,128)(2,1)S(1)} collective-permute-done((bf16[96,512]{1,0:T(8,128)(2,1)S(1)}, bf16[96,512]{1,0:T(8,128)(2,1)S(1)}, u32[]{:S(2)}, u32[]{:S(2)}) %collective-permute-start.18) | collective-permute-done | bytes 98336 | tf_op jit(solution)/shard_map/ppermute | solution.py:371
  48.8 1.0 %collective-permute-done.17.refs_1_ = bf16[96,512]{1,0:T(8,128)(2,1)S(1)} collective-permute-done((bf16[96,512]{1,0:T(8,128)(2,1)S(1)}, bf16[96,512]{1,0:T(8,128)(2,1)S(1)}, u32[]{:S(2)}, u32[]{:S(2)}) %collective-permute-start.17) | collective-permute-done | bytes 98336 | tf_op jit(solution)/shard_map/ppermute | solution.py:375
  49.9 0.6 %collective-permute-done.16.refs_1_ = bf16[64,512]{1,0:T(8,128)(2,1)S(1)} collective-permute-done((bf16[64,512]{1,0:T(8,128)(2,1)S(1)}, bf16[64,512]{1,0:T(8,128)(2,1)S(1)}, u32[]{:S(2)}, u32[]{:S(2)}) %collective-permute-start.16) | collective-permute-done | bytes 65568 | tf_op jit(solution)/shard_map/ppermute | solution.py:375
  50.5 0.7 %finish_conv.1 = (bf16[2,64,512]{2,1,0:T(8,128)(2,1)}, f32[8,128]{1,0:T(8,128)S(1)}) custom-call(bf16[64,512]{1,0:T(8,128)(2,1)S(1)} %conv_scaled.1.refs_0_.refs_4_, bf16[64,512]{1,0:T(8,128)(2,1)S(1)} %collective-permute-done.16.refs_1_), custom_call_target="tpu_custom_call" | custom-call | flops 10000000000 | tf_op jit(solution)/shard_map/finish_conv/pallas_call | solution.py:131
  51.1 0.5 collective-permute-done.20.refs_1_
  51.6 0.9 %finish_res.1 = bf16[2,256,768]{2,1,0:T(8,128)(2,1)} custom-call(bf16[4,96,512]{2,1,0:T(8,128)(2,1)S(1)} %res_in_order.1.refs_0_, bf16[4,96,512]{2,1,0:T(8,128)(2,1)S(1)} %collective-permute-done.20.refs_1_, f32[8,128]{1,0:T(8,128)S(1)} %get-tuple-element.62.refs_2_), custom_call_target="tpu_custom_call" | custom-call | tf_op jit(solution)/shard_map/finish_res/pallas_call | solution.py:131
  (24 shorter events, 1.2 us)
Async XLA Ops:
  0.6 11.5 %collective-permute-start.1 = (bf16[128,512]{1,0:T(8,128)(2,1)}, bf16[128,512]{1,0:T(8,128)(2,1)S(1)}, u32[]{:S(2)}, u32[]{:S(2)}) collective-permute-start(bf16[128,512]{1,0:T(8,128)(2,1)} %bitcast.6), channel_id=1, source_target_pairs={{0,2},{1,3},{2,4},{3,5},{4,6},{5,7},{6,8},{7,9},{8,10},{9,11},{10,... | collective-permute-start | bytes 393224 | tf_op jit(solution)/shard_map/ppermute | solution.py:384
  5.6 8.1 %collective-permute-start = (bf16[128,1280]{1,0:T(8,128)(2,1)S(1)}, bf16[128,1280]{1,0:T(8,128)(2,1)S(1)}, u32[]{:S(2)}, u32[]{:S(2)}) collective-permute-start(bf16[128,1280]{1,0:T(8,128)(2,1)S(1)} %get-tuple-element.33.refs_0_), channel_id=1, source_target_pairs={{0,1},{1,0},{2,3},{3,2},{4,5},{5,4},{6,7},{7,6},{8,9},{9,8},{10,11... | collective-permute-start | bytes 983048 | tf_op jit(solution)/shard_map/ppermute | solution.py:371
  6.4 5.7 %collective-permute-start.2 = (bf16[32,512]{1,0:T(8,128)(2,1)S(1)}, bf16[32,512]{1,0:T(8,128)(2,1)S(1)}, u32[]{:S(2)}, u32[]{:S(2)}) collective-permute-start(bf16[32,512]{1,0:T(8,128)(2,1)S(1)} %slice_bitcast_fusion), channel_id=1, source_target_pairs={{0,4},{1,5},{2,6},{3,7},{4,8},{5,9},{6,10},{7,11},{8,12},{9,13},{1... | collective-permute-start | bytes 98312 | tf_op jit(solution)/shard_map/ppermute | solution.py:384
  12.2 1.5 %collective-permute-start.3 = (bf16[160,512]{1,0:T(8,128)(2,1)S(1)}, bf16[160,512]{1,0:T(8,128)(2,1)S(1)}, u32[]{:S(2)}, u32[]{:S(2)}) collective-permute-start(bf16[160,512]{1,0:T(8,128)(2,1)S(1)} %pack_halo.1.refs_2_), channel_id=1, source_target_pairs={{0,1},{1,0},{2,3},{3,2},{4,5},{5,4},{6,7},{7,6},{8,9},{9,8},{10,11... | collective-permute-start | bytes 491528 | tf_op jit(solution)/shard_map/ppermute | solution.py:371
  15.9 8.7 %collective-permute-start.5 = (bf16[96,512]{1,0:T(8,128)(2,1)S(1)}, bf16[96,512]{1,0:T(8,128)(2,1)S(1)}, u32[]{:S(2)}, u32[]{:S(2)}) collective-permute-start(bf16[96,512]{1,0:T(8,128)(2,1)S(1)} %get-tuple-element.47), channel_id=1, source_target_pairs={{0,16},{16,0},{1,17},{17,1},{2,18},{18,2},{3,19},{19,3},{4,20},{20... | collective-permute-start | bytes 294920 | tf_op jit(solution)/shard_map/ppermute | solution.py:375
  17.5 7.5 %collective-permute-start.6 = (bf16[96,512]{1,0:T(8,128)(2,1)S(1)}, bf16[96,512]{1,0:T(8,128)(2,1)S(1)}, u32[]{:S(2)}, u32[]{:S(2)}) collective-permute-start(bf16[96,512]{1,0:T(8,128)(2,1)S(1)} %get-tuple-element.48), channel_id=1, source_target_pairs={{0,2},{1,3},{2,0},{3,1},{4,6},{5,7},{6,4},{7,5},{8,10},{9,11},{10,... | collective-permute-start | bytes 294920 | tf_op jit(solution)/shard_map/ppermute | solution.py:371
  19.1 6.0 %collective-permute-start.7 = (bf16[96,512]{1,0:T(8,128)(2,1)S(1)}, bf16[96,512]{1,0:T(8,128)(2,1)S(1)}, u32[]{:S(2)}, u32[]{:S(2)}) collective-permute-start(bf16[96,512]{1,0:T(8,128)(2,1)S(1)} %get-tuple-element.49), channel_id=1, source_target_pairs={{0,18},{1,19},{2,16},{3,17},{4,22},{5,23},{6,20},{7,21},{8,26},{9,... | collective-permute-start | bytes 294920 | tf_op jit(solution)/shard_map/ppermute | solution.py:380
  21.5 10.5 %collective-permute-start.10 = (bf16[4,64,512]{2,1,0:T(8,128)(2,1)S(1)}, bf16[4,64,512]{2,1,0:T(8,128)(2,1)S(1)}, u32[]{:S(2)}, u32[]{:S(2)}) collective-permute-start(bf16[4,64,512]{2,1,0:T(8,128)(2,1)S(1)} %get-tuple-element.52), channel_id=1, source_target_pairs={{0,16},{16,0},{1,17},{17,1},{2,18},{18,2},{3,19},{19,3},{4,20},{20... | collective-permute-start | bytes 786440 | tf_op jit(solution)/shard_map/ppermute | solution.py:375
  23.1 9.2 %collective-permute-start.11 = (bf16[4,64,512]{2,1,0:T(8,128)(2,1)S(1)}, bf16[4,64,512]{2,1,0:T(8,128)(2,1)S(1)}, u32[]{:S(2)}, u32[]{:S(2)}) collective-permute-start(bf16[4,64,512]{2,1,0:T(8,128)(2,1)S(1)} %get-tuple-element.53), channel_id=1, source_target_pairs={{0,2},{1,3},{2,0},{3,1},{4,6},{5,7},{6,4},{7,5},{8,10},{9,11},{10,... | collective-permute-start | bytes 786440 | tf_op jit(solution)/shard_map/ppermute | solution.py:371
  24.6 11.3 %collective-permute-start.12 = (bf16[4,64,512]{2,1,0:T(8,128)(2,1)S(1)}, bf16[4,64,512]{2,1,0:T(8,128)(2,1)S(1)}, u32[]{:S(2)}, u32[]{:S(2)}) collective-permute-start(bf16[4,64,512]{2,1,0:T(8,128)(2,1)S(1)} %get-tuple-element.54), channel_id=1, source_target_pairs={{0,18},{1,19},{2,16},{3,17},{4,22},{5,23},{6,20},{7,21},{8,26},{9,... | collective-permute-start | bytes 786440 | tf_op jit(solution)/shard_map/ppermute | solution.py:380
  25.1 5.0 %collective-permute-start.8 = (bf16[128,512]{1,0:T(8,128)(2,1)S(1)}, bf16[128,512]{1,0:T(8,128)(2,1)S(1)}, u32[]{:S(2)}, u32[]{:S(2)}) collective-permute-start(bf16[128,512]{1,0:T(8,128)(2,1)S(1)} %res_sum_xy.1.refs_0_), channel_id=1, source_target_pairs={{0,4},{1,5},{2,6},{3,7},{4,0},{5,1},{6,2},{7,3},{8,12},{9,13},{10,... | collective-permute-start | bytes 393224 | tf_op jit(solution)/shard_map/ppermute | solution.py:371
  30.2 12.1 %collective-permute-start.9 = (bf16[128,512]{1,0:T(8,128)(2,1)S(1)}, bf16[128,512]{1,0:T(8,128)(2,1)S(1)}, u32[]{:S(2)}, u32[]{:S(2)}) collective-permute-start(bf16[128,512]{1,0:T(8,128)(2,1)S(1)} %res_sum_z1.1.refs_4_.refs_0_), channel_id=1, source_target_pairs={{0,8},{1,9},{2,10},{3,11},{4,12},{5,13},{6,14},{7,15},{8,0},{9,1},... | collective-permute-start | bytes 393224 | tf_op jit(solution)/shard_map/ppermute | solution.py:371
  36.1 7.5 %collective-permute-start.13 = (bf16[64,512]{1,0:T(8,128)(2,1)S(1)}, bf16[64,512]{1,0:T(8,128)(2,1)S(1)}, u32[]{:S(2)}, u32[]{:S(2)}) collective-permute-start(bf16[64,512]{1,0:T(8,128)(2,1)S(1)} %get-tuple-element.57), channel_id=1, source_target_pairs={{0,4},{1,5},{2,6},{3,7},{4,0},{5,1},{6,2},{7,3},{8,12},{9,13},{10,... | collective-permute-start | bytes 196616 | tf_op jit(solution)/shard_map/ppermute | solution.py:371
  36.2 9.0 %collective-permute-start.14 = (bf16[64,512]{1,0:T(8,128)(2,1)S(1)}, bf16[64,512]{1,0:T(8,128)(2,1)S(1)}, u32[]{:S(2)}, u32[]{:S(2)}) collective-permute-start(bf16[64,512]{1,0:T(8,128)(2,1)S(1)} %get-tuple-element.58), channel_id=1, source_target_pairs={{0,8},{1,9},{2,10},{3,11},{4,12},{5,13},{6,14},{7,15},{8,0},{9,1},... | collective-permute-start | bytes 196616 | tf_op jit(solution)/shard_map/ppermute | solution.py:371
  38.5 7.3 %collective-permute-start.15 = (bf16[64,512]{1,0:T(8,128)(2,1)S(1)}, bf16[64,512]{1,0:T(8,128)(2,1)S(1)}, u32[]{:S(2)}, u32[]{:S(2)}) collective-permute-start(bf16[64,512]{1,0:T(8,128)(2,1)S(1)} %get-tuple-element.59), channel_id=1, source_target_pairs={{0,12},{1,13},{2,14},{3,15},{4,8},{5,9},{6,10},{7,11},{8,4},{9,5},... | collective-permute-start | bytes 196616 | tf_op jit(solution)/shard_map/ppermute | solution.py:371
  40.5 6.7 %collective-permute-start.4 = (bf16[128,512]{1,0:T(8,128)(2,1)S(1)}, bf16[128,512]{1,0:T(8,128)(2,1)S(1)}, u32[]{:S(2)}, u32[]{:S(2)}) collective-permute-start(bf16[128,512]{1,0:T(8,128)(2,1)S(1)} %get-tuple-element.45), channel_id=1, source_target_pairs={{0,14},{1,15},{2,0},{3,1},{4,2},{5,3},{6,4},{7,5},{8,6},{9,7},{10,... | collective-permute-start | bytes 393224 | tf_op jit(solution)/shard_map/ppermute | solution.py:384
  42.3 5.7 %collective-permute-start.19 = (bf16[96,512]{1,0:T(8,128)(2,1)S(1)}, bf16[96,512]{1,0:T(8,128)(2,1)S(1)}, u32[]{:S(2)}, u32[]{:S(2)}) collective-permute-start(bf16[96,512]{1,0:T(8,128)(2,1)S(1)} %res_sum_z2.1.refs_4_.refs_0_), channel_id=1, source_target_pairs={{0,18},{1,19},{2,16},{3,17},{4,22},{5,23},{6,20},{7,21},{8,26},{9,... | collective-permute-start | bytes 294920 | tf_op jit(solution)/shard_map/ppermute | solution.py:380
  43.6 5.2 %collective-permute-start.18 = (bf16[96,512]{1,0:T(8,128)(2,1)S(1)}, bf16[96,512]{1,0:T(8,128)(2,1)S(1)}, u32[]{:S(2)}, u32[]{:S(2)}) collective-permute-start(bf16[96,512]{1,0:T(8,128)(2,1)S(1)} %res_sum_z2.1.refs_4_.refs_0_), channel_id=1, source_target_pairs={{0,2},{1,3},{2,0},{3,1},{4,6},{5,7},{6,4},{7,5},{8,10},{9,11},{10,... | collective-permute-start | bytes 294920 | tf_op jit(solution)/shard_map/ppermute | solution.py:371
  45.2 4.6 %collective-permute-start.17 = (bf16[96,512]{1,0:T(8,128)(2,1)S(1)}, bf16[96,512]{1,0:T(8,128)(2,1)S(1)}, u32[]{:S(2)}, u32[]{:S(2)}) collective-permute-start(bf16[96,512]{1,0:T(8,128)(2,1)S(1)} %res_sum_z2.1.refs_4_.refs_0_), channel_id=1, source_target_pairs={{0,16},{16,0},{1,17},{17,1},{2,18},{18,2},{3,19},{19,3},{4,20},{20... | collective-permute-start | bytes 294920 | tf_op jit(solution)/shard_map/ppermute | solution.py:375
  45.9 4.6 %collective-permute-start.16 = (bf16[64,512]{1,0:T(8,128)(2,1)S(1)}, bf16[64,512]{1,0:T(8,128)(2,1)S(1)}, u32[]{:S(2)}, u32[]{:S(2)}) collective-permute-start(bf16[64,512]{1,0:T(8,128)(2,1)S(1)} %conv_scaled.1.refs_0_.refs_4_), channel_id=1, source_target_pairs={{0,16},{16,0},{1,17},{17,1},{2,18},{18,2},{3,19},{19,3},{4,20},{20... | collective-permute-start | bytes 196616 | tf_op jit(solution)/shard_map/ppermute | solution.py:375
  49.8 1.8 %collective-permute-start.20 = (bf16[4,96,512]{2,1,0:T(8,128)(2,1)S(1)}, bf16[4,96,512]{2,1,0:T(8,128)(2,1)S(1)}, u32[]{:S(2)}, u32[]{:S(2)}) collective-permute-start(bf16[4,96,512]{2,1,0:T(8,128)(2,1)S(1)} %res_in_order.1.refs_0_), channel_id=1, source_target_pairs={{0,1},{1,0},{2,3},{3,2},{4,5},{5,4},{6,7},{7,6},{8,9},{9,8},{10,11... | collective-permute-start | bytes 1179656 | tf_op jit(solution)/shard_map/ppermute | solution.py:371

commit v6 on v5

--- a/solution.py
+++ b/solution.py
@@ -148,15 +148,7 @@
     return place(lax.axis_index("tm"))
 
 
-def load_kernel(cw, rw, sig, grad, skip, cw_out, rw_out, own_out, sems):
-    width = sig.shape[1]
-    pairs = (
-        (sig, own_out.at[:, 0:width]),
-        (grad, own_out.at[:, width : 2 * width]),
-        (skip, own_out.at[:, 2 * width :]),
-        (cw, cw_out),
-        (rw, rw_out),
-    )
+def copy_all(pairs, sems):
     copies = [pltpu.make_async_copy(src, dst, sems.at[i]) for i, (src, dst) in enumerate(pairs)]
     for copy in copies:
         copy.start()
@@ -164,21 +156,33 @@
         copy.wait()
 
 
-def load(cw, rw, sig, grad, skip):
+def load_slab_kernel(sig, grad, skip, own_out, tail_out, sems):
     t, width = sig.shape
-    in_hbm = [pltpu.with_memory_space_constraint(a, pltpu.HBM) for a in (cw, rw, sig, grad, skip)]
+    near = tail_out.shape[0]
+    pairs = (
+        (sig.at[t - near :, :], tail_out),
+        (sig, own_out.at[:, 0:width]),
+        (grad, own_out.at[:, width : 2 * width]),
+        (skip, own_out.at[:, 2 * width :]),
+    )
+    copy_all(pairs, sems)
+
+
+def load_weights_kernel(cw, rw, cw_out, rw_out, sems):
+    copy_all(((cw, cw_out), (rw, rw_out)), sems)
+
+
+def load(kernel, outs, flops, name, *arrays):
+    in_hbm = [pltpu.with_memory_space_constraint(a, pltpu.HBM) for a in arrays]
     return pl.pallas_call(
-        load_kernel,
-        out_shape=[
-            pltpu.VMEM(cw.shape, BF16), pltpu.VMEM(rw.shape, BF16),
-            pltpu.VMEM((t, 2 * width + skip.shape[1]), BF16),
-        ],
-        in_specs=[pl.BlockSpec(memory_space=pltpu.HBM)] * 5,
-        out_specs=[pl.BlockSpec(memory_space=pltpu.VMEM)] * 3,
-        scratch_shapes=[pltpu.SemaphoreType.DMA((5,))],
+        kernel,
+        out_shape=[pltpu.VMEM(shape, BF16) for shape in outs],
+        in_specs=[pl.BlockSpec(memory_space=pltpu.HBM)] * len(arrays),
+        out_specs=[pl.BlockSpec(memory_space=pltpu.VMEM)] * len(outs),
+        scratch_shapes=[pltpu.SemaphoreType.DMA((4,))],
         compiler_params=pltpu.CompilerParams(vmem_limit_bytes=8 * 1024 * 1024),
-        cost_estimate=pl.CostEstimate(flops=4_000_000_000, bytes_accessed=6_000_000, transcendentals=0),
-        name="load",
+        cost_estimate=pl.CostEstimate(flops=flops, bytes_accessed=0, transcendentals=0),
+        name=name,
     )(*in_hbm)
 
 
@@ -249,14 +253,13 @@
 
 
 def inner_kernel(
-    xin, a, b, x1, dz1, outer, ga, es, cw, rw,
-    mine, by_y, by_x, by_both, own_out, back_out, tail_out,
-    staged, dz,
+    xin, a, b, x1, dz1, outer, es, rw,
+    mine, by_y, by_x, by_both, dz,
+    staged,
 ):
     width = xin.shape[1]
     t = dz1.shape[0] // 2
     near = t // 4
-    _, _, core = here()
     e0 = mm_nt(outer[...], rw[0, :, 0:width])
     e0 = jnp.concatenate([e0[: 2 * t, :], e0[2 * t :, :] + es[...]], axis=0)
     dz0 = jnp.concatenate([e0 * a[...], e0 * b[...]], axis=1).astype(BF16)
@@ -276,6 +279,13 @@
                 staged[c, 2 * x + y, g, 0:half, :] = part0[src, :].astype(BF16)
                 staged[c, 2 * x + y, g, half:, :] = part1[src, :].astype(BF16)
     split_quarters(staged, mine, by_y, by_x, by_both)
+
+
+def signal_kernel(dz, outer, ga, cw, own_out, back_out, tail_out):
+    t = ga.shape[0] // 2
+    near = t // 4
+    width = ga.shape[1]
+    _, _, core = here()
     at = pl.multiple_of(core * t, t)
     long = t + near
     back = dz[pl.ds(at, long), :]
@@ -393,10 +403,17 @@
     factor = float(s_dev * t * 32) ** (-0.5)
 
     far = shift(signal[0], 2)
-    cw, rw, own = load(conv_weight, res_weight, signal[0], grad_out[0], skip_cotangent[0])
+    own, tail = load(
+        load_slab_kernel, [(t, 2 * width + skip_cotangent.shape[2]), (near, width)], 0, "load_slab",
+        signal[0], grad_out[0], skip_cotangent[0],
+    )
+    cw, rw = load(
+        load_weights_kernel, [conv_weight.shape, res_weight.shape], 4_000_000_000, "load_weights",
+        conv_weight, res_weight,
+    )
     own_other = swap(own, 1)
-    tail4 = shift(signal[0, t - near :, :], 4)
-    (halo,) = call(pack_halo_kernel, [shaped((t + near, width))], far, tail4, name="pack_halo")
+    tail4 = shift(tail, 4)
+    (halo,) = call(pack_halo_kernel, [shaped((t + near, width))], far, tail4, after=(cw,), flops=5_000_000_000, name="pack_halo")
     halo_other = swap(halo, 1)
 
     res = shaped((res_rows, width))
@@ -417,16 +434,20 @@
     )
     piece = (2 * half, width)
     part = shaped((4,) + piece)
-    *csplit, own, back, tail = call(
-        inner_kernel,
-        [part, part, part, part, shaped((t, width), F32), shaped((t, width)), shaped((near, width))],
-        xin, a, b, x1, dz1, outer, ga, es, cw, rw,
-        scratch=[pltpu.VMEM((2, 4, 4) + piece, BF16), pltpu.VMEM((4 * t + near, width), BF16)],
-        vmem=16, flops=2_000_000_000, name="inner",
+    *csplit, dz0 = call(
+        inner_kernel, [part, part, part, part, shaped((4 * t + near, width))],
+        xin, a, b, x1, dz1, outer, es, rw,
+        scratch=[pltpu.VMEM((2, 4, 4) + piece, BF16)], vmem=16, flops=2_000_000_000, name="inner",
+    )
+    own, back, tail = call(
+        signal_kernel, [shaped((t, width), F32), shaped((t, width)), shaped((near, width))],
+        dz0, outer, ga, cw, vmem=16, flops=1_000_000_000, name="signal",
     )
 
     def around(by_y, by_x, by_both):
-        return swap_streams(by_y), swap(by_x, 2), swap_both(by_both, 2)
+        both = swap_both(by_both, 2)
+        beside = swap(by_x, 2)
+        return swap_streams(by_y), beside, both
 
     rterms = (rsplit[0],) + around(*rsplit[1:])
     cterms = (csplit[0],) + around(*csplit[1:])
@@ -440,7 +461,7 @@
         groups_kernel, [shaped(piece, F32)] + [shaped(piece)] * 3, *cterms,
         after=(rsum,), scratch=[pltpu.VMEM((4,) + piece, F32)], name="conv_groups",
     )
-    cgot = [swap(send, 4 * k) for k, send in zip((1, 2, 3), csend)]
+    cgot = [swap(csend[k - 1], 4 * k) for k in (2, 3, 1)]
     input_grad, done = call(
         finish_signal_kernel, [shaped((t, width)), shaped((8, 128), F32)], own, come, rgot1, rgot2,
         after=(ckeep,), name="finish_signal",
@@ -448,7 +469,7 @@
     (quarter,) = call(
         functools.partial(sum_z2_kernel, factor), [res], rsum, rgot2, after=(ckeep,), name="res_sum_z2"
     )
-    rparts = (quarter,) + around(quarter, quarter, quarter)
+    rparts = (quarter, swap_streams(quarter), swap(quarter, 2), swap_both(quarter, 2))
     (mine,) = call(
         functools.partial(scaled_sum_kernel, factor), [shaped(piece)], ckeep, *cgot,
         after=(quarter,), flops=10_000_000_000, name="conv_scaled",

time: 52.7 us -> 50.5 us (0.958)
  waiting for transfers between devices: 18.2 us -> 16.1 us
  Pallas kernels: 8.97 us -> 10.1 us
  local copies, waits for them, and re-layouts: 0.76 us -> 0 us
    ppermute x3, waiting for transfers between devices: 4.14 us -> 2.63 us  [shift(): return lax.ppermute(x, 'tm', [(i, (i + distance) % 16) for i in range(16)])]
    ppermute x11, starting transfers between devices: 10.2 us -> 9.12 us  [swap(): return lax.ppermute(x, 'tm', [(i, i ^ distance) for i in range(16)])]
    pallas_call x1 -> x2, Pallas kernels: 1.97 us -> 2.82 us  [load(): pl.pallas_call(kernel, out_shape=[pltpu.VMEM(shape, BF16) for shape in ou...]
    squeeze x1 -> x0, local copies, waits for them, and re-layouts: 0.76 us -> none  [body(): tail4 = shift(signal[0, t - near:, :], 4)]
    ppermute x4, waiting for transfers between devices: 2.5 us -> 1.96 us  [swap_streams(): return lax.ppermute(x, 'dp', [(0, 1), (1, 0)])]
    pallas_call x12 -> x13, Pallas kernels: 7 us -> 7.25 us  [call(): pl.pallas_call(run, out_shape=outs, in_specs=[in_vmem] * n_args + [pl.Blo...]
  transfers between devices with their start and end apart: 21 -> 21, of which waited for: 10 -> 11; matrix products, arithmetic and copies ran while one was open for 1% -> 0% of each run, Pallas kernels for 11% -> 14%
where the time goes in v6:
time: 50.5 us; the launch traced here: 50.3 us
  starting transfers between devices  23.4 us (46%)
  waiting for transfers between devices  16.1 us (32%)
  Pallas kernels  10.1 us (20%)
  between operations  0.76 us (2%)
    ppermute x11, starting transfers between devices, swap(): return lax.ppermute(x, 'tm', [(i, i ^ distance) for i in range(16)])  9.12 us
    ppermute x11, waiting for transfers between devices, swap(): return lax.ppermute(x, 'tm', [(i, i ^ distance) for i in range(16)])  7.87 us
    pallas_call x13, Pallas kernels, call(): pl.pallas_call(run, out_shape=outs, in_specs=[in_vmem] * n_args + [pl.Blo...  7.25 us
    ppermute x3, starting transfers between devices, shift(): return lax.ppermute(x, 'tm', [(i, (i + distance) % 16) for i in range(16)])  6.58 us
    ppermute x4, starting transfers between devices, swap_streams(): return lax.ppermute(x, 'dp', [(0, 1), (1, 0)])  5.26 us
    ppermute x3, waiting for transfers between devices, swap_both(): return lax.ppermute(x, ('dp', 'tm'), route)  3.66 us
    pallas_call x2, Pallas kernels, load(): pl.pallas_call(kernel, out_shape=[pltpu.VMEM(shape, BF16) for shape in ou...  2.82 us
    ppermute x3, waiting for transfers between devices, shift(): return lax.ppermute(x, 'tm', [(i, (i + distance) % 16) for i in range(16)])  2.63 us
  transfers between devices with their start and end apart: 21, of which 11 were waited for; matrix products, arithmetic and copies ran while one was open for 0% of the time, Pallas kernels for 14%

profile of v6, /device:TPU:0, one launch (start us, length us, event | category | flops | bytes accessed | tf_op | source)
XLA Modules:
  0.0 50.3 jit_solution(13730897344323004074)
XLA Ops:
  0.6 3.0 %collective-permute-start.1 = (bf16[128,512]{1,0:T(8,128)(2,1)}, bf16[128,512]{1,0:T(8,128)(2,1)S(1)}, u32[]{:S(2)}, u32[]{:S(2)}) collective-permute-start(bf16[128,512]{1,0:T(8,128)(2,1)} %bitcast.5), channel_id=1, source_target_pairs={{0,2},{1,3},{2,4},{3,5},{4,6},{5,7},{6,8},{7,9},{8,10},{9,11},{10,... | collective-permute-start | bytes 393224 | tf_op jit(solution)/shard_map/ppermute | solution.py:394
  3.6 1.0 %load_slab.1 = (bf16[128,1280]{1,0:T(8,128)(2,1)S(1)}, bf16[32,512]{1,0:T(8,128)(2,1)S(1)}) custom-call(bf16[128,512]{1,0:T(8,128)(2,1)} %bitcast.6, bf16[128,512]{1,0:T(8,128)(2,1)} %bitcast.4, bf16[128,256]{1,0:T(8,128)(2,1)} %bitcast.7), custom_call_target="tpu_custom_call" | custom-call | tf_op jit(solution)/shard_map/load_slab/pallas_call | solution.py:177
  4.7 1.6 %collective-permute-start.2 = (bf16[32,512]{1,0:T(8,128)(2,1)S(1)}, bf16[32,512]{1,0:T(8,128)(2,1)S(1)}, u32[]{:S(2)}, u32[]{:S(2)}) collective-permute-start(bf16[32,512]{1,0:T(8,128)(2,1)S(1)} %get-tuple-element.36), channel_id=1, source_target_pairs={{0,4},{1,5},{2,6},{3,7},{4,8},{5,9},{6,10},{7,11},{8,12},{9,13},{1... | collective-permute-start | bytes 98312 | tf_op jit(solution)/shard_map/ppermute | solution.py:394
  6.3 1.8 %load_weights.1 = (bf16[2,1024,512]{2,1,0:T(8,128)(2,1)S(1)}, bf16[2,256,768]{2,1,0:T(8,128)(2,1)S(1)}) custom-call(bf16[2,1024,512]{2,1,0:T(8,128)(2,1)} %cw.1, bf16[2,256,768]{2,1,0:T(8,128)(2,1)} %rw.1), custom_call_target="tpu_custom_call" | custom-call | flops 4000000000 | tf_op jit(solution)/shard_map/load_weights/pallas_call | solution.py:177
  8.1 2.3 %collective-permute-done.2.refs_1_ = bf16[32,512]{1,0:T(8,128)(2,1)S(1)} collective-permute-done((bf16[32,512]{1,0:T(8,128)(2,1)S(1)}, bf16[32,512]{1,0:T(8,128)(2,1)S(1)}, u32[]{:S(2)}, u32[]{:S(2)}) %collective-permute-start.2) | collective-permute-done | bytes 32800 | tf_op jit(solution)/shard_map/ppermute | solution.py:394
  10.8 1.4 %collective-permute-done.3.refs_3_ = bf16[160,512]{1,0:T(8,128)(2,1)S(1)} collective-permute-done((bf16[160,512]{1,0:T(8,128)(2,1)S(1)}, bf16[160,512]{1,0:T(8,128)(2,1)S(1)}, u32[]{:S(2)}, u32[]{:S(2)}) %collective-permute-start.3) | collective-permute-done | bytes 163872 | tf_op jit(solution)/shard_map/ppermute | solution.py:381
  12.2 2.3 %forward_and_outer.1 = (bf16[96,512]{1,0:T(8,128)(2,1)S(1)}, bf16[96,512]{1,0:T(8,128)(2,1)S(1)}, bf16[96,512]{1,0:T(8,128)(2,1)S(1)}, bf16[96,512]{1,0:T(8,128)...) custom-call(bf16[128,1280]{1,0:T(8,128)(2,1)S(1)} %get-tuple-element, ...), custom_call_target="tpu_custom_call" | custom-call | tf_op jit(solution)/shard_map/forward_and_outer/pallas_call | solution.py:131
  14.5 1.6 %collective-permute-start.5 = (bf16[96,512]{1,0:T(8,128)(2,1)S(1)}, bf16[96,512]{1,0:T(8,128)(2,1)S(1)}, u32[]{:S(2)}, u32[]{:S(2)}) collective-permute-start(bf16[96,512]{1,0:T(8,128)(2,1)S(1)} %get-tuple-element.51), channel_id=1, source_target_pairs={{0,16},{16,0},{1,17},{17,1},{2,18},{18,2},{3,19},{19,3},{4,20},{20... | collective-permute-start | bytes 294920 | tf_op jit(solution)/shard_map/ppermute | solution.py:385
  16.1 1.3 %collective-permute-start.6 = (bf16[96,512]{1,0:T(8,128)(2,1)S(1)}, bf16[96,512]{1,0:T(8,128)(2,1)S(1)}, u32[]{:S(2)}, u32[]{:S(2)}) collective-permute-start(bf16[96,512]{1,0:T(8,128)(2,1)S(1)} %get-tuple-element.52), channel_id=1, source_target_pairs={{0,2},{1,3},{2,0},{3,1},{4,6},{5,7},{6,4},{7,5},{8,10},{9,11},{10,... | collective-permute-start | bytes 294920 | tf_op jit(solution)/shard_map/ppermute | solution.py:381
  17.3 0.7 %collective-permute-start.7 = (bf16[96,512]{1,0:T(8,128)(2,1)S(1)}, bf16[96,512]{1,0:T(8,128)(2,1)S(1)}, u32[]{:S(2)}, u32[]{:S(2)}) collective-permute-start(bf16[96,512]{1,0:T(8,128)(2,1)S(1)} %get-tuple-element.53), channel_id=1, source_target_pairs={{0,18},{1,19},{2,16},{3,17},{4,22},{5,23},{6,20},{7,21},{8,26},{9,... | collective-permute-start | bytes 294920 | tf_op jit(solution)/shard_map/ppermute | solution.py:390
  18.1 1.5 %inner.1 = (bf16[4,64,512]{2,1,0:T(8,128)(2,1)S(1)}, bf16[4,64,512]{2,1,0:T(8,128)(2,1)S(1)}, bf16[4,64,512]{2,1,0:T(8,128)(2,1)S(1)}, bf16[4,64,512]{2,1,0:T(8,128)(2,1)S(1)}, bf16[544,512]{1,0:T(8,128)(2,1)S(1)}) custom-call(bf16[544,512]{1,0:T(8,128)(2,1)S(1)} %get-tuple-element.39.refs_0_, f32[512,256]{1,0:T(8,128)S(1)} %get-tuple-element.40.refs_1_, ...), custom_call_target="tpu_custom_call" | custom-call | flops 2000000000 | tf_op jit(solution)/shard_map/inner/pallas_call | solution.py:131
  19.6 1.6 %collective-permute-start.10 = (bf16[4,64,512]{2,1,0:T(8,128)(2,1)S(1)}, bf16[4,64,512]{2,1,0:T(8,128)(2,1)S(1)}, u32[]{:S(2)}, u32[]{:S(2)}) collective-permute-start(bf16[4,64,512]{2,1,0:T(8,128)(2,1)S(1)} %get-tuple-element.56), channel_id=1, source_target_pairs={{0,16},{16,0},{1,17},{17,1},{2,18},{18,2},{3,19},{19,3},{4,20},{20... | collective-permute-start | bytes 786440 | tf_op jit(solution)/shard_map/ppermute | solution.py:385
  21.2 1.3 %collective-permute-start.11 = (bf16[4,64,512]{2,1,0:T(8,128)(2,1)S(1)}, bf16[4,64,512]{2,1,0:T(8,128)(2,1)S(1)}, u32[]{:S(2)}, u32[]{:S(2)}) collective-permute-start(bf16[4,64,512]{2,1,0:T(8,128)(2,1)S(1)} %get-tuple-element.57), channel_id=1, source_target_pairs={{0,2},{1,3},{2,0},{3,1},{4,6},{5,7},{6,4},{7,5},{8,10},{9,11},{10,... | collective-permute-start | bytes 786440 | tf_op jit(solution)/shard_map/ppermute | solution.py:381
  22.4 0.7 %collective-permute-start.12 = (bf16[4,64,512]{2,1,0:T(8,128)(2,1)S(1)}, bf16[4,64,512]{2,1,0:T(8,128)(2,1)S(1)}, u32[]{:S(2)}, u32[]{:S(2)}) collective-permute-start(bf16[4,64,512]{2,1,0:T(8,128)(2,1)S(1)} %get-tuple-element.58), channel_id=1, source_target_pairs={{0,18},{1,19},{2,16},{3,17},{4,22},{5,23},{6,20},{7,21},{8,26},{9,... | collective-permute-start | bytes 786440 | tf_op jit(solution)/shard_map/ppermute | solution.py:390
  23.2 0.7 %signal.1 = (f32[128,512]{1,0:T(8,128)S(1)}, bf16[128,512]{1,0:T(8,128)(2,1)S(1)}, bf16[32,512]{1,0:T(8,128)(2,1)S(1)}) custom-call(bf16[544,512]{1,0:T(8,128)(2,1)S(1)} %get-tuple-element.46.refs_0_, bf16[512,512]{1,0:T(8,128)(2,1)S(1)} %get-tuple-element.44.refs_5_.refs_1_, f32[256,512]{1,0:T(8,128)S(1)} %get-tuple-element.47.refs_2_, ...), custom_call_target="tpu_custom_call" | custom-call | flops 1000000000 | tf_op jit(solution)/shard_map/signal/pallas_call | solution.py:131
  24.0 5.0 %collective-permute-done.8.refs_1_.refs_2_ = bf16[128,512]{1,0:T(8,128)(2,1)S(1)} collective-permute-done((bf16[128,512]{1,0:T(8,128)(2,1)S(1)}, bf16[128,512]{1,0:T(8,128)(2,1)S(1)}, u32[]{:S(2)}, u32[]{:S(2)}) %collective-permute-start.8) | collective-permute-done | bytes 131104 | tf_op jit(solution)/shard_map/ppermute | solution.py:381
  29.0 0.8 %collective-permute-start.9 = (bf16[128,512]{1,0:T(8,128)(2,1)S(1)}, bf16[128,512]{1,0:T(8,128)(2,1)S(1)}, u32[]{:S(2)}, u32[]{:S(2)}) collective-permute-start(bf16[128,512]{1,0:T(8,128)(2,1)S(1)} %res_sum_z1.1.refs_4_.refs_0_), channel_id=1, source_target_pairs={{0,8},{1,9},{2,10},{3,11},{4,12},{5,13},{6,14},{7,15},{8,0},{9,1},... | collective-permute-start | bytes 393224 | tf_op jit(solution)/shard_map/ppermute | solution.py:381
  30.4 3.7 %collective-permute-done.12.refs_3_ = bf16[4,64,512]{2,1,0:T(8,128)(2,1)S(1)} collective-permute-done((bf16[4,64,512]{2,1,0:T(8,128)(2,1)S(1)}, bf16[4,64,512]{2,1,0:T(8,128)(2,1)S(1)}, u32[]{:S(2)}, u32[]{:S(2)}) %collective-permute-start.12) | collective-permute-done | bytes 262176 | tf_op jit(solution)/shard_map/ppermute | solution.py:390
  34.3 0.9 %collective-permute-start.13 = (bf16[64,512]{1,0:T(8,128)(2,1)S(1)}, bf16[64,512]{1,0:T(8,128)(2,1)S(1)}, u32[]{:S(2)}, u32[]{:S(2)}) collective-permute-start(bf16[64,512]{1,0:T(8,128)(2,1)S(1)} %get-tuple-element.61), channel_id=1, source_target_pairs={{0,8},{1,9},{2,10},{3,11},{4,12},{5,13},{6,14},{7,15},{8,0},{9,1},... | collective-permute-start | bytes 196616 | tf_op jit(solution)/shard_map/ppermute | solution.py:381
  35.2 1.3 %collective-permute-start.14 = (bf16[64,512]{1,0:T(8,128)(2,1)S(1)}, bf16[64,512]{1,0:T(8,128)(2,1)S(1)}, u32[]{:S(2)}, u32[]{:S(2)}) collective-permute-start(bf16[64,512]{1,0:T(8,128)(2,1)S(1)} %get-tuple-element.62), channel_id=1, source_target_pairs={{0,12},{1,13},{2,14},{3,15},{4,8},{5,9},{6,10},{7,11},{8,4},{9,5},... | collective-permute-start | bytes 196616 | tf_op jit(solution)/shard_map/ppermute | solution.py:381
  36.5 1.3 %collective-permute-start.15 = (bf16[64,512]{1,0:T(8,128)(2,1)S(1)}, bf16[64,512]{1,0:T(8,128)(2,1)S(1)}, u32[]{:S(2)}, u32[]{:S(2)}) collective-permute-start(bf16[64,512]{1,0:T(8,128)(2,1)S(1)} %get-tuple-element.63), channel_id=1, source_target_pairs={{0,4},{1,5},{2,6},{3,7},{4,0},{5,1},{6,2},{7,3},{8,12},{9,13},{10,... | collective-permute-start | bytes 196616 | tf_op jit(solution)/shard_map/ppermute | solution.py:381
  37.9 2.0 %collective-permute-start.4 = (bf16[128,512]{1,0:T(8,128)(2,1)S(1)}, bf16[128,512]{1,0:T(8,128)(2,1)S(1)}, u32[]{:S(2)}, u32[]{:S(2)}) collective-permute-start(bf16[128,512]{1,0:T(8,128)(2,1)S(1)} %get-tuple-element.49), channel_id=1, source_target_pairs={{0,14},{1,15},{2,0},{3,1},{4,2},{5,3},{6,4},{7,5},{8,6},{9,7},{10,... | collective-permute-start | bytes 393224 | tf_op jit(solution)/shard_map/ppermute | solution.py:394
  39.9 1.0 %collective-permute-start.19 = (bf16[96,512]{1,0:T(8,128)(2,1)S(1)}, bf16[96,512]{1,0:T(8,128)(2,1)S(1)}, u32[]{:S(2)}, u32[]{:S(2)}) collective-permute-start(bf16[96,512]{1,0:T(8,128)(2,1)S(1)} %res_sum_z2.1.refs_4_.refs_0_), channel_id=1, source_target_pairs={{0,18},{1,19},{2,16},{3,17},{4,22},{5,23},{6,20},{7,21},{8,26},{9,... | collective-permute-start | bytes 294920 | tf_op jit(solution)/shard_map/ppermute | solution.py:390
  40.8 2.1 %collective-permute-start.18 = (bf16[96,512]{1,0:T(8,128)(2,1)S(1)}, bf16[96,512]{1,0:T(8,128)(2,1)S(1)}, u32[]{:S(2)}, u32[]{:S(2)}) collective-permute-start(bf16[96,512]{1,0:T(8,128)(2,1)S(1)} %res_sum_z2.1.refs_4_.refs_0_), channel_id=1, source_target_pairs={{0,2},{1,3},{2,0},{3,1},{4,6},{5,7},{6,4},{7,5},{8,10},{9,11},{10,... | collective-permute-start | bytes 294920 | tf_op jit(solution)/shard_map/ppermute | solution.py:381
  42.9 0.5 %collective-permute-start.17 = (bf16[96,512]{1,0:T(8,128)(2,1)S(1)}, bf16[96,512]{1,0:T(8,128)(2,1)S(1)}, u32[]{:S(2)}, u32[]{:S(2)}) collective-permute-start(bf16[96,512]{1,0:T(8,128)(2,1)S(1)} %res_sum_z2.1.refs_4_.refs_0_), channel_id=1, source_target_pairs={{0,16},{16,0},{1,17},{17,1},{2,18},{18,2},{3,19},{19,3},{4,20},{20... | collective-permute-start | bytes 294920 | tf_op jit(solution)/shard_map/ppermute | solution.py:385
  43.5 1.6 %collective-permute-start.16 = (bf16[64,512]{1,0:T(8,128)(2,1)S(1)}, bf16[64,512]{1,0:T(8,128)(2,1)S(1)}, u32[]{:S(2)}, u32[]{:S(2)}) collective-permute-start(bf16[64,512]{1,0:T(8,128)(2,1)S(1)} %conv_scaled.1.refs_0_.refs_4_), channel_id=1, source_target_pairs={{0,16},{16,0},{1,17},{17,1},{2,18},{18,2},{3,19},{19,3},{4,20},{20... | collective-permute-start | bytes 196616 | tf_op jit(solution)/shard_map/ppermute | solution.py:385
  45.1 0.7 %finish_signal.1 = (bf16[128,512]{1,0:T(8,128)(2,1)}, f32[8,128]{1,0:T(8,128)S(1)}) custom-call(f32[128,512]{1,0:T(8,128)S(1)} %get-tuple-element.48.refs_0_, bf16[128,512]{1,0:T(8,128)(2,1)S(1)} %collective-permute-done.4.refs_1_, bf16[128,512]{1,0:T(8,128)(2,1)S(1)} %collective-permute-done.8.refs_1_.refs_2_, ...), custom_call_target="tpu_custom_call" | custom-call | tf_op jit(solution)/shard_map/finish_signal/pallas_call | solution.py:131
  45.8 0.8 %collective-permute-done.18.refs_2_ = bf16[96,512]{1,0:T(8,128)(2,1)S(1)} collective-permute-done((bf16[96,512]{1,0:T(8,128)(2,1)S(1)}, bf16[96,512]{1,0:T(8,128)(2,1)S(1)}, u32[]{:S(2)}, u32[]{:S(2)}) %collective-permute-start.18) | collective-permute-done | bytes 98336 | tf_op jit(solution)/shard_map/ppermute | solution.py:381
  46.6 1.0 %collective-permute-done.17.refs_1_ = bf16[96,512]{1,0:T(8,128)(2,1)S(1)} collective-permute-done((bf16[96,512]{1,0:T(8,128)(2,1)S(1)}, bf16[96,512]{1,0:T(8,128)(2,1)S(1)}, u32[]{:S(2)}, u32[]{:S(2)}) %collective-permute-start.17) | collective-permute-done | bytes 98336 | tf_op jit(solution)/shard_map/ppermute | solution.py:385
  47.7 0.6 %collective-permute-done.16.refs_1_ = bf16[64,512]{1,0:T(8,128)(2,1)S(1)} collective-permute-done((bf16[64,512]{1,0:T(8,128)(2,1)S(1)}, bf16[64,512]{1,0:T(8,128)(2,1)S(1)}, u32[]{:S(2)}, u32[]{:S(2)}) %collective-permute-start.16) | collective-permute-done | bytes 65568 | tf_op jit(solution)/shard_map/ppermute | solution.py:385
  48.2 0.7 %finish_conv.1 = (bf16[2,64,512]{2,1,0:T(8,128)(2,1)}, f32[8,128]{1,0:T(8,128)S(1)}) custom-call(bf16[64,512]{1,0:T(8,128)(2,1)S(1)} %conv_scaled.1.refs_0_.refs_4_, bf16[64,512]{1,0:T(8,128)(2,1)S(1)} %collective-permute-done.16.refs_1_), custom_call_target="tpu_custom_call" | custom-call | flops 10000000000 | tf_op jit(solution)/shard_map/finish_conv/pallas_call | solution.py:131
  49.4 0.9 %finish_res.1 = bf16[2,256,768]{2,1,0:T(8,128)(2,1)} custom-call(bf16[4,96,512]{2,1,0:T(8,128)(2,1)S(1)} %res_in_order.1.refs_0_, bf16[4,96,512]{2,1,0:T(8,128)(2,1)S(1)} %collective-permute-done.20.refs_1_, f32[8,128]{1,0:T(8,128)S(1)} %get-tuple-element.66.refs_2_), custom_call_target="tpu_custom_call" | custom-call | tf_op jit(solution)/shard_map/finish_res/pallas_call | solution.py:131
  (25 shorter events, 2.1 us)
Async XLA Ops:
  0.6 10.1 %collective-permute-start.1 = (bf16[128,512]{1,0:T(8,128)(2,1)}, bf16[128,512]{1,0:T(8,128)(2,1)S(1)}, u32[]{:S(2)}, u32[]{:S(2)}) collective-permute-start(bf16[128,512]{1,0:T(8,128)(2,1)} %bitcast.5), channel_id=1, source_target_pairs={{0,2},{1,3},{2,4},{3,5},{4,6},{5,7},{6,8},{7,9},{8,10},{9,11},{10,... | collective-permute-start | bytes 393224 | tf_op jit(solution)/shard_map/ppermute | solution.py:394
  4.7 5.8 %collective-permute-start.2 = (bf16[32,512]{1,0:T(8,128)(2,1)S(1)}, bf16[32,512]{1,0:T(8,128)(2,1)S(1)}, u32[]{:S(2)}, u32[]{:S(2)}) collective-permute-start(bf16[32,512]{1,0:T(8,128)(2,1)S(1)} %get-tuple-element.36), channel_id=1, source_target_pairs={{0,4},{1,5},{2,6},{3,7},{4,8},{5,9},{6,10},{7,11},{8,12},{9,13},{1... | collective-permute-start | bytes 98312 | tf_op jit(solution)/shard_map/ppermute | solution.py:394
  6.3 5.9 %collective-permute-start = (bf16[128,1280]{1,0:T(8,128)(2,1)S(1)}, bf16[128,1280]{1,0:T(8,128)(2,1)S(1)}, u32[]{:S(2)}, u32[]{:S(2)}) collective-permute-start(bf16[128,1280]{1,0:T(8,128)(2,1)S(1)} %get-tuple-element.35.refs_0_), channel_id=1, source_target_pairs={{0,1},{1,0},{2,3},{3,2},{4,5},{5,4},{6,7},{7,6},{8,9},{9,8},{10,11... | collective-permute-start | bytes 983048 | tf_op jit(solution)/shard_map/ppermute | solution.py:381
  10.7 1.5 %collective-permute-start.3 = (bf16[160,512]{1,0:T(8,128)(2,1)S(1)}, bf16[160,512]{1,0:T(8,128)(2,1)S(1)}, u32[]{:S(2)}, u32[]{:S(2)}) collective-permute-start(bf16[160,512]{1,0:T(8,128)(2,1)S(1)} %pack_halo.1.refs_2_), channel_id=1, source_target_pairs={{0,1},{1,0},{2,3},{3,2},{4,5},{5,4},{6,7},{7,6},{8,9},{9,8},{10,11... | collective-permute-start | bytes 491528 | tf_op jit(solution)/shard_map/ppermute | solution.py:381
  14.5 7.9 %collective-permute-start.5 = (bf16[96,512]{1,0:T(8,128)(2,1)S(1)}, bf16[96,512]{1,0:T(8,128)(2,1)S(1)}, u32[]{:S(2)}, u32[]{:S(2)}) collective-permute-start(bf16[96,512]{1,0:T(8,128)(2,1)S(1)} %get-tuple-element.51), channel_id=1, source_target_pairs={{0,16},{16,0},{1,17},{17,1},{2,18},{18,2},{3,19},{19,3},{4,20},{20... | collective-permute-start | bytes 294920 | tf_op jit(solution)/shard_map/ppermute | solution.py:385
  16.1 7.8 %collective-permute-start.6 = (bf16[96,512]{1,0:T(8,128)(2,1)S(1)}, bf16[96,512]{1,0:T(8,128)(2,1)S(1)}, u32[]{:S(2)}, u32[]{:S(2)}) collective-permute-start(bf16[96,512]{1,0:T(8,128)(2,1)S(1)} %get-tuple-element.52), channel_id=1, source_target_pairs={{0,2},{1,3},{2,0},{3,1},{4,6},{5,7},{6,4},{7,5},{8,10},{9,11},{10,... | collective-permute-start | bytes 294920 | tf_op jit(solution)/shard_map/ppermute | solution.py:381
  17.3 6.5 %collective-permute-start.7 = (bf16[96,512]{1,0:T(8,128)(2,1)S(1)}, bf16[96,512]{1,0:T(8,128)(2,1)S(1)}, u32[]{:S(2)}, u32[]{:S(2)}) collective-permute-start(bf16[96,512]{1,0:T(8,128)(2,1)S(1)} %get-tuple-element.53), channel_id=1, source_target_pairs={{0,18},{1,19},{2,16},{3,17},{4,22},{5,23},{6,20},{7,21},{8,26},{9,... | collective-permute-start | bytes 294920 | tf_op jit(solution)/shard_map/ppermute | solution.py:390
  19.6 10.6 %collective-permute-start.10 = (bf16[4,64,512]{2,1,0:T(8,128)(2,1)S(1)}, bf16[4,64,512]{2,1,0:T(8,128)(2,1)S(1)}, u32[]{:S(2)}, u32[]{:S(2)}) collective-permute-start(bf16[4,64,512]{2,1,0:T(8,128)(2,1)S(1)} %get-tuple-element.56), channel_id=1, source_target_pairs={{0,16},{16,0},{1,17},{17,1},{2,18},{18,2},{3,19},{19,3},{4,20},{20... | collective-permute-start | bytes 786440 | tf_op jit(solution)/shard_map/ppermute | solution.py:385
  21.2 9.2 %collective-permute-start.11 = (bf16[4,64,512]{2,1,0:T(8,128)(2,1)S(1)}, bf16[4,64,512]{2,1,0:T(8,128)(2,1)S(1)}, u32[]{:S(2)}, u32[]{:S(2)}) collective-permute-start(bf16[4,64,512]{2,1,0:T(8,128)(2,1)S(1)} %get-tuple-element.57), channel_id=1, source_target_pairs={{0,2},{1,3},{2,0},{3,1},{4,6},{5,7},{6,4},{7,5},{8,10},{9,11},{10,... | collective-permute-start | bytes 786440 | tf_op jit(solution)/shard_map/ppermute | solution.py:381
  22.4 11.6 %collective-permute-start.12 = (bf16[4,64,512]{2,1,0:T(8,128)(2,1)S(1)}, bf16[4,64,512]{2,1,0:T(8,128)(2,1)S(1)}, u32[]{:S(2)}, u32[]{:S(2)}) collective-permute-start(bf16[4,64,512]{2,1,0:T(8,128)(2,1)S(1)} %get-tuple-element.58), channel_id=1, source_target_pairs={{0,18},{1,19},{2,16},{3,17},{4,22},{5,23},{6,20},{7,21},{8,26},{9,... | collective-permute-start | bytes 786440 | tf_op jit(solution)/shard_map/ppermute | solution.py:390
  23.9 5.0 %collective-permute-start.8 = (bf16[128,512]{1,0:T(8,128)(2,1)S(1)}, bf16[128,512]{1,0:T(8,128)(2,1)S(1)}, u32[]{:S(2)}, u32[]{:S(2)}) collective-permute-start(bf16[128,512]{1,0:T(8,128)(2,1)S(1)} %res_sum_xy.1.refs_0_), channel_id=1, source_target_pairs={{0,4},{1,5},{2,6},{3,7},{4,0},{5,1},{6,2},{7,3},{8,12},{9,13},{10,... | collective-permute-start | bytes 393224 | tf_op jit(solution)/shard_map/ppermute | solution.py:381
  29.0 10.8 %collective-permute-start.9 = (bf16[128,512]{1,0:T(8,128)(2,1)S(1)}, bf16[128,512]{1,0:T(8,128)(2,1)S(1)}, u32[]{:S(2)}, u32[]{:S(2)}) collective-permute-start(bf16[128,512]{1,0:T(8,128)(2,1)S(1)} %res_sum_z1.1.refs_4_.refs_0_), channel_id=1, source_target_pairs={{0,8},{1,9},{2,10},{3,11},{4,12},{5,13},{6,14},{7,15},{8,0},{9,1},... | collective-permute-start | bytes 393224 | tf_op jit(solution)/shard_map/ppermute | solution.py:381
  34.3 6.5 %collective-permute-start.13 = (bf16[64,512]{1,0:T(8,128)(2,1)S(1)}, bf16[64,512]{1,0:T(8,128)(2,1)S(1)}, u32[]{:S(2)}, u32[]{:S(2)}) collective-permute-start(bf16[64,512]{1,0:T(8,128)(2,1)S(1)} %get-tuple-element.61), channel_id=1, source_target_pairs={{0,8},{1,9},{2,10},{3,11},{4,12},{5,13},{6,14},{7,15},{8,0},{9,1},... | collective-permute-start | bytes 196616 | tf_op jit(solution)/shard_map/ppermute | solution.py:381
  35.2 7.8 %collective-permute-start.14 = (bf16[64,512]{1,0:T(8,128)(2,1)S(1)}, bf16[64,512]{1,0:T(8,128)(2,1)S(1)}, u32[]{:S(2)}, u32[]{:S(2)}) collective-permute-start(bf16[64,512]{1,0:T(8,128)(2,1)S(1)} %get-tuple-element.62), channel_id=1, source_target_pairs={{0,12},{1,13},{2,14},{3,15},{4,8},{5,9},{6,10},{7,11},{8,4},{9,5},... | collective-permute-start | bytes 196616 | tf_op jit(solution)/shard_map/ppermute | solution.py:381
  36.5 6.9 %collective-permute-start.15 = (bf16[64,512]{1,0:T(8,128)(2,1)S(1)}, bf16[64,512]{1,0:T(8,128)(2,1)S(1)}, u32[]{:S(2)}, u32[]{:S(2)}) collective-permute-start(bf16[64,512]{1,0:T(8,128)(2,1)S(1)} %get-tuple-element.63), channel_id=1, source_target_pairs={{0,4},{1,5},{2,6},{3,7},{4,0},{5,1},{6,2},{7,3},{8,12},{9,13},{10,... | collective-permute-start | bytes 196616 | tf_op jit(solution)/shard_map/ppermute | solution.py:381
  37.9 7.2 %collective-permute-start.4 = (bf16[128,512]{1,0:T(8,128)(2,1)S(1)}, bf16[128,512]{1,0:T(8,128)(2,1)S(1)}, u32[]{:S(2)}, u32[]{:S(2)}) collective-permute-start(bf16[128,512]{1,0:T(8,128)(2,1)S(1)} %get-tuple-element.49), channel_id=1, source_target_pairs={{0,14},{1,15},{2,0},{3,1},{4,2},{5,3},{6,4},{7,5},{8,6},{9,7},{10,... | collective-permute-start | bytes 393224 | tf_op jit(solution)/shard_map/ppermute | solution.py:394
  39.9 5.9 %collective-permute-start.19 = (bf16[96,512]{1,0:T(8,128)(2,1)S(1)}, bf16[96,512]{1,0:T(8,128)(2,1)S(1)}, u32[]{:S(2)}, u32[]{:S(2)}) collective-permute-start(bf16[96,512]{1,0:T(8,128)(2,1)S(1)} %res_sum_z2.1.refs_4_.refs_0_), channel_id=1, source_target_pairs={{0,18},{1,19},{2,16},{3,17},{4,22},{5,23},{6,20},{7,21},{8,26},{9,... | collective-permute-start | bytes 294920 | tf_op jit(solution)/shard_map/ppermute | solution.py:390
  40.8 5.7 %collective-permute-start.18 = (bf16[96,512]{1,0:T(8,128)(2,1)S(1)}, bf16[96,512]{1,0:T(8,128)(2,1)S(1)}, u32[]{:S(2)}, u32[]{:S(2)}) collective-permute-start(bf16[96,512]{1,0:T(8,128)(2,1)S(1)} %res_sum_z2.1.refs_4_.refs_0_), channel_id=1, source_target_pairs={{0,2},{1,3},{2,0},{3,1},{4,6},{5,7},{6,4},{7,5},{8,10},{9,11},{10,... | collective-permute-start | bytes 294920 | tf_op jit(solution)/shard_map/ppermute | solution.py:381
  42.9 4.6 %collective-permute-start.17 = (bf16[96,512]{1,0:T(8,128)(2,1)S(1)}, bf16[96,512]{1,0:T(8,128)(2,1)S(1)}, u32[]{:S(2)}, u32[]{:S(2)}) collective-permute-start(bf16[96,512]{1,0:T(8,128)(2,1)S(1)} %res_sum_z2.1.refs_4_.refs_0_), channel_id=1, source_target_pairs={{0,16},{16,0},{1,17},{17,1},{2,18},{18,2},{3,19},{19,3},{4,20},{20... | collective-permute-start | bytes 294920 | tf_op jit(solution)/shard_map/ppermute | solution.py:385
  43.5 4.8 %collective-permute-start.16 = (bf16[64,512]{1,0:T(8,128)(2,1)S(1)}, bf16[64,512]{1,0:T(8,128)(2,1)S(1)}, u32[]{:S(2)}, u32[]{:S(2)}) collective-permute-start(bf16[64,512]{1,0:T(8,128)(2,1)S(1)} %conv_scaled.1.refs_0_.refs_4_), channel_id=1, source_target_pairs={{0,16},{16,0},{1,17},{17,1},{2,18},{18,2},{3,19},{19,3},{4,20},{20... | collective-permute-start | bytes 196616 | tf_op jit(solution)/shard_map/ppermute | solution.py:385
  47.6 1.8 %collective-permute-start.20 = (bf16[4,96,512]{2,1,0:T(8,128)(2,1)S(1)}, bf16[4,96,512]{2,1,0:T(8,128)(2,1)S(1)}, u32[]{:S(2)}, u32[]{:S(2)}) collective-permute-start(bf16[4,96,512]{2,1,0:T(8,128)(2,1)S(1)} %res_in_order.1.refs_0_), channel_id=1, source_target_pairs={{0,1},{1,0},{2,3},{3,2},{4,5},{5,4},{6,7},{7,6},{8,9},{9,8},{10,11... | collective-permute-start | bytes 1179656 | tf_op jit(solution)/shard_map/ppermute | solution.py:381

commit v7 on v6

--- a/solution.py
+++ b/solution.py
@@ -253,8 +253,8 @@
 
 
 def inner_kernel(
-    xin, a, b, x1, dz1, outer, es, rw,
-    mine, by_y, by_x, by_both, dz,
+    xin, a, b, x1, dz1, outer, es, cw, rw,
+    mine, by_y, by_x, by_both, dz, tail,
     staged,
 ):
     width = xin.shape[1]
@@ -265,6 +265,7 @@
     dz0 = jnp.concatenate([e0 * a[...], e0 * b[...]], axis=1).astype(BF16)
     dz[0 : 4 * t, :] = dz0
     dz[4 * t :, :] = jnp.zeros((near, width), BF16)
+    tail[...] = mm_nt(dz0[0:near, :], cw[0, 0:width, :]).astype(BF16)
     half = width // 16
     rows = 2 * half
     blocks = width // rows
@@ -281,7 +282,7 @@
     split_quarters(staged, mine, by_y, by_x, by_both)
 
 
-def signal_kernel(dz, outer, ga, cw, own_out, back_out, tail_out):
+def signal_kernel(dz, outer, ga, cw, own_out, back_out):
     t = ga.shape[0] // 2
     near = t // 4
     width = ga.shape[1]
@@ -290,13 +291,11 @@
     long = t + near
     back = dz[pl.ds(at, long), :]
     here_dz = dz[pl.ds(2 * t + at, long), :]
-    first = mm_nt(dz[0:near, :], cw[0, 0:width, :]).astype(BF16)
     both = jnp.concatenate([back, here_dz], axis=0)
     wp = mm_nt(both, cw[0, 0:width, :]).astype(BF16)
     wx = mm_nt(both, cw[0, width:, :])
     back_out[...] = (outer[pl.ds(at, t), :].astype(F32) + wx[0:t, :] + wp[near:long, :].astype(F32)).astype(BF16)
     own_out[...] = ga[pl.ds(at, t), :] + wx[long : long + t, :] + wp[long + near :, :].astype(F32)
-    tail_out[...] = first
 
 
 def total_of(*refs):
@@ -351,7 +350,7 @@
         conv[1, rows, :] = ref[half:, :]
 
 
-def finish_res_kernel(mine, other, res):
+def finish_kernel(mine, other, own, come, got1, got2, res, grad):
     _, _, core = here()
     eighth = res.shape[1] // 8
     width, part = mine.shape[2], mine.shape[2] // 2
@@ -362,19 +361,19 @@
             res[0, rows, 0:width] = ref[q, eighth : 2 * eighth, :]
             res[1, rows, width:] = ref[q, 2 * eighth :, 0:part]
             res[0, rows, width:] = ref[q, 2 * eighth :, part:]
-
-
-def finish_signal_kernel(own, come, got1, got2, out, done):
-    done[...] = jnp.zeros_like(done)
     t = own.shape[0]
     near = t // 4
     first = got1.shape[0] - near
-    g, _, core = here()
+    g, _, _ = here()
     total = own[...] + jnp.where(lax.axis_index("tm") < 14, come[...].astype(F32), 0.0)
-    out[0 : t - near, :] = total[0 : t - near, :].astype(BF16)
+    grad[0 : t - near, :] = total[0 : t - near, :].astype(BF16)
     last = jnp.where(lax.rem(g, 2) == 0, got1[first:, :], got2[first:, :]).astype(F32)
     last = jnp.where((g < 3) & (core == 1), last, 0.0)
-    out[t - near :, :] = (total[t - near :, :] + last).astype(BF16)
+    grad[t - near :, :] = (total[t - near :, :] + last).astype(BF16)
+
+
+def hold_kernel(a, out):
+    out[...] = a[...]
 
 
 def swap(x, distance):
@@ -434,16 +433,11 @@
     )
     piece = (2 * half, width)
     part = shaped((4,) + piece)
-    *csplit, dz0 = call(
-        inner_kernel, [part, part, part, part, shaped((4 * t + near, width))],
-        xin, a, b, x1, dz1, outer, es, rw,
+    *csplit, dz0, tail = call(
+        inner_kernel, [part, part, part, part, shaped((4 * t + near, width)), shaped((near, width))],
+        xin, a, b, x1, dz1, outer, es, cw, rw,
         scratch=[pltpu.VMEM((2, 4, 4) + piece, BF16)], vmem=16, flops=2_000_000_000, name="inner",
     )
-    own, back, tail = call(
-        signal_kernel, [shaped((t, width), F32), shaped((t, width)), shaped((near, width))],
-        dz0, outer, ga, cw, vmem=16, flops=1_000_000_000, name="signal",
-    )
-
     def around(by_y, by_x, by_both):
         both = swap_both(by_both, 2)
         beside = swap(by_x, 2)
@@ -451,38 +445,40 @@
 
     rterms = (rsplit[0],) + around(*rsplit[1:])
     cterms = (csplit[0],) + around(*csplit[1:])
-    come = shift(back, -2)
     long = shaped((res_rows + near, width))
     (rsum,) = call(sum_xy_kernel, [long], *rterms, tail, after=(csplit[0],), name="res_sum_xy")
     rgot1 = swap(rsum, 4)
+    own, back = call(
+        signal_kernel, [shaped((t, width), F32), shaped((t, width))], dz0, outer, ga, cw,
+        after=(rsum,), vmem=16, flops=1_000_000_000, name="signal",
+    )
     (rsum,) = call(functools.partial(sum_z1_kernel, res_rows), [long], rsum, rgot1, name="res_sum_z1")
     rgot2 = swap(rsum, 8)
     ckeep, *csend = call(
         groups_kernel, [shaped(piece, F32)] + [shaped(piece)] * 3, *cterms,
-        after=(rsum,), scratch=[pltpu.VMEM((4,) + piece, F32)], name="conv_groups",
+        after=(rsum, back), scratch=[pltpu.VMEM((4,) + piece, F32)], name="conv_groups",
     )
     cgot = [swap(csend[k - 1], 4 * k) for k in (2, 3, 1)]
-    input_grad, done = call(
-        finish_signal_kernel, [shaped((t, width)), shaped((8, 128), F32)], own, come, rgot1, rgot2,
-        after=(ckeep,), name="finish_signal",
-    )
     (quarter,) = call(
         functools.partial(sum_z2_kernel, factor), [res], rsum, rgot2, after=(ckeep,), name="res_sum_z2"
     )
     rparts = (quarter, swap_streams(quarter), swap(quarter, 2), swap_both(quarter, 2))
+    (back,) = call(hold_kernel, [shaped((t, width))], back, after=(ckeep,), name="hold")
+    come = shift(back, -2)
     (mine,) = call(
         functools.partial(scaled_sum_kernel, factor), [shaped(piece)], ckeep, *cgot,
         after=(quarter,), flops=10_000_000_000, name="conv_scaled",
     )
     other = swap_streams(mine)
-    (ordered,) = call(in_order_kernel, [shaped((4, res_rows, width))], *rparts, after=(mine, done), name="res_in_order")
+    (ordered,) = call(in_order_kernel, [shaped((4, res_rows, width))], *rparts, after=(mine,), name="res_in_order")
     rgot = swap(ordered, 1)
     conv_grad, conv_done = call(
         finish_conv_kernel, [shaped((2,) + piece), shaped((8, 128), F32)], mine, other,
         flops=10_000_000_000, name="finish_conv",
     )
-    (res_grad,) = call(
-        finish_res_kernel, [shaped(res_weight.shape)], ordered, rgot, after=(conv_done,), name="finish_res"
+    res_grad, input_grad = call(
+        finish_kernel, [shaped(res_weight.shape), shaped((t, width))], ordered, rgot, own, come, rgot1, rgot2,
+        after=(conv_done,), name="finish",
     )
     return (input_grad.reshape(s_dev, t, width), conv_grad, res_grad)
 

time: 50.5 us -> 49.4 us (0.978)
  waiting for transfers between devices: 16.1 us -> 15.2 us
  Pallas kernels: 10.1 us -> 9.33 us
  starting transfers between devices: 23.4 us -> 24 us
    ppermute x11, starting transfers between devices: 9.12 us -> 7.81 us  [swap(): return lax.ppermute(x, 'tm', [(i, i ^ distance) for i in range(16)])]
    ppermute x3, waiting for transfers between devices: 2.63 us -> 3.93 us  [shift(): return lax.ppermute(x, 'tm', [(i, (i + distance) % 16) for i in range(16)])]
    ppermute x3, starting transfers between devices: 2.41 us -> 3.65 us  [swap_both(): return lax.ppermute(x, ('dp', 'tm'), route)]
    ppermute x11, waiting for transfers between devices: 7.87 us -> 6.63 us  [swap(): return lax.ppermute(x, 'tm', [(i, i ^ distance) for i in range(16)])]
    ppermute x4, waiting for transfers between devices: 1.96 us -> 0.98 us  [swap_streams(): return lax.ppermute(x, 'dp', [(0, 1), (1, 0)])]
    pallas_call x13, Pallas kernels: 7.25 us -> 6.51 us  [call(): pl.pallas_call(run, out_shape=outs, in_specs=[in_vmem] * n_args + [pl.Blo...]
    ppermute x3, starting transfers between devices: 6.58 us -> 7.27 us  [shift(): return lax.ppermute(x, 'tm', [(i, (i + distance) % 16) for i in range(16)])]
  transfers between devices with their start and end apart: 21 -> 21, of which waited for: 11 -> 9; matrix products, arithmetic and copies ran while one was open for 0% -> 0% of each run, Pallas kernels for 14% -> 12%
where the time goes in v7:
time: 49.4 us; the launch traced here: 49.2 us
  starting transfers between devices  24 us (49%)
  waiting for transfers between devices  15.2 us (31%)
  Pallas kernels  9.33 us (19%)
  between operations  0.75 us (2%)
    ppermute x11, starting transfers between devices, swap(): return lax.ppermute(x, 'tm', [(i, i ^ distance) for i in range(16)])  7.81 us
    ppermute x3, starting transfers between devices, shift(): return lax.ppermute(x, 'tm', [(i, (i + distance) % 16) for i in range(16)])  7.27 us
    ppermute x11, waiting for transfers between devices, swap(): return lax.ppermute(x, 'tm', [(i, i ^ distance) for i in range(16)])  6.63 us
    pallas_call x13, Pallas kernels, call(): pl.pallas_call(run, out_shape=outs, in_specs=[in_vmem] * n_args + [pl.Blo...  6.51 us
    ppermute x4, starting transfers between devices, swap_streams(): return lax.ppermute(x, 'dp', [(0, 1), (1, 0)])  5.24 us
    ppermute x3, waiting for transfers between devices, shift(): return lax.ppermute(x, 'tm', [(i, (i + distance) % 16) for i in range(16)])  3.93 us
    ppermute x3, starting transfers between devices, swap_both(): return lax.ppermute(x, ('dp', 'tm'), route)  3.65 us
    ppermute x3, waiting for transfers between devices, swap_both(): return lax.ppermute(x, ('dp', 'tm'), route)  3.62 us
  transfers between devices with their start and end apart: 21, of which 9 were waited for; matrix products, arithmetic and copies ran while one was open for 0% of the time, Pallas kernels for 12%

profile of v7, /device:TPU:0, one launch (start us, length us, event | category | flops | bytes accessed | tf_op | source)
XLA Modules:
  0.0 49.2 jit_solution(7136974946858880550)
XLA Ops:
  0.6 3.0 %collective-permute-start.1 = (bf16[128,512]{1,0:T(8,128)(2,1)}, bf16[128,512]{1,0:T(8,128)(2,1)S(1)}, u32[]{:S(2)}, u32[]{:S(2)}) collective-permute-start(bf16[128,512]{1,0:T(8,128)(2,1)} %bitcast.5), channel_id=1, source_target_pairs={{0,2},{1,3},{2,4},{3,5},{4,6},{5,7},{6,8},{7,9},{8,10},{9,11},{10,... | collective-permute-start | bytes 393224 | tf_op jit(solution)/shard_map/ppermute | solution.py:393
  3.6 1.0 %load_slab.1 = (bf16[128,1280]{1,0:T(8,128)(2,1)S(1)}, bf16[32,512]{1,0:T(8,128)(2,1)S(1)}) custom-call(bf16[128,512]{1,0:T(8,128)(2,1)} %bitcast.6, bf16[128,512]{1,0:T(8,128)(2,1)} %bitcast.4, bf16[128,256]{1,0:T(8,128)(2,1)} %bitcast.7), custom_call_target="tpu_custom_call" | custom-call | tf_op jit(solution)/shard_map/load_slab/pallas_call | solution.py:177
  4.7 1.6 %collective-permute-start.2 = (bf16[32,512]{1,0:T(8,128)(2,1)S(1)}, bf16[32,512]{1,0:T(8,128)(2,1)S(1)}, u32[]{:S(2)}, u32[]{:S(2)}) collective-permute-start(bf16[32,512]{1,0:T(8,128)(2,1)S(1)} %get-tuple-element.36), channel_id=1, source_target_pairs={{0,4},{1,5},{2,6},{3,7},{4,8},{5,9},{6,10},{7,11},{8,12},{9,13},{1... | collective-permute-start | bytes 98312 | tf_op jit(solution)/shard_map/ppermute | solution.py:393
  6.3 1.8 %load_weights.1 = (bf16[2,1024,512]{2,1,0:T(8,128)(2,1)S(1)}, bf16[2,256,768]{2,1,0:T(8,128)(2,1)S(1)}) custom-call(bf16[2,1024,512]{2,1,0:T(8,128)(2,1)} %cw.1, bf16[2,256,768]{2,1,0:T(8,128)(2,1)} %rw.1), custom_call_target="tpu_custom_call" | custom-call | flops 4000000000 | tf_op jit(solution)/shard_map/load_weights/pallas_call | solution.py:177
  8.1 2.3 %collective-permute-done.2.refs_1_ = bf16[32,512]{1,0:T(8,128)(2,1)S(1)} collective-permute-done((bf16[32,512]{1,0:T(8,128)(2,1)S(1)}, bf16[32,512]{1,0:T(8,128)(2,1)S(1)}, u32[]{:S(2)}, u32[]{:S(2)}) %collective-permute-start.2) | collective-permute-done | bytes 32800 | tf_op jit(solution)/shard_map/ppermute | solution.py:393
  10.4 0.3 collective-permute-done.1.refs_0_
  10.8 1.4 %collective-permute-done.3.refs_3_ = bf16[160,512]{1,0:T(8,128)(2,1)S(1)} collective-permute-done((bf16[160,512]{1,0:T(8,128)(2,1)S(1)}, bf16[160,512]{1,0:T(8,128)(2,1)S(1)}, u32[]{:S(2)}, u32[]{:S(2)}) %collective-permute-start.3) | collective-permute-done | bytes 163872 | tf_op jit(solution)/shard_map/ppermute | solution.py:380
  12.2 2.3 %forward_and_outer.1 = (bf16[96,512]{1,0:T(8,128)(2,1)S(1)}, bf16[96,512]{1,0:T(8,128)(2,1)S(1)}, bf16[96,512]{1,0:T(8,128)(2,1)S(1)}, bf16[96,512]{1,0:T(8,128)...) custom-call(bf16[128,1280]{1,0:T(8,128)(2,1)S(1)} %get-tuple-element, ...), custom_call_target="tpu_custom_call" | custom-call | tf_op jit(solution)/shard_map/forward_and_outer/pallas_call | solution.py:131
  14.5 1.6 %collective-permute-start.4 = (bf16[96,512]{1,0:T(8,128)(2,1)S(1)}, bf16[96,512]{1,0:T(8,128)(2,1)S(1)}, u32[]{:S(2)}, u32[]{:S(2)}) collective-permute-start(bf16[96,512]{1,0:T(8,128)(2,1)S(1)} %get-tuple-element.40), channel_id=1, source_target_pairs={{0,16},{16,0},{1,17},{17,1},{2,18},{18,2},{3,19},{19,3},{4,20},{20... | collective-permute-start | bytes 294920 | tf_op jit(solution)/shard_map/ppermute | solution.py:384
  16.1 1.3 %collective-permute-start.5 = (bf16[96,512]{1,0:T(8,128)(2,1)S(1)}, bf16[96,512]{1,0:T(8,128)(2,1)S(1)}, u32[]{:S(2)}, u32[]{:S(2)}) collective-permute-start(bf16[96,512]{1,0:T(8,128)(2,1)S(1)} %get-tuple-element.41), channel_id=1, source_target_pairs={{0,2},{1,3},{2,0},{3,1},{4,6},{5,7},{6,4},{7,5},{8,10},{9,11},{10,... | collective-permute-start | bytes 294920 | tf_op jit(solution)/shard_map/ppermute | solution.py:380
  17.3 0.7 %collective-permute-start.6 = (bf16[96,512]{1,0:T(8,128)(2,1)S(1)}, bf16[96,512]{1,0:T(8,128)(2,1)S(1)}, u32[]{:S(2)}, u32[]{:S(2)}) collective-permute-start(bf16[96,512]{1,0:T(8,128)(2,1)S(1)} %get-tuple-element.42), channel_id=1, source_target_pairs={{0,18},{1,19},{2,16},{3,17},{4,22},{5,23},{6,20},{7,21},{8,26},{9,... | collective-permute-start | bytes 294920 | tf_op jit(solution)/shard_map/ppermute | solution.py:389
  18.1 1.6 %inner.1 = (bf16[4,64,512]{2,1,0:T(8,128)(2,1)S(1)}, bf16[4,64,512]{2,1,0:T(8,128)(2,1)S(1)}, bf16[4,64,512]{2,1,0:T(8,128)(2,1)S(1)}, bf16[4,64,512]{2,1,0:T(8,...) custom-call(bf16[544,512]{1,0:T(8,128)(2,1)S(1)} %get-tuple-element.43.refs_0_, ...), custom_call_target="tpu_custom_call" | custom-call | flops 2000000000 | tf_op jit(solution)/shard_map/inner/pallas_call | solution.py:131
  19.6 1.6 %collective-permute-start.9 = (bf16[4,64,512]{2,1,0:T(8,128)(2,1)S(1)}, bf16[4,64,512]{2,1,0:T(8,128)(2,1)S(1)}, u32[]{:S(2)}, u32[]{:S(2)}) collective-permute-start(bf16[4,64,512]{2,1,0:T(8,128)(2,1)S(1)} %get-tuple-element.52), channel_id=1, source_target_pairs={{0,16},{16,0},{1,17},{17,1},{2,18},{18,2},{3,19},{19,3},{4,20},{20... | collective-permute-start | bytes 786440 | tf_op jit(solution)/shard_map/ppermute | solution.py:384
  21.2 1.3 %collective-permute-start.10 = (bf16[4,64,512]{2,1,0:T(8,128)(2,1)S(1)}, bf16[4,64,512]{2,1,0:T(8,128)(2,1)S(1)}, u32[]{:S(2)}, u32[]{:S(2)}) collective-permute-start(bf16[4,64,512]{2,1,0:T(8,128)(2,1)S(1)} %get-tuple-element.53), channel_id=1, source_target_pairs={{0,2},{1,3},{2,0},{3,1},{4,6},{5,7},{6,4},{7,5},{8,10},{9,11},{10,... | collective-permute-start | bytes 786440 | tf_op jit(solution)/shard_map/ppermute | solution.py:380
  22.5 0.7 %collective-permute-start.11 = (bf16[4,64,512]{2,1,0:T(8,128)(2,1)S(1)}, bf16[4,64,512]{2,1,0:T(8,128)(2,1)S(1)}, u32[]{:S(2)}, u32[]{:S(2)}) collective-permute-start(bf16[4,64,512]{2,1,0:T(8,128)(2,1)S(1)} %get-tuple-element.54), channel_id=1, source_target_pairs={{0,18},{1,19},{2,16},{3,17},{4,22},{5,23},{6,20},{7,21},{8,26},{9,... | collective-permute-start | bytes 786440 | tf_op jit(solution)/shard_map/ppermute | solution.py:389
  23.3 5.0 %collective-permute-done.7.refs_1_.refs_4_ = bf16[128,512]{1,0:T(8,128)(2,1)S(1)} collective-permute-done((bf16[128,512]{1,0:T(8,128)(2,1)S(1)}, bf16[128,512]{1,0:T(8,128)(2,1)S(1)}, u32[]{:S(2)}, u32[]{:S(2)}) %collective-permute-start.7) | collective-permute-done | bytes 131104 | tf_op jit(solution)/shard_map/ppermute | solution.py:380
  28.3 0.8 %collective-permute-start.8 = (bf16[128,512]{1,0:T(8,128)(2,1)S(1)}, bf16[128,512]{1,0:T(8,128)(2,1)S(1)}, u32[]{:S(2)}, u32[]{:S(2)}) collective-permute-start(bf16[128,512]{1,0:T(8,128)(2,1)S(1)} %res_sum_z1.1.refs_4_.refs_0_), channel_id=1, source_target_pairs={{0,8},{1,9},{2,10},{3,11},{4,12},{5,13},{6,14},{7,15},{8,0},{9,1},... | collective-permute-start | bytes 393224 | tf_op jit(solution)/shard_map/ppermute | solution.py:380
  29.1 0.5 %signal.1 = (f32[128,512]{1,0:T(8,128)S(1)}, bf16[128,512]{1,0:T(8,128)(2,1)S(1)}) custom-call(bf16[544,512]{1,0:T(8,128)(2,1)S(1)} %get-tuple-element.55.refs_0_, bf16[512,512]{1,0:T(8,128)(2,1)S(1)} %get-tuple-element.48.refs_5_.refs_1_, f32[256,512]{1,0:T(8,128)S(1)} %get-tuple-element.56.refs_2_, ...), custom_call_target="tpu_custom_call" | custom-call | flops 1000000000 | tf_op jit(solution)/shard_map/signal/pallas_call | solution.py:131
  29.6 0.6 %collective-permute-done.9.refs_1_ = bf16[4,64,512]{2,1,0:T(8,128)(2,1)S(1)} collective-permute-done((bf16[4,64,512]{2,1,0:T(8,128)(2,1)S(1)}, bf16[4,64,512]{2,1,0:T(8,128)(2,1)S(1)}, u32[]{:S(2)}, u32[]{:S(2)}) %collective-permute-start.9) | collective-permute-done | bytes 262176 | tf_op jit(solution)/shard_map/ppermute | solution.py:384
  30.5 3.6 %collective-permute-done.11.refs_3_ = bf16[4,64,512]{2,1,0:T(8,128)(2,1)S(1)} collective-permute-done((bf16[4,64,512]{2,1,0:T(8,128)(2,1)S(1)}, bf16[4,64,512]{2,1,0:T(8,128)(2,1)S(1)}, u32[]{:S(2)}, u32[]{:S(2)}) %collective-permute-start.11) | collective-permute-done | bytes 262176 | tf_op jit(solution)/shard_map/ppermute | solution.py:389
  34.3 0.9 %collective-permute-start.15 = (bf16[64,512]{1,0:T(8,128)(2,1)S(1)}, bf16[64,512]{1,0:T(8,128)(2,1)S(1)}, u32[]{:S(2)}, u32[]{:S(2)}) collective-permute-start(bf16[64,512]{1,0:T(8,128)(2,1)S(1)} %get-tuple-element.59), channel_id=1, source_target_pairs={{0,8},{1,9},{2,10},{3,11},{4,12},{5,13},{6,14},{7,15},{8,0},{9,1},... | collective-permute-start | bytes 196616 | tf_op jit(solution)/shard_map/ppermute | solution.py:380
  35.2 1.3 %collective-permute-start.16 = (bf16[64,512]{1,0:T(8,128)(2,1)S(1)}, bf16[64,512]{1,0:T(8,128)(2,1)S(1)}, u32[]{:S(2)}, u32[]{:S(2)}) collective-permute-start(bf16[64,512]{1,0:T(8,128)(2,1)S(1)} %get-tuple-element.60), channel_id=1, source_target_pairs={{0,12},{1,13},{2,14},{3,15},{4,8},{5,9},{6,10},{7,11},{8,4},{9,5},... | collective-permute-start | bytes 196616 | tf_op jit(solution)/shard_map/ppermute | solution.py:380
  36.5 1.3 %collective-permute-start.17 = (bf16[64,512]{1,0:T(8,128)(2,1)S(1)}, bf16[64,512]{1,0:T(8,128)(2,1)S(1)}, u32[]{:S(2)}, u32[]{:S(2)}) collective-permute-start(bf16[64,512]{1,0:T(8,128)(2,1)S(1)} %get-tuple-element.61), channel_id=1, source_target_pairs={{0,4},{1,5},{2,6},{3,7},{4,0},{5,1},{6,2},{7,3},{8,12},{9,13},{10,... | collective-permute-start | bytes 196616 | tf_op jit(solution)/shard_map/ppermute | solution.py:380
  37.9 2.2 %collective-permute-start.14 = (bf16[96,512]{1,0:T(8,128)(2,1)S(1)}, bf16[96,512]{1,0:T(8,128)(2,1)S(1)}, u32[]{:S(2)}, u32[]{:S(2)}) collective-permute-start(bf16[96,512]{1,0:T(8,128)(2,1)S(1)} %res_sum_z2.1.refs_4_.refs_0_), channel_id=1, source_target_pairs={{0,18},{1,19},{2,16},{3,17},{4,22},{5,23},{6,20},{7,21},{8,26},{9,... | collective-permute-start | bytes 294920 | tf_op jit(solution)/shard_map/ppermute | solution.py:389
  40.1 0.8 %collective-permute-start.13 = (bf16[96,512]{1,0:T(8,128)(2,1)S(1)}, bf16[96,512]{1,0:T(8,128)(2,1)S(1)}, u32[]{:S(2)}, u32[]{:S(2)}) collective-permute-start(bf16[96,512]{1,0:T(8,128)(2,1)S(1)} %res_sum_z2.1.refs_4_.refs_0_), channel_id=1, source_target_pairs={{0,2},{1,3},{2,0},{3,1},{4,6},{5,7},{6,4},{7,5},{8,10},{9,11},{10,... | collective-permute-start | bytes 294920 | tf_op jit(solution)/shard_map/ppermute | solution.py:380
  40.9 0.6 %collective-permute-start.12 = (bf16[96,512]{1,0:T(8,128)(2,1)S(1)}, bf16[96,512]{1,0:T(8,128)(2,1)S(1)}, u32[]{:S(2)}, u32[]{:S(2)}) collective-permute-start(bf16[96,512]{1,0:T(8,128)(2,1)S(1)} %res_sum_z2.1.refs_4_.refs_0_), channel_id=1, source_target_pairs={{0,16},{16,0},{1,17},{17,1},{2,18},{18,2},{3,19},{19,3},{4,20},{20... | collective-permute-start | bytes 294920 | tf_op jit(solution)/shard_map/ppermute | solution.py:384
  41.5 1.5 %collective-permute-start.20 = (bf16[64,512]{1,0:T(8,128)(2,1)S(1)}, bf16[64,512]{1,0:T(8,128)(2,1)S(1)}, u32[]{:S(2)}, u32[]{:S(2)}) collective-permute-start(bf16[64,512]{1,0:T(8,128)(2,1)S(1)} %conv_scaled.1.refs_4_.refs_0_), channel_id=1, source_target_pairs={{0,16},{16,0},{1,17},{17,1},{2,18},{18,2},{3,19},{19,3},{4,20},{20... | collective-permute-start | bytes 196616 | tf_op jit(solution)/shard_map/ppermute | solution.py:384
  43.0 2.7 %collective-permute-start.19 = (bf16[128,512]{1,0:T(8,128)(2,1)S(1)}, bf16[128,512]{1,0:T(8,128)(2,1)S(1)}, u32[]{:S(2)}, u32[]{:S(2)}) collective-permute-start(bf16[128,512]{1,0:T(8,128)(2,1)S(1)} %hold.1), channel_id=1, source_target_pairs={{0,14},{1,15},{2,0},{3,1},{4,2},{5,3},{6,4},{7,5},{8,6},{9,7},{10,... | collective-permute-start | bytes 393224 | tf_op jit(solution)/shard_map/ppermute | solution.py:393
  45.8 0.4 collective-permute-done.20.refs_1_
  46.3 0.7 %finish_conv.1 = (bf16[2,64,512]{2,1,0:T(8,128)(2,1)}, f32[8,128]{1,0:T(8,128)S(1)}) custom-call(bf16[64,512]{1,0:T(8,128)(2,1)S(1)} %conv_scaled.1.refs_4_.refs_0_, bf16[64,512]{1,0:T(8,128)(2,1)S(1)} %collective-permute-done.20.refs_1_), custom_call_target="tpu_custom_call" | custom-call | flops 10000000000 | tf_op jit(solution)/shard_map/finish_conv/pallas_call | solution.py:131
  46.9 1.3 %collective-permute-done.19.refs_3_ = bf16[128,512]{1,0:T(8,128)(2,1)S(1)} collective-permute-done((bf16[128,512]{1,0:T(8,128)(2,1)S(1)}, bf16[128,512]{1,0:T(8,128)(2,1)S(1)}, u32[]{:S(2)}, u32[]{:S(2)}) %collective-permute-start.19) | collective-permute-done | bytes 131104 | tf_op jit(solution)/shard_map/ppermute | solution.py:393
  48.2 1.0 %finish.1 = (bf16[2,256,768]{2,1,0:T(8,128)(2,1)}, bf16[128,512]{1,0:T(8,128)(2,1)}) custom-call(bf16[4,96,512]{2,1,0:T(8,128)(2,1)S(1)} %res_in_order.1.refs_0_, bf16[4,96,512]{2,1,0:T(8,128)(2,1)S(1)} %collective-permute-done.18.refs_1_, f32[128,512]{1,0:T(8,128)S(1)} %get-tuple-element.62.refs_2_, bf16[128,512]{1,0:T(8,128)(2,1)S(1)} %collective-permute-done.19.refs_3_, ...), custom_call_target="tpu_custom_call" | custom-call | tf_op jit(solution)/shard_map/finish/pallas_call | solution.py:131
  (25 shorter events, 1.0 us)
Async XLA Ops:
  0.6 10.1 %collective-permute-start.1 = (bf16[128,512]{1,0:T(8,128)(2,1)}, bf16[128,512]{1,0:T(8,128)(2,1)S(1)}, u32[]{:S(2)}, u32[]{:S(2)}) collective-permute-start(bf16[128,512]{1,0:T(8,128)(2,1)} %bitcast.5), channel_id=1, source_target_pairs={{0,2},{1,3},{2,4},{3,5},{4,6},{5,7},{6,8},{7,9},{8,10},{9,11},{10,... | collective-permute-start | bytes 393224 | tf_op jit(solution)/shard_map/ppermute | solution.py:393
  4.7 5.8 %collective-permute-start.2 = (bf16[32,512]{1,0:T(8,128)(2,1)S(1)}, bf16[32,512]{1,0:T(8,128)(2,1)S(1)}, u32[]{:S(2)}, u32[]{:S(2)}) collective-permute-start(bf16[32,512]{1,0:T(8,128)(2,1)S(1)} %get-tuple-element.36), channel_id=1, source_target_pairs={{0,4},{1,5},{2,6},{3,7},{4,8},{5,9},{6,10},{7,11},{8,12},{9,13},{1... | collective-permute-start | bytes 98312 | tf_op jit(solution)/shard_map/ppermute | solution.py:393
  6.3 5.9 %collective-permute-start = (bf16[128,1280]{1,0:T(8,128)(2,1)S(1)}, bf16[128,1280]{1,0:T(8,128)(2,1)S(1)}, u32[]{:S(2)}, u32[]{:S(2)}) collective-permute-start(bf16[128,1280]{1,0:T(8,128)(2,1)S(1)} %get-tuple-element.35.refs_0_), channel_id=1, source_target_pairs={{0,1},{1,0},{2,3},{3,2},{4,5},{5,4},{6,7},{7,6},{8,9},{9,8},{10,11... | collective-permute-start | bytes 983048 | tf_op jit(solution)/shard_map/ppermute | solution.py:380
  10.7 1.5 %collective-permute-start.3 = (bf16[160,512]{1,0:T(8,128)(2,1)S(1)}, bf16[160,512]{1,0:T(8,128)(2,1)S(1)}, u32[]{:S(2)}, u32[]{:S(2)}) collective-permute-start(bf16[160,512]{1,0:T(8,128)(2,1)S(1)} %pack_halo.1.refs_2_), channel_id=1, source_target_pairs={{0,1},{1,0},{2,3},{3,2},{4,5},{5,4},{6,7},{7,6},{8,9},{9,8},{10,11... | collective-permute-start | bytes 491528 | tf_op jit(solution)/shard_map/ppermute | solution.py:380
  14.5 8.0 %collective-permute-start.4 = (bf16[96,512]{1,0:T(8,128)(2,1)S(1)}, bf16[96,512]{1,0:T(8,128)(2,1)S(1)}, u32[]{:S(2)}, u32[]{:S(2)}) collective-permute-start(bf16[96,512]{1,0:T(8,128)(2,1)S(1)} %get-tuple-element.40), channel_id=1, source_target_pairs={{0,16},{16,0},{1,17},{17,1},{2,18},{18,2},{3,19},{19,3},{4,20},{20... | collective-permute-start | bytes 294920 | tf_op jit(solution)/shard_map/ppermute | solution.py:384
  16.1 7.1 %collective-permute-start.5 = (bf16[96,512]{1,0:T(8,128)(2,1)S(1)}, bf16[96,512]{1,0:T(8,128)(2,1)S(1)}, u32[]{:S(2)}, u32[]{:S(2)}) collective-permute-start(bf16[96,512]{1,0:T(8,128)(2,1)S(1)} %get-tuple-element.41), channel_id=1, source_target_pairs={{0,2},{1,3},{2,0},{3,1},{4,6},{5,7},{6,4},{7,5},{8,10},{9,11},{10,... | collective-permute-start | bytes 294920 | tf_op jit(solution)/shard_map/ppermute | solution.py:380
  17.3 5.9 %collective-permute-start.6 = (bf16[96,512]{1,0:T(8,128)(2,1)S(1)}, bf16[96,512]{1,0:T(8,128)(2,1)S(1)}, u32[]{:S(2)}, u32[]{:S(2)}) collective-permute-start(bf16[96,512]{1,0:T(8,128)(2,1)S(1)} %get-tuple-element.42), channel_id=1, source_target_pairs={{0,18},{1,19},{2,16},{3,17},{4,22},{5,23},{6,20},{7,21},{8,26},{9,... | collective-permute-start | bytes 294920 | tf_op jit(solution)/shard_map/ppermute | solution.py:389
  19.6 10.6 %collective-permute-start.9 = (bf16[4,64,512]{2,1,0:T(8,128)(2,1)S(1)}, bf16[4,64,512]{2,1,0:T(8,128)(2,1)S(1)}, u32[]{:S(2)}, u32[]{:S(2)}) collective-permute-start(bf16[4,64,512]{2,1,0:T(8,128)(2,1)S(1)} %get-tuple-element.52), channel_id=1, source_target_pairs={{0,16},{16,0},{1,17},{17,1},{2,18},{18,2},{3,19},{19,3},{4,20},{20... | collective-permute-start | bytes 786440 | tf_op jit(solution)/shard_map/ppermute | solution.py:384
  21.2 9.2 %collective-permute-start.10 = (bf16[4,64,512]{2,1,0:T(8,128)(2,1)S(1)}, bf16[4,64,512]{2,1,0:T(8,128)(2,1)S(1)}, u32[]{:S(2)}, u32[]{:S(2)}) collective-permute-start(bf16[4,64,512]{2,1,0:T(8,128)(2,1)S(1)} %get-tuple-element.53), channel_id=1, source_target_pairs={{0,2},{1,3},{2,0},{3,1},{4,6},{5,7},{6,4},{7,5},{8,10},{9,11},{10,... | collective-permute-start | bytes 786440 | tf_op jit(solution)/shard_map/ppermute | solution.py:380
  22.5 11.6 %collective-permute-start.11 = (bf16[4,64,512]{2,1,0:T(8,128)(2,1)S(1)}, bf16[4,64,512]{2,1,0:T(8,128)(2,1)S(1)}, u32[]{:S(2)}, u32[]{:S(2)}) collective-permute-start(bf16[4,64,512]{2,1,0:T(8,128)(2,1)S(1)} %get-tuple-element.54), channel_id=1, source_target_pairs={{0,18},{1,19},{2,16},{3,17},{4,22},{5,23},{6,20},{7,21},{8,26},{9,... | collective-permute-start | bytes 786440 | tf_op jit(solution)/shard_map/ppermute | solution.py:389
  23.3 5.0 %collective-permute-start.7 = (bf16[128,512]{1,0:T(8,128)(2,1)S(1)}, bf16[128,512]{1,0:T(8,128)(2,1)S(1)}, u32[]{:S(2)}, u32[]{:S(2)}) collective-permute-start(bf16[128,512]{1,0:T(8,128)(2,1)S(1)} %res_sum_xy.1.refs_0_.refs_4_), channel_id=1, source_target_pairs={{0,4},{1,5},{2,6},{3,7},{4,0},{5,1},{6,2},{7,3},{8,12},{9,13},{10,... | collective-permute-start | bytes 393224 | tf_op jit(solution)/shard_map/ppermute | solution.py:380
  28.3 9.5 %collective-permute-start.8 = (bf16[128,512]{1,0:T(8,128)(2,1)S(1)}, bf16[128,512]{1,0:T(8,128)(2,1)S(1)}, u32[]{:S(2)}, u32[]{:S(2)}) collective-permute-start(bf16[128,512]{1,0:T(8,128)(2,1)S(1)} %res_sum_z1.1.refs_4_.refs_0_), channel_id=1, source_target_pairs={{0,8},{1,9},{2,10},{3,11},{4,12},{5,13},{6,14},{7,15},{8,0},{9,1},... | collective-permute-start | bytes 393224 | tf_op jit(solution)/shard_map/ppermute | solution.py:380
  34.3 6.6 %collective-permute-start.15 = (bf16[64,512]{1,0:T(8,128)(2,1)S(1)}, bf16[64,512]{1,0:T(8,128)(2,1)S(1)}, u32[]{:S(2)}, u32[]{:S(2)}) collective-permute-start(bf16[64,512]{1,0:T(8,128)(2,1)S(1)} %get-tuple-element.59), channel_id=1, source_target_pairs={{0,8},{1,9},{2,10},{3,11},{4,12},{5,13},{6,14},{7,15},{8,0},{9,1},... | collective-permute-start | bytes 196616 | tf_op jit(solution)/shard_map/ppermute | solution.py:380
  35.2 6.3 %collective-permute-start.16 = (bf16[64,512]{1,0:T(8,128)(2,1)S(1)}, bf16[64,512]{1,0:T(8,128)(2,1)S(1)}, u32[]{:S(2)}, u32[]{:S(2)}) collective-permute-start(bf16[64,512]{1,0:T(8,128)(2,1)S(1)} %get-tuple-element.60), channel_id=1, source_target_pairs={{0,12},{1,13},{2,14},{3,15},{4,8},{5,9},{6,10},{7,11},{8,4},{9,5},... | collective-permute-start | bytes 196616 | tf_op jit(solution)/shard_map/ppermute | solution.py:380
  36.5 5.0 %collective-permute-start.17 = (bf16[64,512]{1,0:T(8,128)(2,1)S(1)}, bf16[64,512]{1,0:T(8,128)(2,1)S(1)}, u32[]{:S(2)}, u32[]{:S(2)}) collective-permute-start(bf16[64,512]{1,0:T(8,128)(2,1)S(1)} %get-tuple-element.61), channel_id=1, source_target_pairs={{0,4},{1,5},{2,6},{3,7},{4,0},{5,1},{6,2},{7,3},{8,12},{9,13},{10,... | collective-permute-start | bytes 196616 | tf_op jit(solution)/shard_map/ppermute | solution.py:380
  37.9 7.8 %collective-permute-start.14 = (bf16[96,512]{1,0:T(8,128)(2,1)S(1)}, bf16[96,512]{1,0:T(8,128)(2,1)S(1)}, u32[]{:S(2)}, u32[]{:S(2)}) collective-permute-start(bf16[96,512]{1,0:T(8,128)(2,1)S(1)} %res_sum_z2.1.refs_4_.refs_0_), channel_id=1, source_target_pairs={{0,18},{1,19},{2,16},{3,17},{4,22},{5,23},{6,20},{7,21},{8,26},{9,... | collective-permute-start | bytes 294920 | tf_op jit(solution)/shard_map/ppermute | solution.py:389
  40.1 5.6 %collective-permute-start.13 = (bf16[96,512]{1,0:T(8,128)(2,1)S(1)}, bf16[96,512]{1,0:T(8,128)(2,1)S(1)}, u32[]{:S(2)}, u32[]{:S(2)}) collective-permute-start(bf16[96,512]{1,0:T(8,128)(2,1)S(1)} %res_sum_z2.1.refs_4_.refs_0_), channel_id=1, source_target_pairs={{0,2},{1,3},{2,0},{3,1},{4,6},{5,7},{6,4},{7,5},{8,10},{9,11},{10,... | collective-permute-start | bytes 294920 | tf_op jit(solution)/shard_map/ppermute | solution.py:380
  40.9 4.8 %collective-permute-start.12 = (bf16[96,512]{1,0:T(8,128)(2,1)S(1)}, bf16[96,512]{1,0:T(8,128)(2,1)S(1)}, u32[]{:S(2)}, u32[]{:S(2)}) collective-permute-start(bf16[96,512]{1,0:T(8,128)(2,1)S(1)} %res_sum_z2.1.refs_4_.refs_0_), channel_id=1, source_target_pairs={{0,16},{16,0},{1,17},{17,1},{2,18},{18,2},{3,19},{19,3},{4,20},{20... | collective-permute-start | bytes 294920 | tf_op jit(solution)/shard_map/ppermute | solution.py:384
  41.5 4.7 %collective-permute-start.20 = (bf16[64,512]{1,0:T(8,128)(2,1)S(1)}, bf16[64,512]{1,0:T(8,128)(2,1)S(1)}, u32[]{:S(2)}, u32[]{:S(2)}) collective-permute-start(bf16[64,512]{1,0:T(8,128)(2,1)S(1)} %conv_scaled.1.refs_4_.refs_0_), channel_id=1, source_target_pairs={{0,16},{16,0},{1,17},{17,1},{2,18},{18,2},{3,19},{19,3},{4,20},{20... | collective-permute-start | bytes 196616 | tf_op jit(solution)/shard_map/ppermute | solution.py:384
  43.0 5.2 %collective-permute-start.19 = (bf16[128,512]{1,0:T(8,128)(2,1)S(1)}, bf16[128,512]{1,0:T(8,128)(2,1)S(1)}, u32[]{:S(2)}, u32[]{:S(2)}) collective-permute-start(bf16[128,512]{1,0:T(8,128)(2,1)S(1)} %hold.1), channel_id=1, source_target_pairs={{0,14},{1,15},{2,0},{3,1},{4,2},{5,3},{6,4},{7,5},{8,6},{9,7},{10,... | collective-permute-start | bytes 393224 | tf_op jit(solution)/shard_map/ppermute | solution.py:393
  45.8 2.5 %collective-permute-start.18 = (bf16[4,96,512]{2,1,0:T(8,128)(2,1)S(1)}, bf16[4,96,512]{2,1,0:T(8,128)(2,1)S(1)}, u32[]{:S(2)}, u32[]{:S(2)}) collective-permute-start(bf16[4,96,512]{2,1,0:T(8,128)(2,1)S(1)} %res_in_order.1.refs_0_), channel_id=1, source_target_pairs={{0,1},{1,0},{2,3},{3,2},{4,5},{5,4},{6,7},{7,6},{8,9},{9,8},{10,11... | collective-permute-start | bytes 1179656 | tf_op jit(solution)/shard_map/ppermute | solution.py:380

commit v8 on v7

--- a/solution.py
+++ b/solution.py
@@ -194,32 +194,63 @@
 
 
 def split_quarters(staged, mine, by_y, by_x, by_both):
-    _, x, core = here()
+    _, x, _ = here()
     q = 2 * x + lax.axis_index("dp")
-    mine[...] = staged[core, q]
+    mine[...] = staged[q]
     for k, out in ((1, by_y), (2, by_x), (3, by_both)):
-        out[...] = staged[core, lax.bitwise_xor(q, k)]
+        out[...] = staged[lax.bitwise_xor(q, k)]
+
+
+def columns_of(a, core, block):
+    count = a.shape[1] // block
+    return jnp.where(
+        core == 0,
+        jnp.concatenate([a[:, i * block : (i + 1) * block] for i in range(0, count, 2)], axis=1),
+        jnp.concatenate([a[:, i * block : (i + 1) * block] for i in range(1, count, 2)], axis=1),
+    )
+
+
+def own_kernel(own, own_other, cw, rw, sig, gin, skin, z_out, e_out, es_out):
+    t = own.shape[0]
+    near = t // 4
+    width = sig.shape[1]
+    _, _, core = here()
+    for a, c in ((own, core), (own_other, 1 - core)):
+        rows = pl.ds(pl.multiple_of(c * t, t), t)
+        sig[rows, :] = a[:, 0:width]
+        gin[rows, :] = a[:, width : 2 * width]
+        skin[rows, :] = a[:, 2 * width :]
+    z = mm(sig[...], cw[0, width:, :])
+    z_out[0:near, :] = z[0:near, :]
+    z_out[near:, :] = z[near:, :] + mm(sig[...], cw[0, 0:width, :])[: 2 * t - near, :]
+    e_out[...] = mm_nt(gin[...], rw[1, :, 0:width]) + mm_nt(skin[...], rw[1, :, width:])
+    es_out[...] = mm_nt(skin[...], rw[0, :, width:])
 
 
 def forward_and_outer_kernel(
-    own, own_other, halo, halo_other, cw, rw,
-    mine, by_y, by_x, by_both, x_out, a_out, b_out, x1_out, dz_out, o_out, ga_out, es_out,
-    staged, gin, skin,
+    sig, z_own, e1, gin, skin, halo, halo_other, cw, rw,
+    mine, by_y, by_x, by_both, x_out, a_out, b_out, x1_out, dz_out, o_out, ga_out,
+    staged,
 ):
-    t = own.shape[0]
+    t = sig.shape[0] // 2
     near = t // 4
     width = x_out.shape[1]
     gated = rw.shape[1]
     _, _, core = here()
-    for a, h, c in ((own, halo, core), (own_other, halo_other, 1 - core)):
-        rows = pl.ds(pl.multiple_of(c * t, t), t)
+    for h, c in ((halo, core), (halo_other, 1 - core)):
         x_out[pl.ds(pl.multiple_of(near + c * t, near), t), :] = h[0:t, :]
-        x_out[pl.ds(pl.multiple_of(near + (2 + c) * t, near), t), :] = a[:, 0:width]
-        gin[rows, :] = a[:, width : 2 * width]
-        skin[rows, :] = a[:, 2 * width :]
+    x_out[near + 2 * t :, :] = sig[...]
     x_out[0:near, :] = jnp.where(core == 1, halo[t:, :], halo_other[t:, :])
     x0 = x_out[near:, :]
-    z0 = mm(x_out[0 : 4 * t, :], cw[0, 0:width, :]) + mm(x0, cw[0, width:, :])
+    behind = mm(x_out[0 : 2 * t + near, :], cw[0, 0:width, :])
+    z0 = jnp.concatenate(
+        [
+            behind[0 : 2 * t, :] + mm(x_out[near : 2 * t + near, :], cw[0, width:, :]),
+            z_own[0:near, :] + behind[2 * t :, :],
+            z_own[near:, :],
+        ],
+        axis=0,
+    )
     tf = jnp.tanh(z0[:, :gated])
     sg = jax.nn.sigmoid(z0[:, gated:])
     h0 = (tf * sg).astype(BF16)
@@ -233,29 +264,29 @@
     h1 = (tf * sg).astype(BF16)
     g2 = gin[...]
     sk = skin[...]
-    e1 = mm_nt(g2, rw[1, :, 0:width]) + mm_nt(sk, rw[1, :, width:])
-    dz1 = jnp.concatenate([e1 * sg * (1.0 - tf * tf), e1 * tf * sg * (1.0 - sg)], axis=1).astype(BF16)
+    e = e1[...]
+    dz1 = jnp.concatenate([e * sg * (1.0 - tf * tf), e * tf * sg * (1.0 - sg)], axis=1).astype(BF16)
     dz_out[...] = dz1
     dpast = mm_nt(dz1, cw[1, 0:width, :]).astype(BF16)
     ga = g2.astype(F32) + mm_nt(dz1, cw[1, width:, :])
     ga_out[...] = ga
     outer = jnp.concatenate([dpast, ga.astype(BF16)], axis=0)
     o_out[...] = outer
-    es_out[...] = mm_nt(sk, rw[0, :, width:])
-    skips = jnp.concatenate([mm_tn(h1, sk), mm_tn(h0[2 * t :, :], sk)], axis=1)
+    part = gated // 2
+    mine_h0 = jnp.where(core == 0, h0[:, :part], h0[:, part:])
+    mine_h1 = jnp.where(core == 0, h1[:, :part], h1[:, part:])
+    skips = jnp.concatenate([mm_tn(mine_h1, sk), mm_tn(mine_h0[2 * t :, :], sk)], axis=1)
     eighth = gated // 8
-    for which, part in enumerate((mm_tn(h1, g2), mm_tn(h0, outer), skips)):
-        for c in range(2):
-            for q in range(4):
-                rows = slice((4 * c + q) * eighth, (4 * c + q + 1) * eighth)
-                staged[c, q, which * eighth : (which + 1) * eighth, :] = part[rows, :].astype(BF16)
+    for which, part in enumerate((mm_tn(mine_h1, g2), mm_tn(mine_h0, outer), skips)):
+        for q in range(4):
+            staged[q, which * eighth : (which + 1) * eighth, :] = part[q * eighth : (q + 1) * eighth, :].astype(BF16)
     split_quarters(staged, mine, by_y, by_x, by_both)
 
 
 def inner_kernel(
     xin, a, b, x1, dz1, outer, es, cw, rw,
     mine, by_y, by_x, by_both, dz, tail,
-    staged,
+    staged, mine_in,
 ):
     width = xin.shape[1]
     t = dz1.shape[0] // 2
@@ -268,17 +299,20 @@
     tail[...] = mm_nt(dz0[0:near, :], cw[0, 0:width, :]).astype(BF16)
     half = width // 16
     rows = 2 * half
-    blocks = width // rows
+    _, _, core = here()
+    mine_in[...] = columns_of(xin[...], core, rows)
+    mine_x1 = columns_of(x1[...], core, rows)
+    pairs = width // rows // 2
     for base, part0, part1 in (
-        (0, mm_tn(xin[0 : 4 * t, :], dz0), mm_tn(x1[0 : 2 * t, :], dz1[...])),
-        (blocks, mm_tn(xin[near:, :], dz0), mm_tn(x1[2 * t :, :], dz1[...])),
+        (0, mm_tn(mine_in[0 : 4 * t, :], dz0), mm_tn(mine_x1[0 : 2 * t, :], dz1[...])),
+        (pairs, mm_tn(mine_in[near:, :], dz0), mm_tn(mine_x1[2 * t :, :], dz1[...])),
     ):
-        for block in range(blocks):
-            g, x, c = (base + block) // 4, (base + block) // 2 % 2, (base + block) % 2
+        for block in range(pairs):
+            g, x = (base + block) // 2, (base + block) % 2
             for y in range(2):
                 src = slice(block * rows + y * half, block * rows + (y + 1) * half)
-                staged[c, 2 * x + y, g, 0:half, :] = part0[src, :].astype(BF16)
-                staged[c, 2 * x + y, g, half:, :] = part1[src, :].astype(BF16)
+                staged[2 * x + y, g, 0:half, :] = part0[src, :].astype(BF16)
+                staged[2 * x + y, g, half:, :] = part1[src, :].astype(BF16)
     split_quarters(staged, mine, by_y, by_x, by_both)
 
 
@@ -416,27 +450,30 @@
     halo_other = swap(halo, 1)
 
     res = shaped((res_rows, width))
-    *rsplit, xin, a, b, x1, dz1, outer, ga, es = call(
+    sig, gin, skin, z_own, e1, es = call(
+        own_kernel,
+        [
+            shaped((2 * t, width)), shaped((2 * t, width)), shaped((2 * t, gated)), shaped((2 * t, 2 * gated), F32),
+            shaped((2 * t, gated), F32), shaped((2 * t, gated), F32),
+        ],
+        own, own_other, cw, rw, vmem=16, flops=2_000_000_000, name="own",
+    )
+    *rsplit, xin, a, b, x1, dz1, outer, ga = call(
         forward_and_outer_kernel,
         [
             res, res, res, res,
             shaped((4 * t + near, width)), shaped((4 * t, gated), F32), shaped((4 * t, gated), F32),
             shaped((4 * t, width)), shaped((2 * t, width)), shaped((4 * t, width)), shaped((2 * t, width), F32),
-            shaped((2 * t, gated), F32),
         ],
-        own, own_other, halo, halo_other, cw, rw,
-        scratch=[
-            pltpu.VMEM((2, 4, res_rows, width), BF16), pltpu.VMEM((2 * t, width), BF16),
-            pltpu.VMEM((2 * t, gated), BF16),
-        ],
-        vmem=16, name="forward_and_outer",
+        sig, z_own, e1, gin, skin, halo, halo_other, cw, rw,
+        scratch=[pltpu.VMEM((4, res_rows, width), BF16)], vmem=16, name="forward_and_outer",
     )
     piece = (2 * half, width)
     part = shaped((4,) + piece)
     *csplit, dz0, tail = call(
         inner_kernel, [part, part, part, part, shaped((4 * t + near, width)), shaped((near, width))],
         xin, a, b, x1, dz1, outer, es, cw, rw,
-        scratch=[pltpu.VMEM((2, 4, 4) + piece, BF16)], vmem=16, flops=2_000_000_000, name="inner",
+        scratch=[pltpu.VMEM((4, 4) + piece, BF16), pltpu.VMEM((4 * t + near, width // 2), BF16)], vmem=16, flops=2_000_000_000, name="inner",
     )
     def around(by_y, by_x, by_both):
         both = swap_both(by_both, 2)

time: 49.4 us -> 48.6 us (0.984)
    ppermute x3, waiting for transfers between devices: 3.62 us -> 4.62 us  [swap_both(): return lax.ppermute(x, ('dp', 'tm'), route)]
    ppermute x4, waiting for transfers between devices: 0.98 us -> 0.15 us  [swap_streams(): return lax.ppermute(x, 'dp', [(0, 1), (1, 0)])]
    ppermute x11, waiting for transfers between devices: 6.63 us -> 6.08 us  [swap(): return lax.ppermute(x, 'tm', [(i, i ^ distance) for i in range(16)])]
    pallas_call x13 -> x14, Pallas kernels: 6.51 us -> 6.06 us  [call(): pl.pallas_call(run, out_shape=outs, in_specs=[in_vmem] * n_args + [pl.Blo...]
  transfers between devices with their start and end apart: 21 -> 21, of which waited for: 9 -> 9; matrix products, arithmetic and copies ran while one was open for 0% -> 0% of each run, Pallas kernels for 12% -> 13%
where the time goes in v8:
time: 48.6 us; the launch traced here: 48.5 us
  starting transfers between devices  24 us (49%)
  waiting for transfers between devices  14.8 us (30%)
  Pallas kernels  8.88 us (18%)
  between operations  0.76 us (2%)
    ppermute x11, starting transfers between devices, swap(): return lax.ppermute(x, 'tm', [(i, i ^ distance) for i in range(16)])  8.03 us
    ppermute x3, starting transfers between devices, shift(): return lax.ppermute(x, 'tm', [(i, (i + distance) % 16) for i in range(16)])  7.23 us
    ppermute x11, waiting for transfers between devices, swap(): return lax.ppermute(x, 'tm', [(i, i ^ distance) for i in range(16)])  6.08 us
    pallas_call x14, Pallas kernels, call(): pl.pallas_call(run, out_shape=outs, in_specs=[in_vmem] * n_args + [pl.Blo...  6.06 us
    ppermute x4, starting transfers between devices, swap_streams(): return lax.ppermute(x, 'dp', [(0, 1), (1, 0)])  5.25 us
    ppermute x3, waiting for transfers between devices, swap_both(): return lax.ppermute(x, ('dp', 'tm'), route)  4.62 us
    ppermute x3, waiting for transfers between devices, shift(): return lax.ppermute(x, 'tm', [(i, (i + distance) % 16) for i in range(16)])  3.92 us
    ppermute x3, starting transfers between devices, swap_both(): return lax.ppermute(x, ('dp', 'tm'), route)  3.54 us
  transfers between devices with their start and end apart: 21, of which 9 were waited for; matrix products, arithmetic and copies ran while one was open for 0% of the time, Pallas kernels for 13%

profile of v8, /device:TPU:0, one launch (start us, length us, event | category | flops | bytes accessed | tf_op | source)
XLA Modules:
  0.0 48.5 jit_solution(7529922488645148976)
XLA Ops:
  0.6 3.0 %collective-permute-start.1 = (bf16[128,512]{1,0:T(8,128)(2,1)}, bf16[128,512]{1,0:T(8,128)(2,1)S(1)}, u32[]{:S(2)}, u32[]{:S(2)}) collective-permute-start(bf16[128,512]{1,0:T(8,128)(2,1)} %bitcast.5), channel_id=1, source_target_pairs={{0,2},{1,3},{2,4},{3,5},{4,6},{5,7},{6,8},{7,9},{8,10},{9,11},{10,... | collective-permute-start | bytes 393224 | tf_op jit(solution)/shard_map/ppermute | solution.py:427
  3.6 1.0 %load_slab.1 = (bf16[128,1280]{1,0:T(8,128)(2,1)S(1)}, bf16[32,512]{1,0:T(8,128)(2,1)S(1)}) custom-call(bf16[128,512]{1,0:T(8,128)(2,1)} %bitcast.6, bf16[128,512]{1,0:T(8,128)(2,1)} %bitcast.4, bf16[128,256]{1,0:T(8,128)(2,1)} %bitcast.7), custom_call_target="tpu_custom_call" | custom-call | tf_op jit(solution)/shard_map/load_slab/pallas_call | solution.py:177
  4.7 1.6 %collective-permute-start.2 = (bf16[32,512]{1,0:T(8,128)(2,1)S(1)}, bf16[32,512]{1,0:T(8,128)(2,1)S(1)}, u32[]{:S(2)}, u32[]{:S(2)}) collective-permute-start(bf16[32,512]{1,0:T(8,128)(2,1)S(1)} %get-tuple-element.48), channel_id=1, source_target_pairs={{0,4},{1,5},{2,6},{3,7},{4,8},{5,9},{6,10},{7,11},{8,12},{9,13},{1... | collective-permute-start | bytes 98312 | tf_op jit(solution)/shard_map/ppermute | solution.py:427
  6.3 1.8 %load_weights.1 = (bf16[2,1024,512]{2,1,0:T(8,128)(2,1)S(1)}, bf16[2,256,768]{2,1,0:T(8,128)(2,1)S(1)}) custom-call(bf16[2,1024,512]{2,1,0:T(8,128)(2,1)} %cw.1, bf16[2,256,768]{2,1,0:T(8,128)(2,1)} %rw.1), custom_call_target="tpu_custom_call" | custom-call | flops 4000000000 | tf_op jit(solution)/shard_map/load_weights/pallas_call | solution.py:177
  8.1 2.3 %collective-permute-done.2.refs_1_ = bf16[32,512]{1,0:T(8,128)(2,1)S(1)} collective-permute-done((bf16[32,512]{1,0:T(8,128)(2,1)S(1)}, bf16[32,512]{1,0:T(8,128)(2,1)S(1)}, u32[]{:S(2)}, u32[]{:S(2)}) %collective-permute-start.2) | collective-permute-done | bytes 32800 | tf_op jit(solution)/shard_map/ppermute | solution.py:427
  10.4 0.3 collective-permute-done.1.refs_0_
  10.8 0.6 %own.1 = (bf16[256,512]{1,0:T(8,128)(2,1)S(1)}, bf16[256,512]{1,0:T(8,128)(2,1)S(1)}, bf16[256,256]{1,0:T(8,128)(2,1)S(1)}, f32[256,512]{1,0:T(8,128)S(1)}, f32[...) custom-call(bf16[128,1280]{1,0:T(8,128)(2,1)S(1)} %get-tuple-element.40.refs_0_, ...), custom_call_target="tpu_custom_call" | custom-call | flops 2000000000 | tf_op jit(solution)/shard_map/own/pallas_call | solution.py:131
  11.4 0.8 %collective-permute-done.3.refs_6_ = bf16[160,512]{1,0:T(8,128)(2,1)S(1)} collective-permute-done((bf16[160,512]{1,0:T(8,128)(2,1)S(1)}, bf16[160,512]{1,0:T(8,128)(2,1)S(1)}, u32[]{:S(2)}, u32[]{:S(2)}) %collective-permute-start.3) | collective-permute-done | bytes 163872 | tf_op jit(solution)/shard_map/ppermute | solution.py:414
  12.2 1.7 %forward_and_outer.1 = (bf16[96,512]{1,0:T(8,128)(2,1)S(1)}, bf16[96,512]{1,0:T(8,128)(2,1)S(1)}, bf16[96,512]{1,0:T(8,128)(2,1)S(1)}, bf16[96,512]{1,0:T(8,128)...) custom-call(bf16[256,512]{1,0:T(8,128)(2,1)S(1)} %get-tuple-element., ...), custom_call_target="tpu_custom_call" | custom-call | tf_op jit(solution)/shard_map/forward_and_outer/pallas_call | solution.py:131
  13.9 1.6 %collective-permute-start.4 = (bf16[96,512]{1,0:T(8,128)(2,1)S(1)}, bf16[96,512]{1,0:T(8,128)(2,1)S(1)}, u32[]{:S(2)}, u32[]{:S(2)}) collective-permute-start(bf16[96,512]{1,0:T(8,128)(2,1)S(1)} %get-tuple-element.50), channel_id=1, source_target_pairs={{0,16},{16,0},{1,17},{17,1},{2,18},{18,2},{3,19},{19,3},{4,20},{20... | collective-permute-start | bytes 294920 | tf_op jit(solution)/shard_map/ppermute | solution.py:418
  15.5 1.2 %collective-permute-start.5 = (bf16[96,512]{1,0:T(8,128)(2,1)S(1)}, bf16[96,512]{1,0:T(8,128)(2,1)S(1)}, u32[]{:S(2)}, u32[]{:S(2)}) collective-permute-start(bf16[96,512]{1,0:T(8,128)(2,1)S(1)} %get-tuple-element.51), channel_id=1, source_target_pairs={{0,2},{1,3},{2,0},{3,1},{4,6},{5,7},{6,4},{7,5},{8,10},{9,11},{10,... | collective-permute-start | bytes 294920 | tf_op jit(solution)/shard_map/ppermute | solution.py:414
  16.7 0.7 %collective-permute-start.6 = (bf16[96,512]{1,0:T(8,128)(2,1)S(1)}, bf16[96,512]{1,0:T(8,128)(2,1)S(1)}, u32[]{:S(2)}, u32[]{:S(2)}) collective-permute-start(bf16[96,512]{1,0:T(8,128)(2,1)S(1)} %get-tuple-element.52), channel_id=1, source_target_pairs={{0,18},{1,19},{2,16},{3,17},{4,22},{5,23},{6,20},{7,21},{8,26},{9,... | collective-permute-start | bytes 294920 | tf_op jit(solution)/shard_map/ppermute | solution.py:423
  17.4 1.2 %inner.1 = (bf16[4,64,512]{2,1,0:T(8,128)(2,1)S(1)}, bf16[4,64,512]{2,1,0:T(8,128)(2,1)S(1)}, bf16[4,64,512]{2,1,0:T(8,128)(2,1)S(1)}, bf16[4,64,512]{2,1,0:T(8,...) custom-call(bf16[544,512]{1,0:T(8,128)(2,1)S(1)} %get-tuple-element.53.refs_0_, ...), custom_call_target="tpu_custom_call" | custom-call | flops 2000000000 | tf_op jit(solution)/shard_map/inner/pallas_call | solution.py:131
  18.6 1.6 %collective-permute-start.9 = (bf16[4,64,512]{2,1,0:T(8,128)(2,1)S(1)}, bf16[4,64,512]{2,1,0:T(8,128)(2,1)S(1)}, u32[]{:S(2)}, u32[]{:S(2)}) collective-permute-start(bf16[4,64,512]{2,1,0:T(8,128)(2,1)S(1)} %get-tuple-element.62), channel_id=1, source_target_pairs={{0,16},{16,0},{1,17},{17,1},{2,18},{18,2},{3,19},{19,3},{4,20},{20... | collective-permute-start | bytes 786440 | tf_op jit(solution)/shard_map/ppermute | solution.py:418
  20.2 1.3 %collective-permute-start.10 = (bf16[4,64,512]{2,1,0:T(8,128)(2,1)S(1)}, bf16[4,64,512]{2,1,0:T(8,128)(2,1)S(1)}, u32[]{:S(2)}, u32[]{:S(2)}) collective-permute-start(bf16[4,64,512]{2,1,0:T(8,128)(2,1)S(1)} %get-tuple-element.63), channel_id=1, source_target_pairs={{0,2},{1,3},{2,0},{3,1},{4,6},{5,7},{6,4},{7,5},{8,10},{9,11},{10,... | collective-permute-start | bytes 786440 | tf_op jit(solution)/shard_map/ppermute | solution.py:414
  21.5 0.7 %collective-permute-start.11 = (bf16[4,64,512]{2,1,0:T(8,128)(2,1)S(1)}, bf16[4,64,512]{2,1,0:T(8,128)(2,1)S(1)}, u32[]{:S(2)}, u32[]{:S(2)}) collective-permute-start(bf16[4,64,512]{2,1,0:T(8,128)(2,1)S(1)} %get-tuple-element.64), channel_id=1, source_target_pairs={{0,18},{1,19},{2,16},{3,17},{4,22},{5,23},{6,20},{7,21},{8,26},{9,... | collective-permute-start | bytes 786440 | tf_op jit(solution)/shard_map/ppermute | solution.py:423
  22.2 0.6 %collective-permute-done.6.refs_3_ = bf16[96,512]{1,0:T(8,128)(2,1)S(1)} collective-permute-done((bf16[96,512]{1,0:T(8,128)(2,1)S(1)}, bf16[96,512]{1,0:T(8,128)(2,1)S(1)}, u32[]{:S(2)}, u32[]{:S(2)}) %collective-permute-start.6) | collective-permute-done | bytes 98336 | tf_op jit(solution)/shard_map/ppermute | solution.py:423
  22.9 5.0 %collective-permute-done.7.refs_1_.refs_4_ = bf16[128,512]{1,0:T(8,128)(2,1)S(1)} collective-permute-done((bf16[128,512]{1,0:T(8,128)(2,1)S(1)}, bf16[128,512]{1,0:T(8,128)(2,1)S(1)}, u32[]{:S(2)}, u32[]{:S(2)}) %collective-permute-start.7) | collective-permute-done | bytes 131104 | tf_op jit(solution)/shard_map/ppermute | solution.py:414
  27.9 1.0 %collective-permute-start.8 = (bf16[128,512]{1,0:T(8,128)(2,1)S(1)}, bf16[128,512]{1,0:T(8,128)(2,1)S(1)}, u32[]{:S(2)}, u32[]{:S(2)}) collective-permute-start(bf16[128,512]{1,0:T(8,128)(2,1)S(1)} %res_sum_z1.1.refs_4_.refs_0_), channel_id=1, source_target_pairs={{0,8},{1,9},{2,10},{3,11},{4,12},{5,13},{6,14},{7,15},{8,0},{9,1},... | collective-permute-start | bytes 393224 | tf_op jit(solution)/shard_map/ppermute | solution.py:414
  28.9 0.5 %signal.1 = (f32[128,512]{1,0:T(8,128)S(1)}, bf16[128,512]{1,0:T(8,128)(2,1)S(1)}) custom-call(bf16[544,512]{1,0:T(8,128)(2,1)S(1)} %get-tuple-element.65.refs_0_, bf16[512,512]{1,0:T(8,128)(2,1)S(1)} %get-tuple-element.58.refs_5_.refs_1_, f32[256,512]{1,0:T(8,128)S(1)} %get-tuple-element.66.refs_2_, ...), custom_call_target="tpu_custom_call" | custom-call | flops 1000000000 | tf_op jit(solution)/shard_map/signal/pallas_call | solution.py:131
  29.4 4.0 %collective-permute-done.11.refs_3_ = bf16[4,64,512]{2,1,0:T(8,128)(2,1)S(1)} collective-permute-done((bf16[4,64,512]{2,1,0:T(8,128)(2,1)S(1)}, bf16[4,64,512]{2,1,0:T(8,128)(2,1)S(1)}, u32[]{:S(2)}, u32[]{:S(2)}) %collective-permute-start.11) | collective-permute-done | bytes 262176 | tf_op jit(solution)/shard_map/ppermute | solution.py:423
  33.7 0.9 %collective-permute-start.15 = (bf16[64,512]{1,0:T(8,128)(2,1)S(1)}, bf16[64,512]{1,0:T(8,128)(2,1)S(1)}, u32[]{:S(2)}, u32[]{:S(2)}) collective-permute-start(bf16[64,512]{1,0:T(8,128)(2,1)S(1)} %get-tuple-element.69), channel_id=1, source_target_pairs={{0,8},{1,9},{2,10},{3,11},{4,12},{5,13},{6,14},{7,15},{8,0},{9,1},... | collective-permute-start | bytes 196616 | tf_op jit(solution)/shard_map/ppermute | solution.py:414
  34.5 1.3 %collective-permute-start.16 = (bf16[64,512]{1,0:T(8,128)(2,1)S(1)}, bf16[64,512]{1,0:T(8,128)(2,1)S(1)}, u32[]{:S(2)}, u32[]{:S(2)}) collective-permute-start(bf16[64,512]{1,0:T(8,128)(2,1)S(1)} %get-tuple-element.70), channel_id=1, source_target_pairs={{0,12},{1,13},{2,14},{3,15},{4,8},{5,9},{6,10},{7,11},{8,4},{9,5},... | collective-permute-start | bytes 196616 | tf_op jit(solution)/shard_map/ppermute | solution.py:414
  35.9 1.3 %collective-permute-start.17 = (bf16[64,512]{1,0:T(8,128)(2,1)S(1)}, bf16[64,512]{1,0:T(8,128)(2,1)S(1)}, u32[]{:S(2)}, u32[]{:S(2)}) collective-permute-start(bf16[64,512]{1,0:T(8,128)(2,1)S(1)} %get-tuple-element.71), channel_id=1, source_target_pairs={{0,4},{1,5},{2,6},{3,7},{4,0},{5,1},{6,2},{7,3},{8,12},{9,13},{10,... | collective-permute-start | bytes 196616 | tf_op jit(solution)/shard_map/ppermute | solution.py:414
  37.3 2.1 %collective-permute-start.14 = (bf16[96,512]{1,0:T(8,128)(2,1)S(1)}, bf16[96,512]{1,0:T(8,128)(2,1)S(1)}, u32[]{:S(2)}, u32[]{:S(2)}) collective-permute-start(bf16[96,512]{1,0:T(8,128)(2,1)S(1)} %res_sum_z2.1.refs_4_.refs_0_), channel_id=1, source_target_pairs={{0,18},{1,19},{2,16},{3,17},{4,22},{5,23},{6,20},{7,21},{8,26},{9,... | collective-permute-start | bytes 294920 | tf_op jit(solution)/shard_map/ppermute | solution.py:423
  39.4 0.8 %collective-permute-start.13 = (bf16[96,512]{1,0:T(8,128)(2,1)S(1)}, bf16[96,512]{1,0:T(8,128)(2,1)S(1)}, u32[]{:S(2)}, u32[]{:S(2)}) collective-permute-start(bf16[96,512]{1,0:T(8,128)(2,1)S(1)} %res_sum_z2.1.refs_4_.refs_0_), channel_id=1, source_target_pairs={{0,2},{1,3},{2,0},{3,1},{4,6},{5,7},{6,4},{7,5},{8,10},{9,11},{10,... | collective-permute-start | bytes 294920 | tf_op jit(solution)/shard_map/ppermute | solution.py:414
  40.2 0.7 %collective-permute-start.12 = (bf16[96,512]{1,0:T(8,128)(2,1)S(1)}, bf16[96,512]{1,0:T(8,128)(2,1)S(1)}, u32[]{:S(2)}, u32[]{:S(2)}) collective-permute-start(bf16[96,512]{1,0:T(8,128)(2,1)S(1)} %res_sum_z2.1.refs_4_.refs_0_), channel_id=1, source_target_pairs={{0,16},{16,0},{1,17},{17,1},{2,18},{18,2},{3,19},{19,3},{4,20},{20... | collective-permute-start | bytes 294920 | tf_op jit(solution)/shard_map/ppermute | solution.py:418
  40.9 1.4 %collective-permute-start.20 = (bf16[64,512]{1,0:T(8,128)(2,1)S(1)}, bf16[64,512]{1,0:T(8,128)(2,1)S(1)}, u32[]{:S(2)}, u32[]{:S(2)}) collective-permute-start(bf16[64,512]{1,0:T(8,128)(2,1)S(1)} %conv_scaled.1.refs_4_.refs_0_), channel_id=1, source_target_pairs={{0,16},{16,0},{1,17},{17,1},{2,18},{18,2},{3,19},{19,3},{4,20},{20... | collective-permute-start | bytes 196616 | tf_op jit(solution)/shard_map/ppermute | solution.py:418
  42.3 2.6 %collective-permute-start.19 = (bf16[128,512]{1,0:T(8,128)(2,1)S(1)}, bf16[128,512]{1,0:T(8,128)(2,1)S(1)}, u32[]{:S(2)}, u32[]{:S(2)}) collective-permute-start(bf16[128,512]{1,0:T(8,128)(2,1)S(1)} %hold.1), channel_id=1, source_target_pairs={{0,14},{1,15},{2,0},{3,1},{4,2},{5,3},{6,4},{7,5},{8,6},{9,7},{10,... | collective-permute-start | bytes 393224 | tf_op jit(solution)/shard_map/ppermute | solution.py:427
  45.5 0.7 %finish_conv.1 = (bf16[2,64,512]{2,1,0:T(8,128)(2,1)}, f32[8,128]{1,0:T(8,128)S(1)}) custom-call(bf16[64,512]{1,0:T(8,128)(2,1)S(1)} %conv_scaled.1.refs_4_.refs_0_, bf16[64,512]{1,0:T(8,128)(2,1)S(1)} %collective-permute-done.20.refs_1_), custom_call_target="tpu_custom_call" | custom-call | flops 10000000000 | tf_op jit(solution)/shard_map/finish_conv/pallas_call | solution.py:131
  46.2 1.3 %collective-permute-done.19.refs_3_ = bf16[128,512]{1,0:T(8,128)(2,1)S(1)} collective-permute-done((bf16[128,512]{1,0:T(8,128)(2,1)S(1)}, bf16[128,512]{1,0:T(8,128)(2,1)S(1)}, u32[]{:S(2)}, u32[]{:S(2)}) %collective-permute-start.19) | collective-permute-done | bytes 131104 | tf_op jit(solution)/shard_map/ppermute | solution.py:427
  47.5 1.0 %finish.1 = (bf16[2,256,768]{2,1,0:T(8,128)(2,1)}, bf16[128,512]{1,0:T(8,128)(2,1)}) custom-call(bf16[4,96,512]{2,1,0:T(8,128)(2,1)S(1)} %res_in_order.1.refs_0_, bf16[4,96,512]{2,1,0:T(8,128)(2,1)S(1)} %collective-permute-done.18.refs_1_, f32[128,512]{1,0:T(8,128)S(1)} %get-tuple-element.72.refs_2_, bf16[128,512]{1,0:T(8,128)(2,1)S(1)} %collective-permute-done.19.refs_3_, ...), custom_call_target="tpu_custom_call" | custom-call | tf_op jit(solution)/shard_map/finish/pallas_call | solution.py:131
  (26 shorter events, 1.2 us)
Async XLA Ops:
  0.6 10.1 %collective-permute-start.1 = (bf16[128,512]{1,0:T(8,128)(2,1)}, bf16[128,512]{1,0:T(8,128)(2,1)S(1)}, u32[]{:S(2)}, u32[]{:S(2)}) collective-permute-start(bf16[128,512]{1,0:T(8,128)(2,1)} %bitcast.5), channel_id=1, source_target_pairs={{0,2},{1,3},{2,4},{3,5},{4,6},{5,7},{6,8},{7,9},{8,10},{9,11},{10,... | collective-permute-start | bytes 393224 | tf_op jit(solution)/shard_map/ppermute | solution.py:427
  4.7 5.8 %collective-permute-start.2 = (bf16[32,512]{1,0:T(8,128)(2,1)S(1)}, bf16[32,512]{1,0:T(8,128)(2,1)S(1)}, u32[]{:S(2)}, u32[]{:S(2)}) collective-permute-start(bf16[32,512]{1,0:T(8,128)(2,1)S(1)} %get-tuple-element.48), channel_id=1, source_target_pairs={{0,4},{1,5},{2,6},{3,7},{4,8},{5,9},{6,10},{7,11},{8,12},{9,13},{1... | collective-permute-start | bytes 98312 | tf_op jit(solution)/shard_map/ppermute | solution.py:427
  6.3 4.5 %collective-permute-start = (bf16[128,1280]{1,0:T(8,128)(2,1)S(1)}, bf16[128,1280]{1,0:T(8,128)(2,1)S(1)}, u32[]{:S(2)}, u32[]{:S(2)}) collective-permute-start(bf16[128,1280]{1,0:T(8,128)(2,1)S(1)} %get-tuple-element.40.refs_0_), channel_id=1, source_target_pairs={{0,1},{1,0},{2,3},{3,2},{4,5},{5,4},{6,7},{7,6},{8,9},{9,8},{10,11... | collective-permute-start | bytes 983048 | tf_op jit(solution)/shard_map/ppermute | solution.py:414
  10.7 1.5 %collective-permute-start.3 = (bf16[160,512]{1,0:T(8,128)(2,1)S(1)}, bf16[160,512]{1,0:T(8,128)(2,1)S(1)}, u32[]{:S(2)}, u32[]{:S(2)}) collective-permute-start(bf16[160,512]{1,0:T(8,128)(2,1)S(1)} %pack_halo.1.refs_5_), channel_id=1, source_target_pairs={{0,1},{1,0},{2,3},{3,2},{4,5},{5,4},{6,7},{7,6},{8,9},{9,8},{10,11... | collective-permute-start | bytes 491528 | tf_op jit(solution)/shard_map/ppermute | solution.py:414
  13.9 7.6 %collective-permute-start.4 = (bf16[96,512]{1,0:T(8,128)(2,1)S(1)}, bf16[96,512]{1,0:T(8,128)(2,1)S(1)}, u32[]{:S(2)}, u32[]{:S(2)}) collective-permute-start(bf16[96,512]{1,0:T(8,128)(2,1)S(1)} %get-tuple-element.50), channel_id=1, source_target_pairs={{0,16},{16,0},{1,17},{17,1},{2,18},{18,2},{3,19},{19,3},{4,20},{20... | collective-permute-start | bytes 294920 | tf_op jit(solution)/shard_map/ppermute | solution.py:418
  15.5 6.7 %collective-permute-start.5 = (bf16[96,512]{1,0:T(8,128)(2,1)S(1)}, bf16[96,512]{1,0:T(8,128)(2,1)S(1)}, u32[]{:S(2)}, u32[]{:S(2)}) collective-permute-start(bf16[96,512]{1,0:T(8,128)(2,1)S(1)} %get-tuple-element.51), channel_id=1, source_target_pairs={{0,2},{1,3},{2,0},{3,1},{4,6},{5,7},{6,4},{7,5},{8,10},{9,11},{10,... | collective-permute-start | bytes 294920 | tf_op jit(solution)/shard_map/ppermute | solution.py:414
  16.7 6.0 %collective-permute-start.6 = (bf16[96,512]{1,0:T(8,128)(2,1)S(1)}, bf16[96,512]{1,0:T(8,128)(2,1)S(1)}, u32[]{:S(2)}, u32[]{:S(2)}) collective-permute-start(bf16[96,512]{1,0:T(8,128)(2,1)S(1)} %get-tuple-element.52), channel_id=1, source_target_pairs={{0,18},{1,19},{2,16},{3,17},{4,22},{5,23},{6,20},{7,21},{8,26},{9,... | collective-permute-start | bytes 294920 | tf_op jit(solution)/shard_map/ppermute | solution.py:423
  18.6 10.8 %collective-permute-start.9 = (bf16[4,64,512]{2,1,0:T(8,128)(2,1)S(1)}, bf16[4,64,512]{2,1,0:T(8,128)(2,1)S(1)}, u32[]{:S(2)}, u32[]{:S(2)}) collective-permute-start(bf16[4,64,512]{2,1,0:T(8,128)(2,1)S(1)} %get-tuple-element.62), channel_id=1, source_target_pairs={{0,16},{16,0},{1,17},{17,1},{2,18},{18,2},{3,19},{19,3},{4,20},{20... | collective-permute-start | bytes 786440 | tf_op jit(solution)/shard_map/ppermute | solution.py:418
  20.2 9.2 %collective-permute-start.10 = (bf16[4,64,512]{2,1,0:T(8,128)(2,1)S(1)}, bf16[4,64,512]{2,1,0:T(8,128)(2,1)S(1)}, u32[]{:S(2)}, u32[]{:S(2)}) collective-permute-start(bf16[4,64,512]{2,1,0:T(8,128)(2,1)S(1)} %get-tuple-element.63), channel_id=1, source_target_pairs={{0,2},{1,3},{2,0},{3,1},{4,6},{5,7},{6,4},{7,5},{8,10},{9,11},{10,... | collective-permute-start | bytes 786440 | tf_op jit(solution)/shard_map/ppermute | solution.py:414
  21.5 12.0 %collective-permute-start.11 = (bf16[4,64,512]{2,1,0:T(8,128)(2,1)S(1)}, bf16[4,64,512]{2,1,0:T(8,128)(2,1)S(1)}, u32[]{:S(2)}, u32[]{:S(2)}) collective-permute-start(bf16[4,64,512]{2,1,0:T(8,128)(2,1)S(1)} %get-tuple-element.64), channel_id=1, source_target_pairs={{0,18},{1,19},{2,16},{3,17},{4,22},{5,23},{6,20},{7,21},{8,26},{9,... | collective-permute-start | bytes 786440 | tf_op jit(solution)/shard_map/ppermute | solution.py:423
  22.8 5.0 %collective-permute-start.7 = (bf16[128,512]{1,0:T(8,128)(2,1)S(1)}, bf16[128,512]{1,0:T(8,128)(2,1)S(1)}, u32[]{:S(2)}, u32[]{:S(2)}) collective-permute-start(bf16[128,512]{1,0:T(8,128)(2,1)S(1)} %res_sum_xy.1.refs_0_.refs_4_), channel_id=1, source_target_pairs={{0,4},{1,5},{2,6},{3,7},{4,0},{5,1},{6,2},{7,3},{8,12},{9,13},{10,... | collective-permute-start | bytes 393224 | tf_op jit(solution)/shard_map/ppermute | solution.py:414
  27.9 9.4 %collective-permute-start.8 = (bf16[128,512]{1,0:T(8,128)(2,1)S(1)}, bf16[128,512]{1,0:T(8,128)(2,1)S(1)}, u32[]{:S(2)}, u32[]{:S(2)}) collective-permute-start(bf16[128,512]{1,0:T(8,128)(2,1)S(1)} %res_sum_z1.1.refs_4_.refs_0_), channel_id=1, source_target_pairs={{0,8},{1,9},{2,10},{3,11},{4,12},{5,13},{6,14},{7,15},{8,0},{9,1},... | collective-permute-start | bytes 393224 | tf_op jit(solution)/shard_map/ppermute | solution.py:414
  33.7 6.5 %collective-permute-start.15 = (bf16[64,512]{1,0:T(8,128)(2,1)S(1)}, bf16[64,512]{1,0:T(8,128)(2,1)S(1)}, u32[]{:S(2)}, u32[]{:S(2)}) collective-permute-start(bf16[64,512]{1,0:T(8,128)(2,1)S(1)} %get-tuple-element.69), channel_id=1, source_target_pairs={{0,8},{1,9},{2,10},{3,11},{4,12},{5,13},{6,14},{7,15},{8,0},{9,1},... | collective-permute-start | bytes 196616 | tf_op jit(solution)/shard_map/ppermute | solution.py:414
  34.5 6.3 %collective-permute-start.16 = (bf16[64,512]{1,0:T(8,128)(2,1)S(1)}, bf16[64,512]{1,0:T(8,128)(2,1)S(1)}, u32[]{:S(2)}, u32[]{:S(2)}) collective-permute-start(bf16[64,512]{1,0:T(8,128)(2,1)S(1)} %get-tuple-element.70), channel_id=1, source_target_pairs={{0,12},{1,13},{2,14},{3,15},{4,8},{5,9},{6,10},{7,11},{8,4},{9,5},... | collective-permute-start | bytes 196616 | tf_op jit(solution)/shard_map/ppermute | solution.py:414
  35.9 5.0 %collective-permute-start.17 = (bf16[64,512]{1,0:T(8,128)(2,1)S(1)}, bf16[64,512]{1,0:T(8,128)(2,1)S(1)}, u32[]{:S(2)}, u32[]{:S(2)}) collective-permute-start(bf16[64,512]{1,0:T(8,128)(2,1)S(1)} %get-tuple-element.71), channel_id=1, source_target_pairs={{0,4},{1,5},{2,6},{3,7},{4,0},{5,1},{6,2},{7,3},{8,12},{9,13},{10,... | collective-permute-start | bytes 196616 | tf_op jit(solution)/shard_map/ppermute | solution.py:414
  37.3 7.7 %collective-permute-start.14 = (bf16[96,512]{1,0:T(8,128)(2,1)S(1)}, bf16[96,512]{1,0:T(8,128)(2,1)S(1)}, u32[]{:S(2)}, u32[]{:S(2)}) collective-permute-start(bf16[96,512]{1,0:T(8,128)(2,1)S(1)} %res_sum_z2.1.refs_4_.refs_0_), channel_id=1, source_target_pairs={{0,18},{1,19},{2,16},{3,17},{4,22},{5,23},{6,20},{7,21},{8,26},{9,... | collective-permute-start | bytes 294920 | tf_op jit(solution)/shard_map/ppermute | solution.py:423
  39.4 5.8 %collective-permute-start.13 = (bf16[96,512]{1,0:T(8,128)(2,1)S(1)}, bf16[96,512]{1,0:T(8,128)(2,1)S(1)}, u32[]{:S(2)}, u32[]{:S(2)}) collective-permute-start(bf16[96,512]{1,0:T(8,128)(2,1)S(1)} %res_sum_z2.1.refs_4_.refs_0_), channel_id=1, source_target_pairs={{0,2},{1,3},{2,0},{3,1},{4,6},{5,7},{6,4},{7,5},{8,10},{9,11},{10,... | collective-permute-start | bytes 294920 | tf_op jit(solution)/shard_map/ppermute | solution.py:414
  40.2 5.0 %collective-permute-start.12 = (bf16[96,512]{1,0:T(8,128)(2,1)S(1)}, bf16[96,512]{1,0:T(8,128)(2,1)S(1)}, u32[]{:S(2)}, u32[]{:S(2)}) collective-permute-start(bf16[96,512]{1,0:T(8,128)(2,1)S(1)} %res_sum_z2.1.refs_4_.refs_0_), channel_id=1, source_target_pairs={{0,16},{16,0},{1,17},{17,1},{2,18},{18,2},{3,19},{19,3},{4,20},{20... | collective-permute-start | bytes 294920 | tf_op jit(solution)/shard_map/ppermute | solution.py:418
  40.9 4.6 %collective-permute-start.20 = (bf16[64,512]{1,0:T(8,128)(2,1)S(1)}, bf16[64,512]{1,0:T(8,128)(2,1)S(1)}, u32[]{:S(2)}, u32[]{:S(2)}) collective-permute-start(bf16[64,512]{1,0:T(8,128)(2,1)S(1)} %conv_scaled.1.refs_4_.refs_0_), channel_id=1, source_target_pairs={{0,16},{16,0},{1,17},{17,1},{2,18},{18,2},{3,19},{19,3},{4,20},{20... | collective-permute-start | bytes 196616 | tf_op jit(solution)/shard_map/ppermute | solution.py:418
  42.3 5.1 %collective-permute-start.19 = (bf16[128,512]{1,0:T(8,128)(2,1)S(1)}, bf16[128,512]{1,0:T(8,128)(2,1)S(1)}, u32[]{:S(2)}, u32[]{:S(2)}) collective-permute-start(bf16[128,512]{1,0:T(8,128)(2,1)S(1)} %hold.1), channel_id=1, source_target_pairs={{0,14},{1,15},{2,0},{3,1},{4,2},{5,3},{6,4},{7,5},{8,6},{9,7},{10,... | collective-permute-start | bytes 393224 | tf_op jit(solution)/shard_map/ppermute | solution.py:427
  45.3 2.2 %collective-permute-start.18 = (bf16[4,96,512]{2,1,0:T(8,128)(2,1)S(1)}, bf16[4,96,512]{2,1,0:T(8,128)(2,1)S(1)}, u32[]{:S(2)}, u32[]{:S(2)}) collective-permute-start(bf16[4,96,512]{2,1,0:T(8,128)(2,1)S(1)} %res_in_order.1.refs_0_), channel_id=1, source_target_pairs={{0,1},{1,0},{2,3},{3,2},{4,5},{5,4},{6,7},{7,6},{8,9},{9,8},{10,11... | collective-permute-start | bytes 1179656 | tf_op jit(solution)/shard_map/ppermute | solution.py:414

commit v9 on v8

--- a/solution.py
+++ b/solution.py
@@ -210,7 +210,7 @@
     )
 
 
-def own_kernel(own, own_other, cw, rw, sig, gin, skin, z_out, e_out, es_out):
+def own_kernel(own, own_other, halo, cw, rw, sig, gin, skin, z_out, e_out, es_out, far_out, behind_out):
     t = own.shape[0]
     near = t // 4
     width = sig.shape[1]
@@ -225,12 +225,14 @@
     z_out[near:, :] = z[near:, :] + mm(sig[...], cw[0, 0:width, :])[: 2 * t - near, :]
     e_out[...] = mm_nt(gin[...], rw[1, :, 0:width]) + mm_nt(skin[...], rw[1, :, width:])
     es_out[...] = mm_nt(skin[...], rw[0, :, width:])
+    far_out[...] = mm(halo[0:t, :], cw[0, width:, :])
+    behind_out[...] = mm(halo[...], cw[0, 0:width, :])
 
 
 def forward_and_outer_kernel(
-    sig, z_own, e1, gin, skin, halo, halo_other, cw, rw,
+    sig, z_own, e1, gin, skin, far_own, behind_own, halo, halo_other, cw, rw,
     mine, by_y, by_x, by_both, x_out, a_out, b_out, x1_out, dz_out, o_out, ga_out,
-    staged,
+    staged, far, behind,
 ):
     t = sig.shape[0] // 2
     near = t // 4
@@ -242,14 +244,14 @@
     x_out[near + 2 * t :, :] = sig[...]
     x_out[0:near, :] = jnp.where(core == 1, halo[t:, :], halo_other[t:, :])
     x0 = x_out[near:, :]
-    behind = mm(x_out[0 : 2 * t + near, :], cw[0, 0:width, :])
+    far_other = mm(halo_other[0:t, :], cw[0, width:, :])
+    behind_other = mm(halo_other[...], cw[0, 0:width, :])
+    behind[0:near, :] = jnp.where(core == 1, behind_own[t:, :], behind_other[t:, :])
+    for f, p, c in ((far_own[...], behind_own[0:t, :], core), (far_other, behind_other[0:t, :], 1 - core)):
+        behind[pl.ds(pl.multiple_of(near + c * t, near), t), :] = p
+        far[pl.ds(pl.multiple_of(c * t, t), t), :] = f
     z0 = jnp.concatenate(
-        [
-            behind[0 : 2 * t, :] + mm(x_out[near : 2 * t + near, :], cw[0, width:, :]),
-            z_own[0:near, :] + behind[2 * t :, :],
-            z_own[near:, :],
-        ],
-        axis=0,
+        [far[...] + behind[0 : 2 * t, :], z_own[0:near, :] + behind[2 * t :, :], z_own[near:, :]], axis=0
     )
     tf = jnp.tanh(z0[:, :gated])
     sg = jax.nn.sigmoid(z0[:, gated:])
@@ -339,7 +341,7 @@
     return total
 
 
-def sum_xy_kernel(mine, by_y, by_x, by_both, tail, out):
+def sum_xy_kernel(mine, by_both, by_x, by_y, tail, out):
     rows = mine.shape[0]
     out[0:rows, :] = total_of(mine, by_y, by_x, by_both).astype(BF16)
     out[rows:, :] = tail[...]
@@ -347,7 +349,7 @@
 
 def sum_z1_kernel(rows, mine, got, out):
     out[0:rows, :] = total_of(mine.at[0:rows, :], got.at[0:rows, :]).astype(BF16)
-    out[rows:, :] = got[rows:, :]
+    out[rows:, :] = mine[rows:, :]
 
 
 def sum_z2_kernel(factor, mine, got, out):
@@ -450,13 +452,14 @@
     halo_other = swap(halo, 1)
 
     res = shaped((res_rows, width))
-    sig, gin, skin, z_own, e1, es = call(
+    sig, gin, skin, z_own, e1, es, far_own, behind_own = call(
         own_kernel,
         [
             shaped((2 * t, width)), shaped((2 * t, width)), shaped((2 * t, gated)), shaped((2 * t, 2 * gated), F32),
             shaped((2 * t, gated), F32), shaped((2 * t, gated), F32),
+            shaped((t, 2 * gated), F32), shaped((t + near, 2 * gated), F32),
         ],
-        own, own_other, cw, rw, vmem=16, flops=2_000_000_000, name="own",
+        own, own_other, halo, cw, rw, vmem=16, flops=2_000_000_000, name="own",
     )
     *rsplit, xin, a, b, x1, dz1, outer, ga = call(
         forward_and_outer_kernel,
@@ -465,8 +468,11 @@
             shaped((4 * t + near, width)), shaped((4 * t, gated), F32), shaped((4 * t, gated), F32),
             shaped((4 * t, width)), shaped((2 * t, width)), shaped((4 * t, width)), shaped((2 * t, width), F32),
         ],
-        sig, z_own, e1, gin, skin, halo, halo_other, cw, rw,
-        scratch=[pltpu.VMEM((4, res_rows, width), BF16)], vmem=16, name="forward_and_outer",
+        sig, z_own, e1, gin, skin, far_own, behind_own, halo, halo_other, cw, rw,
+        scratch=[
+            pltpu.VMEM((4, res_rows, width), BF16), pltpu.VMEM((2 * t, 2 * gated), F32),
+            pltpu.VMEM((2 * t + near, 2 * gated), F32),
+        ], vmem=16, name="forward_and_outer",
     )
     piece = (2 * half, width)
     part = shaped((4,) + piece)
@@ -480,7 +486,7 @@
         beside = swap(by_x, 2)
         return swap_streams(by_y), beside, both
 
-    rterms = (rsplit[0],) + around(*rsplit[1:])
+    rterms = (rsplit[0],) + around(*rsplit[1:])[::-1]
     cterms = (csplit[0],) + around(*csplit[1:])
     long = shaped((res_rows + near, width))
     (rsum,) = call(sum_xy_kernel, [long], *rterms, tail, after=(csplit[0],), name="res_sum_xy")
@@ -490,7 +496,7 @@
         after=(rsum,), vmem=16, flops=1_000_000_000, name="signal",
     )
     (rsum,) = call(functools.partial(sum_z1_kernel, res_rows), [long], rsum, rgot1, name="res_sum_z1")
-    rgot2 = swap(rsum, 8)
+    rgot2 = swap(rsum, 12)
     ckeep, *csend = call(
         groups_kernel, [shaped(piece, F32)] + [shaped(piece)] * 3, *cterms,
         after=(rsum, back), scratch=[pltpu.VMEM((4,) + piece, F32)], name="conv_groups",

time: 48.6 us -> 48.4 us (level)
  waiting for transfers between devices: 14.8 us -> 13 us
  starting transfers between devices: 24 us -> 25.4 us
    ppermute x3, waiting for transfers between devices: 4.62 us -> 0.01 us  [swap_both(): return lax.ppermute(x, ('dp', 'tm'), route)]
    ppermute x4, waiting for transfers between devices: 0.15 us -> 3.47 us  [swap_streams(): return lax.ppermute(x, 'dp', [(0, 1), (1, 0)])]
    ppermute x3, starting transfers between devices: 3.54 us -> 5.67 us  [swap_both(): return lax.ppermute(x, ('dp', 'tm'), route)]
    ppermute x4, starting transfers between devices: 5.25 us -> 4.18 us  [swap_streams(): return lax.ppermute(x, 'dp', [(0, 1), (1, 0)])]
  transfers between devices with their start and end apart: 21 -> 21, of which waited for: 9 -> 7; matrix products, arithmetic and copies ran while one was open for 0% -> 0% of each run, Pallas kernels for 13% -> 13%
where the time goes in v9:
time: 48.4 us; the launch traced here: 48.2 us
  starting transfers between devices  25.4 us (52%)
  waiting for transfers between devices  13 us (27%)
  Pallas kernels  9.03 us (19%)
  between operations  0.77 us (2%)
    ppermute x11, starting transfers between devices, swap(): return lax.ppermute(x, 'tm', [(i, i ^ distance) for i in range(16)])  8.3 us
    ppermute x3, starting transfers between devices, shift(): return lax.ppermute(x, 'tm', [(i, (i + distance) % 16) for i in range(16)])  7.29 us
    pallas_call x14, Pallas kernels, call(): pl.pallas_call(run, out_shape=outs, in_specs=[in_vmem] * n_args + [pl.Blo...  6.21 us
    ppermute x3, starting transfers between devices, swap_both(): return lax.ppermute(x, ('dp', 'tm'), route)  5.67 us
    ppermute x11, waiting for transfers between devices, swap(): return lax.ppermute(x, 'tm', [(i, i ^ distance) for i in range(16)])  5.6 us
    ppermute x4, starting transfers between devices, swap_streams(): return lax.ppermute(x, 'dp', [(0, 1), (1, 0)])  4.18 us
    ppermute x3, waiting for transfers between devices, shift(): return lax.ppermute(x, 'tm', [(i, (i + distance) % 16) for i in range(16)])  3.91 us
    ppermute x4, waiting for transfers between devices, swap_streams(): return lax.ppermute(x, 'dp', [(0, 1), (1, 0)])  3.47 us
  transfers between devices with their start and end apart: 21, of which 7 were waited for; matrix products, arithmetic and copies ran while one was open for 0% of the time, Pallas kernels for 13%

profile of v9, /device:TPU:0, one launch (start us, length us, event | category | flops | bytes accessed | tf_op | source)
XLA Modules:
  0.0 48.2 jit_solution(15161926312828904359)
XLA Ops:
  0.6 3.0 %collective-permute-start.1 = (bf16[128,512]{1,0:T(8,128)(2,1)}, bf16[128,512]{1,0:T(8,128)(2,1)S(1)}, u32[]{:S(2)}, u32[]{:S(2)}) collective-permute-start(bf16[128,512]{1,0:T(8,128)(2,1)} %bitcast.5), channel_id=1, source_target_pairs={{0,2},{1,3},{2,4},{3,5},{4,6},{5,7},{6,8},{7,9},{8,10},{9,11},{10,... | collective-permute-start | bytes 393224 | tf_op jit(solution)/shard_map/ppermute | solution.py:429
  3.6 1.0 %load_slab.1 = (bf16[128,1280]{1,0:T(8,128)(2,1)S(1)}, bf16[32,512]{1,0:T(8,128)(2,1)S(1)}) custom-call(bf16[128,512]{1,0:T(8,128)(2,1)} %bitcast.6, bf16[128,512]{1,0:T(8,128)(2,1)} %bitcast.4, bf16[128,256]{1,0:T(8,128)(2,1)} %bitcast.7), custom_call_target="tpu_custom_call" | custom-call | tf_op jit(solution)/shard_map/load_slab/pallas_call | solution.py:177
  4.7 1.6 %collective-permute-start.2 = (bf16[32,512]{1,0:T(8,128)(2,1)S(1)}, bf16[32,512]{1,0:T(8,128)(2,1)S(1)}, u32[]{:S(2)}, u32[]{:S(2)}) collective-permute-start(bf16[32,512]{1,0:T(8,128)(2,1)S(1)} %get-tuple-element.43), channel_id=1, source_target_pairs={{0,4},{1,5},{2,6},{3,7},{4,8},{5,9},{6,10},{7,11},{8,12},{9,13},{1... | collective-permute-start | bytes 98312 | tf_op jit(solution)/shard_map/ppermute | solution.py:429
  6.3 1.8 %load_weights.1 = (bf16[2,1024,512]{2,1,0:T(8,128)(2,1)S(1)}, bf16[2,256,768]{2,1,0:T(8,128)(2,1)S(1)}) custom-call(bf16[2,1024,512]{2,1,0:T(8,128)(2,1)} %cw.1, bf16[2,256,768]{2,1,0:T(8,128)(2,1)} %rw.1), custom_call_target="tpu_custom_call" | custom-call | flops 4000000000 | tf_op jit(solution)/shard_map/load_weights/pallas_call | solution.py:177
  8.1 2.3 %collective-permute-done.2.refs_1_ = bf16[32,512]{1,0:T(8,128)(2,1)S(1)} collective-permute-done((bf16[32,512]{1,0:T(8,128)(2,1)S(1)}, bf16[32,512]{1,0:T(8,128)(2,1)S(1)}, u32[]{:S(2)}, u32[]{:S(2)}) %collective-permute-start.2) | collective-permute-done | bytes 32800 | tf_op jit(solution)/shard_map/ppermute | solution.py:429
  10.4 0.3 collective-permute-done.1.refs_0_
  10.8 0.7 %own.1 = (bf16[256,512]{1,0:T(8,128)(2,1)S(1)}, bf16[256,512]{1,0:T(8,128)(2,1)S(1)}, bf16[256,256]{1,0:T(8,128)(2,1)S(1)}, f32[256,512]{1,0:T(8,128)S(1)}, f32[...) custom-call(bf16[128,1280]{1,0:T(8,128)(2,1)S(1)} %get-tuple-element.42.refs_0_, ...), custom_call_target="tpu_custom_call" | custom-call | flops 2000000000 | tf_op jit(solution)/shard_map/own/pallas_call | solution.py:131
  11.6 0.6 %collective-permute-done.3.refs_8_ = bf16[160,512]{1,0:T(8,128)(2,1)S(1)} collective-permute-done((bf16[160,512]{1,0:T(8,128)(2,1)S(1)}, bf16[160,512]{1,0:T(8,128)(2,1)S(1)}, u32[]{:S(2)}, u32[]{:S(2)}) %collective-permute-start.3) | collective-permute-done | bytes 163872 | tf_op jit(solution)/shard_map/ppermute | solution.py:416
  12.2 1.7 %forward_and_outer.1 = (bf16[96,512]{1,0:T(8,128)(2,1)S(1)}, bf16[96,512]{1,0:T(8,128)(2,1)S(1)}, bf16[96,512]{1,0:T(8,128)(2,1)S(1)}, bf16[96,512]{1,0:T(8,128)...) custom-call(bf16[256,512]{1,0:T(8,128)(2,1)S(1)} %get-tuple-element., ...), custom_call_target="tpu_custom_call" | custom-call | tf_op jit(solution)/shard_map/forward_and_outer/pallas_call | solution.py:131
  13.9 2.3 %collective-permute-start.4 = (bf16[96,512]{1,0:T(8,128)(2,1)S(1)}, bf16[96,512]{1,0:T(8,128)(2,1)S(1)}, u32[]{:S(2)}, u32[]{:S(2)}) collective-permute-start(bf16[96,512]{1,0:T(8,128)(2,1)S(1)} %get-tuple-element.54), channel_id=1, source_target_pairs={{0,18},{1,19},{2,16},{3,17},{4,22},{5,23},{6,20},{7,21},{8,26},{9,... | collective-permute-start | bytes 294920 | tf_op jit(solution)/shard_map/ppermute | solution.py:425
  16.1 0.8 %collective-permute-start.5 = (bf16[96,512]{1,0:T(8,128)(2,1)S(1)}, bf16[96,512]{1,0:T(8,128)(2,1)S(1)}, u32[]{:S(2)}, u32[]{:S(2)}) collective-permute-start(bf16[96,512]{1,0:T(8,128)(2,1)S(1)} %get-tuple-element.55), channel_id=1, source_target_pairs={{0,2},{1,3},{2,0},{3,1},{4,6},{5,7},{6,4},{7,5},{8,10},{9,11},{10,... | collective-permute-start | bytes 294920 | tf_op jit(solution)/shard_map/ppermute | solution.py:416
  16.9 0.5 %collective-permute-start.6 = (bf16[96,512]{1,0:T(8,128)(2,1)S(1)}, bf16[96,512]{1,0:T(8,128)(2,1)S(1)}, u32[]{:S(2)}, u32[]{:S(2)}) collective-permute-start(bf16[96,512]{1,0:T(8,128)(2,1)S(1)} %get-tuple-element.56), channel_id=1, source_target_pairs={{0,16},{16,0},{1,17},{17,1},{2,18},{18,2},{3,19},{19,3},{4,20},{20... | collective-permute-start | bytes 294920 | tf_op jit(solution)/shard_map/ppermute | solution.py:420
  17.4 1.2 %inner.1 = (bf16[4,64,512]{2,1,0:T(8,128)(2,1)S(1)}, bf16[4,64,512]{2,1,0:T(8,128)(2,1)S(1)}, bf16[4,64,512]{2,1,0:T(8,128)(2,1)S(1)}, bf16[4,64,512]{2,1,0:T(8,...) custom-call(bf16[544,512]{1,0:T(8,128)(2,1)S(1)} %get-tuple-element.57.refs_0_, ...), custom_call_target="tpu_custom_call" | custom-call | flops 2000000000 | tf_op jit(solution)/shard_map/inner/pallas_call | solution.py:131
  18.6 1.6 %collective-permute-start.9 = (bf16[4,64,512]{2,1,0:T(8,128)(2,1)S(1)}, bf16[4,64,512]{2,1,0:T(8,128)(2,1)S(1)}, u32[]{:S(2)}, u32[]{:S(2)}) collective-permute-start(bf16[4,64,512]{2,1,0:T(8,128)(2,1)S(1)} %get-tuple-element.66), channel_id=1, source_target_pairs={{0,16},{16,0},{1,17},{17,1},{2,18},{18,2},{3,19},{19,3},{4,20},{20... | collective-permute-start | bytes 786440 | tf_op jit(solution)/shard_map/ppermute | solution.py:420
  20.2 1.3 %collective-permute-start.10 = (bf16[4,64,512]{2,1,0:T(8,128)(2,1)S(1)}, bf16[4,64,512]{2,1,0:T(8,128)(2,1)S(1)}, u32[]{:S(2)}, u32[]{:S(2)}) collective-permute-start(bf16[4,64,512]{2,1,0:T(8,128)(2,1)S(1)} %get-tuple-element.67), channel_id=1, source_target_pairs={{0,2},{1,3},{2,0},{3,1},{4,6},{5,7},{6,4},{7,5},{8,10},{9,11},{10,... | collective-permute-start | bytes 786440 | tf_op jit(solution)/shard_map/ppermute | solution.py:416
  21.5 1.2 %collective-permute-start.11 = (bf16[4,64,512]{2,1,0:T(8,128)(2,1)S(1)}, bf16[4,64,512]{2,1,0:T(8,128)(2,1)S(1)}, u32[]{:S(2)}, u32[]{:S(2)}) collective-permute-start(bf16[4,64,512]{2,1,0:T(8,128)(2,1)S(1)} %get-tuple-element.68), channel_id=1, source_target_pairs={{0,18},{1,19},{2,16},{3,17},{4,22},{5,23},{6,20},{7,21},{8,26},{9,... | collective-permute-start | bytes 786440 | tf_op jit(solution)/shard_map/ppermute | solution.py:425
  22.8 5.0 %collective-permute-done.7.refs_1_.refs_4_ = bf16[128,512]{1,0:T(8,128)(2,1)S(1)} collective-permute-done((bf16[128,512]{1,0:T(8,128)(2,1)S(1)}, bf16[128,512]{1,0:T(8,128)(2,1)S(1)}, u32[]{:S(2)}, u32[]{:S(2)}) %collective-permute-start.7) | collective-permute-done | bytes 131104 | tf_op jit(solution)/shard_map/ppermute | solution.py:416
  27.8 1.7 %collective-permute-start.8 = (bf16[128,512]{1,0:T(8,128)(2,1)S(1)}, bf16[128,512]{1,0:T(8,128)(2,1)S(1)}, u32[]{:S(2)}, u32[]{:S(2)}) collective-permute-start(bf16[128,512]{1,0:T(8,128)(2,1)S(1)} %res_sum_z1.1.refs_4_.refs_0_), channel_id=1, source_target_pairs={{0,12},{1,13},{2,14},{3,15},{4,8},{5,9},{6,10},{7,11},{8,4},{9,5},... | collective-permute-start | bytes 393224 | tf_op jit(solution)/shard_map/ppermute | solution.py:416
  29.5 0.5 %signal.1 = (f32[128,512]{1,0:T(8,128)S(1)}, bf16[128,512]{1,0:T(8,128)(2,1)S(1)}) custom-call(bf16[544,512]{1,0:T(8,128)(2,1)S(1)} %get-tuple-element.69.refs_0_, bf16[512,512]{1,0:T(8,128)(2,1)S(1)} %get-tuple-element.62.refs_5_.refs_1_, f32[256,512]{1,0:T(8,128)S(1)} %get-tuple-element.70.refs_2_, ...), custom_call_target="tpu_custom_call" | custom-call | flops 1000000000 | tf_op jit(solution)/shard_map/signal/pallas_call | solution.py:131
  30.1 3.0 %collective-permute-done.9.refs_1_ = bf16[4,64,512]{2,1,0:T(8,128)(2,1)S(1)} collective-permute-done((bf16[4,64,512]{2,1,0:T(8,128)(2,1)S(1)}, bf16[4,64,512]{2,1,0:T(8,128)(2,1)S(1)}, u32[]{:S(2)}, u32[]{:S(2)}) %collective-permute-start.9) | collective-permute-done | bytes 262176 | tf_op jit(solution)/shard_map/ppermute | solution.py:420
  33.4 0.8 %collective-permute-start.15 = (bf16[64,512]{1,0:T(8,128)(2,1)S(1)}, bf16[64,512]{1,0:T(8,128)(2,1)S(1)}, u32[]{:S(2)}, u32[]{:S(2)}) collective-permute-start(bf16[64,512]{1,0:T(8,128)(2,1)S(1)} %get-tuple-element.73), channel_id=1, source_target_pairs={{0,8},{1,9},{2,10},{3,11},{4,12},{5,13},{6,14},{7,15},{8,0},{9,1},... | collective-permute-start | bytes 196616 | tf_op jit(solution)/shard_map/ppermute | solution.py:416
  34.1 1.4 %collective-permute-start.16 = (bf16[64,512]{1,0:T(8,128)(2,1)S(1)}, bf16[64,512]{1,0:T(8,128)(2,1)S(1)}, u32[]{:S(2)}, u32[]{:S(2)}) collective-permute-start(bf16[64,512]{1,0:T(8,128)(2,1)S(1)} %get-tuple-element.74), channel_id=1, source_target_pairs={{0,12},{1,13},{2,14},{3,15},{4,8},{5,9},{6,10},{7,11},{8,4},{9,5},... | collective-permute-start | bytes 196616 | tf_op jit(solution)/shard_map/ppermute | solution.py:416
  35.5 1.4 %collective-permute-start.17 = (bf16[64,512]{1,0:T(8,128)(2,1)S(1)}, bf16[64,512]{1,0:T(8,128)(2,1)S(1)}, u32[]{:S(2)}, u32[]{:S(2)}) collective-permute-start(bf16[64,512]{1,0:T(8,128)(2,1)S(1)} %get-tuple-element.75), channel_id=1, source_target_pairs={{0,4},{1,5},{2,6},{3,7},{4,0},{5,1},{6,2},{7,3},{8,12},{9,13},{10,... | collective-permute-start | bytes 196616 | tf_op jit(solution)/shard_map/ppermute | solution.py:416
  37.0 2.2 %collective-permute-start.14 = (bf16[96,512]{1,0:T(8,128)(2,1)S(1)}, bf16[96,512]{1,0:T(8,128)(2,1)S(1)}, u32[]{:S(2)}, u32[]{:S(2)}) collective-permute-start(bf16[96,512]{1,0:T(8,128)(2,1)S(1)} %res_sum_z2.1.refs_4_.refs_0_), channel_id=1, source_target_pairs={{0,18},{1,19},{2,16},{3,17},{4,22},{5,23},{6,20},{7,21},{8,26},{9,... | collective-permute-start | bytes 294920 | tf_op jit(solution)/shard_map/ppermute | solution.py:425
  39.1 0.8 %collective-permute-start.13 = (bf16[96,512]{1,0:T(8,128)(2,1)S(1)}, bf16[96,512]{1,0:T(8,128)(2,1)S(1)}, u32[]{:S(2)}, u32[]{:S(2)}) collective-permute-start(bf16[96,512]{1,0:T(8,128)(2,1)S(1)} %res_sum_z2.1.refs_4_.refs_0_), channel_id=1, source_target_pairs={{0,2},{1,3},{2,0},{3,1},{4,6},{5,7},{6,4},{7,5},{8,10},{9,11},{10,... | collective-permute-start | bytes 294920 | tf_op jit(solution)/shard_map/ppermute | solution.py:416
  39.9 0.6 %collective-permute-start.12 = (bf16[96,512]{1,0:T(8,128)(2,1)S(1)}, bf16[96,512]{1,0:T(8,128)(2,1)S(1)}, u32[]{:S(2)}, u32[]{:S(2)}) collective-permute-start(bf16[96,512]{1,0:T(8,128)(2,1)S(1)} %res_sum_z2.1.refs_4_.refs_0_), channel_id=1, source_target_pairs={{0,16},{16,0},{1,17},{17,1},{2,18},{18,2},{3,19},{19,3},{4,20},{20... | collective-permute-start | bytes 294920 | tf_op jit(solution)/shard_map/ppermute | solution.py:420
  40.6 1.5 %collective-permute-start.20 = (bf16[64,512]{1,0:T(8,128)(2,1)S(1)}, bf16[64,512]{1,0:T(8,128)(2,1)S(1)}, u32[]{:S(2)}, u32[]{:S(2)}) collective-permute-start(bf16[64,512]{1,0:T(8,128)(2,1)S(1)} %conv_scaled.1.refs_4_.refs_0_), channel_id=1, source_target_pairs={{0,16},{16,0},{1,17},{17,1},{2,18},{18,2},{3,19},{19,3},{4,20},{20... | collective-permute-start | bytes 196616 | tf_op jit(solution)/shard_map/ppermute | solution.py:420
  42.0 2.7 %collective-permute-start.19 = (bf16[128,512]{1,0:T(8,128)(2,1)S(1)}, bf16[128,512]{1,0:T(8,128)(2,1)S(1)}, u32[]{:S(2)}, u32[]{:S(2)}) collective-permute-start(bf16[128,512]{1,0:T(8,128)(2,1)S(1)} %hold.1), channel_id=1, source_target_pairs={{0,14},{1,15},{2,0},{3,1},{4,2},{5,3},{6,4},{7,5},{8,6},{9,7},{10,... | collective-permute-start | bytes 393224 | tf_op jit(solution)/shard_map/ppermute | solution.py:429
  44.9 0.4 collective-permute-done.20.refs_1_
  45.3 0.7 %finish_conv.1 = (bf16[2,64,512]{2,1,0:T(8,128)(2,1)}, f32[8,128]{1,0:T(8,128)S(1)}) custom-call(bf16[64,512]{1,0:T(8,128)(2,1)S(1)} %conv_scaled.1.refs_4_.refs_0_, bf16[64,512]{1,0:T(8,128)(2,1)S(1)} %collective-permute-done.20.refs_1_), custom_call_target="tpu_custom_call" | custom-call | flops 10000000000 | tf_op jit(solution)/shard_map/finish_conv/pallas_call | solution.py:131
  46.0 1.3 %collective-permute-done.19.refs_3_ = bf16[128,512]{1,0:T(8,128)(2,1)S(1)} collective-permute-done((bf16[128,512]{1,0:T(8,128)(2,1)S(1)}, bf16[128,512]{1,0:T(8,128)(2,1)S(1)}, u32[]{:S(2)}, u32[]{:S(2)}) %collective-permute-start.19) | collective-permute-done | bytes 131104 | tf_op jit(solution)/shard_map/ppermute | solution.py:429
  47.2 1.0 %finish.1 = (bf16[2,256,768]{2,1,0:T(8,128)(2,1)}, bf16[128,512]{1,0:T(8,128)(2,1)}) custom-call(bf16[4,96,512]{2,1,0:T(8,128)(2,1)S(1)} %res_in_order.1.refs_0_, bf16[4,96,512]{2,1,0:T(8,128)(2,1)S(1)} %collective-permute-done.18.refs_1_, f32[128,512]{1,0:T(8,128)S(1)} %get-tuple-element.76.refs_2_, bf16[128,512]{1,0:T(8,128)(2,1)S(1)} %collective-permute-done.19.refs_3_, ...), custom_call_target="tpu_custom_call" | custom-call | tf_op jit(solution)/shard_map/finish/pallas_call | solution.py:131
  (26 shorter events, 0.7 us)
Async XLA Ops:
  0.6 10.1 %collective-permute-start.1 = (bf16[128,512]{1,0:T(8,128)(2,1)}, bf16[128,512]{1,0:T(8,128)(2,1)S(1)}, u32[]{:S(2)}, u32[]{:S(2)}) collective-permute-start(bf16[128,512]{1,0:T(8,128)(2,1)} %bitcast.5), channel_id=1, source_target_pairs={{0,2},{1,3},{2,4},{3,5},{4,6},{5,7},{6,8},{7,9},{8,10},{9,11},{10,... | collective-permute-start | bytes 393224 | tf_op jit(solution)/shard_map/ppermute | solution.py:429
  4.7 5.8 %collective-permute-start.2 = (bf16[32,512]{1,0:T(8,128)(2,1)S(1)}, bf16[32,512]{1,0:T(8,128)(2,1)S(1)}, u32[]{:S(2)}, u32[]{:S(2)}) collective-permute-start(bf16[32,512]{1,0:T(8,128)(2,1)S(1)} %get-tuple-element.43), channel_id=1, source_target_pairs={{0,4},{1,5},{2,6},{3,7},{4,8},{5,9},{6,10},{7,11},{8,12},{9,13},{1... | collective-permute-start | bytes 98312 | tf_op jit(solution)/shard_map/ppermute | solution.py:429
  6.3 4.5 %collective-permute-start = (bf16[128,1280]{1,0:T(8,128)(2,1)S(1)}, bf16[128,1280]{1,0:T(8,128)(2,1)S(1)}, u32[]{:S(2)}, u32[]{:S(2)}) collective-permute-start(bf16[128,1280]{1,0:T(8,128)(2,1)S(1)} %get-tuple-element.42.refs_0_), channel_id=1, source_target_pairs={{0,1},{1,0},{2,3},{3,2},{4,5},{5,4},{6,7},{7,6},{8,9},{9,8},{10,11... | collective-permute-start | bytes 983048 | tf_op jit(solution)/shard_map/ppermute | solution.py:416
  10.7 1.5 %collective-permute-start.3 = (bf16[160,512]{1,0:T(8,128)(2,1)S(1)}, bf16[160,512]{1,0:T(8,128)(2,1)S(1)}, u32[]{:S(2)}, u32[]{:S(2)}) collective-permute-start(bf16[160,512]{1,0:T(8,128)(2,1)S(1)} %pack_halo.1.refs_2_.refs_7_), channel_id=1, source_target_pairs={{0,1},{1,0},{2,3},{3,2},{4,5},{5,4},{6,7},{7,6},{8,9},{9,8},{10,11... | collective-permute-start | bytes 491528 | tf_op jit(solution)/shard_map/ppermute | solution.py:416
  13.9 7.6 %collective-permute-start.4 = (bf16[96,512]{1,0:T(8,128)(2,1)S(1)}, bf16[96,512]{1,0:T(8,128)(2,1)S(1)}, u32[]{:S(2)}, u32[]{:S(2)}) collective-permute-start(bf16[96,512]{1,0:T(8,128)(2,1)S(1)} %get-tuple-element.54), channel_id=1, source_target_pairs={{0,18},{1,19},{2,16},{3,17},{4,22},{5,23},{6,20},{7,21},{8,26},{9,... | collective-permute-start | bytes 294920 | tf_op jit(solution)/shard_map/ppermute | solution.py:425
  16.1 6.5 %collective-permute-start.5 = (bf16[96,512]{1,0:T(8,128)(2,1)S(1)}, bf16[96,512]{1,0:T(8,128)(2,1)S(1)}, u32[]{:S(2)}, u32[]{:S(2)}) collective-permute-start(bf16[96,512]{1,0:T(8,128)(2,1)S(1)} %get-tuple-element.55), channel_id=1, source_target_pairs={{0,2},{1,3},{2,0},{3,1},{4,6},{5,7},{6,4},{7,5},{8,10},{9,11},{10,... | collective-permute-start | bytes 294920 | tf_op jit(solution)/shard_map/ppermute | solution.py:416
  16.9 5.8 %collective-permute-start.6 = (bf16[96,512]{1,0:T(8,128)(2,1)S(1)}, bf16[96,512]{1,0:T(8,128)(2,1)S(1)}, u32[]{:S(2)}, u32[]{:S(2)}) collective-permute-start(bf16[96,512]{1,0:T(8,128)(2,1)S(1)} %get-tuple-element.56), channel_id=1, source_target_pairs={{0,16},{16,0},{1,17},{17,1},{2,18},{18,2},{3,19},{19,3},{4,20},{20... | collective-permute-start | bytes 294920 | tf_op jit(solution)/shard_map/ppermute | solution.py:420
  18.6 14.5 %collective-permute-start.9 = (bf16[4,64,512]{2,1,0:T(8,128)(2,1)S(1)}, bf16[4,64,512]{2,1,0:T(8,128)(2,1)S(1)}, u32[]{:S(2)}, u32[]{:S(2)}) collective-permute-start(bf16[4,64,512]{2,1,0:T(8,128)(2,1)S(1)} %get-tuple-element.66), channel_id=1, source_target_pairs={{0,16},{16,0},{1,17},{17,1},{2,18},{18,2},{3,19},{19,3},{4,20},{20... | collective-permute-start | bytes 786440 | tf_op jit(solution)/shard_map/ppermute | solution.py:420
  20.2 12.9 %collective-permute-start.10 = (bf16[4,64,512]{2,1,0:T(8,128)(2,1)S(1)}, bf16[4,64,512]{2,1,0:T(8,128)(2,1)S(1)}, u32[]{:S(2)}, u32[]{:S(2)}) collective-permute-start(bf16[4,64,512]{2,1,0:T(8,128)(2,1)S(1)} %get-tuple-element.67), channel_id=1, source_target_pairs={{0,2},{1,3},{2,0},{3,1},{4,6},{5,7},{6,4},{7,5},{8,10},{9,11},{10,... | collective-permute-start | bytes 786440 | tf_op jit(solution)/shard_map/ppermute | solution.py:416
  21.5 11.7 %collective-permute-start.11 = (bf16[4,64,512]{2,1,0:T(8,128)(2,1)S(1)}, bf16[4,64,512]{2,1,0:T(8,128)(2,1)S(1)}, u32[]{:S(2)}, u32[]{:S(2)}) collective-permute-start(bf16[4,64,512]{2,1,0:T(8,128)(2,1)S(1)} %get-tuple-element.68), channel_id=1, source_target_pairs={{0,18},{1,19},{2,16},{3,17},{4,22},{5,23},{6,20},{7,21},{8,26},{9,... | collective-permute-start | bytes 786440 | tf_op jit(solution)/shard_map/ppermute | solution.py:425
  22.8 5.0 %collective-permute-start.7 = (bf16[128,512]{1,0:T(8,128)(2,1)S(1)}, bf16[128,512]{1,0:T(8,128)(2,1)S(1)}, u32[]{:S(2)}, u32[]{:S(2)}) collective-permute-start(bf16[128,512]{1,0:T(8,128)(2,1)S(1)} %res_sum_xy.1.refs_0_.refs_4_), channel_id=1, source_target_pairs={{0,4},{1,5},{2,6},{3,7},{4,0},{5,1},{6,2},{7,3},{8,12},{9,13},{10,... | collective-permute-start | bytes 393224 | tf_op jit(solution)/shard_map/ppermute | solution.py:416
  27.8 9.1 %collective-permute-start.8 = (bf16[128,512]{1,0:T(8,128)(2,1)S(1)}, bf16[128,512]{1,0:T(8,128)(2,1)S(1)}, u32[]{:S(2)}, u32[]{:S(2)}) collective-permute-start(bf16[128,512]{1,0:T(8,128)(2,1)S(1)} %res_sum_z1.1.refs_4_.refs_0_), channel_id=1, source_target_pairs={{0,12},{1,13},{2,14},{3,15},{4,8},{5,9},{6,10},{7,11},{8,4},{9,5},... | collective-permute-start | bytes 393224 | tf_op jit(solution)/shard_map/ppermute | solution.py:416
  33.4 6.5 %collective-permute-start.15 = (bf16[64,512]{1,0:T(8,128)(2,1)S(1)}, bf16[64,512]{1,0:T(8,128)(2,1)S(1)}, u32[]{:S(2)}, u32[]{:S(2)}) collective-permute-start(bf16[64,512]{1,0:T(8,128)(2,1)S(1)} %get-tuple-element.73), channel_id=1, source_target_pairs={{0,8},{1,9},{2,10},{3,11},{4,12},{5,13},{6,14},{7,15},{8,0},{9,1},... | collective-permute-start | bytes 196616 | tf_op jit(solution)/shard_map/ppermute | solution.py:416
  34.1 6.4 %collective-permute-start.16 = (bf16[64,512]{1,0:T(8,128)(2,1)S(1)}, bf16[64,512]{1,0:T(8,128)(2,1)S(1)}, u32[]{:S(2)}, u32[]{:S(2)}) collective-permute-start(bf16[64,512]{1,0:T(8,128)(2,1)S(1)} %get-tuple-element.74), channel_id=1, source_target_pairs={{0,12},{1,13},{2,14},{3,15},{4,8},{5,9},{6,10},{7,11},{8,4},{9,5},... | collective-permute-start | bytes 196616 | tf_op jit(solution)/shard_map/ppermute | solution.py:416
  35.5 5.0 %collective-permute-start.17 = (bf16[64,512]{1,0:T(8,128)(2,1)S(1)}, bf16[64,512]{1,0:T(8,128)(2,1)S(1)}, u32[]{:S(2)}, u32[]{:S(2)}) collective-permute-start(bf16[64,512]{1,0:T(8,128)(2,1)S(1)} %get-tuple-element.75), channel_id=1, source_target_pairs={{0,4},{1,5},{2,6},{3,7},{4,0},{5,1},{6,2},{7,3},{8,12},{9,13},{10,... | collective-permute-start | bytes 196616 | tf_op jit(solution)/shard_map/ppermute | solution.py:416
  37.0 7.8 %collective-permute-start.14 = (bf16[96,512]{1,0:T(8,128)(2,1)S(1)}, bf16[96,512]{1,0:T(8,128)(2,1)S(1)}, u32[]{:S(2)}, u32[]{:S(2)}) collective-permute-start(bf16[96,512]{1,0:T(8,128)(2,1)S(1)} %res_sum_z2.1.refs_4_.refs_0_), channel_id=1, source_target_pairs={{0,18},{1,19},{2,16},{3,17},{4,22},{5,23},{6,20},{7,21},{8,26},{9,... | collective-permute-start | bytes 294920 | tf_op jit(solution)/shard_map/ppermute | solution.py:425
  39.1 5.6 %collective-permute-start.13 = (bf16[96,512]{1,0:T(8,128)(2,1)S(1)}, bf16[96,512]{1,0:T(8,128)(2,1)S(1)}, u32[]{:S(2)}, u32[]{:S(2)}) collective-permute-start(bf16[96,512]{1,0:T(8,128)(2,1)S(1)} %res_sum_z2.1.refs_4_.refs_0_), channel_id=1, source_target_pairs={{0,2},{1,3},{2,0},{3,1},{4,6},{5,7},{6,4},{7,5},{8,10},{9,11},{10,... | collective-permute-start | bytes 294920 | tf_op jit(solution)/shard_map/ppermute | solution.py:416
  39.9 4.8 %collective-permute-start.12 = (bf16[96,512]{1,0:T(8,128)(2,1)S(1)}, bf16[96,512]{1,0:T(8,128)(2,1)S(1)}, u32[]{:S(2)}, u32[]{:S(2)}) collective-permute-start(bf16[96,512]{1,0:T(8,128)(2,1)S(1)} %res_sum_z2.1.refs_4_.refs_0_), channel_id=1, source_target_pairs={{0,16},{16,0},{1,17},{17,1},{2,18},{18,2},{3,19},{19,3},{4,20},{20... | collective-permute-start | bytes 294920 | tf_op jit(solution)/shard_map/ppermute | solution.py:420
  40.6 4.7 %collective-permute-start.20 = (bf16[64,512]{1,0:T(8,128)(2,1)S(1)}, bf16[64,512]{1,0:T(8,128)(2,1)S(1)}, u32[]{:S(2)}, u32[]{:S(2)}) collective-permute-start(bf16[64,512]{1,0:T(8,128)(2,1)S(1)} %conv_scaled.1.refs_4_.refs_0_), channel_id=1, source_target_pairs={{0,16},{16,0},{1,17},{17,1},{2,18},{18,2},{3,19},{19,3},{4,20},{20... | collective-permute-start | bytes 196616 | tf_op jit(solution)/shard_map/ppermute | solution.py:420
  42.0 5.2 %collective-permute-start.19 = (bf16[128,512]{1,0:T(8,128)(2,1)S(1)}, bf16[128,512]{1,0:T(8,128)(2,1)S(1)}, u32[]{:S(2)}, u32[]{:S(2)}) collective-permute-start(bf16[128,512]{1,0:T(8,128)(2,1)S(1)} %hold.1), channel_id=1, source_target_pairs={{0,14},{1,15},{2,0},{3,1},{4,2},{5,3},{6,4},{7,5},{8,6},{9,7},{10,... | collective-permute-start | bytes 393224 | tf_op jit(solution)/shard_map/ppermute | solution.py:429
  44.8 2.5 %collective-permute-start.18 = (bf16[4,96,512]{2,1,0:T(8,128)(2,1)S(1)}, bf16[4,96,512]{2,1,0:T(8,128)(2,1)S(1)}, u32[]{:S(2)}, u32[]{:S(2)}) collective-permute-start(bf16[4,96,512]{2,1,0:T(8,128)(2,1)S(1)} %res_in_order.1.refs_0_), channel_id=1, source_target_pairs={{0,1},{1,0},{2,3},{3,2},{4,5},{5,4},{6,7},{7,6},{8,9},{9,8},{10,11... | collective-permute-start | bytes 1179656 | tf_op jit(solution)/shard_map/ppermute | solution.py:416

commit v10 on v8

--- a/solution.py
+++ b/solution.py
@@ -339,7 +339,7 @@
     return total
 
 
-def sum_xy_kernel(mine, by_y, by_x, by_both, tail, out):
+def sum_xy_kernel(mine, by_both, by_x, by_y, tail, out):
     rows = mine.shape[0]
     out[0:rows, :] = total_of(mine, by_y, by_x, by_both).astype(BF16)
     out[rows:, :] = tail[...]
@@ -347,7 +347,7 @@
 
 def sum_z1_kernel(rows, mine, got, out):
     out[0:rows, :] = total_of(mine.at[0:rows, :], got.at[0:rows, :]).astype(BF16)
-    out[rows:, :] = got[rows:, :]
+    out[rows:, :] = mine[rows:, :]
 
 
 def sum_z2_kernel(factor, mine, got, out):
@@ -480,7 +480,7 @@
         beside = swap(by_x, 2)
         return swap_streams(by_y), beside, both
 
-    rterms = (rsplit[0],) + around(*rsplit[1:])
+    rterms = (rsplit[0],) + around(*rsplit[1:])[::-1]
     cterms = (csplit[0],) + around(*csplit[1:])
     long = shaped((res_rows + near, width))
     (rsum,) = call(sum_xy_kernel, [long], *rterms, tail, after=(csplit[0],), name="res_sum_xy")
@@ -490,7 +490,7 @@
         after=(rsum,), vmem=16, flops=1_000_000_000, name="signal",
     )
     (rsum,) = call(functools.partial(sum_z1_kernel, res_rows), [long], rsum, rgot1, name="res_sum_z1")
-    rgot2 = swap(rsum, 8)
+    rgot2 = swap(rsum, 12)
     ckeep, *csend = call(
         groups_kernel, [shaped(piece, F32)] + [shaped(piece)] * 3, *cterms,
         after=(rsum, back), scratch=[pltpu.VMEM((4,) + piece, F32)], name="conv_groups",

time: 48.6 us -> 48.4 us (level)
  waiting for transfers between devices: 14.8 us -> 13.1 us
  starting transfers between devices: 24 us -> 25.4 us
    ppermute x3, waiting for transfers between devices: 4.62 us -> 0.01 us  [swap_both(): return lax.ppermute(x, ('dp', 'tm'), route)]
    ppermute x4, waiting for transfers between devices: 0.15 us -> 3.48 us  [swap_streams(): return lax.ppermute(x, 'dp', [(0, 1), (1, 0)])]
    ppermute x3, starting transfers between devices: 3.54 us -> 5.66 us  [swap_both(): return lax.ppermute(x, ('dp', 'tm'), route)]
    ppermute x4, starting transfers between devices: 5.25 us -> 4.18 us  [swap_streams(): return lax.ppermute(x, 'dp', [(0, 1), (1, 0)])]
  transfers between devices with their start and end apart: 21 -> 21, of which waited for: 9 -> 7; matrix products, arithmetic and copies ran while one was open for 0% -> 0% of each run, Pallas kernels for 13% -> 13%
where the time goes in v10:
time: 48.4 us; the launch traced here: 48.2 us
  starting transfers between devices  25.4 us (52%)
  waiting for transfers between devices  13.1 us (27%)
  Pallas kernels  8.88 us (18%)
  between operations  0.77 us (2%)
    ppermute x11, starting transfers between devices, swap(): return lax.ppermute(x, 'tm', [(i, i ^ distance) for i in range(16)])  8.3 us
    ppermute x3, starting transfers between devices, shift(): return lax.ppermute(x, 'tm', [(i, (i + distance) % 16) for i in range(16)])  7.28 us
    pallas_call x14, Pallas kernels, call(): pl.pallas_call(run, out_shape=outs, in_specs=[in_vmem] * n_args + [pl.Blo...  6.06 us
    ppermute x11, waiting for transfers between devices, swap(): return lax.ppermute(x, 'tm', [(i, i ^ distance) for i in range(16)])  5.75 us
    ppermute x3, starting transfers between devices, swap_both(): return lax.ppermute(x, ('dp', 'tm'), route)  5.66 us
    ppermute x4, starting transfers between devices, swap_streams(): return lax.ppermute(x, 'dp', [(0, 1), (1, 0)])  4.18 us
    ppermute x3, waiting for transfers between devices, shift(): return lax.ppermute(x, 'tm', [(i, (i + distance) % 16) for i in range(16)])  3.91 us
    ppermute x4, waiting for transfers between devices, swap_streams(): return lax.ppermute(x, 'dp', [(0, 1), (1, 0)])  3.48 us
  transfers between devices with their start and end apart: 21, of which 7 were waited for; matrix products, arithmetic and copies ran while one was open for 0% of the time, Pallas kernels for 13%

profile of v10, /device:TPU:0, one launch (start us, length us, event | category | flops | bytes accessed | tf_op | source)
XLA Modules:
  0.0 48.2 jit_solution(4730335707496193872)
XLA Ops:
  0.6 3.0 %collective-permute-start.1 = (bf16[128,512]{1,0:T(8,128)(2,1)}, bf16[128,512]{1,0:T(8,128)(2,1)S(1)}, u32[]{:S(2)}, u32[]{:S(2)}) collective-permute-start(bf16[128,512]{1,0:T(8,128)(2,1)} %bitcast.5), channel_id=1, source_target_pairs={{0,2},{1,3},{2,4},{3,5},{4,6},{5,7},{6,8},{7,9},{8,10},{9,11},{10,... | collective-permute-start | bytes 393224 | tf_op jit(solution)/shard_map/ppermute | solution.py:427
  3.6 1.0 %load_slab.1 = (bf16[128,1280]{1,0:T(8,128)(2,1)S(1)}, bf16[32,512]{1,0:T(8,128)(2,1)S(1)}) custom-call(bf16[128,512]{1,0:T(8,128)(2,1)} %bitcast.6, bf16[128,512]{1,0:T(8,128)(2,1)} %bitcast.4, bf16[128,256]{1,0:T(8,128)(2,1)} %bitcast.7), custom_call_target="tpu_custom_call" | custom-call | tf_op jit(solution)/shard_map/load_slab/pallas_call | solution.py:177
  4.7 1.6 %collective-permute-start.2 = (bf16[32,512]{1,0:T(8,128)(2,1)S(1)}, bf16[32,512]{1,0:T(8,128)(2,1)S(1)}, u32[]{:S(2)}, u32[]{:S(2)}) collective-permute-start(bf16[32,512]{1,0:T(8,128)(2,1)S(1)} %get-tuple-element.48), channel_id=1, source_target_pairs={{0,4},{1,5},{2,6},{3,7},{4,8},{5,9},{6,10},{7,11},{8,12},{9,13},{1... | collective-permute-start | bytes 98312 | tf_op jit(solution)/shard_map/ppermute | solution.py:427
  6.3 1.8 %load_weights.1 = (bf16[2,1024,512]{2,1,0:T(8,128)(2,1)S(1)}, bf16[2,256,768]{2,1,0:T(8,128)(2,1)S(1)}) custom-call(bf16[2,1024,512]{2,1,0:T(8,128)(2,1)} %cw.1, bf16[2,256,768]{2,1,0:T(8,128)(2,1)} %rw.1), custom_call_target="tpu_custom_call" | custom-call | flops 4000000000 | tf_op jit(solution)/shard_map/load_weights/pallas_call | solution.py:177
  8.1 2.3 %collective-permute-done.2.refs_1_ = bf16[32,512]{1,0:T(8,128)(2,1)S(1)} collective-permute-done((bf16[32,512]{1,0:T(8,128)(2,1)S(1)}, bf16[32,512]{1,0:T(8,128)(2,1)S(1)}, u32[]{:S(2)}, u32[]{:S(2)}) %collective-permute-start.2) | collective-permute-done | bytes 32800 | tf_op jit(solution)/shard_map/ppermute | solution.py:427
  10.4 0.3 collective-permute-done.1.refs_0_
  10.8 0.6 %own.1 = (bf16[256,512]{1,0:T(8,128)(2,1)S(1)}, bf16[256,512]{1,0:T(8,128)(2,1)S(1)}, bf16[256,256]{1,0:T(8,128)(2,1)S(1)}, f32[256,512]{1,0:T(8,128)S(1)}, f32[...) custom-call(bf16[128,1280]{1,0:T(8,128)(2,1)S(1)} %get-tuple-element.40.refs_0_, ...), custom_call_target="tpu_custom_call" | custom-call | flops 2000000000 | tf_op jit(solution)/shard_map/own/pallas_call | solution.py:131
  11.4 0.8 %collective-permute-done.3.refs_6_ = bf16[160,512]{1,0:T(8,128)(2,1)S(1)} collective-permute-done((bf16[160,512]{1,0:T(8,128)(2,1)S(1)}, bf16[160,512]{1,0:T(8,128)(2,1)S(1)}, u32[]{:S(2)}, u32[]{:S(2)}) %collective-permute-start.3) | collective-permute-done | bytes 163872 | tf_op jit(solution)/shard_map/ppermute | solution.py:414
  12.2 1.7 %forward_and_outer.1 = (bf16[96,512]{1,0:T(8,128)(2,1)S(1)}, bf16[96,512]{1,0:T(8,128)(2,1)S(1)}, bf16[96,512]{1,0:T(8,128)(2,1)S(1)}, bf16[96,512]{1,0:T(8,128)...) custom-call(bf16[256,512]{1,0:T(8,128)(2,1)S(1)} %get-tuple-element., ...), custom_call_target="tpu_custom_call" | custom-call | tf_op jit(solution)/shard_map/forward_and_outer/pallas_call | solution.py:131
  13.9 2.3 %collective-permute-start.4 = (bf16[96,512]{1,0:T(8,128)(2,1)S(1)}, bf16[96,512]{1,0:T(8,128)(2,1)S(1)}, u32[]{:S(2)}, u32[]{:S(2)}) collective-permute-start(bf16[96,512]{1,0:T(8,128)(2,1)S(1)} %get-tuple-element.50), channel_id=1, source_target_pairs={{0,18},{1,19},{2,16},{3,17},{4,22},{5,23},{6,20},{7,21},{8,26},{9,... | collective-permute-start | bytes 294920 | tf_op jit(solution)/shard_map/ppermute | solution.py:423
  16.1 0.8 %collective-permute-start.5 = (bf16[96,512]{1,0:T(8,128)(2,1)S(1)}, bf16[96,512]{1,0:T(8,128)(2,1)S(1)}, u32[]{:S(2)}, u32[]{:S(2)}) collective-permute-start(bf16[96,512]{1,0:T(8,128)(2,1)S(1)} %get-tuple-element.51), channel_id=1, source_target_pairs={{0,2},{1,3},{2,0},{3,1},{4,6},{5,7},{6,4},{7,5},{8,10},{9,11},{10,... | collective-permute-start | bytes 294920 | tf_op jit(solution)/shard_map/ppermute | solution.py:414
  16.9 0.5 %collective-permute-start.6 = (bf16[96,512]{1,0:T(8,128)(2,1)S(1)}, bf16[96,512]{1,0:T(8,128)(2,1)S(1)}, u32[]{:S(2)}, u32[]{:S(2)}) collective-permute-start(bf16[96,512]{1,0:T(8,128)(2,1)S(1)} %get-tuple-element.52), channel_id=1, source_target_pairs={{0,16},{16,0},{1,17},{17,1},{2,18},{18,2},{3,19},{19,3},{4,20},{20... | collective-permute-start | bytes 294920 | tf_op jit(solution)/shard_map/ppermute | solution.py:418
  17.4 1.2 %inner.1 = (bf16[4,64,512]{2,1,0:T(8,128)(2,1)S(1)}, bf16[4,64,512]{2,1,0:T(8,128)(2,1)S(1)}, bf16[4,64,512]{2,1,0:T(8,128)(2,1)S(1)}, bf16[4,64,512]{2,1,0:T(8,...) custom-call(bf16[544,512]{1,0:T(8,128)(2,1)S(1)} %get-tuple-element.53.refs_0_, ...), custom_call_target="tpu_custom_call" | custom-call | flops 2000000000 | tf_op jit(solution)/shard_map/inner/pallas_call | solution.py:131
  18.6 1.6 %collective-permute-start.9 = (bf16[4,64,512]{2,1,0:T(8,128)(2,1)S(1)}, bf16[4,64,512]{2,1,0:T(8,128)(2,1)S(1)}, u32[]{:S(2)}, u32[]{:S(2)}) collective-permute-start(bf16[4,64,512]{2,1,0:T(8,128)(2,1)S(1)} %get-tuple-element.62), channel_id=1, source_target_pairs={{0,16},{16,0},{1,17},{17,1},{2,18},{18,2},{3,19},{19,3},{4,20},{20... | collective-permute-start | bytes 786440 | tf_op jit(solution)/shard_map/ppermute | solution.py:418
  20.2 1.3 %collective-permute-start.10 = (bf16[4,64,512]{2,1,0:T(8,128)(2,1)S(1)}, bf16[4,64,512]{2,1,0:T(8,128)(2,1)S(1)}, u32[]{:S(2)}, u32[]{:S(2)}) collective-permute-start(bf16[4,64,512]{2,1,0:T(8,128)(2,1)S(1)} %get-tuple-element.63), channel_id=1, source_target_pairs={{0,2},{1,3},{2,0},{3,1},{4,6},{5,7},{6,4},{7,5},{8,10},{9,11},{10,... | collective-permute-start | bytes 786440 | tf_op jit(solution)/shard_map/ppermute | solution.py:414
  21.5 1.2 %collective-permute-start.11 = (bf16[4,64,512]{2,1,0:T(8,128)(2,1)S(1)}, bf16[4,64,512]{2,1,0:T(8,128)(2,1)S(1)}, u32[]{:S(2)}, u32[]{:S(2)}) collective-permute-start(bf16[4,64,512]{2,1,0:T(8,128)(2,1)S(1)} %get-tuple-element.64), channel_id=1, source_target_pairs={{0,18},{1,19},{2,16},{3,17},{4,22},{5,23},{6,20},{7,21},{8,26},{9,... | collective-permute-start | bytes 786440 | tf_op jit(solution)/shard_map/ppermute | solution.py:423
  22.8 5.0 %collective-permute-done.7.refs_1_.refs_4_ = bf16[128,512]{1,0:T(8,128)(2,1)S(1)} collective-permute-done((bf16[128,512]{1,0:T(8,128)(2,1)S(1)}, bf16[128,512]{1,0:T(8,128)(2,1)S(1)}, u32[]{:S(2)}, u32[]{:S(2)}) %collective-permute-start.7) | collective-permute-done | bytes 131104 | tf_op jit(solution)/shard_map/ppermute | solution.py:414
  27.8 1.7 %collective-permute-start.8 = (bf16[128,512]{1,0:T(8,128)(2,1)S(1)}, bf16[128,512]{1,0:T(8,128)(2,1)S(1)}, u32[]{:S(2)}, u32[]{:S(2)}) collective-permute-start(bf16[128,512]{1,0:T(8,128)(2,1)S(1)} %res_sum_z1.1.refs_4_.refs_0_), channel_id=1, source_target_pairs={{0,12},{1,13},{2,14},{3,15},{4,8},{5,9},{6,10},{7,11},{8,4},{9,5},... | collective-permute-start | bytes 393224 | tf_op jit(solution)/shard_map/ppermute | solution.py:414
  29.5 0.5 %signal.1 = (f32[128,512]{1,0:T(8,128)S(1)}, bf16[128,512]{1,0:T(8,128)(2,1)S(1)}) custom-call(bf16[544,512]{1,0:T(8,128)(2,1)S(1)} %get-tuple-element.65.refs_0_, bf16[512,512]{1,0:T(8,128)(2,1)S(1)} %get-tuple-element.58.refs_5_.refs_1_, f32[256,512]{1,0:T(8,128)S(1)} %get-tuple-element.66.refs_2_, ...), custom_call_target="tpu_custom_call" | custom-call | flops 1000000000 | tf_op jit(solution)/shard_map/signal/pallas_call | solution.py:131
  30.1 3.1 %collective-permute-done.9.refs_1_ = bf16[4,64,512]{2,1,0:T(8,128)(2,1)S(1)} collective-permute-done((bf16[4,64,512]{2,1,0:T(8,128)(2,1)S(1)}, bf16[4,64,512]{2,1,0:T(8,128)(2,1)S(1)}, u32[]{:S(2)}, u32[]{:S(2)}) %collective-permute-start.9) | collective-permute-done | bytes 262176 | tf_op jit(solution)/shard_map/ppermute | solution.py:418
  33.4 0.8 %collective-permute-start.15 = (bf16[64,512]{1,0:T(8,128)(2,1)S(1)}, bf16[64,512]{1,0:T(8,128)(2,1)S(1)}, u32[]{:S(2)}, u32[]{:S(2)}) collective-permute-start(bf16[64,512]{1,0:T(8,128)(2,1)S(1)} %get-tuple-element.69), channel_id=1, source_target_pairs={{0,8},{1,9},{2,10},{3,11},{4,12},{5,13},{6,14},{7,15},{8,0},{9,1},... | collective-permute-start | bytes 196616 | tf_op jit(solution)/shard_map/ppermute | solution.py:414
  34.1 1.4 %collective-permute-start.16 = (bf16[64,512]{1,0:T(8,128)(2,1)S(1)}, bf16[64,512]{1,0:T(8,128)(2,1)S(1)}, u32[]{:S(2)}, u32[]{:S(2)}) collective-permute-start(bf16[64,512]{1,0:T(8,128)(2,1)S(1)} %get-tuple-element.70), channel_id=1, source_target_pairs={{0,12},{1,13},{2,14},{3,15},{4,8},{5,9},{6,10},{7,11},{8,4},{9,5},... | collective-permute-start | bytes 196616 | tf_op jit(solution)/shard_map/ppermute | solution.py:414
  35.5 1.4 %collective-permute-start.17 = (bf16[64,512]{1,0:T(8,128)(2,1)S(1)}, bf16[64,512]{1,0:T(8,128)(2,1)S(1)}, u32[]{:S(2)}, u32[]{:S(2)}) collective-permute-start(bf16[64,512]{1,0:T(8,128)(2,1)S(1)} %get-tuple-element.71), channel_id=1, source_target_pairs={{0,4},{1,5},{2,6},{3,7},{4,0},{5,1},{6,2},{7,3},{8,12},{9,13},{10,... | collective-permute-start | bytes 196616 | tf_op jit(solution)/shard_map/ppermute | solution.py:414
  37.0 2.2 %collective-permute-start.14 = (bf16[96,512]{1,0:T(8,128)(2,1)S(1)}, bf16[96,512]{1,0:T(8,128)(2,1)S(1)}, u32[]{:S(2)}, u32[]{:S(2)}) collective-permute-start(bf16[96,512]{1,0:T(8,128)(2,1)S(1)} %res_sum_z2.1.refs_4_.refs_0_), channel_id=1, source_target_pairs={{0,18},{1,19},{2,16},{3,17},{4,22},{5,23},{6,20},{7,21},{8,26},{9,... | collective-permute-start | bytes 294920 | tf_op jit(solution)/shard_map/ppermute | solution.py:423
  39.1 0.8 %collective-permute-start.13 = (bf16[96,512]{1,0:T(8,128)(2,1)S(1)}, bf16[96,512]{1,0:T(8,128)(2,1)S(1)}, u32[]{:S(2)}, u32[]{:S(2)}) collective-permute-start(bf16[96,512]{1,0:T(8,128)(2,1)S(1)} %res_sum_z2.1.refs_4_.refs_0_), channel_id=1, source_target_pairs={{0,2},{1,3},{2,0},{3,1},{4,6},{5,7},{6,4},{7,5},{8,10},{9,11},{10,... | collective-permute-start | bytes 294920 | tf_op jit(solution)/shard_map/ppermute | solution.py:414
  39.9 0.6 %collective-permute-start.12 = (bf16[96,512]{1,0:T(8,128)(2,1)S(1)}, bf16[96,512]{1,0:T(8,128)(2,1)S(1)}, u32[]{:S(2)}, u32[]{:S(2)}) collective-permute-start(bf16[96,512]{1,0:T(8,128)(2,1)S(1)} %res_sum_z2.1.refs_4_.refs_0_), channel_id=1, source_target_pairs={{0,16},{16,0},{1,17},{17,1},{2,18},{18,2},{3,19},{19,3},{4,20},{20... | collective-permute-start | bytes 294920 | tf_op jit(solution)/shard_map/ppermute | solution.py:418
  40.6 1.5 %collective-permute-start.20 = (bf16[64,512]{1,0:T(8,128)(2,1)S(1)}, bf16[64,512]{1,0:T(8,128)(2,1)S(1)}, u32[]{:S(2)}, u32[]{:S(2)}) collective-permute-start(bf16[64,512]{1,0:T(8,128)(2,1)S(1)} %conv_scaled.1.refs_4_.refs_0_), channel_id=1, source_target_pairs={{0,16},{16,0},{1,17},{17,1},{2,18},{18,2},{3,19},{19,3},{4,20},{20... | collective-permute-start | bytes 196616 | tf_op jit(solution)/shard_map/ppermute | solution.py:418
  42.0 2.7 %collective-permute-start.19 = (bf16[128,512]{1,0:T(8,128)(2,1)S(1)}, bf16[128,512]{1,0:T(8,128)(2,1)S(1)}, u32[]{:S(2)}, u32[]{:S(2)}) collective-permute-start(bf16[128,512]{1,0:T(8,128)(2,1)S(1)} %hold.1), channel_id=1, source_target_pairs={{0,14},{1,15},{2,0},{3,1},{4,2},{5,3},{6,4},{7,5},{8,6},{9,7},{10,... | collective-permute-start | bytes 393224 | tf_op jit(solution)/shard_map/ppermute | solution.py:427
  44.9 0.4 collective-permute-done.20.refs_1_
  45.3 0.7 %finish_conv.1 = (bf16[2,64,512]{2,1,0:T(8,128)(2,1)}, f32[8,128]{1,0:T(8,128)S(1)}) custom-call(bf16[64,512]{1,0:T(8,128)(2,1)S(1)} %conv_scaled.1.refs_4_.refs_0_, bf16[64,512]{1,0:T(8,128)(2,1)S(1)} %collective-permute-done.20.refs_1_), custom_call_target="tpu_custom_call" | custom-call | flops 10000000000 | tf_op jit(solution)/shard_map/finish_conv/pallas_call | solution.py:131
  45.9 1.3 %collective-permute-done.19.refs_3_ = bf16[128,512]{1,0:T(8,128)(2,1)S(1)} collective-permute-done((bf16[128,512]{1,0:T(8,128)(2,1)S(1)}, bf16[128,512]{1,0:T(8,128)(2,1)S(1)}, u32[]{:S(2)}, u32[]{:S(2)}) %collective-permute-start.19) | collective-permute-done | bytes 131104 | tf_op jit(solution)/shard_map/ppermute | solution.py:427
  47.2 1.0 %finish.1 = (bf16[2,256,768]{2,1,0:T(8,128)(2,1)}, bf16[128,512]{1,0:T(8,128)(2,1)}) custom-call(bf16[4,96,512]{2,1,0:T(8,128)(2,1)S(1)} %res_in_order.1.refs_0_, bf16[4,96,512]{2,1,0:T(8,128)(2,1)S(1)} %collective-permute-done.18.refs_1_, f32[128,512]{1,0:T(8,128)S(1)} %get-tuple-element.72.refs_2_, bf16[128,512]{1,0:T(8,128)(2,1)S(1)} %collective-permute-done.19.refs_3_, ...), custom_call_target="tpu_custom_call" | custom-call | tf_op jit(solution)/shard_map/finish/pallas_call | solution.py:131
  (26 shorter events, 0.7 us)
Async XLA Ops:
  0.6 10.1 %collective-permute-start.1 = (bf16[128,512]{1,0:T(8,128)(2,1)}, bf16[128,512]{1,0:T(8,128)(2,1)S(1)}, u32[]{:S(2)}, u32[]{:S(2)}) collective-permute-start(bf16[128,512]{1,0:T(8,128)(2,1)} %bitcast.5), channel_id=1, source_target_pairs={{0,2},{1,3},{2,4},{3,5},{4,6},{5,7},{6,8},{7,9},{8,10},{9,11},{10,... | collective-permute-start | bytes 393224 | tf_op jit(solution)/shard_map/ppermute | solution.py:427
  4.7 5.8 %collective-permute-start.2 = (bf16[32,512]{1,0:T(8,128)(2,1)S(1)}, bf16[32,512]{1,0:T(8,128)(2,1)S(1)}, u32[]{:S(2)}, u32[]{:S(2)}) collective-permute-start(bf16[32,512]{1,0:T(8,128)(2,1)S(1)} %get-tuple-element.48), channel_id=1, source_target_pairs={{0,4},{1,5},{2,6},{3,7},{4,8},{5,9},{6,10},{7,11},{8,12},{9,13},{1... | collective-permute-start | bytes 98312 | tf_op jit(solution)/shard_map/ppermute | solution.py:427
  6.3 4.5 %collective-permute-start = (bf16[128,1280]{1,0:T(8,128)(2,1)S(1)}, bf16[128,1280]{1,0:T(8,128)(2,1)S(1)}, u32[]{:S(2)}, u32[]{:S(2)}) collective-permute-start(bf16[128,1280]{1,0:T(8,128)(2,1)S(1)} %get-tuple-element.40.refs_0_), channel_id=1, source_target_pairs={{0,1},{1,0},{2,3},{3,2},{4,5},{5,4},{6,7},{7,6},{8,9},{9,8},{10,11... | collective-permute-start | bytes 983048 | tf_op jit(solution)/shard_map/ppermute | solution.py:414
  10.7 1.5 %collective-permute-start.3 = (bf16[160,512]{1,0:T(8,128)(2,1)S(1)}, bf16[160,512]{1,0:T(8,128)(2,1)S(1)}, u32[]{:S(2)}, u32[]{:S(2)}) collective-permute-start(bf16[160,512]{1,0:T(8,128)(2,1)S(1)} %pack_halo.1.refs_5_), channel_id=1, source_target_pairs={{0,1},{1,0},{2,3},{3,2},{4,5},{5,4},{6,7},{7,6},{8,9},{9,8},{10,11... | collective-permute-start | bytes 491528 | tf_op jit(solution)/shard_map/ppermute | solution.py:414
  13.9 7.6 %collective-permute-start.4 = (bf16[96,512]{1,0:T(8,128)(2,1)S(1)}, bf16[96,512]{1,0:T(8,128)(2,1)S(1)}, u32[]{:S(2)}, u32[]{:S(2)}) collective-permute-start(bf16[96,512]{1,0:T(8,128)(2,1)S(1)} %get-tuple-element.50), channel_id=1, source_target_pairs={{0,18},{1,19},{2,16},{3,17},{4,22},{5,23},{6,20},{7,21},{8,26},{9,... | collective-permute-start | bytes 294920 | tf_op jit(solution)/shard_map/ppermute | solution.py:423
  16.1 6.5 %collective-permute-start.5 = (bf16[96,512]{1,0:T(8,128)(2,1)S(1)}, bf16[96,512]{1,0:T(8,128)(2,1)S(1)}, u32[]{:S(2)}, u32[]{:S(2)}) collective-permute-start(bf16[96,512]{1,0:T(8,128)(2,1)S(1)} %get-tuple-element.51), channel_id=1, source_target_pairs={{0,2},{1,3},{2,0},{3,1},{4,6},{5,7},{6,4},{7,5},{8,10},{9,11},{10,... | collective-permute-start | bytes 294920 | tf_op jit(solution)/shard_map/ppermute | solution.py:414
  16.9 5.8 %collective-permute-start.6 = (bf16[96,512]{1,0:T(8,128)(2,1)S(1)}, bf16[96,512]{1,0:T(8,128)(2,1)S(1)}, u32[]{:S(2)}, u32[]{:S(2)}) collective-permute-start(bf16[96,512]{1,0:T(8,128)(2,1)S(1)} %get-tuple-element.52), channel_id=1, source_target_pairs={{0,16},{16,0},{1,17},{17,1},{2,18},{18,2},{3,19},{19,3},{4,20},{20... | collective-permute-start | bytes 294920 | tf_op jit(solution)/shard_map/ppermute | solution.py:418
  18.6 14.5 %collective-permute-start.9 = (bf16[4,64,512]{2,1,0:T(8,128)(2,1)S(1)}, bf16[4,64,512]{2,1,0:T(8,128)(2,1)S(1)}, u32[]{:S(2)}, u32[]{:S(2)}) collective-permute-start(bf16[4,64,512]{2,1,0:T(8,128)(2,1)S(1)} %get-tuple-element.62), channel_id=1, source_target_pairs={{0,16},{16,0},{1,17},{17,1},{2,18},{18,2},{3,19},{19,3},{4,20},{20... | collective-permute-start | bytes 786440 | tf_op jit(solution)/shard_map/ppermute | solution.py:418
  20.2 12.9 %collective-permute-start.10 = (bf16[4,64,512]{2,1,0:T(8,128)(2,1)S(1)}, bf16[4,64,512]{2,1,0:T(8,128)(2,1)S(1)}, u32[]{:S(2)}, u32[]{:S(2)}) collective-permute-start(bf16[4,64,512]{2,1,0:T(8,128)(2,1)S(1)} %get-tuple-element.63), channel_id=1, source_target_pairs={{0,2},{1,3},{2,0},{3,1},{4,6},{5,7},{6,4},{7,5},{8,10},{9,11},{10,... | collective-permute-start | bytes 786440 | tf_op jit(solution)/shard_map/ppermute | solution.py:414
  21.5 11.7 %collective-permute-start.11 = (bf16[4,64,512]{2,1,0:T(8,128)(2,1)S(1)}, bf16[4,64,512]{2,1,0:T(8,128)(2,1)S(1)}, u32[]{:S(2)}, u32[]{:S(2)}) collective-permute-start(bf16[4,64,512]{2,1,0:T(8,128)(2,1)S(1)} %get-tuple-element.64), channel_id=1, source_target_pairs={{0,18},{1,19},{2,16},{3,17},{4,22},{5,23},{6,20},{7,21},{8,26},{9,... | collective-permute-start | bytes 786440 | tf_op jit(solution)/shard_map/ppermute | solution.py:423
  22.7 5.0 %collective-permute-start.7 = (bf16[128,512]{1,0:T(8,128)(2,1)S(1)}, bf16[128,512]{1,0:T(8,128)(2,1)S(1)}, u32[]{:S(2)}, u32[]{:S(2)}) collective-permute-start(bf16[128,512]{1,0:T(8,128)(2,1)S(1)} %res_sum_xy.1.refs_0_.refs_4_), channel_id=1, source_target_pairs={{0,4},{1,5},{2,6},{3,7},{4,0},{5,1},{6,2},{7,3},{8,12},{9,13},{10,... | collective-permute-start | bytes 393224 | tf_op jit(solution)/shard_map/ppermute | solution.py:414
  27.8 9.1 %collective-permute-start.8 = (bf16[128,512]{1,0:T(8,128)(2,1)S(1)}, bf16[128,512]{1,0:T(8,128)(2,1)S(1)}, u32[]{:S(2)}, u32[]{:S(2)}) collective-permute-start(bf16[128,512]{1,0:T(8,128)(2,1)S(1)} %res_sum_z1.1.refs_4_.refs_0_), channel_id=1, source_target_pairs={{0,12},{1,13},{2,14},{3,15},{4,8},{5,9},{6,10},{7,11},{8,4},{9,5},... | collective-permute-start | bytes 393224 | tf_op jit(solution)/shard_map/ppermute | solution.py:414
  33.4 6.5 %collective-permute-start.15 = (bf16[64,512]{1,0:T(8,128)(2,1)S(1)}, bf16[64,512]{1,0:T(8,128)(2,1)S(1)}, u32[]{:S(2)}, u32[]{:S(2)}) collective-permute-start(bf16[64,512]{1,0:T(8,128)(2,1)S(1)} %get-tuple-element.69), channel_id=1, source_target_pairs={{0,8},{1,9},{2,10},{3,11},{4,12},{5,13},{6,14},{7,15},{8,0},{9,1},... | collective-permute-start | bytes 196616 | tf_op jit(solution)/shard_map/ppermute | solution.py:414
  34.1 6.4 %collective-permute-start.16 = (bf16[64,512]{1,0:T(8,128)(2,1)S(1)}, bf16[64,512]{1,0:T(8,128)(2,1)S(1)}, u32[]{:S(2)}, u32[]{:S(2)}) collective-permute-start(bf16[64,512]{1,0:T(8,128)(2,1)S(1)} %get-tuple-element.70), channel_id=1, source_target_pairs={{0,12},{1,13},{2,14},{3,15},{4,8},{5,9},{6,10},{7,11},{8,4},{9,5},... | collective-permute-start | bytes 196616 | tf_op jit(solution)/shard_map/ppermute | solution.py:414
  35.5 5.0 %collective-permute-start.17 = (bf16[64,512]{1,0:T(8,128)(2,1)S(1)}, bf16[64,512]{1,0:T(8,128)(2,1)S(1)}, u32[]{:S(2)}, u32[]{:S(2)}) collective-permute-start(bf16[64,512]{1,0:T(8,128)(2,1)S(1)} %get-tuple-element.71), channel_id=1, source_target_pairs={{0,4},{1,5},{2,6},{3,7},{4,0},{5,1},{6,2},{7,3},{8,12},{9,13},{10,... | collective-permute-start | bytes 196616 | tf_op jit(solution)/shard_map/ppermute | solution.py:414
  37.0 7.8 %collective-permute-start.14 = (bf16[96,512]{1,0:T(8,128)(2,1)S(1)}, bf16[96,512]{1,0:T(8,128)(2,1)S(1)}, u32[]{:S(2)}, u32[]{:S(2)}) collective-permute-start(bf16[96,512]{1,0:T(8,128)(2,1)S(1)} %res_sum_z2.1.refs_4_.refs_0_), channel_id=1, source_target_pairs={{0,18},{1,19},{2,16},{3,17},{4,22},{5,23},{6,20},{7,21},{8,26},{9,... | collective-permute-start | bytes 294920 | tf_op jit(solution)/shard_map/ppermute | solution.py:423
  39.1 5.6 %collective-permute-start.13 = (bf16[96,512]{1,0:T(8,128)(2,1)S(1)}, bf16[96,512]{1,0:T(8,128)(2,1)S(1)}, u32[]{:S(2)}, u32[]{:S(2)}) collective-permute-start(bf16[96,512]{1,0:T(8,128)(2,1)S(1)} %res_sum_z2.1.refs_4_.refs_0_), channel_id=1, source_target_pairs={{0,2},{1,3},{2,0},{3,1},{4,6},{5,7},{6,4},{7,5},{8,10},{9,11},{10,... | collective-permute-start | bytes 294920 | tf_op jit(solution)/shard_map/ppermute | solution.py:414
  39.9 4.8 %collective-permute-start.12 = (bf16[96,512]{1,0:T(8,128)(2,1)S(1)}, bf16[96,512]{1,0:T(8,128)(2,1)S(1)}, u32[]{:S(2)}, u32[]{:S(2)}) collective-permute-start(bf16[96,512]{1,0:T(8,128)(2,1)S(1)} %res_sum_z2.1.refs_4_.refs_0_), channel_id=1, source_target_pairs={{0,16},{16,0},{1,17},{17,1},{2,18},{18,2},{3,19},{19,3},{4,20},{20... | collective-permute-start | bytes 294920 | tf_op jit(solution)/shard_map/ppermute | solution.py:418
  40.6 4.7 %collective-permute-start.20 = (bf16[64,512]{1,0:T(8,128)(2,1)S(1)}, bf16[64,512]{1,0:T(8,128)(2,1)S(1)}, u32[]{:S(2)}, u32[]{:S(2)}) collective-permute-start(bf16[64,512]{1,0:T(8,128)(2,1)S(1)} %conv_scaled.1.refs_4_.refs_0_), channel_id=1, source_target_pairs={{0,16},{16,0},{1,17},{17,1},{2,18},{18,2},{3,19},{19,3},{4,20},{20... | collective-permute-start | bytes 196616 | tf_op jit(solution)/shard_map/ppermute | solution.py:418
  42.0 5.2 %collective-permute-start.19 = (bf16[128,512]{1,0:T(8,128)(2,1)S(1)}, bf16[128,512]{1,0:T(8,128)(2,1)S(1)}, u32[]{:S(2)}, u32[]{:S(2)}) collective-permute-start(bf16[128,512]{1,0:T(8,128)(2,1)S(1)} %hold.1), channel_id=1, source_target_pairs={{0,14},{1,15},{2,0},{3,1},{4,2},{5,3},{6,4},{7,5},{8,6},{9,7},{10,... | collective-permute-start | bytes 393224 | tf_op jit(solution)/shard_map/ppermute | solution.py:427
  44.8 2.5 %collective-permute-start.18 = (bf16[4,96,512]{2,1,0:T(8,128)(2,1)S(1)}, bf16[4,96,512]{2,1,0:T(8,128)(2,1)S(1)}, u32[]{:S(2)}, u32[]{:S(2)}) collective-permute-start(bf16[4,96,512]{2,1,0:T(8,128)(2,1)S(1)} %res_in_order.1.refs_0_), channel_id=1, source_target_pairs={{0,1},{1,0},{2,3},{3,2},{4,5},{5,4},{6,7},{7,6},{8,9},{9,8},{10,11... | collective-permute-start | bytes 1179656 | tf_op jit(solution)/shard_map/ppermute | solution.py:414
